TPU v7x, 32 devices: a whole 2x2x4 slice. The times are simulated.
32 devices in a mesh: replica: 8 (over z, y), tensor: 4 (over x, core).
Axes of the slice: x: 2, y: 2, z: 4, core: 2. Of those that a mesh axis runs over, the one named last changes fastest.
Arguments:
- grad_q: bfloat16 [16384, 2048], P('replica', 'tensor'), may hold values from -6 to 6
- error_q: bfloat16 [16384, 2048], P('replica', 'tensor'), may hold values from -6 to 6
- qfac_q: bfloat16 [2048, 32], P('tensor'), may hold values from -0.25 to 0.25
- ginv_q: float32 [128, 32], P('tensor'), as said below
- weight_q: float32 [2048, 2048], P('replica', 'tensor'), may hold values from -6 to 6
- momentum_q: float32 [2048, 2048], P('replica', 'tensor'), may hold values from -4 to 4
- grad_o: bfloat16 [16384, 2048], P(('replica', 'tensor')), may hold values from -6 to 6
- error_o: bfloat16 [16384, 2048], P(('replica', 'tensor')), may hold values from -6 to 6
- qfac_o: bfloat16 [8192, 32], P('tensor'), may hold values from -0.125 to 0.125
- ginv_o: float32 [128, 32], P('tensor'), as said below
- weight_o: float32 [2048, 2048], P('tensor', 'replica'), may hold values from -6 to 6
- momentum_o: float32 [2048, 2048], P('tensor', 'replica'), may hold values from -4 to 4
- norm_grads: bfloat16 [8, 4, 4096], P('replica', 'tensor'), may hold values from -24 to 24
Outputs:
- error_q_new: bfloat16 [16384, 2048], P('replica', 'tensor')
- qfac_q_new: bfloat16 [2048, 32], P('tensor')
- momentum_q_new: float32 [2048, 2048], P('replica', 'tensor')
- weight_q_new: float32 [2048, 2048], P('replica', 'tensor')
- error_o_new: bfloat16 [16384, 2048], P(('replica', 'tensor'))
- qfac_o_new: bfloat16 [8192, 32], P('tensor')
- momentum_o_new: float32 [2048, 2048], P('tensor', 'replica')
- weight_o_new: float32 [2048, 2048], P('tensor', 'replica')
- norm_mean: float32 [4096], replicated
Inputs may be any that keep to these rules, and one draw needn't show every extreme that they name: `ginv_q`: each block of 32 rows is an upper-triangular matrix with a positive diagonal. `ginv_o`: each block of 32 rows is an upper-triangular matrix with a positive diagonal.
All inputs are finite; a program needn't handle non-finite values.
Results may differ from a plain program's by a relative error of at most 0.0085.
Values may be sent and summed in bfloat16 or wider, within the bound.
No kernel may reach another device: no remote copies, remote signals or barrier semaphores. Data moves between devices by JAX's collectives and lax.ppermute only.
A program may use at most 64 MiB of HBM per device.

v0:
```python
import jax
import jax.numpy as jnp
from jax import lax
from jax.sharding import PartitionSpec as P

momentum_decay = 0.9
step_size = 0.5


def left_factor(matrix, factor):
    return jnp.dot(matrix, factor, preferred_element_type=jnp.float32)


def right_factor(matrix, p_hat):
    return lax.dot_general(
        matrix, p_hat, (((0,), (0,)), ((), ())), preferred_element_type=jnp.float32
    )


def orthonormal(p_part, gram):
    return jnp.dot(p_part, gram, precision=lax.Precision.HIGHEST).astype(jnp.bfloat16)


def on_device(
    grad_q,
    error_q,
    qfac_q,
    ginv_q,
    weight_q,
    momentum_q,
    grad_o,
    error_o,
    qfac_o,
    ginv_o,
    weight_o,
    momentum_o,
    norm_grads,
):
    replicas = lax.axis_size("replica")
    tensors = lax.axis_size("tensor")
    mat_q = (grad_q.astype(jnp.float32) + error_q.astype(jnp.float32)).astype(jnp.bfloat16)
    mat_o = (grad_o.astype(jnp.float32) + error_o.astype(jnp.float32)).astype(jnp.bfloat16)
    p_q = left_factor(mat_q, qfac_q)
    p_o = left_factor(mat_o, qfac_o)
    norm_part = norm_grads.reshape(-1).astype(jnp.float32)
    norm_total = lax.psum(norm_part, ("replica", "tensor"))
    sum_q, sum_o = lax.psum((p_q, p_o), "replica")
    phat_q = orthonormal(sum_q, ginv_q)
    phat_o = orthonormal(sum_o, ginv_o)
    qpart_q = right_factor(mat_q, phat_q)
    qpart_o = right_factor(mat_o, phat_o)
    qsum_q, qsum_o = lax.psum((qpart_q, qpart_o), "replica")
    qnew_q = (qsum_q / replicas).astype(jnp.bfloat16)
    qnew_o = (qsum_o / replicas).astype(jnp.bfloat16)
    approx_q = lax.dot_general(
        phat_q, qnew_q, (((1,), (1,)), ((), ())), preferred_element_type=jnp.float32
    )
    approx_o = lax.dot_general(
        phat_o, qnew_o, (((1,), (1,)), ((), ())), preferred_element_type=jnp.float32
    )
    error_q_new = (mat_q.astype(jnp.float32) - approx_q).astype(jnp.bfloat16)
    error_o_new = (mat_o.astype(jnp.float32) - approx_o).astype(jnp.bfloat16)
    replica_index = lax.axis_index("replica")
    piece_rows = weight_q.shape[0]
    piece_q = lax.dynamic_slice_in_dim(approx_q, replica_index * piece_rows, piece_rows, 0)
    piece_cols = weight_o.shape[1]
    piece_o = lax.dynamic_slice_in_dim(approx_o, replica_index * piece_cols, piece_cols, 1)
    momentum_q_new = momentum_decay * momentum_q + piece_q
    weight_q_new = weight_q - step_size * momentum_q_new
    momentum_o_new = momentum_decay * momentum_o + piece_o
    weight_o_new = weight_o - step_size * momentum_o_new
    norm_mean = norm_total / (replicas * tensors)
    return (
        error_q_new,
        qnew_q,
        momentum_q_new,
        weight_q_new,
        error_o_new,
        qnew_o,
        momentum_o_new,
        weight_o_new,
        norm_mean,
    )


def solution(mesh):
    in_specs = (
        P("replica", "tensor"),
        P("replica", "tensor"),
        P("tensor", None),
        P("tensor", None),
        P("replica", "tensor"),
        P("replica", "tensor"),
        P(("replica", "tensor"), None),
        P(("replica", "tensor"), None),
        P("tensor", None),
        P("tensor", None),
        P("tensor", "replica"),
        P("tensor", "replica"),
        P("replica", "tensor", None),
    )
    out_specs = (
        P("replica", "tensor"),
        P("tensor", None),
        P("replica", "tensor"),
        P("replica", "tensor"),
        P(("replica", "tensor"), None),
        P("tensor", None),
        P("tensor", "replica"),
        P("tensor", "replica"),
        P(),
    )
    return jax.shard_map(
        on_device, mesh=mesh, in_specs=in_specs, out_specs=out_specs, check_vma=False
    )
```

profile of v0, /device:TPU:0, one launch (start us, length us, event | category | flops | bytes accessed | tf_op | source)
XLA Modules:
  0.0 193.6 jit_solution(17981295365880007924)
XLA Ops:
  7.2 0.0 copy-start
  7.2 0.0 all-reduce.7.cloned.1.call-start
  7.3 4.0 %fusion.1 = f32[2048,32]{1,0:T(8,128)} fusion(bf16[512,32]{0,1:T(8,128)(2,1)} %param.15, bf16[2048,512]{1,0:T(8,128)(2,1)} %param.14, bf16[2048,512]{1,0:T(8,128)(2,1)} %param.13), kind=kOutput, calls=%fused_computation.14 | convolution fusion | flops 71303168 | bytes 4489216 | tf_op jit(solution)/shard_map/dot_general | solution.py:11
  11.3 0.0 copy-start.16
  11.3 1.4 fusion.3
  12.7 0.0 all-reduce.7.cloned.1.call-update
  12.8 0.0 all-reduce.5.cloned.1.call-start
  12.8 86.6 %all-reduce.7.cloned.1.call-done = (f32[2048,32]{1,0:T(8,128)}, f32[512,32]{1,0:T(8,128)}) async-done(((f32[2048,32]{1,0:T(8,128)}, f32[512,32]{1,0:T(8,128)}), (f32[2048,32]{1,0:T(8,128)}, f32[512,32]{1,0:T(8,128)})) %all-reduce.7.cloned.1.call-update) | async-done | bytes 327696 | tf_op jit(solution)/shard_map/psum | solution.py:47
  99.4 2.5 %convolution_convert_fusion = bf16[2048,32]{0,1:T(8,128)(2,1)S(1)} fusion(f32[2048,32]{1,0:T(8,128)} %get-tuple-element.11, f32[32,32]{1,0:T(8,128)S(1)} %copy-done.16), kind=kOutput, calls=%fused_computation.4 | convolution fusion | flops 25231360 | bytes 397312 | tf_op jit(solution)/shard_map/dot_general | solution.py:21
  101.9 3.0 %fusion = f32[512,32]{0,1:T(8,128)} fusion(bf16[2048,32]{0,1:T(8,128)(2,1)S(1)} %convolution_convert_fusion, bf16[2048,512]{1,0:T(8,128)(2,1)S(1)} %copy-done.1, bf16[2048,512]{1,0:T(8,128)(2,1)} %param.13), kind=kOutput, calls=%fused_computation.13 | convolution fusion | flops 71303168 | bytes 4390912 | tf_op jit(solution)/shard_map/dot_general | solution.py:15
  105.0 0.4 convolution_convert_fusion.1
  105.3 0.0 copy-done.3
  105.4 1.4 fusion.2
  106.8 0.0 all-reduce.5.cloned.1.call-update
  106.8 40.0 %psum.39 = f32[4096]{0:T(1024)S(1)} all-reduce(f32[4096]{0:T(1024)S(1)} %bitcast.13), channel_id=1, replica_groups=mesh['replica'=8,'tensor'=4] {'replica','tensor'}, use_global_device_ids=true, to_apply=%region_4.0 | all-reduce | flops 4096 | bytes 32768 | tf_op jit(solution)/shard_map/psum | solution.py:46
  146.8 0.6 broadcast_multiply_fusion
  147.4 29.8 %all-reduce.5.cloned.1.call-done = (f32[512,32]{0,1:T(8,128)}, f32[2048,32]{0,1:T(8,128)}) async-done(((f32[512,32]{0,1:T(8,128)}, f32[2048,32]{0,1:T(8,128)}), (f32[512,32]{0,1:T(8,128)}, f32[2048,32]{0,1:T(8,128)})) %all-reduce.5.cloned.1.call-update) | async-done | bytes 327696 | tf_op jit(solution)/shard_map/psum | solution.py:52
  177.3 0.8 multiply_convert_fusion.1
  178.1 3.8 %subtract_convert_fusion.1 = (bf16[2048,512]{1,0:T(8,128)(2,1)}, f32[2048,512]{1,0:T(8,128)S(1)}) fusion(bf16[2048,512]{1,0:T(8,128)(2,1)S(1)} %copy-done.1, bf16[2048,512]{1,0:T(8,128)(2,1)} %param.13, bf16[2048,32]{0,1:T(8,128)(2,1)S(1)} %convolution_convert_fusion, bf16[512,32]{0,1:T(8,128)(2,1)S(1)} %multiply_convert_fusion.1), kind=kOutput, calls=%fused_computation.2 | convolution fusion | flops 74448896 | bytes 10649600 | tf_op jit(solution)/shard_map/dot_general | solution.py:55
  182.0 0.0 copy-start.12
  182.1 2.1 %subtract_convert_fusion = (bf16[512,2048]{1,0:T(8,128)(2,1)}, f32[512,2048]{1,0:T(8,128)S(1)}) fusion(bf16[512,2048]{1,0:T(8,128)(2,1)S(1)} %copy-done.4, bf16[512,2048]{1,0:T(8,128)(2,1)S(1)} %copy-done.7, bf16[512,32]{0,1:T(8,128)(2,1)S(1)} %convolution_convert_fusion.1, bf16[2048,32]{0,1:T(8,128)(2,1)S(1)} %multiply_convert_fusion), kind=kOutput, calls=%fused_computation | convolution fusion | flops 74448896 | bytes 10649600 | tf_op jit(solution)/shard_map/dot_general | solution.py:58
  184.2 1.1 multiply_subtract_fusion.1
  185.3 0.3 copy-done.11
  185.6 1.1 multiply_subtract_fusion
  (35 shorter events, 0.1 us)
Async XLA Ops:
  7.2 4.1 %copy-start = (bf16[2048,32]{0,1:T(8,128)(2,1)S(1)}, bf16[2048,32]{0,1:T(8,128)(2,1)}, u32[]{:S(2)}) copy-start(bf16[2048,32]{0,1:T(8,128)(2,1)} %param.21) | copy-start | bytes 393220
  7.2 4.1 %copy-start.2 = (bf16[512,2048]{1,0:T(8,128)(2,1)S(1)}, bf16[512,2048]{1,0:T(8,128)(2,1)}, u32[]{:S(2)}) copy-start(bf16[512,2048]{1,0:T(8,128)(2,1)} %param.20) | copy-start | bytes 6291460
  7.2 92.2 %all-reduce.7.cloned.1.call-start = ((), (), s32[]{:S(2)}) async-start(), calls=%async_computation.1 | async-start | bytes 2621440 | tf_op jit(solution)/shard_map/psum | solution.py:47
  7.2 4.1 %copy-start.5 = (bf16[512,2048]{1,0:T(8,128)(2,1)S(1)}, bf16[512,2048]{1,0:T(8,128)(2,1)}, u32[]{:S(2)}) copy-start(bf16[512,2048]{1,0:T(8,128)(2,1)} %param.19) | copy-start | bytes 6291460
  11.3 88.1 %copy-start.16 = (f32[32,32]{1,0:T(8,128)S(1)}, f32[32,32]{1,0:T(8,128)}, u32[]{:S(2)}) copy-start(f32[32,32]{1,0:T(8,128)} %param.16) | copy-start | bytes 12292
  12.7 89.2 %copy-start.1 = (bf16[2048,512]{1,0:T(8,128)(2,1)S(1)}, bf16[2048,512]{1,0:T(8,128)(2,1)}, u32[]{:S(2)}) copy-start(bf16[2048,512]{1,0:T(8,128)(2,1)} %param.14) | copy-start | bytes 6291460
  12.8 164.5 %all-reduce.5.cloned.1.call-start = ((), (), s32[]{:S(2)}) async-start(), calls=%async_computation | async-start | bytes 655360 | tf_op jit(solution)/shard_map/psum | solution.py:52
  99.4 5.6 %copy-start.14 = (f32[512,32]{1,0:T(8,128)S(1)}, f32[512,32]{1,0:T(8,128)}, u32[]{:S(2)}) copy-start(f32[512,32]{1,0:T(8,128)} %get-tuple-element.12) | copy-start | bytes 196612
  101.9 3.1 %copy-start.17 = (f32[32,32]{1,0:T(8,128)S(1)}, f32[32,32]{1,0:T(8,128)}, u32[]{:S(2)}) copy-start(f32[32,32]{1,0:T(8,128)} %param.22) | copy-start | bytes 12292
  101.9 3.4 %copy-start.3 = (bf16[512,2048]{1,0:T(8,128)(2,1)S(1)}, bf16[512,2048]{1,0:T(8,128)(2,1)}, u32[]{:S(2)}) copy-start(bf16[512,2048]{1,0:T(8,128)(2,1)} %param.20) | copy-start | bytes 6291460
  101.9 3.4 %copy-start.6 = (bf16[512,2048]{1,0:T(8,128)(2,1)S(1)}, bf16[512,2048]{1,0:T(8,128)(2,1)}, u32[]{:S(2)}) copy-start(bf16[512,2048]{1,0:T(8,128)(2,1)} %param.19) | copy-start | bytes 6291460
  105.4 1.4 copy-start.18
  178.1 3.9 %copy-start.15 = (bf16[512,32]{0,1:T(8,128)(2,1)}, bf16[512,32]{0,1:T(8,128)(2,1)S(1)}, u32[]{:S(2)}) copy-start(bf16[512,32]{0,1:T(8,128)(2,1)S(1)} %multiply_convert_fusion.1) | copy-start | bytes 98308
  178.1 3.9 %copy-start.13 = (f32[2048,32]{0,1:T(8,128)S(1)}, f32[2048,32]{0,1:T(8,128)}, u32[]{:S(2)}) copy-start(f32[2048,32]{0,1:T(8,128)} %get-tuple-element.10) | copy-start | bytes 786436
  178.1 3.9 %copy-start.4 = (bf16[512,2048]{1,0:T(8,128)(2,1)S(1)}, bf16[512,2048]{1,0:T(8,128)(2,1)}, u32[]{:S(2)}) copy-start(bf16[512,2048]{1,0:T(8,128)(2,1)} %param.20) | copy-start | bytes 6291460
  178.1 3.9 %copy-start.7 = (bf16[512,2048]{1,0:T(8,128)(2,1)S(1)}, bf16[512,2048]{1,0:T(8,128)(2,1)}, u32[]{:S(2)}) copy-start(bf16[512,2048]{1,0:T(8,128)(2,1)} %param.19) | copy-start | bytes 6291460
  182.0 2.2 %copy-start.12 = (bf16[2048,32]{0,1:T(8,128)(2,1)}, bf16[2048,32]{0,1:T(8,128)(2,1)S(1)}, u32[]{:S(2)}) copy-start(bf16[2048,32]{0,1:T(8,128)(2,1)S(1)} %multiply_convert_fusion) | copy-start | bytes 393220
  182.0 2.2 %copy-start.8 = (f32[256,512]{1,0:T(8,128)S(1)}, f32[256,512]{1,0:T(8,128)}, u32[]{:S(2)}) copy-start(f32[256,512]{1,0:T(8,128)} %param.17) | copy-start | bytes 1572868
  182.0 2.2 %copy-start.9 = (f32[256,512]{1,0:T(8,128)S(1)}, f32[256,512]{1,0:T(8,128)}, u32[]{:S(2)}) copy-start(f32[256,512]{1,0:T(8,128)} %param.18) | copy-start | bytes 1572868
  184.2 1.2 copy-start.10
  184.2 1.5 copy-start.11
Sparse Core Ops, SparseCore 0:
  12.9 86.4 all-reduce.6
  106.9 70.2 all-reduce.4
where the time goes:
time: 194 us
  waiting for transfers between devices  116 us (60%)
  blocking collectives  40 us (21%)
  matrix products  18.7 us (10%)
  between operations  14.3 us (7%)
  other arithmetic  3.76 us (2%)
    psum x1, waiting for transfers between devices, on_device(): sum_q, sum_o = lax.psum((p_q, p_o), 'replica')  86.6 us
    psum x1, blocking collectives, on_device(): norm_total = lax.psum(norm_part, ('replica', 'tensor'))  40 us
    psum x1, waiting for transfers between devices, on_device(): qsum_q, qsum_o = lax.psum((qpart_q, qpart_o), 'replica')  29.8 us
    dot_general x2, matrix products, left_factor(): return jnp.dot(matrix, factor, preferred_element_type=jnp.float32)  5.46 us
    dot_general x2, matrix products, right_factor(): lax.dot_general(matrix, p_hat, (((0,), (0,)), ((), ())), preferred_elemen...  4.4 us
  transfers between devices with their start and end apart: 2, of which 2 were waited for; matrix products, arithmetic and copies ran while one was open for 0% of the time, Pallas kernels for 0%

commit v1 on v0

v1 whole, which is shorter than its diff:
```python
import jax
import jax.numpy as jnp
from jax import lax
from jax.sharding import PartitionSpec as P

momentum_decay = 0.9
step_size = 0.5


def contract(left, right, left_dim, right_dim):
    return lax.dot_general(
        left, right, (((left_dim,), (right_dim,)), ((), ())), preferred_element_type=jnp.float32
    )


def shifts(count, step):
    return [(source, (source + step) % count) for source in range(count)]


def exchange(pieces, axis, count):
    me = lax.axis_index(axis)
    got = [lax.dynamic_index_in_dim(pieces, me, 0, keepdims=False)]
    for step in range(1, count):
        piece = lax.dynamic_index_in_dim(pieces, (me + step) % count, 0, keepdims=False)
        got.append(lax.ppermute(piece, axis, shifts(count, step)))
    return got


def gather(piece, axis, count):
    me = lax.axis_index(axis)
    got = [piece]
    for step in range(1, count):
        got.append(lax.ppermute(piece, axis, shifts(count, step)))
    stacked = jnp.stack(got[::-1])
    return jnp.roll(stacked, me + 1, axis=0)


def cut(factor, count):
    rank, size = factor.shape
    return factor.reshape(rank, count, size // count).transpose(1, 0, 2)


def join(pieces):
    count, rank, size = pieces.shape
    return pieces.transpose(1, 0, 2).reshape(rank, count * size)


def on_device(
    grad_q,
    error_q,
    qfac_q,
    ginv_q,
    weight_q,
    momentum_q,
    grad_o,
    error_o,
    qfac_o,
    ginv_o,
    weight_o,
    momentum_o,
    norm_grads,
):
    replicas = lax.axis_size("replica")
    tensors = lax.axis_size("tensor")
    rank = qfac_q.shape[1]
    mat_q = (grad_q.astype(jnp.float32) + error_q.astype(jnp.float32)).astype(jnp.bfloat16)
    mat_o = (grad_o.astype(jnp.float32) + error_o.astype(jnp.float32)).astype(jnp.bfloat16)
    p_q = contract(qfac_q.T, mat_q, 1, 1)
    p_o = contract(qfac_o.T, mat_o, 1, 1)
    norm = norm_grads.reshape(replicas, rank, -1)
    send = jnp.concatenate(
        [cut(p_q, replicas).astype(jnp.bfloat16), cut(p_o, replicas).astype(jnp.bfloat16), norm], axis=2
    )
    got = exchange(send, "replica", replicas)
    total = sum(part.astype(jnp.float32) for part in got)
    q_size = p_q.shape[1] // replicas
    o_size = p_o.shape[1] // replicas
    sum_q = total[:, :q_size]
    sum_o = total[:, q_size:q_size + o_size]
    sum_norm = total[:, q_size + o_size:]
    hat_q = jnp.dot(ginv_q.T, sum_q, precision=lax.Precision.HIGHEST).astype(jnp.bfloat16)
    hat_o = jnp.dot(ginv_o.T, sum_o, precision=lax.Precision.HIGHEST).astype(jnp.bfloat16)
    hats = gather(jnp.concatenate([hat_q, hat_o], axis=1), "replica", replicas)
    phat_q = join(hats[:, :, :q_size])
    phat_o = join(hats[:, :, q_size:])

    norm_parts = gather(sum_norm, "tensor", tensors)
    norm_piece = jnp.sum(norm_parts, axis=0) / (replicas * tensors)
    norm_mean = gather(norm_piece, "replica", replicas).reshape(-1)

    q_q = contract(phat_q, mat_q, 1, 0)
    q_o = contract(phat_o, mat_o, 1, 0)
    send = jnp.concatenate(
        [cut(q_q, replicas).astype(jnp.bfloat16), cut(q_o, replicas).astype(jnp.bfloat16)], axis=2
    )
    got = lax.all_to_all(send, "replica", 0, 0, tiled=True)
    total = jnp.sum(got.astype(jnp.float32), axis=0)
    piece = (total / replicas).astype(jnp.bfloat16)
    news = lax.all_to_all(
        jnp.broadcast_to(piece[None], (replicas,) + piece.shape), "replica", 0, 0, tiled=True
    )
    q_size = q_q.shape[1] // replicas
    new_q = join(news[:, :, :q_size])
    new_o = join(news[:, :, q_size:])
    approx_q = contract(phat_q, new_q, 0, 0)
    approx_o = contract(phat_o, new_o, 0, 0)
    error_q_new = (mat_q.astype(jnp.float32) - approx_q).astype(jnp.bfloat16)
    error_o_new = (mat_o.astype(jnp.float32) - approx_o).astype(jnp.bfloat16)
    replica_index = lax.axis_index("replica")
    piece_rows = weight_q.shape[0]
    piece_cols = weight_o.shape[1]
    hat_q_mine = lax.dynamic_slice_in_dim(phat_q, replica_index * piece_rows, piece_rows, 1)
    new_o_mine = lax.dynamic_slice_in_dim(new_o, replica_index * piece_cols, piece_cols, 1)
    momentum_q_new = momentum_decay * momentum_q + contract(hat_q_mine, new_q, 0, 0)
    weight_q_new = weight_q - step_size * momentum_q_new
    momentum_o_new = momentum_decay * momentum_o + contract(phat_o, new_o_mine, 0, 0)
    weight_o_new = weight_o - step_size * momentum_o_new
    return (
        error_q_new,
        new_q.T,
        momentum_q_new,
        weight_q_new,
        error_o_new,
        new_o.T,
        momentum_o_new,
        weight_o_new,
        norm_mean,
    )


def solution(mesh):
    in_specs = (
        P("replica", "tensor"),
        P("replica", "tensor"),
        P("tensor", None),
        P("tensor", None),
        P("replica", "tensor"),
        P("replica", "tensor"),
        P(("replica", "tensor"), None),
        P(("replica", "tensor"), None),
        P("tensor", None),
        P("tensor", None),
        P("tensor", "replica"),
        P("tensor", "replica"),
        P("replica", "tensor", None),
    )
    out_specs = (
        P("replica", "tensor"),
        P("tensor", None),
        P("replica", "tensor"),
        P("replica", "tensor"),
        P(("replica", "tensor"), None),
        P("tensor", None),
        P("tensor", "replica"),
        P("tensor", "replica"),
        P(),
    )
    return jax.shard_map(
        on_device, mesh=mesh, in_specs=in_specs, out_specs=out_specs, check_vma=False
    )
```

time: 194 us -> 134 us (0.69)
  waiting for transfers between devices: 116 us -> 48.1 us
  starting transfers between devices: 0.08 us -> 47.8 us
  blocking collectives: 40 us -> 0 us
  between operations: 14.3 us -> 1.31 us
  local copies, waits for them, and re-layouts: 0.43 us -> 11.6 us
  other arithmetic: 3.76 us -> 6.71 us
    psum x2 -> x0, waiting for transfers between devices: 116 us -> none  [the longest x1 86.6 us: on_device(): sum_q, sum_o = lax.psum((p_q, p_o), 'replica')]
    psum x1 -> x0, blocking collectives: 40 us -> none  [on_device(): norm_total = lax.psum(norm_part, ('replica', 'tensor'))]
    ppermute x0 -> x24, starting transfers between devices: none -> 37.7 us  [the longest x17 24.9 us: gather(): got.append(lax.ppermute(piece, axis, shifts(count, step)))]
    ppermute x0 -> x24, waiting for transfers between devices: none -> 33.1 us  [the longest x17 33.1 us: gather(): got.append(lax.ppermute(piece, axis, shifts(count, step)))]
    all_to_all x0 -> x2, waiting for transfers between devices: none -> 15 us  [the longest x1 8.12 us: on_device(): got = lax.all_to_all(send, 'replica', 0, 0, tiled=True)]
    all_to_all x0 -> x2, starting transfers between devices: none -> 10.1 us  [the longest x1 6.67 us: on_device(): got = lax.all_to_all(send, 'replica', 0, 0, tiled=True)]
    dot_general x0 -> x2, local copies, waits for them, and re-layouts: none -> 7.91 us  [contract(): lax.dot_general(left, right, (((left_dim,), (right_dim,)), ((), ())), pre...]
    dot_general x0 -> x2, other arithmetic: none -> 5.61 us  [contract(): lax.dot_general(left, right, (((left_dim,), (right_dim,)), ((), ())), pre...]
  transfers between devices with their start and end apart: 2 -> 26, of which waited for: 2 -> 12; matrix products, arithmetic and copies ran while one was open for 0% -> 11% of each run, Pallas kernels for 0% -> 0%
where the time goes in v1:
time: 134 us; the launch traced here: 133 us
  waiting for transfers between devices  48.1 us (36%)
  starting transfers between devices  47.8 us (36%)
  matrix products  17.7 us (13%)
  local copies, waits for them, and re-layouts  11.6 us (9%)
  other arithmetic  6.71 us (5%)
    ppermute x17, waiting for transfers between devices, gather(): got.append(lax.ppermute(piece, axis, shifts(count, step)))  33.1 us
    ppermute x17, starting transfers between devices, gather(): got.append(lax.ppermute(piece, axis, shifts(count, step)))  24.9 us
    dot_general x8, matrix products, contract(): lax.dot_general(left, right, (((left_dim,), (right_dim,)), ((), ())), pre...  17.3 us
    ppermute x7, starting transfers between devices, exchange(): got.append(lax.ppermute(piece, axis, shifts(count, step)))  12.9 us
    all_to_all x1, waiting for transfers between devices, on_device(): got = lax.all_to_all(send, 'replica', 0, 0, tiled=True)  8.12 us
    dot_general x2, local copies, waits for them, and re-layouts, contract(): lax.dot_general(left, right, (((left_dim,), (right_dim,)), ((), ())), pre...  7.91 us
    all_to_all x1, waiting for transfers between devices, on_device(): lax.all_to_all(jnp.broadcast_to(piece[None], (replicas,) + piece.shape),...  6.84 us
    all_to_all x1, starting transfers between devices, on_device(): got = lax.all_to_all(send, 'replica', 0, 0, tiled=True)  6.67 us
  transfers between devices with their start and end apart: 26, of which 12 were waited for; matrix products, arithmetic and copies ran while one was open for 11% of the time, Pallas kernels for 0%

profile of v1, /device:TPU:0, one launch (start us, length us, event | category | flops | bytes accessed | tf_op | source)
XLA Modules:
  0.0 133.2 jit_solution(7368812364596330338)
XLA Ops:
  1.6 3.1 %fusion.2 = bf16[32,512]{1,0:T(8,128)(2,1)S(1)} fusion(bf16[2048,32]{0,1:T(8,128)(2,1)S(1)} %copy-done, bf16[512,2048]{1,0:T(8,128)(2,1)} %param.20, bf16[512,2048]{1,0:T(8,128)(2,1)} %param.19), kind=kOutput, calls=%fused_computation.12 | convolution fusion | flops 71319552 | bytes 4358144 | tf_op jit(solution)/shard_map/dot_general | solution.py:11
  7.5 3.0 %collective-permute-start = (bf16[32,336]{1,0:T(8,128)(2,1)S(1)}, bf16[32,336]{1,0:T(8,128)(2,1)S(1)}, u32[]{:S(2)}, u32[]{:S(2)}) collective-permute-start(bf16[32,336]{1,0:T(8,128)(2,1)S(1)} %get-tuple-element.11), channel_id=1, source_target_pairs={{0,4},{4,8},{8,12},{12,16},{16,20},{20,24},{24,28},{28,0},{1,5},{5... | collective-permute-start | bytes 64520 | tf_op jit(solution)/shard_map/ppermute | solution.py:25
  10.5 3.1 %collective-permute-start.6 = (bf16[32,336]{1,0:T(8,128)(2,1)S(1)}, bf16[32,336]{1,0:T(8,128)(2,1)S(1)}, u32[]{:S(2)}, u32[]{:S(2)}) collective-permute-start(bf16[32,336]{1,0:T(8,128)(2,1)S(1)} %get-tuple-element.12), channel_id=1, source_target_pairs={{0,28},{4,0},{8,4},{12,8},{16,12},{20,16},{24,20},{28,24},{1,29},{... | collective-permute-start | bytes 64520 | tf_op jit(solution)/shard_map/ppermute | solution.py:25
  15.5 3.0 %collective-permute-start.3 = (bf16[32,336]{1,0:T(8,128)(2,1)S(1)}, bf16[32,336]{1,0:T(8,128)(2,1)S(1)}, u32[]{:S(2)}, u32[]{:S(2)}) collective-permute-start(bf16[32,336]{1,0:T(8,128)(2,1)S(1)} %get-tuple-element.15), channel_id=1, source_target_pairs={{0,16},{4,20},{8,24},{12,28},{16,0},{20,4},{24,8},{28,12},{1,17},{... | collective-permute-start | bytes 64520 | tf_op jit(solution)/shard_map/ppermute | solution.py:25
  18.5 3.5 %fusion.17 = bf16[512,2048]{0,1:T(8,128)(2,1)} fusion(bf16[2048,512]{1,0:T(8,128)(2,1)S(1)} %copy-done.1, bf16[2048,512]{1,0:T(8,128)(2,1)} %param.13), kind=kLoop, calls=%fused_computation.94 | loop fusion | flops 4194304 | bytes 6291456 | tf_op jit(solution)/shard_map/dot_general | solution.py:11
  26.0 4.0 %copy.40 = bf16[512,2048]{1,0:T(8,128)(2,1)} copy(bf16[512,2048]{0,1:T(8,128)(2,1)} %fusion.17) | data formatting | bytes 4194304 | tf_op jit(solution)/shard_map/dot_general | solution.py:11
  29.9 3.9 %copy.45 = bf16[2048,512]{1,0:T(8,128)(2,1)} copy(bf16[2048,512]{0,1:T(8,128)(2,1)} %fusion.18) | data formatting | bytes 4194304 | tf_op jit(solution)/shard_map/dot_general | solution.py:11
  38.6 3.1 %collective-permute-start.17 = (f32[32,16]{1,0:T(8,128)S(1)}, f32[32,16]{1,0:T(8,128)S(1)}, u32[]{:S(2)}, u32[]{:S(2)}) collective-permute-start(f32[32,16]{1,0:T(8,128)S(1)} %broadcast_multiply_fusion), channel_id=1, source_target_pairs={{0,28},{4,0},{8,4},{12,8},{16,12},{20,16},{24,20},{28,24},{1,29},{... | collective-permute-start | bytes 6152 | tf_op jit(solution)/shard_map/ppermute | solution.py:33
  44.2 2.9 %collective-permute-start.10 = (bf16[32,320]{1,0:T(8,128)(2,1)S(1)}, bf16[32,320]{1,0:T(8,128)(2,1)S(1)}, u32[]{:S(2)}, u32[]{:S(2)}) collective-permute-start(bf16[32,320]{1,0:T(8,128)(2,1)S(1)} %pad_maximum_fusion.2), channel_id=1, source_target_pairs={{0,16},{4,20},{8,24},{12,28},{16,0},{20,4},{24,8},{28,12},{1,17},{... | collective-permute-start | bytes 61448 | tf_op jit(solution)/shard_map/ppermute | solution.py:33
  47.0 2.9 %collective-permute-start.18 = (f32[32,16]{1,0:T(8,128)S(1)}, f32[32,16]{1,0:T(8,128)S(1)}, u32[]{:S(2)}, u32[]{:S(2)}) collective-permute-start(f32[32,16]{1,0:T(8,128)S(1)} %broadcast_multiply_fusion), channel_id=1, source_target_pairs={{0,24},{4,28},{8,0},{12,4},{16,8},{20,12},{24,16},{28,20},{1,25},{... | collective-permute-start | bytes 6152 | tf_op jit(solution)/shard_map/ppermute | solution.py:33
  52.0 4.0 %collective-permute-done.19 = f32[32,16]{1,0:T(8,128)S(1)} collective-permute-done((f32[32,16]{1,0:T(8,128)S(1)}, f32[32,16]{1,0:T(8,128)S(1)}, u32[]{:S(2)}, u32[]{:S(2)}) %collective-permute-start.19) | collective-permute-done | bytes 2080 | tf_op jit(solution)/shard_map/ppermute | solution.py:33
  57.3 3.4 %collective-permute-done.20 = f32[32,16]{1,0:T(8,128)S(1)} collective-permute-done((f32[32,16]{1,0:T(8,128)S(1)}, f32[32,16]{1,0:T(8,128)S(1)}, u32[]{:S(2)}, u32[]{:S(2)}) %collective-permute-start.20) | collective-permute-done | bytes 2080 | tf_op jit(solution)/shard_map/ppermute | solution.py:33
  63.3 2.9 %collective-permute-done.21 = f32[32,16]{1,0:T(8,128)S(1)} collective-permute-done((f32[32,16]{1,0:T(8,128)S(1)}, f32[32,16]{1,0:T(8,128)S(1)}, u32[]{:S(2)}, u32[]{:S(2)}) %collective-permute-start.21) | collective-permute-done | bytes 2080 | tf_op jit(solution)/shard_map/ppermute | solution.py:33
  66.2 3.5 %collective-permute-start.22 = (f32[32,16]{1,0:T(8,128)S(1)}, f32[32,16]{1,0:T(8,128)S(1)}, u32[]{:S(2)}, u32[]{:S(2)}) collective-permute-start(f32[32,16]{1,0:T(8,128)S(1)} %broadcast_multiply_fusion), channel_id=1, source_target_pairs={{0,8},{4,12},{8,16},{12,20},{16,24},{20,28},{24,0},{28,4},{1,9},{5... | collective-permute-start | bytes 6152 | tf_op jit(solution)/shard_map/ppermute | solution.py:33
  69.8 4.2 %collective-permute-done.22 = f32[32,16]{1,0:T(8,128)S(1)} collective-permute-done((f32[32,16]{1,0:T(8,128)S(1)}, f32[32,16]{1,0:T(8,128)S(1)}, u32[]{:S(2)}, u32[]{:S(2)}) %collective-permute-start.22) | collective-permute-done | bytes 2080 | tf_op jit(solution)/shard_map/ppermute | solution.py:33
  75.3 5.1 %collective-permute-done.23 = f32[32,16]{1,0:T(8,128)S(1)} collective-permute-done((f32[32,16]{1,0:T(8,128)S(1)}, f32[32,16]{1,0:T(8,128)S(1)}, u32[]{:S(2)}, u32[]{:S(2)}) %collective-permute-start.23) | collective-permute-done | bytes 2080 | tf_op jit(solution)/shard_map/ppermute | solution.py:33
  80.5 3.8 %collective-permute-done.7 = bf16[32,320]{1,0:T(8,128)(2,1)S(1)} collective-permute-done((bf16[32,320]{1,0:T(8,128)(2,1)S(1)}, bf16[32,320]{1,0:T(8,128)(2,1)S(1)}, u32[]{:S(2)}, u32[]{:S(2)}) %collective-permute-start.7) | collective-permute-done | bytes 20512 | tf_op jit(solution)/shard_map/ppermute | solution.py:33
  84.3 3.7 %collective-permute-done.8 = bf16[32,320]{1,0:T(8,128)(2,1)S(1)} collective-permute-done((bf16[32,320]{1,0:T(8,128)(2,1)S(1)}, bf16[32,320]{1,0:T(8,128)(2,1)S(1)}, u32[]{:S(2)}, u32[]{:S(2)}) %collective-permute-start.8) | collective-permute-done | bytes 20512 | tf_op jit(solution)/shard_map/ppermute | solution.py:33
  89.3 3.5 %collective-permute-done.9 = bf16[32,320]{1,0:T(8,128)(2,1)S(1)} collective-permute-done((bf16[32,320]{1,0:T(8,128)(2,1)S(1)}, bf16[32,320]{1,0:T(8,128)(2,1)S(1)}, u32[]{:S(2)}, u32[]{:S(2)}) %collective-permute-start.9) | collective-permute-done | bytes 20512 | tf_op jit(solution)/shard_map/ppermute | solution.py:33
  97.8 6.7 %all-to-all-start = ((bf16[8,32,320]{2,1,0:T(8,128)(2,1)}), bf16[8,32,320]{2,1,0:T(8,128)(2,1)S(1)}, u32[]{:S(2)}, u32[]{:S(2)}) async-start(bf16[8,32,320]{2,1,0:T(8,128)(2,1)} %pad_maximum_fusion.1), calls=%async_computation | async-start | bytes 393216 | tf_op jit(solution)/shard_map/all_to_all | solution.py:96
  104.5 8.1 %all-to-all-done = bf16[8,32,320]{2,1,0:T(8,128)(2,1)S(1)} async-done(((bf16[8,32,320]{2,1,0:T(8,128)(2,1)}), bf16[8,32,320]{2,1,0:T(8,128)(2,1)S(1)}, u32[]{:S(2)}, u32[]{:S(2)}) %all-to-all-start) | async-done | bytes 163872 | tf_op jit(solution)/shard_map/all_to_all | solution.py:96
  113.3 3.4 %all-to-all-start.1 = ((bf16[8,32,320]{2,1,0:T(8,128)(2,1)}), bf16[8,32,320]{2,1,0:T(8,128)(2,1)S(1)}, u32[]{:S(2)}, u32[]{:S(2)}) async-start(bf16[8,32,320]{2,1,0:T(8,128)(2,1)} %broadcast_in_dim.2), calls=%async_computation.1 | async-start | bytes 393216 | tf_op jit(solution)/shard_map/all_to_all | solution.py:99
  117.6 6.8 %all-to-all-done.1 = bf16[8,32,320]{2,1,0:T(8,128)(2,1)S(1)} async-done(((bf16[8,32,320]{2,1,0:T(8,128)(2,1)}), bf16[8,32,320]{2,1,0:T(8,128)(2,1)S(1)}, u32[]{:S(2)}, u32[]{:S(2)}) %all-to-all-start.1) | async-done | bytes 163872 | tf_op jit(solution)/shard_map/all_to_all | solution.py:99
  124.8 3.8 %subtract_convert_fusion.1 = bf16[2048,512]{1,0:T(8,128)(2,1)} fusion(bf16[32,2048]{1,0:T(8,128)(2,1)S(1)} %bitcast.139, bf16[32,512]{1,0:T(8,128)(2,1)S(1)} %reshape.62, bf16[2048,512]{1,0:T(8,128)(2,1)S(1)} %copy-done.1, bf16[2048,512]{1,0:T(8,128)(2,1)} %param.13), kind=kOutput, calls=%fused_computation.1 | convolution fusion | flops 74448896 | bytes 6455296 | tf_op jit(solution)/shard_map/dot_general | solution.py:11
  (147 shorter events, 36.4 us)
Async XLA Ops:
  7.5 14.5 %collective-permute-start = (bf16[32,336]{1,0:T(8,128)(2,1)S(1)}, bf16[32,336]{1,0:T(8,128)(2,1)S(1)}, u32[]{:S(2)}, u32[]{:S(2)}) collective-permute-start(bf16[32,336]{1,0:T(8,128)(2,1)S(1)} %get-tuple-element.11), channel_id=1, source_target_pairs={{0,4},{4,8},{8,12},{12,16},{16,20},{20,24},{24,28},{28,0},{1,5},{5... | collective-permute-start | bytes 64520 | tf_op jit(solution)/shard_map/ppermute | solution.py:25
  10.5 11.6 %collective-permute-start.6 = (bf16[32,336]{1,0:T(8,128)(2,1)S(1)}, bf16[32,336]{1,0:T(8,128)(2,1)S(1)}, u32[]{:S(2)}, u32[]{:S(2)}) collective-permute-start(bf16[32,336]{1,0:T(8,128)(2,1)S(1)} %get-tuple-element.12), channel_id=1, source_target_pairs={{0,28},{4,0},{8,4},{12,8},{16,12},{20,16},{24,20},{28,24},{1,29},{... | collective-permute-start | bytes 64520 | tf_op jit(solution)/shard_map/ppermute | solution.py:25
  13.6 20.3 %collective-permute-start.5 = (bf16[32,336]{1,0:T(8,128)(2,1)S(1)}, bf16[32,336]{1,0:T(8,128)(2,1)S(1)}, u32[]{:S(2)}, u32[]{:S(2)}) collective-permute-start(bf16[32,336]{1,0:T(8,128)(2,1)S(1)} %get-tuple-element.13), channel_id=1, source_target_pairs={{0,24},{4,28},{8,0},{12,4},{16,8},{20,12},{24,16},{28,20},{1,25},{... | collective-permute-start | bytes 64520 | tf_op jit(solution)/shard_map/ppermute | solution.py:25
  15.5 18.4 %collective-permute-start.4 = (bf16[32,336]{1,0:T(8,128)(2,1)S(1)}, bf16[32,336]{1,0:T(8,128)(2,1)S(1)}, u32[]{:S(2)}, u32[]{:S(2)}) collective-permute-start(bf16[32,336]{1,0:T(8,128)(2,1)S(1)} %get-tuple-element.14), channel_id=1, source_target_pairs={{0,20},{4,24},{8,28},{12,0},{16,4},{20,8},{24,12},{28,16},{1,21},{... | collective-permute-start | bytes 64520 | tf_op jit(solution)/shard_map/ppermute | solution.py:25
  15.5 18.4 %collective-permute-start.3 = (bf16[32,336]{1,0:T(8,128)(2,1)S(1)}, bf16[32,336]{1,0:T(8,128)(2,1)S(1)}, u32[]{:S(2)}, u32[]{:S(2)}) collective-permute-start(bf16[32,336]{1,0:T(8,128)(2,1)S(1)} %get-tuple-element.15), channel_id=1, source_target_pairs={{0,16},{4,20},{8,24},{12,28},{16,0},{20,4},{24,8},{28,12},{1,17},{... | collective-permute-start | bytes 64520 | tf_op jit(solution)/shard_map/ppermute | solution.py:25
  22.0 11.9 %collective-permute-start.2 = (bf16[32,336]{1,0:T(8,128)(2,1)S(1)}, bf16[32,336]{1,0:T(8,128)(2,1)S(1)}, u32[]{:S(2)}, u32[]{:S(2)}) collective-permute-start(bf16[32,336]{1,0:T(8,128)(2,1)S(1)} %get-tuple-element.16), channel_id=1, source_target_pairs={{0,12},{4,16},{8,20},{12,24},{16,28},{20,0},{24,4},{28,8},{1,13},{... | collective-permute-start | bytes 64520 | tf_op jit(solution)/shard_map/ppermute | solution.py:25
  22.1 11.8 %collective-permute-start.1 = (bf16[32,336]{1,0:T(8,128)(2,1)S(1)}, bf16[32,336]{1,0:T(8,128)(2,1)S(1)}, u32[]{:S(2)}, u32[]{:S(2)}) collective-permute-start(bf16[32,336]{1,0:T(8,128)(2,1)S(1)} %get-tuple-element.17), channel_id=1, source_target_pairs={{0,8},{4,12},{8,16},{12,20},{16,24},{20,28},{24,0},{28,4},{1,9},{5... | collective-permute-start | bytes 64520 | tf_op jit(solution)/shard_map/ppermute | solution.py:25
  34.0 4.4 %collective-permute-start.16 = (f32[32,16]{1,0:T(8,128)S(1)}, f32[32,16]{1,0:T(8,128)S(1)}, u32[]{:S(2)}, u32[]{:S(2)}) collective-permute-start(f32[32,16]{1,0:T(8,128)S(1)} %slice.32), channel_id=1, source_target_pairs={{0,1},{1,2},{2,3},{3,0},{4,5},{5,6},{6,7},{7,4},{8,9},{9,10},{10,1... | collective-permute-start | bytes 6152 | tf_op jit(solution)/shard_map/ppermute | solution.py:33
  34.0 4.4 %collective-permute-start.15 = (f32[32,16]{1,0:T(8,128)S(1)}, f32[32,16]{1,0:T(8,128)S(1)}, u32[]{:S(2)}, u32[]{:S(2)}) collective-permute-start(f32[32,16]{1,0:T(8,128)S(1)} %slice.32), channel_id=1, source_target_pairs={{0,2},{1,3},{2,0},{3,1},{4,6},{5,7},{6,4},{7,5},{8,10},{9,11},{10,... | collective-permute-start | bytes 6152 | tf_op jit(solution)/shard_map/ppermute | solution.py:33
  38.6 8.4 %collective-permute-start.17 = (f32[32,16]{1,0:T(8,128)S(1)}, f32[32,16]{1,0:T(8,128)S(1)}, u32[]{:S(2)}, u32[]{:S(2)}) collective-permute-start(f32[32,16]{1,0:T(8,128)S(1)} %broadcast_multiply_fusion), channel_id=1, source_target_pairs={{0,28},{4,0},{8,4},{12,8},{16,12},{20,16},{24,20},{28,24},{1,29},{... | collective-permute-start | bytes 6152 | tf_op jit(solution)/shard_map/ppermute | solution.py:33
  41.8 51.1 %collective-permute-start.13 = (bf16[32,320]{1,0:T(8,128)(2,1)S(1)}, bf16[32,320]{1,0:T(8,128)(2,1)S(1)}, u32[]{:S(2)}, u32[]{:S(2)}) collective-permute-start(bf16[32,320]{1,0:T(8,128)(2,1)S(1)} %pad_maximum_fusion.2), channel_id=1, source_target_pairs={{0,4},{4,8},{8,12},{12,16},{16,20},{20,24},{24,28},{28,0},{1,5},{5... | collective-permute-start | bytes 61448 | tf_op jit(solution)/shard_map/ppermute | solution.py:33
  41.8 51.1 %collective-permute-start.12 = (bf16[32,320]{1,0:T(8,128)(2,1)S(1)}, bf16[32,320]{1,0:T(8,128)(2,1)S(1)}, u32[]{:S(2)}, u32[]{:S(2)}) collective-permute-start(bf16[32,320]{1,0:T(8,128)(2,1)S(1)} %pad_maximum_fusion.2), channel_id=1, source_target_pairs={{0,8},{4,12},{8,16},{12,20},{16,24},{20,28},{24,0},{28,4},{1,9},{5... | collective-permute-start | bytes 61448 | tf_op jit(solution)/shard_map/ppermute | solution.py:33
  42.3 50.5 %collective-permute-start.11 = (bf16[32,320]{1,0:T(8,128)(2,1)S(1)}, bf16[32,320]{1,0:T(8,128)(2,1)S(1)}, u32[]{:S(2)}, u32[]{:S(2)}) collective-permute-start(bf16[32,320]{1,0:T(8,128)(2,1)S(1)} %pad_maximum_fusion.2), channel_id=1, source_target_pairs={{0,12},{4,16},{8,20},{12,24},{16,28},{20,0},{24,4},{28,8},{1,13},{... | collective-permute-start | bytes 61448 | tf_op jit(solution)/shard_map/ppermute | solution.py:33
  44.2 48.6 %collective-permute-start.10 = (bf16[32,320]{1,0:T(8,128)(2,1)S(1)}, bf16[32,320]{1,0:T(8,128)(2,1)S(1)}, u32[]{:S(2)}, u32[]{:S(2)}) collective-permute-start(bf16[32,320]{1,0:T(8,128)(2,1)S(1)} %pad_maximum_fusion.2), channel_id=1, source_target_pairs={{0,16},{4,20},{8,24},{12,28},{16,0},{20,4},{24,8},{28,12},{1,17},{... | collective-permute-start | bytes 61448 | tf_op jit(solution)/shard_map/ppermute | solution.py:33
  47.0 4.4 %collective-permute-start.18 = (f32[32,16]{1,0:T(8,128)S(1)}, f32[32,16]{1,0:T(8,128)S(1)}, u32[]{:S(2)}, u32[]{:S(2)}) collective-permute-start(f32[32,16]{1,0:T(8,128)S(1)} %broadcast_multiply_fusion), channel_id=1, source_target_pairs={{0,24},{4,28},{8,0},{12,4},{16,8},{20,12},{24,16},{28,20},{1,25},{... | collective-permute-start | bytes 6152 | tf_op jit(solution)/shard_map/ppermute | solution.py:33
  51.4 4.6 %collective-permute-start.19 = (f32[32,16]{1,0:T(8,128)S(1)}, f32[32,16]{1,0:T(8,128)S(1)}, u32[]{:S(2)}, u32[]{:S(2)}) collective-permute-start(f32[32,16]{1,0:T(8,128)S(1)} %broadcast_multiply_fusion), channel_id=1, source_target_pairs={{0,20},{4,24},{8,28},{12,0},{16,4},{20,8},{24,12},{28,16},{1,21},{... | collective-permute-start | bytes 6152 | tf_op jit(solution)/shard_map/ppermute | solution.py:33
  56.0 4.6 %collective-permute-start.20 = (f32[32,16]{1,0:T(8,128)S(1)}, f32[32,16]{1,0:T(8,128)S(1)}, u32[]{:S(2)}, u32[]{:S(2)}) collective-permute-start(f32[32,16]{1,0:T(8,128)S(1)} %broadcast_multiply_fusion), channel_id=1, source_target_pairs={{0,16},{4,20},{8,24},{12,28},{16,0},{20,4},{24,8},{28,12},{1,17},{... | collective-permute-start | bytes 6152 | tf_op jit(solution)/shard_map/ppermute | solution.py:33
  60.7 5.5 %collective-permute-start.21 = (f32[32,16]{1,0:T(8,128)S(1)}, f32[32,16]{1,0:T(8,128)S(1)}, u32[]{:S(2)}, u32[]{:S(2)}) collective-permute-start(f32[32,16]{1,0:T(8,128)S(1)} %broadcast_multiply_fusion), channel_id=1, source_target_pairs={{0,12},{4,16},{8,20},{12,24},{16,28},{20,0},{24,4},{28,8},{1,13},{... | collective-permute-start | bytes 6152 | tf_op jit(solution)/shard_map/ppermute | solution.py:33
  66.2 7.8 %collective-permute-start.22 = (f32[32,16]{1,0:T(8,128)S(1)}, f32[32,16]{1,0:T(8,128)S(1)}, u32[]{:S(2)}, u32[]{:S(2)}) collective-permute-start(f32[32,16]{1,0:T(8,128)S(1)} %broadcast_multiply_fusion), channel_id=1, source_target_pairs={{0,8},{4,12},{8,16},{12,20},{16,24},{20,28},{24,0},{28,4},{1,9},{5... | collective-permute-start | bytes 6152 | tf_op jit(solution)/shard_map/ppermute | solution.py:33
  74.0 6.4 %collective-permute-start.23 = (f32[32,16]{1,0:T(8,128)S(1)}, f32[32,16]{1,0:T(8,128)S(1)}, u32[]{:S(2)}, u32[]{:S(2)}) collective-permute-start(f32[32,16]{1,0:T(8,128)S(1)} %broadcast_multiply_fusion), channel_id=1, source_target_pairs={{0,4},{4,8},{8,12},{12,16},{16,20},{20,24},{24,28},{28,0},{1,5},{5... | collective-permute-start | bytes 6152 | tf_op jit(solution)/shard_map/ppermute | solution.py:33
  80.4 3.8 %collective-permute-start.7 = (bf16[32,320]{1,0:T(8,128)(2,1)S(1)}, bf16[32,320]{1,0:T(8,128)(2,1)S(1)}, u32[]{:S(2)}, u32[]{:S(2)}) collective-permute-start(bf16[32,320]{1,0:T(8,128)(2,1)S(1)} %pad_maximum_fusion.2), channel_id=1, source_target_pairs={{0,28},{4,0},{8,4},{12,8},{16,12},{20,16},{24,20},{28,24},{1,29},{... | collective-permute-start | bytes 61448 | tf_op jit(solution)/shard_map/ppermute | solution.py:33
  88.1 4.7 %collective-permute-start.9 = (bf16[32,320]{1,0:T(8,128)(2,1)S(1)}, bf16[32,320]{1,0:T(8,128)(2,1)S(1)}, u32[]{:S(2)}, u32[]{:S(2)}) collective-permute-start(bf16[32,320]{1,0:T(8,128)(2,1)S(1)} %pad_maximum_fusion.2), channel_id=1, source_target_pairs={{0,20},{4,24},{8,28},{12,0},{16,4},{20,8},{24,12},{28,16},{1,21},{... | collective-permute-start | bytes 61448 | tf_op jit(solution)/shard_map/ppermute | solution.py:33
  97.8 14.8 %all-to-all-start = ((bf16[8,32,320]{2,1,0:T(8,128)(2,1)}), bf16[8,32,320]{2,1,0:T(8,128)(2,1)S(1)}, u32[]{:S(2)}, u32[]{:S(2)}) async-start(bf16[8,32,320]{2,1,0:T(8,128)(2,1)} %pad_maximum_fusion.1), calls=%async_computation | async-start | bytes 393216 | tf_op jit(solution)/shard_map/all_to_all | solution.py:96
  113.3 11.1 %all-to-all-start.1 = ((bf16[8,32,320]{2,1,0:T(8,128)(2,1)}), bf16[8,32,320]{2,1,0:T(8,128)(2,1)S(1)}, u32[]{:S(2)}, u32[]{:S(2)}) async-start(bf16[8,32,320]{2,1,0:T(8,128)(2,1)} %broadcast_in_dim.2), calls=%async_computation.1 | async-start | bytes 393216 | tf_op jit(solution)/shard_map/all_to_all | solution.py:99
  (19 other events, 79.2 us)

commit v2 on v0

v2 whole, which is shorter than its diff:
```python
import functools

import jax
import jax.numpy as jnp
from jax import lax
from jax.experimental import pallas as pl
from jax.experimental.pallas import tpu as pltpu
from jax.sharding import PartitionSpec as P

momentum_decay = 0.9
step_size = 0.5
norm_lanes = 64
low_row = 8
mib = 1024 * 1024

whole = pl.BlockSpec(memory_space=pltpu.VMEM)
in_place = pl.BlockSpec(memory_space=pl.ANY)


def dot(left, right, left_dim, right_dim, precision=None):
    return lax.dot_general(
        left,
        right,
        (((left_dim,), (right_dim,)), ((), ())),
        precision=precision,
        preferred_element_type=jnp.float32,
    )


def padded(width):
    return -(-width // 128) * 128


def project_kernel(
    chunks, fac_q, fac_o, norm, grad_q, error_q, grad_o, error_o, send, mat_q, mat_o,
    grad_q_v, error_q_v, grad_o_v, error_o_v, p_q, p_o, sems
):
    rows_q = grad_q.shape[0] // chunks
    rows_o = grad_o.shape[0] // chunks
    copies = []
    for chunk in range(chunks):
        part_q = pl.ds(chunk * rows_q, rows_q)
        part_o = pl.ds(chunk * rows_o, rows_o)
        quad = (
            (grad_q, grad_q_v, part_q),
            (error_q, error_q_v, part_q),
            (grad_o, grad_o_v, part_o),
            (error_o, error_o_v, part_o),
        )
        group = []
        for slot, (source, target, part) in enumerate(quad):
            copy = pltpu.make_async_copy(source.at[part], target.at[part], sems.at[chunk, slot])
            copy.start()
            group.append(copy)
        copies.append(group)
    for chunk in range(chunks):
        part_q = pl.ds(chunk * rows_q, rows_q)
        part_o = pl.ds(chunk * rows_o, rows_o)
        copies[chunk][0].wait()
        copies[chunk][1].wait()
        block = (
            grad_q_v[part_q].astype(jnp.float32) + error_q_v[part_q].astype(jnp.float32)
        ).astype(jnp.bfloat16)
        mat_q[part_q] = block
        p_q[:, part_q] = dot(fac_q[...], block, 1, 1)
        copies[chunk][2].wait()
        copies[chunk][3].wait()
        block = (
            grad_o_v[part_o].astype(jnp.float32) + error_o_v[part_o].astype(jnp.float32)
        ).astype(jnp.bfloat16)
        mat_o[part_o] = block
        p_o[:, part_o] = dot(fac_o[...], block, 1, 1)
    count = send.shape[0]
    size_q = p_q.shape[1] // count
    size_o = p_o.shape[1] // count
    for slot in range(count):
        send[slot, :, :size_q] = p_q[:, slot * size_q:(slot + 1) * size_q].astype(jnp.bfloat16)
        send[slot, :, size_q:size_q + size_o] = p_o[
            :, slot * size_o:(slot + 1) * size_o
        ].astype(jnp.bfloat16)
        send[slot, :, size_q + size_o:size_q + size_o + norm_lanes] = norm[slot]


def project(grad_q, error_q, grad_o, error_o, fac_q, fac_o, norm):
    rank = fac_q.shape[0]
    count = norm.shape[0]
    width = padded((grad_q.shape[0] + grad_o.shape[0]) // count + norm_lanes)
    chunks = 4
    return pl.pallas_call(
        functools.partial(project_kernel, chunks),
        out_shape=(
            jax.ShapeDtypeStruct((count, rank, width), jnp.bfloat16),
            pltpu.VMEM(grad_q.shape, jnp.bfloat16),
            pltpu.VMEM(grad_o.shape, jnp.bfloat16),
        ),
        in_specs=[whole] * 3 + [in_place] * 4,
        out_specs=(whole, whole, whole),
        scratch_shapes=[
            pltpu.VMEM(grad_q.shape, jnp.bfloat16),
            pltpu.VMEM(grad_q.shape, jnp.bfloat16),
            pltpu.VMEM(grad_o.shape, jnp.bfloat16),
            pltpu.VMEM(grad_o.shape, jnp.bfloat16),
            pltpu.VMEM((rank, grad_q.shape[0]), jnp.float32),
            pltpu.VMEM((rank, grad_o.shape[0]), jnp.float32),
            pltpu.SemaphoreType.DMA((chunks, 4)),
        ],
        compiler_params=pltpu.CompilerParams(vmem_limit_bytes=24 * mib),
        name="project",
    )(fac_q, fac_o, norm, grad_q, error_q, grad_o, error_o)


def total_of(got):
    total = got[0].astype(jnp.float32)
    for slot in range(1, got.shape[0]):
        total = total + got[slot].astype(jnp.float32)
    return total


def hat_kernel(size_q, size_o, got, ginv_q, ginv_o, send):
    total = total_of(got)
    highest = lax.Precision.HIGHEST
    hat_q = dot(ginv_q[...].T, total[:, :size_q], 1, 0, highest)
    hat_o = dot(ginv_o[...].T, total[:, size_q:size_q + size_o], 1, 0, highest)
    part = total[:, size_q + size_o:size_q + size_o + norm_lanes]
    high = part.astype(jnp.bfloat16).astype(jnp.float32)
    low = pltpu.roll(part - high, low_row, 0)
    row = lax.broadcasted_iota(jnp.int32, part.shape, 0)
    norm = jnp.where(row < low_row, high, low).astype(jnp.bfloat16)
    hat_q = hat_q.astype(jnp.bfloat16)
    hat_o = hat_o.astype(jnp.bfloat16)
    for slot in range(send.shape[0]):
        send[slot, :, :size_q] = hat_q
        send[slot, :, size_q:size_q + size_o] = hat_o
        send[slot, :, size_q + size_o:size_q + size_o + norm_lanes] = norm


def hats(got, ginv_q, ginv_o, size_q, size_o):
    return pl.pallas_call(
        functools.partial(hat_kernel, size_q, size_o),
        out_shape=jax.ShapeDtypeStruct(got.shape, jnp.bfloat16),
        in_specs=[whole] * 3,
        out_specs=whole,
        compiler_params=pltpu.CompilerParams(vmem_limit_bytes=16 * mib),
        name="hats",
    )(got, ginv_q, ginv_o)


def right_kernel(got, mat_q, mat_o, hat_q, hat_o, send, norm):
    count = got.shape[0]
    size_q = hat_q.shape[1] // count
    size_o = hat_o.shape[1] // count
    for slot in range(count):
        hat_q[:, slot * size_q:(slot + 1) * size_q] = got[slot, :, :size_q]
        hat_o[:, slot * size_o:(slot + 1) * size_o] = got[slot, :, size_q:size_q + size_o]
        part = got[slot, :, size_q + size_o:size_q + size_o + norm_lanes].astype(jnp.float32)
        norm[slot] = part[:low_row] + part[low_row:2 * low_row]
    q_q = dot(hat_q[...], mat_q[...], 1, 0)
    q_o = dot(hat_o[...], mat_o[...], 1, 0)
    size_q = q_q.shape[1] // count
    size_o = q_o.shape[1] // count
    for slot in range(count):
        send[slot, :, :size_o] = q_o[:, slot * size_o:(slot + 1) * size_o].astype(jnp.bfloat16)
        send[slot, :, size_o:size_o + size_q] = q_q[
            :, slot * size_q:(slot + 1) * size_q
        ].astype(jnp.bfloat16)


def right(got, mat_q, mat_o):
    count, rank, _ = got.shape
    width = padded((mat_q.shape[1] + mat_o.shape[1]) // count)
    return pl.pallas_call(
        right_kernel,
        out_shape=(
            jax.ShapeDtypeStruct((rank, mat_q.shape[0]), jnp.bfloat16),
            jax.ShapeDtypeStruct((rank, mat_o.shape[0]), jnp.bfloat16),
            jax.ShapeDtypeStruct((count, rank, width), jnp.bfloat16),
            jax.ShapeDtypeStruct((count, low_row, norm_lanes), jnp.float32),
        ),
        in_specs=[whole] * 3,
        out_specs=(whole,) * 4,
        compiler_params=pltpu.CompilerParams(vmem_limit_bytes=16 * mib),
        name="right",
    )(got, mat_q, mat_o)


def mean_kernel(got, send):
    mean = (total_of(got) / got.shape[0]).astype(jnp.bfloat16)
    for slot in range(send.shape[0]):
        send[slot] = mean


def means(got):
    return pl.pallas_call(
        mean_kernel,
        out_shape=jax.ShapeDtypeStruct(got.shape, jnp.bfloat16),
        in_specs=[whole],
        out_specs=whole,
        compiler_params=pltpu.CompilerParams(vmem_limit_bytes=16 * mib),
        name="means",
    )(got)


def finish_kernel(
    chunks, got_hat, got_new, hat_q, hat_o, mat_q, mat_o, weight_q, momentum_q, weight_o, momentum_o,
    error_q_new, new_q, momentum_q_new, weight_q_new,
    error_o_new, new_o, momentum_o_new, weight_o_new,
    error_q_v, error_o_v, sems
):
    count = got_new.shape[0]
    me = lax.axis_index("replica")
    size_q = new_q.shape[1] // count
    size_o = new_o.shape[1] // count
    for slot in range(count):
        new_o[:, slot * size_o:(slot + 1) * size_o] = got_new[slot, :, :size_o]
        new_q[:, slot * size_q:(slot + 1) * size_q] = got_new[slot, :, size_o:size_o + size_q]
    copies = []
    rows_q = mat_q.shape[0] // chunks
    rows_o = mat_o.shape[0] // chunks
    for chunk in range(chunks):
        part = pl.ds(chunk * rows_q, rows_q)
        approx = dot(hat_q[:, part], new_q[...], 0, 0)
        error_q_v[part] = (mat_q[part].astype(jnp.float32) - approx).astype(jnp.bfloat16)
        copy = pltpu.make_async_copy(error_q_v.at[part], error_q_new.at[part], sems.at[chunk, 0])
        copy.start()
        copies.append(copy)
        part = pl.ds(chunk * rows_o, rows_o)
        approx = dot(hat_o[:, part], new_o[...], 0, 0)
        error_o_v[part] = (mat_o[part].astype(jnp.float32) - approx).astype(jnp.bfloat16)
        copy = pltpu.make_async_copy(error_o_v.at[part], error_o_new.at[part], sems.at[chunk, 1])
        copy.start()
        copies.append(copy)
    mine = got_hat[me][:, :weight_q.shape[0]]
    moved = momentum_decay * momentum_q[...] + dot(mine, new_q[...], 0, 0)
    momentum_q_new[...] = moved
    weight_q_new[...] = weight_q[...] - step_size * moved
    mine = got_new[me][:, :weight_o.shape[1]]
    moved = momentum_decay * momentum_o[...] + dot(hat_o[...], mine, 0, 0)
    momentum_o_new[...] = moved
    weight_o_new[...] = weight_o[...] - step_size * moved
    for copy in copies:
        copy.wait()


def finish(got_hat, got_new, hat_q, hat_o, mat_q, mat_o, weight_q, momentum_q, weight_o, momentum_o):
    rank = hat_q.shape[0]
    chunks = 4
    f32 = jnp.float32
    bf16 = jnp.bfloat16
    return pl.pallas_call(
        functools.partial(finish_kernel, chunks),
        out_shape=(
            jax.ShapeDtypeStruct(mat_q.shape, bf16),
            jax.ShapeDtypeStruct((rank, mat_q.shape[1]), bf16),
            jax.ShapeDtypeStruct(weight_q.shape, f32),
            jax.ShapeDtypeStruct(weight_q.shape, f32),
            jax.ShapeDtypeStruct(mat_o.shape, bf16),
            jax.ShapeDtypeStruct((rank, mat_o.shape[1]), bf16),
            jax.ShapeDtypeStruct(weight_o.shape, f32),
            jax.ShapeDtypeStruct(weight_o.shape, f32),
        ),
        in_specs=[whole] * 10,
        out_specs=(in_place, whole, whole, whole) * 2,
        scratch_shapes=[
            pltpu.VMEM(mat_q.shape, bf16),
            pltpu.VMEM(mat_o.shape, bf16),
            pltpu.SemaphoreType.DMA((chunks, 2)),
        ],
        compiler_params=pltpu.CompilerParams(vmem_limit_bytes=24 * mib),
        name="finish",
    )(got_hat, got_new, hat_q, hat_o, mat_q, mat_o, weight_q, momentum_q, weight_o, momentum_o)


def spread(send):
    return lax.all_to_all(send, "replica", 0, 0, tiled=True)


def keep(value):
    return pltpu.with_memory_space_constraint(value, pltpu.VMEM)


def on_device(
    grad_q,
    error_q,
    qfac_q,
    ginv_q,
    weight_q,
    momentum_q,
    grad_o,
    error_o,
    qfac_o,
    ginv_o,
    weight_o,
    momentum_o,
    norm_grads,
):
    replicas = lax.axis_size("replica")
    tensors = lax.axis_size("tensor")
    rank = qfac_q.shape[1]
    norm_rows = norm_grads.size // (replicas * norm_lanes)
    norm = norm_grads.reshape(replicas, norm_rows, norm_lanes)
    norm = jnp.pad(norm, ((0, 0), (0, rank - norm_rows), (0, 0)))
    size_q = grad_q.shape[0] // replicas
    size_o = grad_o.shape[0] // replicas
    send, mat_q, mat_o = project(grad_q, error_q, grad_o, error_o, qfac_q.T, qfac_o.T, norm)
    got_hat = spread(hats(spread(send), ginv_q, ginv_o, size_q, size_o))
    hat_q, hat_o, send, norm_part = right(got_hat, keep(mat_q), keep(mat_o))
    got_new = spread(means(spread(send)))
    norm_total = norm_part
    for step in range(1, tensors):
        pairs = [(source, (source + step) % tensors) for source in range(tensors)]
        norm_total = norm_total + lax.ppermute(norm_part, "tensor", pairs)
    norm_mean = (norm_total[:, :norm_rows] / (replicas * tensors)).reshape(-1)
    (
        error_q_new, new_q, momentum_q_new, weight_q_new,
        error_o_new, new_o, momentum_o_new, weight_o_new,
    ) = finish(
        got_hat, got_new, hat_q, hat_o, keep(mat_q), keep(mat_o),
        keep(weight_q), keep(momentum_q), keep(weight_o), keep(momentum_o),
    )
    return (
        error_q_new,
        new_q.T,
        momentum_q_new,
        weight_q_new,
        error_o_new,
        new_o.T,
        momentum_o_new,
        weight_o_new,
        norm_mean,
    )


def solution(mesh):
    in_specs = (
        P("replica", "tensor"),
        P("replica", "tensor"),
        P("tensor", None),
        P("tensor", None),
        P("replica", "tensor"),
        P("replica", "tensor"),
        P(("replica", "tensor"), None),
        P(("replica", "tensor"), None),
        P("tensor", None),
        P("tensor", None),
        P("tensor", "replica"),
        P("tensor", "replica"),
        P("replica", "tensor", None),
    )
    out_specs = (
        P("replica", "tensor"),
        P("tensor", None),
        P("replica", "tensor"),
        P("replica", "tensor"),
        P(("replica", "tensor"), None),
        P("tensor", None),
        P("tensor", "replica"),
        P("tensor", "replica"),
        P(),
    )
    return jax.shard_map(
        on_device, mesh=mesh, in_specs=in_specs, out_specs=out_specs, check_vma=False
    )
```

time: 194 us -> 73.9 us (0.38)
  waiting for transfers between devices: 116 us -> 3.39 us
  matrix products: 18.7 us -> 0 us
  local copies, waits for them, and re-layouts: 0.43 us -> 15.5 us
  between operations: 14.3 us -> 0.75 us
  Pallas kernels: 0 us -> 9.64 us
  starting transfers between devices: 0.08 us -> 5.17 us
  blocking collectives: 40 us -> 36.3 us
    psum x2 -> x0, waiting for transfers between devices: 116 us -> none  [the longest x1 86.6 us: on_device(): sum_q, sum_o = lax.psum((p_q, p_o), 'replica')]
    psum x1 -> x0, blocking collectives: 40 us -> none  [on_device(): norm_total = lax.psum(norm_part, ('replica', 'tensor'))]
    all_to_all x0 -> x3, blocking collectives: none -> 36.3 us  [spread(): return lax.all_to_all(send, 'replica', 0, 0, tiled=True)]
    dot_general x8 -> x0, matrix products: 18.7 us -> none  [the longest x2 5.46 us: left_factor(): return jnp.dot(matrix, factor, preferred_element_type=jnp.float32)]
    unnamed x38, local copies, waits for them, and re-layouts: 0.43 us -> 14 us
    pallas_call x0 -> x5, Pallas kernels: none -> 9.64 us  [the longest x1 3.99 us: project(): pl.pallas_call(functools.partial(project_kernel, chunks), out_shape=(jax....]
    all_to_all x0 -> x1, starting transfers between devices: none -> 3.39 us  [spread(): return lax.all_to_all(send, 'replica', 0, 0, tiled=True)]
    ppermute x0 -> x3, waiting for transfers between devices: none -> 3.38 us  [on_device(): norm_total = norm_total + lax.ppermute(norm_part, 'tensor', pairs)]
  transfers between devices with their start and end apart: 2 -> 4, of which waited for: 2 -> 3; matrix products, arithmetic and copies ran while one was open for 0% -> 4% of each run, Pallas kernels for 0% -> 0%
where the time goes in v2:
time: 73.9 us; the launch traced here: 73 us
  blocking collectives  36.3 us (49%)
  local copies, waits for them, and re-layouts  15.5 us (21%)
  Pallas kernels  9.64 us (13%)
  starting transfers between devices  5.17 us (7%)
  waiting for transfers between devices  3.39 us (5%)
  other arithmetic  2.15 us (3%)
  between operations  0.75 us (1%)
    all_to_all x3, blocking collectives, spread(): return lax.all_to_all(send, 'replica', 0, 0, tiled=True)  36.3 us
    unnamed x38, local copies, waits for them, and re-layouts  14 us
    pallas_call x1, Pallas kernels, project(): pl.pallas_call(functools.partial(project_kernel, chunks), out_shape=(jax....  3.99 us
    pallas_call x1, Pallas kernels, finish(): pl.pallas_call(functools.partial(finish_kernel, chunks), out_shape=(jax.S...  3.85 us
    all_to_all x1, starting transfers between devices, spread(): return lax.all_to_all(send, 'replica', 0, 0, tiled=True)  3.39 us
    ppermute x3, waiting for transfers between devices, on_device(): norm_total = norm_total + lax.ppermute(norm_part, 'tensor', pairs)  3.38 us
    ppermute x3, starting transfers between devices, on_device(): norm_total = norm_total + lax.ppermute(norm_part, 'tensor', pairs)  1.78 us
  transfers between devices with their start and end apart: 4, of which 3 were waited for; matrix products, arithmetic and copies ran while one was open for 4% of the time, Pallas kernels for 0%

profile of v2, /device:TPU:0, one launch (start us, length us, event | category | flops | bytes accessed | tf_op | source)
XLA Modules:
  0.0 73.0 jit_solution(2286991141508299532)
XLA Ops:
  0.6 0.8 %reduce = bf16[4096]{0:T(1024)(128)(2,1)S(1)} reduce(bf16[1,1,4096]{2,1,0:T(2,128)(2,1)} %param.25, bf16[]{:T(256)} %constant.9), dimensions={0,1}, to_apply=%param.25.reduce_sub_computation | reduce | bytes 16386 | tf_op args[12]
  1.5 1.6 %copy-done.2 = bf16[2048,512]{1,0:T(8,128)(2,1)S(1)} copy-done((bf16[2048,512]{1,0:T(8,128)(2,1)S(1)}, bf16[2048,512]{1,0:T(8,128)(2,1)}, u32[]{:S(2)}) %copy-start.2) | copy-done | bytes 2097176
  3.1 1.6 %copy-done.3 = bf16[2048,512]{1,0:T(8,128)(2,1)S(1)} copy-done((bf16[2048,512]{1,0:T(8,128)(2,1)S(1)}, bf16[2048,512]{1,0:T(8,128)(2,1)}, u32[]{:S(2)}) %copy-start.3) | copy-done | bytes 2097176
  4.7 1.6 %copy-done.4 = bf16[512,2048]{1,0:T(8,128)(2,1)S(1)} copy-done((bf16[512,2048]{1,0:T(8,128)(2,1)S(1)}, bf16[512,2048]{1,0:T(8,128)(2,1)}, u32[]{:S(2)}) %copy-start.4) | copy-done | bytes 2097176
  6.3 1.6 %copy-done.5 = bf16[512,2048]{1,0:T(8,128)(2,1)S(1)} copy-done((bf16[512,2048]{1,0:T(8,128)(2,1)S(1)}, bf16[512,2048]{1,0:T(8,128)(2,1)}, u32[]{:S(2)}) %copy-start.5) | copy-done | bytes 2097176
  7.9 0.9 %copy-done.10 = bf16[2048,32]{0,1:T(8,128)(2,1)S(1)} copy-done((bf16[2048,32]{0,1:T(8,128)(2,1)S(1)}, bf16[2048,32]{0,1:T(8,128)(2,1)}, u32[]{:S(2)}) %copy-start.10) | copy-done | bytes 131096
  8.8 0.8 %copy-done.13 = bf16[512,32]{0,1:T(8,128)(2,1)S(1)} copy-done((bf16[512,32]{0,1:T(8,128)(2,1)S(1)}, bf16[512,32]{0,1:T(8,128)(2,1)}, u32[]{:S(2)}) %copy-start.13) | copy-done | bytes 32792
  9.6 4.0 %project.1 = (bf16[8,32,384]{2,1,0:T(8,128)(2,1)S(1)}, bf16[2048,512]{1,0:T(8,128)(2,1)S(1)}, bf16[512,2048]{1,0:T(8,128)(2,1)S(1)}) custom-call(bf16[32,512]{1,0:T(8,128)(2,1)S(1)} %bitcast.5, bf16[32,2048]{1,0:T(8,128)(2,1)S(1)} %bitcast.4, bf16[8,32,64]{2,1,0:T(8,128)(2,1)S(1)} %pad.4.norm, bf16[2048,512]{1,0:T(8,128)(2,1)S(1)} %copy-done.2, ...), custom_call_target="tpu_custom_call" | custom-call | tf_op jit(solution)/shard_map/project/pallas_call | solution.py:89
  13.6 15.0 %all_to_all.20.got = bf16[8,32,384]{2,1,0:T(8,128)(2,1)S(1)} all-to-all(bf16[8,32,384]{2,1,0:T(8,128)(2,1)S(1)} %get-tuple-element.24), channel_id=1, replica_groups=mesh['replica'=8,'tensor'=4] {'replica'}, dimensions={0} | all-to-all | bytes 393216 | tf_op jit(solution)/shard_map/all_to_all | solution.py:274
  28.9 10.7 %all_to_all.21.got.got_hat = bf16[8,32,384]{2,1,0:T(8,128)(2,1)S(1)} all-to-all(bf16[8,32,384]{2,1,0:T(8,128)(2,1)S(1)} %hats.1), channel_id=1, replica_groups=mesh['replica'=8,'tensor'=4] {'replica'}, dimensions={0} | all-to-all | bytes 393216 | tf_op jit(solution)/shard_map/all_to_all | solution.py:274
  39.6 0.8 %right.1 = (bf16[32,2048]{1,0:T(8,128)(2,1)S(1)}, bf16[32,512]{1,0:T(8,128)(2,1)S(1)}, bf16[8,32,384]{2,1,0:T(8,128)(2,1)S(1)}, f32[8,8,64]{2,1,0:T(8,128)S(1)}) custom-call(bf16[8,32,384]{2,1,0:T(8,128)(2,1)S(1)} %all_to_all.21.got.got_hat, bf16[2048,512]{1,0:T(8,128)(2,1)S(1)} %get-tuple-element.25.mat_q, bf16[512,2048]{1,0:T(8,128)(2,1)S(1)} %get-tuple-element.26.mat_o), custom_call_target="tpu_custom_call" | custom-call | tf_op jit(solution)/shard_map/right/pallas_call | solution.py:171
  41.1 10.6 %all_to_all.22.got = bf16[8,32,384]{2,1,0:T(8,128)(2,1)S(1)} all-to-all(bf16[8,32,384]{2,1,0:T(8,128)(2,1)S(1)} %get-tuple-element.27), channel_id=1, replica_groups=mesh['replica'=8,'tensor'=4] {'replica'}, dimensions={0} | all-to-all | bytes 393216 | tf_op jit(solution)/shard_map/all_to_all | solution.py:274
  52.4 3.4 %all-to-all-start.3 = ((bf16[8,32,384]{2,1,0:T(8,128)(2,1)}), bf16[8,32,384]{2,1,0:T(8,128)(2,1)S(1)}, u32[]{:S(2)}, u32[]{:S(2)}) async-start(bf16[8,32,384]{2,1,0:T(8,128)(2,1)} %means.1), calls=%async_computation.3 | async-start | bytes 393216 | tf_op jit(solution)/shard_map/all_to_all | solution.py:274
  55.8 1.6 %collective-permute-start.1 = (f32[8,8,64]{2,1,0:T(8,128)}, f32[8,8,64]{2,1,0:T(8,128)S(1)}, u32[]{:S(2)}, u32[]{:S(2)}) collective-permute-start(f32[8,8,64]{2,1,0:T(8,128)} %copy-done.16), channel_id=1, source_target_pairs={{0,2},{1,3},{2,0},{3,1},{4,6},{5,7},{6,4},{7,5},{8,10},{9,11},{10,... | collective-permute-start | bytes 49160 | tf_op jit(solution)/shard_map/ppermute | solution.py:311
  57.7 2.4 %collective-permute-done.1 = f32[8,8,64]{2,1,0:T(8,128)S(1)} collective-permute-done((f32[8,8,64]{2,1,0:T(8,128)}, f32[8,8,64]{2,1,0:T(8,128)S(1)}, u32[]{:S(2)}, u32[]{:S(2)}) %collective-permute-start.1) | collective-permute-done | bytes 16416 | tf_op jit(solution)/shard_map/ppermute | solution.py:311
  60.1 0.8 %collective-permute-done = f32[8,8,64]{2,1,0:T(8,128)S(1)} collective-permute-done((f32[8,8,64]{2,1,0:T(8,128)}, f32[8,8,64]{2,1,0:T(8,128)S(1)}, u32[]{:S(2)}, u32[]{:S(2)}) %collective-permute-start) | collective-permute-done | bytes 16416 | tf_op jit(solution)/shard_map/ppermute | solution.py:311
  60.9 1.4 %add_multiply_fusion = f32[8,8,64]{2,1,0:T(8,128)} fusion(f32[8,8,64]{2,1,0:T(8,128)S(1)} %collective-permute-done.2, f32[8,8,64]{2,1,0:T(8,128)S(1)} %collective-permute-done.1, f32[8,8,64]{2,1,0:T(8,128)} %copy-done.16, f32[8,8,64]{2,1,0:T(8,128)S(1)} %collective-permute-done), kind=kLoop, calls=%fused_computation | loop fusion | flops 16384 | bytes 81920 | tf_op jit(solution)/shard_map/div | solution.py:312
  62.3 1.4 %reshape.25 = f32[4096]{0:T(1024)} reshape(f32[8,8,64]{2,1,0:T(8,128)} %add_multiply_fusion) | data formatting | bytes 32768 | tf_op jit(solution)/shard_map/reshape | solution.py:312
  63.8 1.6 %copy-done.1 = bf16[512,2048]{1,0:T(8,128)(2,1)S(1)} copy-done((bf16[512,2048]{1,0:T(8,128)(2,1)S(1)}, bf16[512,2048]{1,0:T(8,128)(2,1)}, u32[]{:S(2)}) %copy-start.1) | copy-done | bytes 2097176
  65.4 1.0 %copy-done.8 = f32[512,256]{1,0:T(8,128)S(1)} copy-done((f32[512,256]{1,0:T(8,128)S(1)}, f32[512,256]{1,0:T(8,128)}, u32[]{:S(2)}) %copy-start.8) | copy-done | bytes 524312
  66.4 1.0 %copy-done.9 = f32[512,256]{1,0:T(8,128)S(1)} copy-done((f32[512,256]{1,0:T(8,128)S(1)}, f32[512,256]{1,0:T(8,128)}, u32[]{:S(2)}) %copy-start.9) | copy-done | bytes 524312
  67.5 0.9 %copy-done.12 = bf16[32,2048]{1,0:T(8,128)(2,1)S(1)} copy-done((bf16[32,2048]{1,0:T(8,128)(2,1)S(1)}, bf16[32,2048]{1,0:T(8,128)(2,1)}, u32[]{:S(2)}) %copy-start.12) | copy-done | bytes 131096
  68.4 0.8 %copy-done.15 = bf16[32,512]{1,0:T(8,128)(2,1)S(1)} copy-done((bf16[32,512]{1,0:T(8,128)(2,1)S(1)}, bf16[32,512]{1,0:T(8,128)(2,1)}, u32[]{:S(2)}) %copy-start.15) | copy-done | bytes 32792
  69.1 3.9 %finish.1 = (bf16[2048,512]{1,0:T(8,128)(2,1)}, bf16[32,512]{1,0:T(8,128)(2,1)}, f32[256,512]{1,0:T(8,128)}, f32[256,512]{1,0:T(8,128)}, bf16[512,2048]{1,0:T(8,...) custom-call(bf16[8,32,384]{2,1,0:T(8,128)(2,1)S(1)} %all_to_all.21.got.got_hat, ...), custom_call_target="tpu_custom_call" | custom-call | tf_op jit(solution)/shard_map/finish/pallas_call | solution.py:249
  (35 shorter events, 2.1 us)
Async XLA Ops:
  1.5 1.6 %copy-start.2 = (bf16[2048,512]{1,0:T(8,128)(2,1)S(1)}, bf16[2048,512]{1,0:T(8,128)(2,1)}, u32[]{:S(2)}) copy-start(bf16[2048,512]{1,0:T(8,128)(2,1)} %grad_q.1) | copy-start | bytes 6291460
  3.1 1.6 %copy-start.3 = (bf16[2048,512]{1,0:T(8,128)(2,1)S(1)}, bf16[2048,512]{1,0:T(8,128)(2,1)}, u32[]{:S(2)}) copy-start(bf16[2048,512]{1,0:T(8,128)(2,1)} %error_q.1) | copy-start | bytes 6291460
  4.7 1.6 %copy-start.4 = (bf16[512,2048]{1,0:T(8,128)(2,1)S(1)}, bf16[512,2048]{1,0:T(8,128)(2,1)}, u32[]{:S(2)}) copy-start(bf16[512,2048]{1,0:T(8,128)(2,1)} %grad_o.1) | copy-start | bytes 6291460
  6.3 1.6 %copy-start.5 = (bf16[512,2048]{1,0:T(8,128)(2,1)S(1)}, bf16[512,2048]{1,0:T(8,128)(2,1)}, u32[]{:S(2)}) copy-start(bf16[512,2048]{1,0:T(8,128)(2,1)} %error_o.1) | copy-start | bytes 6291460
  7.9 0.9 %copy-start.10 = (bf16[2048,32]{0,1:T(8,128)(2,1)S(1)}, bf16[2048,32]{0,1:T(8,128)(2,1)}, u32[]{:S(2)}) copy-start(bf16[2048,32]{0,1:T(8,128)(2,1)} %param.21) | copy-start | bytes 393220
  8.8 0.8 %copy-start.13 = (bf16[512,32]{0,1:T(8,128)(2,1)S(1)}, bf16[512,32]{0,1:T(8,128)(2,1)}, u32[]{:S(2)}) copy-start(bf16[512,32]{0,1:T(8,128)(2,1)} %param.15) | copy-start | bytes 98308
  9.5 19.0 %copy-start.17 = (f32[32,32]{1,0:T(8,128)S(1)}, f32[32,32]{1,0:T(8,128)}, u32[]{:S(2)}) copy-start(f32[32,32]{1,0:T(8,128)} %ginv_q.1) | copy-start | bytes 12292
  9.6 19.1 %copy-start.18 = (f32[32,32]{1,0:T(8,128)S(1)}, f32[32,32]{1,0:T(8,128)}, u32[]{:S(2)}) copy-start(f32[32,32]{1,0:T(8,128)} %ginv_o.1) | copy-start | bytes 12292
  13.6 26.9 %copy-start = (bf16[512,2048]{1,0:T(8,128)(2,1)}, bf16[512,2048]{1,0:T(8,128)(2,1)S(1)}, u32[]{:S(2)}) copy-start(bf16[512,2048]{1,0:T(8,128)(2,1)S(1)} %get-tuple-element.26.mat_o) | copy-start | bytes 6291460
  39.6 24.2 %copy-start.6 = (f32[256,512]{1,0:T(8,128)S(1)}, f32[256,512]{1,0:T(8,128)}, u32[]{:S(2)}) copy-start(f32[256,512]{1,0:T(8,128)} %weight_q.1) | copy-start | bytes 1572868
  39.6 24.2 %copy-start.7 = (f32[256,512]{1,0:T(8,128)S(1)}, f32[256,512]{1,0:T(8,128)}, u32[]{:S(2)}) copy-start(f32[256,512]{1,0:T(8,128)} %momentum_q.1) | copy-start | bytes 1572868
  40.4 0.6 copy-start.16
  41.1 11.3 %copy-start.11 = (bf16[32,2048]{1,0:T(8,128)(2,1)}, bf16[32,2048]{1,0:T(8,128)(2,1)S(1)}, u32[]{:S(2)}) copy-start(bf16[32,2048]{1,0:T(8,128)(2,1)S(1)} %get-tuple-element.28.hat_q) | copy-start | bytes 393220
  41.1 11.3 %copy-start.14 = (bf16[32,512]{1,0:T(8,128)(2,1)}, bf16[32,512]{1,0:T(8,128)(2,1)S(1)}, u32[]{:S(2)}) copy-start(bf16[32,512]{1,0:T(8,128)(2,1)S(1)} %get-tuple-element.29.hat_o) | copy-start | bytes 98308
  52.4 11.4 %all-to-all-start.3 = ((bf16[8,32,384]{2,1,0:T(8,128)(2,1)}), bf16[8,32,384]{2,1,0:T(8,128)(2,1)S(1)}, u32[]{:S(2)}, u32[]{:S(2)}) async-start(bf16[8,32,384]{2,1,0:T(8,128)(2,1)} %means.1), calls=%async_computation.3 | async-start | bytes 393216 | tf_op jit(solution)/shard_map/all_to_all | solution.py:274
  55.8 2.0 %collective-permute-start.2 = (f32[8,8,64]{2,1,0:T(8,128)}, f32[8,8,64]{2,1,0:T(8,128)S(1)}, u32[]{:S(2)}, u32[]{:S(2)}) collective-permute-start(f32[8,8,64]{2,1,0:T(8,128)} %copy-done.16), channel_id=1, source_target_pairs={{0,3},{1,0},{2,1},{3,2},{4,7},{5,4},{6,5},{7,6},{8,11},{9,8},{10,9... | collective-permute-start | bytes 49160 | tf_op jit(solution)/shard_map/ppermute | solution.py:311
  55.8 4.3 %collective-permute-start.1 = (f32[8,8,64]{2,1,0:T(8,128)}, f32[8,8,64]{2,1,0:T(8,128)S(1)}, u32[]{:S(2)}, u32[]{:S(2)}) collective-permute-start(f32[8,8,64]{2,1,0:T(8,128)} %copy-done.16), channel_id=1, source_target_pairs={{0,2},{1,3},{2,0},{3,1},{4,6},{5,7},{6,4},{7,5},{8,10},{9,11},{10,... | collective-permute-start | bytes 49160 | tf_op jit(solution)/shard_map/ppermute | solution.py:311
  57.4 3.6 %collective-permute-start = (f32[8,8,64]{2,1,0:T(8,128)}, f32[8,8,64]{2,1,0:T(8,128)S(1)}, u32[]{:S(2)}, u32[]{:S(2)}) collective-permute-start(f32[8,8,64]{2,1,0:T(8,128)} %copy-done.16), channel_id=1, source_target_pairs={{0,1},{1,2},{2,3},{3,0},{4,5},{5,6},{6,7},{7,4},{8,9},{9,10},{10,1... | collective-permute-start | bytes 49160 | tf_op jit(solution)/shard_map/ppermute | solution.py:311
  63.8 1.6 %copy-start.1 = (bf16[512,2048]{1,0:T(8,128)(2,1)S(1)}, bf16[512,2048]{1,0:T(8,128)(2,1)}, u32[]{:S(2)}) copy-start(bf16[512,2048]{1,0:T(8,128)(2,1)} %copy-done) | copy-start | bytes 6291460
  65.4 1.0 %copy-start.8 = (f32[512,256]{1,0:T(8,128)S(1)}, f32[512,256]{1,0:T(8,128)}, u32[]{:S(2)}) copy-start(f32[512,256]{1,0:T(8,128)} %weight_o.1) | copy-start | bytes 1572868
  66.4 1.0 %copy-start.9 = (f32[512,256]{1,0:T(8,128)S(1)}, f32[512,256]{1,0:T(8,128)}, u32[]{:S(2)}) copy-start(f32[512,256]{1,0:T(8,128)} %momentum_o.1) | copy-start | bytes 1572868
  67.5 0.9 %copy-start.12 = (bf16[32,2048]{1,0:T(8,128)(2,1)S(1)}, bf16[32,2048]{1,0:T(8,128)(2,1)}, u32[]{:S(2)}) copy-start(bf16[32,2048]{1,0:T(8,128)(2,1)} %copy-done.11) | copy-start | bytes 393220
  68.4 0.8 %copy-start.15 = (bf16[32,512]{1,0:T(8,128)(2,1)S(1)}, bf16[32,512]{1,0:T(8,128)(2,1)}, u32[]{:S(2)}) copy-start(bf16[32,512]{1,0:T(8,128)(2,1)} %copy-done.14) | copy-start | bytes 98308

commit v3 on v0

v3 whole, which is shorter than its diff:
```python
import functools

import jax
import jax.numpy as jnp
from jax import lax
from jax.experimental import pallas as pl
from jax.experimental.pallas import tpu as pltpu
from jax.sharding import PartitionSpec as P

momentum_decay = 0.9
step_size = 0.5
lanes = 128
mib = 1024 * 1024
bf16 = jnp.bfloat16
f32 = jnp.float32

whole = pl.BlockSpec(memory_space=pltpu.VMEM)
in_place = pl.BlockSpec(memory_space=pl.ANY)


def dot(left, right, left_dim, right_dim, precision=None):
    return lax.dot_general(
        left,
        right,
        (((left_dim,), (right_dim,)), ((), ())),
        precision=precision,
        preferred_element_type=f32,
    )


def params(limit):
    return pltpu.CompilerParams(vmem_limit_bytes=limit * mib)


def cost(flops, moved):
    return pl.CostEstimate(flops=flops, bytes_accessed=moved, transcendentals=0)


def in_hbm(value):
    return pltpu.with_memory_space_constraint(value, pltpu.HBM)


def in_vmem(value):
    return pltpu.with_memory_space_constraint(value, pltpu.VMEM)


def parity():
    return lax.rem(lax.axis_index("replica"), 2)


def half_at(which, size):
    return pl.ds(pl.multiple_of(which * size, size), size)


def load(source, target, sem):
    copy = pltpu.make_async_copy(source, target, sem)
    copy.start()
    return copy


def split_norm(total):
    high = total.astype(bf16)
    low = (total - high.astype(f32)).astype(bf16)
    return jnp.concatenate([high, low], axis=0)


def join_norm(pair):
    rows = pair.shape[0] // 2
    return pair[:rows].astype(f32) + pair[rows:].astype(f32)


def project_half(
    which, fac_q_h, fac_o_h, grad_q, error_q, grad_o, error_o, mat_q, mat_o, store,
    fac_q, fac_o, grad_q_v, error_q_v, grad_o_v, error_o_v, sems,
):
    half_q, half_o = mat_q.shape[0], mat_o.shape[0]
    jobs = []
    fac_copies = [load(fac_q_h, fac_q, sems.at[0]), load(fac_o_h, fac_o, sems.at[1])]
    chunks_q, chunks_o = 4, 2
    rows_q, rows_o = half_q // chunks_q, half_o // chunks_o
    slot = 2
    for chunk in range(chunks_q):
        part = pl.ds(chunk * rows_q, rows_q)
        there = pl.ds(pl.multiple_of(which * half_q + chunk * rows_q, rows_q), rows_q)
        jobs.append((grad_q_v, error_q_v, mat_q, fac_q, part, chunk * rows_q, (
            load(grad_q.at[there], grad_q_v.at[part], sems.at[slot]),
            load(error_q.at[there], error_q_v.at[part], sems.at[slot + 1]),
        )))
        slot += 2
        if chunk % 2 == 0:
            continue
        chunk = chunk // 2
        part = pl.ds(chunk * rows_o, rows_o)
        there = pl.ds(pl.multiple_of(which * half_o + chunk * rows_o, rows_o), rows_o)
        jobs.append((grad_o_v, error_o_v, mat_o, fac_o, part, half_q + chunk * rows_o, (
            load(grad_o.at[there], grad_o_v.at[part], sems.at[slot]),
            load(error_o.at[there], error_o_v.at[part], sems.at[slot + 1]),
        )))
        slot += 2
    for copy in fac_copies:
        copy.wait()
    for grad_v, error_v, mat, fac, part, column, copies in jobs:
        for copy in copies:
            copy.wait()
        block = (grad_v[part].astype(f32) + error_v[part].astype(f32)).astype(bf16)
        mat[part] = block
        store(column, dot(fac[...], block, 1, 1))


def far_kernel(
    fac_q_h, fac_o_h, norm_grads, grad_q, error_q, grad_o, error_o,
    mat_q, mat_o, send, norm_near, norm_rows, *scratch
):
    far = 1 - parity()
    values = norm_grads[0].astype(f32)
    rows = norm_rows.shape[0]
    for row in range(rows):
        norm_rows[row:row + 1, :] = values[:, row * lanes:(row + 1) * lanes]
    half = rows // 2
    norm_near[...] = norm_rows[half_at(1 - far, half), :]
    columns = mat_q.shape[0] + mat_o.shape[0]
    given = norm_rows[half_at(far, half), :]
    send[:, columns:] = jnp.concatenate([given, jnp.zeros_like(given)], axis=0).astype(bf16)

    def store(column, value):
        send[:, column:column + value.shape[1]] = value.astype(bf16)

    project_half(
        far, fac_q_h, fac_o_h, grad_q, error_q, grad_o, error_o, mat_q, mat_o, store, *scratch
    )


def near_kernel(
    fac_q_h, fac_o_h, grad_q, error_q, grad_o, error_o, mat_q, mat_o, part, *scratch
):
    def store(column, value):
        part[:, column:column + value.shape[1]] = value

    project_half(
        parity(), fac_q_h, fac_o_h, grad_q, error_q, grad_o, error_o, mat_q, mat_o, store, *scratch
    )


def project(grad_q, error_q, grad_o, error_o, fac_q, fac_o, norm_grads):
    rank = fac_q.shape[0]
    half_q = (grad_q.shape[0] // 2, grad_q.shape[1])
    half_o = (grad_o.shape[0] // 2, grad_o.shape[1])
    columns = half_q[0] + half_o[0]
    norm_rows = norm_grads.size // lanes
    mats = (pltpu.VMEM(half_q, bf16), pltpu.VMEM(half_o, bf16))
    scratch = [
        pltpu.VMEM(fac_q.shape, bf16),
        pltpu.VMEM(fac_o.shape, bf16),
        pltpu.VMEM(half_q, bf16),
        pltpu.VMEM(half_q, bf16),
        pltpu.VMEM(half_o, bf16),
        pltpu.VMEM(half_o, bf16),
        pltpu.SemaphoreType.DMA((14,)),
    ]
    big = [in_hbm(value) for value in (grad_q, error_q, grad_o, error_o)]
    facs = [in_hbm(fac_q), in_hbm(fac_o)]
    effort = cost(2 * rank * (grad_q.size + grad_o.size) // 2, 4 * grad_q.size)
    mat_q_far, mat_o_far, send, norm_near = pl.pallas_call(
        far_kernel,
        out_shape=mats + (
            jax.ShapeDtypeStruct((rank, columns + lanes), bf16),
            jax.ShapeDtypeStruct((norm_rows // 2, lanes), f32),
        ),
        in_specs=[in_place] * 2 + [whole] + [in_place] * 4,
        out_specs=(whole,) * 4,
        scratch_shapes=[pltpu.VMEM((norm_rows, lanes), f32)] + scratch,
        compiler_params=params(16),
        cost_estimate=effort,
        name="project_far",
    )(*facs, in_hbm(norm_grads), *big)
    mat_q_near, mat_o_near, part = pl.pallas_call(
        near_kernel,
        out_shape=mats + (jax.ShapeDtypeStruct((rank, columns), f32),),
        in_specs=[in_place] * 6,
        out_specs=(whole,) * 3,
        scratch_shapes=scratch,
        compiler_params=params(16),
        cost_estimate=effort,
        name="project_near",
    )(*facs, *big)
    return mat_q_far, mat_o_far, send, norm_near, mat_q_near, mat_o_near, part


def first_sum_kernel(part, norm_near, got, state):
    columns = part.shape[1]
    state[:, :columns] = (part[...] + got[:, :columns].astype(f32)).astype(bf16)
    rows = norm_near.shape[0]
    state[:, columns:] = split_norm(norm_near[...] + got[:rows, columns:].astype(f32))


def first_sum(part, norm_near, got):
    return pl.pallas_call(
        first_sum_kernel,
        out_shape=jax.ShapeDtypeStruct(got.shape, bf16),
        in_specs=[whole] * 3,
        out_specs=whole,
        compiler_params=params(8),
        name="first_sum",
    )(part, norm_near, got)


def norm_sum_kernel(mine, got, state):
    columns = mine.shape[1] - lanes
    state[:, :columns] = (
        mine[:, :columns].astype(f32) + got[:, :columns].astype(f32)
    ).astype(bf16)
    state[:, columns:] = split_norm(join_norm(mine[:, columns:]) + join_norm(got[:, columns:]))


def plain_sum_kernel(mine, got, state):
    state[...] = (mine[...].astype(f32) + got[...].astype(f32)).astype(bf16)


def pair_sum(kernel, mine, got, name):
    return pl.pallas_call(
        kernel,
        out_shape=jax.ShapeDtypeStruct(got.shape, bf16),
        in_specs=[whole] * 2,
        out_specs=whole,
        compiler_params=params(8),
        name=name,
    )(mine, got)


def hat_kernel(size_q, mine, got, ginv_q, ginv_o, state):
    columns = mine.shape[1] - lanes
    total = mine[:, :columns].astype(f32) + got[:, :columns].astype(f32)
    highest = lax.Precision.HIGHEST
    state[:, :size_q] = dot(ginv_q[...].T, total[:, :size_q], 1, 0, highest).astype(bf16)
    state[:, size_q:columns] = dot(ginv_o[...].T, total[:, size_q:], 1, 0, highest).astype(bf16)
    state[:, columns:] = split_norm(join_norm(mine[:, columns:]) + join_norm(got[:, columns:]))


def hats(mine, got, ginv_q, ginv_o, size_q):
    return pl.pallas_call(
        functools.partial(hat_kernel, size_q),
        out_shape=jax.ShapeDtypeStruct(got.shape, bf16),
        in_specs=[whole] * 4,
        out_specs=whole,
        compiler_params=params(8),
        name="hats",
    )(mine, got, ginv_q, ginv_o)


def right_near_kernel(hat, mat_q, mat_o, part_q, part_o):
    size_q, size_o = mat_q.shape[0], mat_o.shape[0]
    part_q[...] = dot(hat[:, :size_q], mat_q[...], 1, 0)
    part_o[...] = dot(hat[:, size_q:size_q + size_o], mat_o[...], 1, 0)


def right_near(hat, mat_q, mat_o):
    rank = hat.shape[0]
    return pl.pallas_call(
        right_near_kernel,
        out_shape=(
            jax.ShapeDtypeStruct((rank, mat_q.shape[1]), f32),
            jax.ShapeDtypeStruct((rank, mat_o.shape[1]), f32),
        ),
        in_specs=[whole] * 3,
        out_specs=(whole,) * 2,
        compiler_params=params(8),
        cost_estimate=cost(2 * rank * (mat_q.size + mat_o.size), 2 * (mat_q.size + mat_o.size)),
        name="right_near",
    )(hat, in_vmem(mat_q), in_vmem(mat_o))


def right_far_kernel(hat, mat_q, mat_o, part_q, part_o, hat_near, send, near, norm, all_q, all_o):
    size_q, size_o = mat_q.shape[0], mat_o.shape[0]
    all_q[...] = part_q[...] + dot(hat[:, :size_q], mat_q[...], 1, 0)
    all_o[...] = part_o[...] + dot(hat[:, size_q:size_q + size_o], mat_o[...], 1, 0)
    mine = parity()
    half_q, half_o = all_q.shape[1] // 2, all_o.shape[1] // 2
    send[:, :half_q] = all_q[:, half_at(1 - mine, half_q)].astype(bf16)
    send[:, half_q:] = all_o[:, half_at(1 - mine, half_o)].astype(bf16)
    near[:, :half_q] = all_q[:, half_at(mine, half_q)]
    near[:, half_q:] = all_o[:, half_at(mine, half_o)]
    columns = size_q + size_o
    half = norm.shape[0] // 2
    norm[half_at(mine, half), :] = join_norm(hat_near[:, columns:])
    norm[half_at(1 - mine, half), :] = join_norm(hat[:, columns:])


def right_far(hat, mat_q, mat_o, part_q, part_o, hat_near, norm_rows):
    rank = hat.shape[0]
    columns = (mat_q.shape[1] + mat_o.shape[1]) // 2
    return pl.pallas_call(
        right_far_kernel,
        out_shape=(
            jax.ShapeDtypeStruct((rank, columns), bf16),
            jax.ShapeDtypeStruct((rank, columns), f32),
            jax.ShapeDtypeStruct((norm_rows, lanes), f32),
        ),
        in_specs=[whole] * 6,
        out_specs=(whole,) * 3,
        scratch_shapes=[pltpu.VMEM(part_q.shape, f32), pltpu.VMEM(part_o.shape, f32)],
        compiler_params=params(8),
        cost_estimate=cost(2 * rank * (mat_q.size + mat_o.size), 2 * (mat_q.size + mat_o.size)),
        name="right_far",
    )(hat, in_vmem(mat_q), in_vmem(mat_o), part_q, part_o, hat_near)


def near_sum_kernel(near, got, norm, state, norm_out):
    state[...] = (near[...] + got[...].astype(f32)).astype(bf16)
    norm_out[...] = norm[...]


def near_sum(near, got, norm):
    return pl.pallas_call(
        near_sum_kernel,
        out_shape=(
            jax.ShapeDtypeStruct(got.shape, bf16),
            jax.ShapeDtypeStruct(norm.shape, f32),
        ),
        in_specs=[whole] * 3,
        out_specs=(whole,) * 2,
        compiler_params=params(8),
        name="near_sum",
    )(near, got, norm)


def mean_kernel(count, mine, got, state):
    state[...] = ((mine[...].astype(f32) + got[...].astype(f32)) / count).astype(bf16)


def error_columns(column, hat, hat_row, half, mat_q, mat_o, new, error_q, error_o, stage_q, stage_o, sems, slot):
    size_q, size_o = mat_q.shape[0], mat_o.shape[0]
    wide_q, wide_o = stage_q.shape[1], stage_o.shape[1]
    copies = []
    chunk_q, chunk_o = size_q // 2, size_o // 2
    cols_q, cols_o = half_at(column, wide_q), half_at(column, wide_o)
    for chunk in range(2):
        part = pl.ds(chunk * chunk_q, chunk_q)
        stage = pl.ds(hat_row * size_q + chunk * chunk_q, chunk_q)
        approx = dot(hat[:, part], new[:, :wide_q], 0, 0)
        stage_q[stage] = (mat_q[part, cols_q].astype(f32) - approx).astype(bf16)
        there = pl.ds(pl.multiple_of(half * size_q + chunk * chunk_q, chunk_q), chunk_q)
        copies.append(load(stage_q.at[stage], error_q.at[there, cols_q], sems.at[slot]))
        part = pl.ds(chunk * chunk_o, chunk_o)
        stage = pl.ds(hat_row * size_o + chunk * chunk_o, chunk_o)
        approx = dot(hat[:, size_q + chunk * chunk_o:size_q + (chunk + 1) * chunk_o], new[:, wide_q:], 0, 0)
        stage_o[stage] = (mat_o[part, cols_o].astype(f32) - approx).astype(bf16)
        there = pl.ds(pl.multiple_of(half * size_o + chunk * chunk_o, chunk_o), chunk_o)
        copies.append(load(stage_o.at[stage], error_o.at[there, cols_o], sems.at[slot + 1]))
        slot += 2
    return copies


def finish_near_kernel(
    hat_near, hat_far, mat_q_near, mat_o_near, mat_q_far, mat_o_far, new,
    error_q, error_o, stage_q, stage_o, sems
):
    mine = parity()
    copies = error_columns(
        mine, hat_near, 0, mine, mat_q_near, mat_o_near, new, error_q, error_o, stage_q, stage_o, sems, 0
    ) + error_columns(
        mine, hat_far, 1, 1 - mine, mat_q_far, mat_o_far, new, error_q, error_o, stage_q, stage_o, sems, 4
    )
    for copy in copies:
        copy.wait()


def piece_of(near, far, index, count, pieces):
    half = count // 2
    size = pieces.shape[2]
    here = index // half == parity()
    chosen = jnp.where(here, near.astype(f32), far.astype(f32))
    for slot in range(half):
        pieces[slot] = chosen[:, slot * size:(slot + 1) * size]
    return pieces[lax.rem(index, half)].astype(bf16)


def finish_far_kernel(
    count, hat_near, hat_far, mat_q_near, mat_o_near, mat_q_far, mat_o_far, new_near, new_far,
    error_q_in, error_o_in, weight_q, momentum_q, weight_o, momentum_o,
    error_q, error_o, new_q, new_o, momentum_q_new, weight_q_new, momentum_o_new, weight_o_new,
    stage_q, stage_o, weight_q_v, momentum_q_v, weight_o_v, momentum_o_v, pieces_q, pieces_o,
    sems, in_sems, out_sems
):
    mine = parity()
    me = lax.axis_index("replica")
    loads = [
        load(source, target, in_sems.at[slot])
        for slot, (source, target) in enumerate((
            (weight_q, weight_q_v), (momentum_q, momentum_q_v),
            (weight_o, weight_o_v), (momentum_o, momentum_o_v),
        ))
    ]
    wide_q, wide_o = stage_q.shape[1], stage_o.shape[1]
    size_q = mat_q_near.shape[0]
    size_o = mat_o_near.shape[0]
    new_q[:, half_at(mine, wide_q)] = new_near[:, :wide_q]
    new_q[:, half_at(1 - mine, wide_q)] = new_far[:, :wide_q]
    new_o[:, half_at(mine, wide_o)] = new_near[:, wide_q:]
    new_o[:, half_at(1 - mine, wide_o)] = new_far[:, wide_q:]
    copies = error_columns(
        1 - mine, hat_near, 0, mine, mat_q_near, mat_o_near, new_far,
        error_q, error_o, stage_q, stage_o, sems, 0
    ) + error_columns(
        1 - mine, hat_far, 1, 1 - mine, mat_q_far, mat_o_far, new_far,
        error_q, error_o, stage_q, stage_o, sems, 4
    )
    hat_piece = piece_of(hat_near[:, :size_q], hat_far[:, :size_q], me, count, pieces_q)
    new_piece = piece_of(new_near[:, wide_q:], new_far[:, wide_q:], me, count, pieces_o)
    for copy in loads:
        copy.wait()
    moved = momentum_decay * momentum_q_v[...] + dot(hat_piece, new_q[...], 0, 0)
    momentum_q_v[...] = moved
    weight_q_v[...] = weight_q_v[...] - step_size * moved
    copies.append(load(momentum_q_v, momentum_q_new, out_sems.at[0]))
    copies.append(load(weight_q_v, weight_q_new, out_sems.at[1]))
    half = mine * size_o
    rows = pl.ds(pl.multiple_of(half, size_o), size_o)
    moved = momentum_decay * momentum_o_v[rows] + dot(
        hat_near[:, size_q:size_q + size_o], new_piece, 0, 0
    )
    momentum_o_v[rows] = moved
    weight_o_v[rows] = weight_o_v[rows] - step_size * moved
    rows = pl.ds(pl.multiple_of((1 - mine) * size_o, size_o), size_o)
    moved = momentum_decay * momentum_o_v[rows] + dot(
        hat_far[:, size_q:size_q + size_o], new_piece, 0, 0
    )
    momentum_o_v[rows] = moved
    weight_o_v[rows] = weight_o_v[rows] - step_size * moved
    copies.append(load(momentum_o_v, momentum_o_new, out_sems.at[2]))
    copies.append(load(weight_o_v, weight_o_new, out_sems.at[3]))
    for copy in copies:
        copy.wait()


def finish(
    count, hat_near, hat_far, mats, new_near, send_far, weight_q, momentum_q, weight_o, momentum_o
):
    mat_q, mat_o = mats[0], mats[1]
    rank = hat_near.shape[0]
    size_q, size_o = mat_q.shape[0], mat_o.shape[0]
    error_q = jax.ShapeDtypeStruct((2 * size_q, mat_q.shape[1]), bf16)
    error_o = jax.ShapeDtypeStruct((2 * size_o, mat_o.shape[1]), bf16)
    stages = [
        pltpu.VMEM((2 * size_q, mat_q.shape[1] // 2), bf16),
        pltpu.VMEM((2 * size_o, mat_o.shape[1] // 2), bf16),
    ]
    moved = 4 * (mat_q.size + mat_o.size)
    mats = [in_vmem(mat) for mat in mats]
    new_far = send_far(new_near)
    error_q_part, error_o_part = pl.pallas_call(
        finish_near_kernel,
        out_shape=(error_q, error_o),
        in_specs=[whole] * 7,
        out_specs=(in_place,) * 2,
        scratch_shapes=stages + [pltpu.SemaphoreType.DMA((8,))],
        compiler_params=params(12),
        cost_estimate=cost(2 * rank * (mat_q.size + mat_o.size), moved),
        name="finish_near",
    )(hat_near, hat_far, *mats, new_near)
    piece_q = weight_q.shape[0]
    piece_o = weight_o.shape[1]
    return pl.pallas_call(
        functools.partial(finish_far_kernel, count),
        out_shape=(
            error_q,
            error_o,
            jax.ShapeDtypeStruct((rank, mat_q.shape[1]), bf16),
            jax.ShapeDtypeStruct((rank, mat_o.shape[1]), bf16),
            jax.ShapeDtypeStruct(weight_q.shape, f32),
            jax.ShapeDtypeStruct(weight_q.shape, f32),
            jax.ShapeDtypeStruct(weight_o.shape, f32),
            jax.ShapeDtypeStruct(weight_o.shape, f32),
        ),
        in_specs=[whole] * 8 + [in_place] * 6,
        out_specs=(in_place, in_place, whole, whole) + (in_place,) * 4,
        scratch_shapes=stages + [
            pltpu.VMEM(weight_q.shape, f32),
            pltpu.VMEM(weight_q.shape, f32),
            pltpu.VMEM(weight_o.shape, f32),
            pltpu.VMEM(weight_o.shape, f32),
            pltpu.VMEM((count // 2, rank, piece_q), f32),
            pltpu.VMEM((count // 2, rank, piece_o), f32),
            pltpu.SemaphoreType.DMA((8,)),
            pltpu.SemaphoreType.DMA((4,)),
            pltpu.SemaphoreType.DMA((4,)),
        ],
        input_output_aliases={8: 0, 9: 1},
        compiler_params=params(16),
        cost_estimate=cost(2 * rank * (mat_q.size + mat_o.size), moved),
        name="finish_far",
    )(
        hat_near, hat_far, *mats, new_near, new_far, error_q_part, error_o_part,
        in_hbm(weight_q), in_hbm(momentum_q), in_hbm(weight_o), in_hbm(momentum_o),
    )


def norm_mean_kernel(count, *refs):
    total = refs[0][...]
    for ref in refs[1:-1]:
        total = total + ref[...]
    refs[-1][...] = total / count


def swap(value, bit):
    count = lax.axis_size("replica")
    return lax.ppermute(value, "replica", [(source, source ^ bit) for source in range(count)])


def on_device(
    grad_q,
    error_q,
    qfac_q,
    ginv_q,
    weight_q,
    momentum_q,
    grad_o,
    error_o,
    qfac_o,
    ginv_o,
    weight_o,
    momentum_o,
    norm_grads,
):
    replicas = lax.axis_size("replica")
    tensors = lax.axis_size("tensor")
    bits = [1 << place for place in range(1, replicas.bit_length() - 1)]
    half_q = grad_q.shape[0] // 2
    norm_rows = norm_grads.size // lanes
    mat_q_far, mat_o_far, send, norm_near, mat_q_near, mat_o_near, part = project(
        grad_q, error_q, grad_o, error_o, qfac_q.T, qfac_o.T, norm_grads
    )
    state = first_sum(part, norm_near, swap(send, 1))
    for bit in bits[:-1]:
        state = pair_sum(norm_sum_kernel, state, swap(state, bit), "norm_sum")
    hat_near = hats(state, swap(state, bits[-1]), ginv_q, ginv_o, half_q)
    hat_far = swap(hat_near, 1)
    part_q, part_o = right_near(hat_near, mat_q_near, mat_o_near)
    send, near, norm = right_far(
        hat_far, mat_q_far, mat_o_far, part_q, part_o, hat_near, norm_rows
    )
    state, norm = near_sum(near, swap(send, 1), norm)
    norms = [norm]
    for step in range(1, tensors):
        pairs = [(source, (source + step) % tensors) for source in range(tensors)]
        norms.append(lax.ppermute(norm, "tensor", pairs))
    for bit in bits[:-1]:
        state = pair_sum(plain_sum_kernel, state, swap(state, bit), "plain_sum")
    new_near = pair_sum(
        functools.partial(mean_kernel, replicas), state, swap(state, bits[-1]), "mean"
    )
    (
        error_q_new, error_o_new, new_q, new_o,
        momentum_q_new, weight_q_new, momentum_o_new, weight_o_new,
    ) = finish(
        replicas, hat_near, hat_far, (mat_q_near, mat_o_near, mat_q_far, mat_o_far),
        new_near, lambda value: swap(value, 1), weight_q, momentum_q, weight_o, momentum_o,
    )
    norm_mean = pl.pallas_call(
        functools.partial(norm_mean_kernel, replicas * tensors),
        out_shape=jax.ShapeDtypeStruct(norm.shape, f32),
        in_specs=[whole] * tensors,
        out_specs=whole,
        compiler_params=params(4),
        name="norm_mean",
    )(*norms)
    return (
        error_q_new,
        new_q.T,
        momentum_q_new,
        weight_q_new,
        error_o_new,
        new_o.T,
        momentum_o_new,
        weight_o_new,
        norm_mean.reshape(-1),
    )


def solution(mesh):
    in_specs = (
        P("replica", "tensor"),
        P("replica", "tensor"),
        P("tensor", None),
        P("tensor", None),
        P("replica", "tensor"),
        P("replica", "tensor"),
        P(("replica", "tensor"), None),
        P(("replica", "tensor"), None),
        P("tensor", None),
        P("tensor", None),
        P("tensor", "replica"),
        P("tensor", "replica"),
        P("replica", "tensor", None),
    )
    out_specs = (
        P("replica", "tensor"),
        P("tensor", None),
        P("replica", "tensor"),
        P("replica", "tensor"),
        P(("replica", "tensor"), None),
        P("tensor", None),
        P("tensor", "replica"),
        P("tensor", "replica"),
        P(),
    )
    return jax.shard_map(
        on_device, mesh=mesh, in_specs=in_specs, out_specs=out_specs, check_vma=False
    )
```

time: 194 us -> 54.8 us (0.28)
  waiting for transfers between devices: 116 us -> 21.5 us
  blocking collectives: 40 us -> 0 us
  matrix products: 18.7 us -> 0 us
  starting transfers between devices: 0.08 us -> 16.6 us
  Pallas kernels: 0 us -> 15.7 us
  between operations: 14.3 us -> 0.73 us
  other arithmetic: 3.76 us -> 0 us
    psum x2 -> x0, waiting for transfers between devices: 116 us -> none  [the longest x1 86.6 us: on_device(): sum_q, sum_o = lax.psum((p_q, p_o), 'replica')]
    psum x1 -> x0, blocking collectives: 40 us -> none  [on_device(): norm_total = lax.psum(norm_part, ('replica', 'tensor'))]
    ppermute x0 -> x11, waiting for transfers between devices: none -> 21.5 us  [the longest x8 18.6 us: swap(): lax.ppermute(value, 'replica', [(source, source ^ bit) for source in rang...]
    dot_general x8 -> x0, matrix products: 18.7 us -> none  [the longest x2 5.46 us: left_factor(): return jnp.dot(matrix, factor, preferred_element_type=jnp.float32)]
    ppermute x0 -> x11, starting transfers between devices: none -> 16.6 us  [the longest x8 14.9 us: swap(): lax.ppermute(value, 'replica', [(source, source ^ bit) for source in rang...]
    pallas_call x0 -> x13, Pallas kernels: none -> 15.7 us  [the longest x1 5.04 us: finish(): pl.pallas_call(functools.partial(finish_far_kernel, count), out_shape=(er...]
    sub x2 -> x0, other arithmetic: 2.27 us -> none  [the longest x1 1.14 us: on_device(): weight_q_new = weight_q - step_size * momentum_q_new]
  transfers between devices with their start and end apart: 2 -> 11, of which waited for: 2 -> 8; matrix products, arithmetic and copies ran while one was open for 0% -> 0% of each run, Pallas kernels for 0% -> 11%
where the time goes in v3:
time: 54.8 us; the launch traced here: 54.5 us
  waiting for transfers between devices  21.5 us (39%)
  starting transfers between devices  16.6 us (30%)
  Pallas kernels  15.7 us (29%)
  between operations  0.73 us (1%)
    ppermute x8, waiting for transfers between devices, swap(): lax.ppermute(value, 'replica', [(source, source ^ bit) for source in rang...  18.6 us
    ppermute x8, starting transfers between devices, swap(): lax.ppermute(value, 'replica', [(source, source ^ bit) for source in rang...  14.9 us
    pallas_call x1, Pallas kernels, finish(): pl.pallas_call(functools.partial(finish_far_kernel, count), out_shape=(er...  5.04 us
    pallas_call x1, Pallas kernels, project(): pl.pallas_call(far_kernel, out_shape=mats + (jax.ShapeDtypeStruct((rank,...  3.82 us
    pallas_call x1, Pallas kernels, project(): pl.pallas_call(near_kernel, out_shape=mats + (jax.ShapeDtypeStruct((rank,...  3.08 us
    ppermute x3, waiting for transfers between devices, on_device(): norms.append(lax.ppermute(norm, 'tensor', pairs))  2.94 us
    ppermute x3, starting transfers between devices, on_device(): norms.append(lax.ppermute(norm, 'tensor', pairs))  1.72 us
    pallas_call x1, Pallas kernels, finish(): pl.pallas_call(finish_near_kernel, out_shape=(error_q, error_o), in_specs...  1.72 us
  transfers between devices with their start and end apart: 11, of which 8 were waited for; matrix products, arithmetic and copies ran while one was open for 0% of the time, Pallas kernels for 11%

profile of v3, /device:TPU:0, one launch (start us, length us, event | category | flops | bytes accessed | tf_op | source)
XLA Modules:
  0.0 54.5 jit_solution(6226693237016108727)
XLA Ops:
  0.6 3.8 %project_far.1 = (bf16[1024,512]{1,0:T(8,128)(2,1)S(1)}, bf16[256,2048]{1,0:T(8,128)(2,1)S(1)}, bf16[32,1408]{1,0:T(8,128)(2,1)S(1)}, f32[16,128]{1,0:T(8,128)S(1)}) custom-call(bf16[32,512]{1,0:T(8,128)(2,1)} %bitcast.7, bf16[32,2048]{1,0:T(8,128)(2,1)} %bitcast.5, bf16[1,1,4096]{2,1,0:T(2,128)(2,1)} %norm_grads.1, bf16[2048,512]{1,0:T(8,128)(2,1)} %grad_q.3, ...), custom_call_target="tpu_custom_call" | custom-call | flops 67108864 | bytes 4194304 | tf_op jit(solution)/shard_map/project_far/pallas_call | solution.py:163
  4.5 3.0 %collective-permute-start = (bf16[32,1408]{1,0:T(8,128)(2,1)S(1)}, bf16[32,1408]{1,0:T(8,128)(2,1)S(1)}, u32[]{:S(2)}, u32[]{:S(2)}) collective-permute-start(bf16[32,1408]{1,0:T(8,128)(2,1)S(1)} %get-tuple-element.35), channel_id=1, source_target_pairs={{0,4},{4,0},{8,12},{12,8},{16,20},{20,16},{24,28},{28,24},{1,5},{5... | collective-permute-start | bytes 270344 | tf_op jit(solution)/shard_map/ppermute | solution.py:506
  7.5 3.1 %project_near.1 = (bf16[1024,512]{1,0:T(8,128)(2,1)S(1)}, bf16[256,2048]{1,0:T(8,128)(2,1)S(1)}, f32[32,1280]{1,0:T(8,128)S(1)}) custom-call(bf16[32,512]{1,0:T(8,128)(2,1)} %bitcast.8, bf16[32,2048]{1,0:T(8,128)(2,1)} %bitcast.6, bf16[2048,512]{1,0:T(8,128)(2,1)} %grad_q.3, bf16[2048,512]{1,0:T(8,128)(2,1)} %error_q.3, bf16[512,2048]{1,0:T(8,128)(2,1)} %grad_o.3, ...), custom_call_target="tpu_custom_call" | custom-call | flops 67108864 | bytes 4194304 | tf_op jit(solution)/shard_map/project_near/pallas_call | solution.py:176
  10.6 1.6 %collective-permute-start.1 = (bf16[32,1408]{1,0:T(8,128)(2,1)S(1)}, bf16[32,1408]{1,0:T(8,128)(2,1)S(1)}, u32[]{:S(2)}, u32[]{:S(2)}) collective-permute-start(bf16[32,1408]{1,0:T(8,128)(2,1)S(1)} %first_sum.1.mine), channel_id=1, source_target_pairs={{0,8},{4,12},{8,0},{12,4},{16,24},{20,28},{24,16},{28,20},{1,9},{5... | collective-permute-start | bytes 270344 | tf_op jit(solution)/shard_map/ppermute | solution.py:506
  12.3 3.0 %collective-permute-done.1.got = bf16[32,1408]{1,0:T(8,128)(2,1)S(1)} collective-permute-done((bf16[32,1408]{1,0:T(8,128)(2,1)S(1)}, bf16[32,1408]{1,0:T(8,128)(2,1)S(1)}, u32[]{:S(2)}, u32[]{:S(2)}) %collective-permute-start.1) | collective-permute-done | bytes 90144 | tf_op jit(solution)/shard_map/ppermute | solution.py:506
  15.3 2.7 %collective-permute-start.2 = (bf16[32,1408]{1,0:T(8,128)(2,1)S(1)}, bf16[32,1408]{1,0:T(8,128)(2,1)S(1)}, u32[]{:S(2)}, u32[]{:S(2)}) collective-permute-start(bf16[32,1408]{1,0:T(8,128)(2,1)S(1)} %norm_sum.1.mine), channel_id=1, source_target_pairs={{0,16},{4,20},{8,24},{12,28},{16,0},{20,4},{24,8},{28,12},{1,17},{... | collective-permute-start | bytes 270344 | tf_op jit(solution)/shard_map/ppermute | solution.py:506
  17.9 2.8 %collective-permute-done.2.got = bf16[32,1408]{1,0:T(8,128)(2,1)S(1)} collective-permute-done((bf16[32,1408]{1,0:T(8,128)(2,1)S(1)}, bf16[32,1408]{1,0:T(8,128)(2,1)S(1)}, u32[]{:S(2)}, u32[]{:S(2)}) %collective-permute-start.2) | collective-permute-done | bytes 90144 | tf_op jit(solution)/shard_map/ppermute | solution.py:506
  21.1 1.5 %collective-permute-start.3 = (bf16[32,1408]{1,0:T(8,128)(2,1)S(1)}, bf16[32,1408]{1,0:T(8,128)(2,1)S(1)}, u32[]{:S(2)}, u32[]{:S(2)}) collective-permute-start(bf16[32,1408]{1,0:T(8,128)(2,1)S(1)} %hats.1.hat.hat_near), channel_id=1, source_target_pairs={{0,4},{4,0},{8,12},{12,8},{16,20},{20,16},{24,28},{28,24},{1,5},{5... | collective-permute-start | bytes 270344 | tf_op jit(solution)/shard_map/ppermute | solution.py:506
  22.6 0.5 right_near.1
  23.0 3.4 %collective-permute-done.3.hat.hat_far = bf16[32,1408]{1,0:T(8,128)(2,1)S(1)} collective-permute-done((bf16[32,1408]{1,0:T(8,128)(2,1)S(1)}, bf16[32,1408]{1,0:T(8,128)(2,1)S(1)}, u32[]{:S(2)}, u32[]{:S(2)}) %collective-permute-start.3) | collective-permute-done | bytes 90144 | tf_op jit(solution)/shard_map/ppermute | solution.py:506
  26.4 0.5 right_far.1
  26.9 1.0 %collective-permute-start.4 = (bf16[32,1280]{1,0:T(8,128)(2,1)S(1)}, bf16[32,1280]{1,0:T(8,128)(2,1)S(1)}, u32[]{:S(2)}, u32[]{:S(2)}) collective-permute-start(bf16[32,1280]{1,0:T(8,128)(2,1)S(1)} %get-tuple-element.43), channel_id=1, source_target_pairs={{0,4},{4,0},{8,12},{12,8},{16,20},{20,16},{24,28},{28,24},{1,5},{5... | collective-permute-start | bytes 245768 | tf_op jit(solution)/shard_map/ppermute | solution.py:506
  27.9 3.5 %collective-permute-done.4.got = bf16[32,1280]{1,0:T(8,128)(2,1)S(1)} collective-permute-done((bf16[32,1280]{1,0:T(8,128)(2,1)S(1)}, bf16[32,1280]{1,0:T(8,128)(2,1)S(1)}, u32[]{:S(2)}, u32[]{:S(2)}) %collective-permute-start.4) | collective-permute-done | bytes 81952 | tf_op jit(solution)/shard_map/ppermute | solution.py:506
  31.5 1.5 %collective-permute-start.5 = (bf16[32,1280]{1,0:T(8,128)(2,1)S(1)}, bf16[32,1280]{1,0:T(8,128)(2,1)S(1)}, u32[]{:S(2)}, u32[]{:S(2)}) collective-permute-start(bf16[32,1280]{1,0:T(8,128)(2,1)S(1)} %get-tuple-element.45.mine), channel_id=1, source_target_pairs={{0,8},{4,12},{8,0},{12,4},{16,24},{20,28},{24,16},{28,20},{1,9},{5... | collective-permute-start | bytes 245768 | tf_op jit(solution)/shard_map/ppermute | solution.py:506
  32.9 3.3 %collective-permute-done.5.got = bf16[32,1280]{1,0:T(8,128)(2,1)S(1)} collective-permute-done((bf16[32,1280]{1,0:T(8,128)(2,1)S(1)}, bf16[32,1280]{1,0:T(8,128)(2,1)S(1)}, u32[]{:S(2)}, u32[]{:S(2)}) %collective-permute-start.5) | collective-permute-done | bytes 81952 | tf_op jit(solution)/shard_map/ppermute | solution.py:506
  36.2 2.8 %collective-permute-start.6 = (bf16[32,1280]{1,0:T(8,128)(2,1)S(1)}, bf16[32,1280]{1,0:T(8,128)(2,1)S(1)}, u32[]{:S(2)}, u32[]{:S(2)}) collective-permute-start(bf16[32,1280]{1,0:T(8,128)(2,1)S(1)} %plain_sum.1.mine), channel_id=1, source_target_pairs={{0,16},{4,20},{8,24},{12,28},{16,0},{20,4},{24,8},{28,12},{1,17},{... | collective-permute-start | bytes 245768 | tf_op jit(solution)/shard_map/ppermute | solution.py:506
  39.0 2.6 %collective-permute-done.6.got = bf16[32,1280]{1,0:T(8,128)(2,1)S(1)} collective-permute-done((bf16[32,1280]{1,0:T(8,128)(2,1)S(1)}, bf16[32,1280]{1,0:T(8,128)(2,1)S(1)}, u32[]{:S(2)}, u32[]{:S(2)}) %collective-permute-start.6) | collective-permute-done | bytes 81952 | tf_op jit(solution)/shard_map/ppermute | solution.py:506
  41.7 0.8 %collective-permute-start.7 = (bf16[32,1280]{1,0:T(8,128)(2,1)S(1)}, bf16[32,1280]{1,0:T(8,128)(2,1)S(1)}, u32[]{:S(2)}, u32[]{:S(2)}) collective-permute-start(bf16[32,1280]{1,0:T(8,128)(2,1)S(1)} %mean.1.new.new_near), channel_id=1, source_target_pairs={{0,4},{4,0},{8,12},{12,8},{16,20},{20,16},{24,28},{28,24},{1,5},{5... | collective-permute-start | bytes 245768 | tf_op jit(solution)/shard_map/ppermute | solution.py:506
  42.5 1.5 %collective-permute-start.9 = (f32[32,128]{1,0:T(8,128)S(1)}, f32[32,128]{1,0:T(8,128)S(1)}, u32[]{:S(2)}, u32[]{:S(2)}) collective-permute-start(f32[32,128]{1,0:T(8,128)S(1)} %get-tuple-element.56.refs_0_), channel_id=1, source_target_pairs={{0,2},{1,3},{2,0},{3,1},{4,6},{5,7},{6,4},{7,5},{8,10},{9,11},{10,... | collective-permute-start | bytes 49160 | tf_op jit(solution)/shard_map/ppermute | solution.py:545
  44.2 2.0 %collective-permute-done.9.refs_2_ = f32[32,128]{1,0:T(8,128)S(1)} collective-permute-done((f32[32,128]{1,0:T(8,128)S(1)}, f32[32,128]{1,0:T(8,128)S(1)}, u32[]{:S(2)}, u32[]{:S(2)}) %collective-permute-start.9) | collective-permute-done | bytes 16416 | tf_op jit(solution)/shard_map/ppermute | solution.py:545
  46.2 0.9 %collective-permute-done.8.refs_1_ = f32[32,128]{1,0:T(8,128)S(1)} collective-permute-done((f32[32,128]{1,0:T(8,128)S(1)}, f32[32,128]{1,0:T(8,128)S(1)}, u32[]{:S(2)}, u32[]{:S(2)}) %collective-permute-start.8) | collective-permute-done | bytes 16416 | tf_op jit(solution)/shard_map/ppermute | solution.py:545
  47.1 0.6 %norm_mean.1 = f32[32,128]{1,0:T(8,128)} custom-call(f32[32,128]{1,0:T(8,128)S(1)} %get-tuple-element.56.refs_0_, f32[32,128]{1,0:T(8,128)S(1)} %collective-permute-done.8.refs_1_, f32[32,128]{1,0:T(8,128)S(1)} %collective-permute-done.9.refs_2_, f32[32,128]{1,0:T(8,128)S(1)} %collective-permute-done.10.refs_3_), custom_call_target="tpu_custom_call" | custom-call | tf_op jit(solution)/shard_map/norm_mean/pallas_call | solution.py:558
  47.8 1.7 %finish_near.1 = (bf16[2048,512]{1,0:T(8,128)(2,1)}, bf16[512,2048]{1,0:T(8,128)(2,1)}) custom-call(bf16[32,1408]{1,0:T(8,128)(2,1)S(1)} %hats.1.hat.hat_near, bf16[32,1408]{1,0:T(8,128)(2,1)S(1)} %collective-permute-done.3.hat.hat_far, bf16[1024,512]{1,0:T(8,128)(2,1)S(1)} %get-tuple-element.36.mat_q.mat_q_near, ...), custom_call_target="tpu_custom_call" | custom-call | flops 67108864 | bytes 4194304 | tf_op jit(solution)/shard_map/finish_near/pallas_call | solution.py:450
  49.5 5.0 %finish_far.1 = (bf16[2048,512]{1,0:T(8,128)(2,1)}, bf16[512,2048]{1,0:T(8,128)(2,1)}, bf16[32,512]{1,0:T(8,128)(2,1)}, bf16[32,2048]{1,0:T(8,128)(2,1)}, f32[25...) custom-call(bf16[32,1408]{1,0:T(8,128)(2,1)S(1)} %hats.1.hat.hat_nea, ...), custom_call_target="tpu_custom_call", output_to_operand_aliasing={{0}: (8, {}), {1}: (9, {})} | custom-call | flops 67108864 | bytes 4194304 | tf_op jit(solution)/shard_map/finish_far/pallas_call | solution.py:462
  (15 shorter events, 0.7 us)
Async XLA Ops:
  4.5 16.3 %copy-start = (f32[32,32]{1,0:T(8,128)S(1)}, f32[32,32]{1,0:T(8,128)}, u32[]{:S(2)}) copy-start(f32[32,32]{1,0:T(8,128)} %ginv_q.1) | copy-start | bytes 12292
  4.5 16.3 %copy-start.1 = (f32[32,32]{1,0:T(8,128)S(1)}, f32[32,32]{1,0:T(8,128)}, u32[]{:S(2)}) copy-start(f32[32,32]{1,0:T(8,128)} %ginv_o.1) | copy-start | bytes 12292
  4.5 6.1 %collective-permute-start = (bf16[32,1408]{1,0:T(8,128)(2,1)S(1)}, bf16[32,1408]{1,0:T(8,128)(2,1)S(1)}, u32[]{:S(2)}, u32[]{:S(2)}) collective-permute-start(bf16[32,1408]{1,0:T(8,128)(2,1)S(1)} %get-tuple-element.35), channel_id=1, source_target_pairs={{0,4},{4,0},{8,12},{12,8},{16,20},{20,16},{24,28},{28,24},{1,5},{5... | collective-permute-start | bytes 270344 | tf_op jit(solution)/shard_map/ppermute | solution.py:506
  10.6 4.6 %collective-permute-start.1 = (bf16[32,1408]{1,0:T(8,128)(2,1)S(1)}, bf16[32,1408]{1,0:T(8,128)(2,1)S(1)}, u32[]{:S(2)}, u32[]{:S(2)}) collective-permute-start(bf16[32,1408]{1,0:T(8,128)(2,1)S(1)} %first_sum.1.mine), channel_id=1, source_target_pairs={{0,8},{4,12},{8,0},{12,4},{16,24},{20,28},{24,16},{28,20},{1,9},{5... | collective-permute-start | bytes 270344 | tf_op jit(solution)/shard_map/ppermute | solution.py:506
  15.3 5.5 %collective-permute-start.2 = (bf16[32,1408]{1,0:T(8,128)(2,1)S(1)}, bf16[32,1408]{1,0:T(8,128)(2,1)S(1)}, u32[]{:S(2)}, u32[]{:S(2)}) collective-permute-start(bf16[32,1408]{1,0:T(8,128)(2,1)S(1)} %norm_sum.1.mine), channel_id=1, source_target_pairs={{0,16},{4,20},{8,24},{12,28},{16,0},{20,4},{24,8},{28,12},{1,17},{... | collective-permute-start | bytes 270344 | tf_op jit(solution)/shard_map/ppermute | solution.py:506
  21.1 5.3 %collective-permute-start.3 = (bf16[32,1408]{1,0:T(8,128)(2,1)S(1)}, bf16[32,1408]{1,0:T(8,128)(2,1)S(1)}, u32[]{:S(2)}, u32[]{:S(2)}) collective-permute-start(bf16[32,1408]{1,0:T(8,128)(2,1)S(1)} %hats.1.hat.hat_near), channel_id=1, source_target_pairs={{0,4},{4,0},{8,12},{12,8},{16,20},{20,16},{24,28},{28,24},{1,5},{5... | collective-permute-start | bytes 270344 | tf_op jit(solution)/shard_map/ppermute | solution.py:506
  26.9 4.5 %collective-permute-start.4 = (bf16[32,1280]{1,0:T(8,128)(2,1)S(1)}, bf16[32,1280]{1,0:T(8,128)(2,1)S(1)}, u32[]{:S(2)}, u32[]{:S(2)}) collective-permute-start(bf16[32,1280]{1,0:T(8,128)(2,1)S(1)} %get-tuple-element.43), channel_id=1, source_target_pairs={{0,4},{4,0},{8,12},{12,8},{16,20},{20,16},{24,28},{28,24},{1,5},{5... | collective-permute-start | bytes 245768 | tf_op jit(solution)/shard_map/ppermute | solution.py:506
  31.5 4.7 %collective-permute-start.5 = (bf16[32,1280]{1,0:T(8,128)(2,1)S(1)}, bf16[32,1280]{1,0:T(8,128)(2,1)S(1)}, u32[]{:S(2)}, u32[]{:S(2)}) collective-permute-start(bf16[32,1280]{1,0:T(8,128)(2,1)S(1)} %get-tuple-element.45.mine), channel_id=1, source_target_pairs={{0,8},{4,12},{8,0},{12,4},{16,24},{20,28},{24,16},{28,20},{1,9},{5... | collective-permute-start | bytes 245768 | tf_op jit(solution)/shard_map/ppermute | solution.py:506
  36.2 5.4 %collective-permute-start.6 = (bf16[32,1280]{1,0:T(8,128)(2,1)S(1)}, bf16[32,1280]{1,0:T(8,128)(2,1)S(1)}, u32[]{:S(2)}, u32[]{:S(2)}) collective-permute-start(bf16[32,1280]{1,0:T(8,128)(2,1)S(1)} %plain_sum.1.mine), channel_id=1, source_target_pairs={{0,16},{4,20},{8,24},{12,28},{16,0},{20,4},{24,8},{28,12},{1,17},{... | collective-permute-start | bytes 245768 | tf_op jit(solution)/shard_map/ppermute | solution.py:506
  41.7 7.8 %collective-permute-start.7 = (bf16[32,1280]{1,0:T(8,128)(2,1)S(1)}, bf16[32,1280]{1,0:T(8,128)(2,1)S(1)}, u32[]{:S(2)}, u32[]{:S(2)}) collective-permute-start(bf16[32,1280]{1,0:T(8,128)(2,1)S(1)} %mean.1.new.new_near), channel_id=1, source_target_pairs={{0,4},{4,0},{8,12},{12,8},{16,20},{20,16},{24,28},{28,24},{1,5},{5... | collective-permute-start | bytes 245768 | tf_op jit(solution)/shard_map/ppermute | solution.py:506
  42.5 1.7 %collective-permute-start.10 = (f32[32,128]{1,0:T(8,128)S(1)}, f32[32,128]{1,0:T(8,128)S(1)}, u32[]{:S(2)}, u32[]{:S(2)}) collective-permute-start(f32[32,128]{1,0:T(8,128)S(1)} %get-tuple-element.56.refs_0_), channel_id=1, source_target_pairs={{0,3},{1,0},{2,1},{3,2},{4,7},{5,4},{6,5},{7,6},{8,11},{9,8},{10,9... | collective-permute-start | bytes 49160 | tf_op jit(solution)/shard_map/ppermute | solution.py:545
  42.5 3.7 %collective-permute-start.9 = (f32[32,128]{1,0:T(8,128)S(1)}, f32[32,128]{1,0:T(8,128)S(1)}, u32[]{:S(2)}, u32[]{:S(2)}) collective-permute-start(f32[32,128]{1,0:T(8,128)S(1)} %get-tuple-element.56.refs_0_), channel_id=1, source_target_pairs={{0,2},{1,3},{2,0},{3,1},{4,6},{5,7},{6,4},{7,5},{8,10},{9,11},{10,... | collective-permute-start | bytes 49160 | tf_op jit(solution)/shard_map/ppermute | solution.py:545
  44.0 3.2 %collective-permute-start.8 = (f32[32,128]{1,0:T(8,128)S(1)}, f32[32,128]{1,0:T(8,128)S(1)}, u32[]{:S(2)}, u32[]{:S(2)}) collective-permute-start(f32[32,128]{1,0:T(8,128)S(1)} %get-tuple-element.56.refs_0_), channel_id=1, source_target_pairs={{0,1},{1,2},{2,3},{3,0},{4,5},{5,6},{6,7},{7,4},{8,9},{9,10},{10,1... | collective-permute-start | bytes 49160 | tf_op jit(solution)/shard_map/ppermute | solution.py:545

commit v4 on v0

v4 whole, which is shorter than its diff:
```python
import functools

import jax
import jax.numpy as jnp
from jax import lax
from jax.experimental import pallas as pl
from jax.experimental.pallas import tpu as pltpu
from jax.sharding import PartitionSpec as P

momentum_decay = 0.9
step_size = 0.5
lanes = 128
mib = 1024 * 1024
bf16 = jnp.bfloat16
f32 = jnp.float32

whole = pl.BlockSpec(memory_space=pltpu.VMEM)
in_place = pl.BlockSpec(memory_space=pl.ANY)


def dot(left, right, left_dim, right_dim, precision=None):
    return lax.dot_general(
        left,
        right,
        (((left_dim,), (right_dim,)), ((), ())),
        precision=precision,
        preferred_element_type=f32,
    )


def params(limit):
    return pltpu.CompilerParams(vmem_limit_bytes=limit * mib)


brief = pl.CostEstimate(flops=1, bytes_accessed=1, transcendentals=0)


def in_hbm(value):
    return pltpu.with_memory_space_constraint(value, pltpu.HBM)


def in_vmem(value):
    return pltpu.with_memory_space_constraint(value, pltpu.VMEM)


def launch(kernel, operands, after=(), **options):
    count = len(operands)
    specs = options.pop("in_specs")

    def body(*refs):
        kernel(*refs[:count], *refs[count + len(after):])

    return pl.pallas_call(
        body, in_specs=list(specs) + [in_place] * len(after), cost_estimate=brief, **options
    )(
        *operands, *after
    )


def shaped(shape, dtype):
    return jax.ShapeDtypeStruct(shape, dtype)


def parity():
    return lax.rem(lax.axis_index("replica"), 2)


def half_at(which, size):
    return pl.ds(pl.multiple_of(which * size, size), size)


def load(source, target, sem):
    copy = pltpu.make_async_copy(source, target, sem)
    copy.start()
    return copy


def split_norm(total):
    high = total.astype(bf16)
    low = (total - high.astype(f32)).astype(bf16)
    return jnp.concatenate([high, low], axis=0)


def join_norm(pair):
    rows = pair.shape[0] // 2
    return pair[:rows].astype(f32) + pair[rows:].astype(f32)


def project_half(which, chunks, fac_h, grad, error, mat, store, fac, grad_v, error_v, sems):
    half = mat.shape[0]
    rows = half // chunks
    fac_copy = load(fac_h, fac, sems.at[0])
    jobs = []
    for chunk in range(chunks):
        part = pl.ds(chunk * rows, rows)
        there = pl.ds(pl.multiple_of(which * half + chunk * rows, rows), rows)
        jobs.append((part, chunk * rows, (
            load(grad.at[there], grad_v.at[part], sems.at[1 + 2 * chunk]),
            load(error.at[there], error_v.at[part], sems.at[2 + 2 * chunk]),
        )))
    fac_copy.wait()
    for part, column, copies in jobs:
        for copy in copies:
            copy.wait()
        block = (grad_v[part].astype(f32) + error_v[part].astype(f32)).astype(bf16)
        mat[part] = block
        store(column, dot(fac[...], block, 1, 1))


def far_kernel(chunks, fac_h, grad, error, mat, send, *scratch):
    def store(column, value):
        send[:, column:column + value.shape[1]] = value.astype(bf16)

    project_half(1 - parity(), chunks, fac_h, grad, error, mat, store, *scratch)


def far_norm_kernel(
    chunks, fac_h, grad, error, norm_grads, mat, send, norm_near, norm_rows, *scratch
):
    far = 1 - parity()
    values = norm_grads[0].astype(f32)
    rows = norm_rows.shape[0]
    for row in range(rows):
        norm_rows[row:row + 1, :] = values[:, row * lanes:(row + 1) * lanes]
    half = rows // 2
    norm_near[...] = norm_rows[half_at(1 - far, half), :]
    given = norm_rows[half_at(far, half), :]
    send[:, mat.shape[0]:] = jnp.concatenate([given, jnp.zeros_like(given)], axis=0).astype(bf16)
    far_kernel(chunks, fac_h, grad, error, mat, send, *scratch)


def near_kernel(chunks, fac_h, grad, error, mat, part, *scratch):
    def store(column, value):
        part[:, column:column + value.shape[1]] = value

    project_half(parity(), chunks, fac_h, grad, error, mat, store, *scratch)


def project(kernel, chunks, name, grad, error, fac, outs, norm=(), after=()):
    half = (grad.shape[0] // 2, grad.shape[1])
    rank = fac.shape[0]
    scratch = [
        pltpu.VMEM(fac.shape, bf16),
        pltpu.VMEM(half, bf16),
        pltpu.VMEM(half, bf16),
        pltpu.SemaphoreType.DMA((1 + 2 * chunks,)),
    ]
    if norm:
        scratch = [pltpu.VMEM((norm[0].size // lanes, lanes), f32)] + scratch
    return launch(
        functools.partial(kernel, chunks),
        (in_hbm(fac), in_hbm(grad), in_hbm(error), *norm),
        after,
        out_shape=(pltpu.VMEM(half, bf16),) + outs,
        in_specs=[in_place] * 3 + [whole] * len(norm),
        out_specs=(whole,) * (1 + len(outs)),
        scratch_shapes=scratch,
        compiler_params=params(12),
        name=name,
    )


def small(kernel, name, outs, *operands, after=()):
    return launch(
        kernel,
        operands,
        after,
        out_shape=outs,
        in_specs=[whole] * len(operands),
        out_specs=(whole,) * len(outs) if isinstance(outs, tuple) else whole,
        compiler_params=params(8),
        name=name,
    )


def first_sum_kernel(part, got, state):
    state[...] = (part[...] + got[...].astype(f32)).astype(bf16)


def first_norm_sum_kernel(part, norm_near, got, state):
    columns = part.shape[1]
    state[:, :columns] = (part[...] + got[:, :columns].astype(f32)).astype(bf16)
    rows = norm_near.shape[0]
    state[:, columns:] = split_norm(norm_near[...] + got[:rows, columns:].astype(f32))


def sum_kernel(mine, got, state):
    state[...] = (mine[...].astype(f32) + got[...].astype(f32)).astype(bf16)


def norm_sum_kernel(mine, got, state):
    columns = mine.shape[1] - lanes
    state[:, :columns] = (
        mine[:, :columns].astype(f32) + got[:, :columns].astype(f32)
    ).astype(bf16)
    state[:, columns:] = split_norm(join_norm(mine[:, columns:]) + join_norm(got[:, columns:]))


def hat_kernel(columns, mine, got, ginv, state):
    total = mine[:, :columns].astype(f32) + got[:, :columns].astype(f32)
    state[:, :columns] = dot(
        ginv[...].T, total, 1, 0, lax.Precision.HIGHEST
    ).astype(bf16)
    if columns < mine.shape[1]:
        state[:, columns:] = split_norm(join_norm(mine[:, columns:]) + join_norm(got[:, columns:]))


def mean_kernel(count, mine, got, state):
    state[...] = ((mine[...].astype(f32) + got[...].astype(f32)) / count).astype(bf16)


def right_near_kernel(hat, mat, part):
    part[...] = dot(hat[:, :mat.shape[0]], mat[...], 1, 0)


def right_near(name, hat, mat, after=()):
    rank = hat.shape[0]
    return launch(
        right_near_kernel,
        (hat, in_vmem(mat)),
        after,
        out_shape=shaped((rank, mat.shape[1]), f32),
        in_specs=[whole] * 2,
        out_specs=whole,
        compiler_params=params(8),
        name=name,
    )


def right_far_kernel(hat, mat, part, send, near, full):
    full[...] = part[...] + dot(hat[:, :mat.shape[0]], mat[...], 1, 0)
    mine = parity()
    half = full.shape[1] // 2
    send[...] = full[:, half_at(1 - mine, half)].astype(bf16)
    near[...] = full[:, half_at(mine, half)]


def right_far(name, hat, mat, part, after=()):
    rank = hat.shape[0]
    half = mat.shape[1] // 2
    return launch(
        right_far_kernel,
        (hat, in_vmem(mat), part),
        after,
        out_shape=(shaped((rank, half), bf16), shaped((rank, half), f32)),
        in_specs=[whole] * 3,
        out_specs=(whole,) * 2,
        scratch_shapes=[pltpu.VMEM(part.shape, f32)],
        compiler_params=params(8),
        name=name,
    )


def norm_join_kernel(columns, hat_near, hat_far, norm):
    half = norm.shape[0] // 2
    mine = parity()
    norm[half_at(mine, half), :] = join_norm(hat_near[:, columns:])
    norm[half_at(1 - mine, half), :] = join_norm(hat_far[:, columns:])


def norm_add_kernel(count, mine, got, total):
    total[...] = (mine[...] + got[...]) / count


def error_columns(chunks, column, hat, hat_row, half, mat, new, error, stage, sems, slot):
    size = mat.shape[0]
    rows = size // chunks
    columns = half_at(column, stage.shape[1])
    copies = []
    for chunk in range(chunks):
        part = pl.ds(chunk * rows, rows)
        staged = pl.ds(hat_row * size + chunk * rows, rows)
        approx = dot(hat[:, part], new[...], 0, 0)
        stage[staged] = (mat[part, columns].astype(f32) - approx).astype(bf16)
        there = pl.ds(pl.multiple_of(half * size + chunk * rows, rows), rows)
        copies.append(load(stage.at[staged], error.at[there, columns], sems.at[slot + chunk]))
    return copies


def finish_near_kernel(chunks, hat_near, hat_far, mat_near, mat_far, new, error, stage, sems):
    mine = parity()
    copies = error_columns(
        chunks, mine, hat_near, 0, mine, mat_near, new, error, stage, sems, 0
    ) + error_columns(
        chunks, mine, hat_far, 1, 1 - mine, mat_far, new, error, stage, sems, chunks
    )
    for copy in copies:
        copy.wait()


def piece_of(near, far, width, size, index, count, pieces):
    half = count // 2
    here = index // half == parity()
    slot = lax.rem(index, half)
    if size % lanes == 0:
        part = half_at(slot, size)
        return jnp.where(here, near[:, part].astype(f32), far[:, part].astype(f32)).astype(bf16)
    chosen = jnp.where(here, near[:, :width].astype(f32), far[:, :width].astype(f32))
    for place in range(half):
        pieces[place] = chosen[:, place * size:(place + 1) * size]
    return pieces[slot].astype(bf16)


def finish_far_kernel(
    chunks, count, by_rows, hat_near, hat_far, mat_near, mat_far, new_near, new_far, error_in,
    weight_v, momentum_v, error, new, momentum_new, weight_new,
    stage, moved_v, stepped_v, pieces, sems, out_sems
):
    mine = parity()
    me = lax.axis_index("replica")
    wide = stage.shape[1]
    size = mat_near.shape[0]
    new[:, half_at(mine, wide)] = new_near[...]
    new[:, half_at(1 - mine, wide)] = new_far[...]
    if by_rows:
        piece = piece_of(hat_near, hat_far, size, weight_v.shape[0], me, count, pieces)
        moved = momentum_decay * momentum_v[...] + dot(piece, new[...], 0, 0)
        moved_v[...] = moved
        stepped_v[...] = weight_v[...] - step_size * moved
    else:
        piece = piece_of(new_near, new_far, wide, weight_v.shape[1], me, count, pieces)
        for which, hat in ((mine, hat_near), (1 - mine, hat_far)):
            rows = half_at(which, size)
            moved = momentum_decay * momentum_v[rows] + dot(hat[:, :size], piece, 0, 0)
            moved_v[rows] = moved
            stepped_v[rows] = weight_v[rows] - step_size * moved
    copies = [
        load(moved_v, momentum_new, out_sems.at[0]),
        load(stepped_v, weight_new, out_sems.at[1]),
    ]
    copies += error_columns(
        chunks, 1 - mine, hat_near, 0, mine, mat_near, new_far, error, stage, sems, 0
    ) + error_columns(
        chunks, 1 - mine, hat_far, 1, 1 - mine, mat_far, new_far, error, stage, sems, chunks
    )
    for copy in copies:
        copy.wait()


def finish_near(name, chunks, hat_near, hat_far, mat_near, mat_far, new_near, after=()):
    size, width = mat_near.shape
    return launch(
        functools.partial(finish_near_kernel, chunks),
        (hat_near, hat_far, in_vmem(mat_near), in_vmem(mat_far), new_near),
        after,
        out_shape=shaped((2 * size, width), bf16),
        in_specs=[whole] * 5,
        out_specs=in_place,
        scratch_shapes=[
            pltpu.VMEM((2 * size, width // 2), bf16),
            pltpu.SemaphoreType.DMA((2 * chunks,)),
        ],
        compiler_params=params(12),
        name=name,
    )


def finish_far(
    name, chunks, count, by_rows,
    hat_near, hat_far, mat_near, mat_far, new_near, new_far, error, weight_v, momentum_v, after=()
):
    size, width = mat_near.shape
    rank = hat_near.shape[0]
    weight = weight_v.shape
    piece = weight[0] if by_rows else weight[1]
    return launch(
        functools.partial(finish_far_kernel, chunks, count, by_rows),
        (
            hat_near, hat_far, in_vmem(mat_near), in_vmem(mat_far), new_near, new_far, error,
            in_vmem(weight_v), in_vmem(momentum_v),
        ),
        after,
        out_shape=(
            shaped((2 * size, width), bf16),
            shaped((rank, width), bf16),
            shaped(weight, f32),
            shaped(weight, f32),
        ),
        in_specs=[whole] * 6 + [in_place] + [whole] * 2,
        out_specs=(in_place, whole, in_place, in_place),
        scratch_shapes=[
            pltpu.VMEM((2 * size, width // 2), bf16),
            pltpu.VMEM(weight, f32),
            pltpu.VMEM(weight, f32),
            pltpu.VMEM((count // 2, rank, piece), f32),
            pltpu.SemaphoreType.DMA((2 * chunks,)),
            pltpu.SemaphoreType.DMA((2,)),
        ],
        input_output_aliases={6: 0},
        compiler_params=params(16),
        name=name,
    )


def swap(value, bit, axis="replica"):
    count = lax.axis_size(axis)
    return lax.ppermute(value, axis, [(source, source ^ bit) for source in range(count)])


def bits_of(count):
    return [1 << place for place in range(1, count.bit_length() - 1)]


def on_device(
    grad_q,
    error_q,
    qfac_q,
    ginv_q,
    weight_q,
    momentum_q,
    grad_o,
    error_o,
    qfac_o,
    ginv_o,
    weight_o,
    momentum_o,
    norm_grads,
):
    replicas = lax.axis_size("replica")
    tensors = lax.axis_size("tensor")
    rank = qfac_q.shape[1]
    half_q = grad_q.shape[0] // 2
    half_o = grad_o.shape[0] // 2
    norm_rows = norm_grads.size // lanes
    fac_q, fac_o = qfac_q.T, qfac_o.T
    wide_q = (rank, half_q)
    wide_o = (rank, half_o + lanes)
    mat_q_far, send_q = project(
        far_kernel, 4, "project_far_q", grad_q, error_q, fac_q, (shaped(wide_q, bf16),)
    )
    got_q = swap(send_q, 1)
    mat_o_far, send_o, norm_near = project(
        far_norm_kernel, 2, "project_far_o", grad_o, error_o, fac_o,
        (shaped(wide_o, bf16), shaped((norm_rows // 2, lanes), f32)), (in_hbm(norm_grads),),
    )
    got_o = swap(send_o, 1)
    mat_q_near, part_q = project(
        near_kernel, 4, "project_near_q", grad_q, error_q, fac_q, (shaped(wide_q, f32),),
    )
    state_q = small(first_sum_kernel, "first_sum_q", shaped(wide_q, bf16), part_q, got_q)
    mat_o_near, part_o = project(
        near_kernel, 2, "project_near_o", grad_o, error_o, fac_o, (shaped((rank, half_o), f32),),
    )
    state_o = small(
        first_norm_sum_kernel, "first_sum_o", shaped(wide_o, bf16), part_o, norm_near, got_o
    )
    bits = bits_of(replicas)
    for bit in bits[:-1]:
        got_q = swap(state_q, bit)
        got_o = swap(state_o, bit)
        state_q = small(
            sum_kernel, "sum_q", shaped(wide_q, bf16), state_q, got_q
        )
        state_o = small(
            norm_sum_kernel, "sum_o", shaped(wide_o, bf16), state_o, got_o
        )
    got_q = swap(state_q, bits[-1])
    got_o = swap(state_o, bits[-1])
    hat_q = small(
        functools.partial(hat_kernel, half_q), "hat_q", shaped(wide_q, bf16),
        state_q, got_q, ginv_q,
    )
    hat_q_far = swap(hat_q, 1)
    part_q = right_near("right_near_q", hat_q, mat_q_near)
    hat_o = small(
        functools.partial(hat_kernel, half_o), "hat_o", shaped(wide_o, bf16),
        state_o, got_o, ginv_o,
    )
    hat_o_far = swap(hat_o, 1)
    part_o = right_near("right_near_o", hat_o, mat_o_near)
    send_q, near_q = right_far("right_far_q", hat_q_far, mat_q_far, part_q)
    got_q = swap(send_q, 1)
    send_o, near_o = right_far("right_far_o", hat_o_far, mat_o_far, part_o)
    got_o = swap(send_o, 1)
    state_q = small(
        first_sum_kernel, "first_sum_q", shaped(got_q.shape, bf16), near_q, got_q
    )
    state_o = small(
        first_sum_kernel, "first_sum_o", shaped(got_o.shape, bf16), near_o, got_o
    )
    norm = small(
        functools.partial(norm_join_kernel, half_o), "norm_join", shaped((norm_rows, lanes), f32),
        hat_o, hat_o_far, after=(state_o,),
    )
    for bit in bits[:-1]:
        got_q = swap(state_q, bit)
        got_o = swap(state_o, bit)
        state_q = small(
            sum_kernel, "sum_q", shaped(got_q.shape, bf16), state_q, got_q
        )
        state_o = small(
            sum_kernel, "sum_o", shaped(got_o.shape, bf16), state_o, got_o
        )
    got_q = swap(state_q, bits[-1])
    got_o = swap(state_o, bits[-1])
    mean = functools.partial(mean_kernel, replicas)
    new_q = small(mean, "mean_q", shaped(got_q.shape, bf16), state_q, got_q)
    new_q_far = swap(new_q, 1)
    chain_q = (hat_q, hat_q_far, mat_q_near, mat_q_far, new_q)
    error_q_part = finish_near("finish_near_q", 2, *chain_q)
    new_o = small(mean, "mean_o", shaped(got_o.shape, bf16), state_o, got_o)
    new_o_far = swap(new_o, 1)
    chain_o = (hat_o, hat_o_far, mat_o_near, mat_o_far, new_o)
    waits = [(state_o,), (new_o,)]
    bit = 1
    while bit < tensors:
        last = 2 * bit >= tensors
        norm = small(
            functools.partial(norm_add_kernel, replicas * tensors if last else 1), "norm_add",
            shaped(norm.shape, f32), norm, swap(norm, bit, "tensor"), after=waits[last],
        )
        bit *= 2
    error_q_new, qfac_q_new, momentum_q_new, weight_q_new = finish_far(
        "finish_far_q", 2, replicas, True, *chain_q, new_q_far, error_q_part,
        weight_q, momentum_q,
    )
    error_o_part = finish_near("finish_near_o", 2, *chain_o)
    error_o_new, qfac_o_new, momentum_o_new, weight_o_new = finish_far(
        "finish_far_o", 2, replicas, False, *chain_o, new_o_far, error_o_part,
        weight_o, momentum_o,
    )
    return (
        error_q_new,
        qfac_q_new.T,
        momentum_q_new,
        weight_q_new,
        error_o_new,
        qfac_o_new.T,
        momentum_o_new,
        weight_o_new,
        norm.reshape(-1),
    )


def solution(mesh):
    in_specs = (
        P("replica", "tensor"),
        P("replica", "tensor"),
        P("tensor", None),
        P("tensor", None),
        P("replica", "tensor"),
        P("replica", "tensor"),
        P(("replica", "tensor"), None),
        P(("replica", "tensor"), None),
        P("tensor", None),
        P("tensor", None),
        P("tensor", "replica"),
        P("tensor", "replica"),
        P("replica", "tensor", None),
    )
    out_specs = (
        P("replica", "tensor"),
        P("tensor", None),
        P("replica", "tensor"),
        P("replica", "tensor"),
        P(("replica", "tensor"), None),
        P("tensor", None),
        P("tensor", "replica"),
        P("tensor", "replica"),
        P(),
    )
    return jax.shard_map(
        on_device, mesh=mesh, in_specs=in_specs, out_specs=out_specs, check_vma=False
    )
```

time: 194 us -> 61.1 us (0.31)
  waiting for transfers between devices: 116 us -> 10.4 us
  blocking collectives: 40 us -> 0 us
  starting transfers between devices: 0.08 us -> 30.7 us
  Pallas kernels: 0 us -> 18.9 us
  matrix products: 18.7 us -> 0 us
  between operations: 14.3 us -> 0.86 us
  other arithmetic: 3.76 us -> 0 us
    psum x2 -> x0, waiting for transfers between devices: 116 us -> none  [the longest x1 86.6 us: on_device(): sum_q, sum_o = lax.psum((p_q, p_o), 'replica')]
    psum x1 -> x0, blocking collectives: 40 us -> none  [on_device(): norm_total = lax.psum(norm_part, ('replica', 'tensor'))]
    ppermute x0 -> x18, starting transfers between devices: none -> 30.7 us  [swap(): lax.ppermute(value, axis, [(source, source ^ bit) for source in range(cou...]
    pallas_call x0 -> x27, Pallas kernels: none -> 18.9 us  [launch(): pl.pallas_call(body, in_specs=list(specs) + [in_place] * len(after), cost...]
    dot_general x8 -> x0, matrix products: 18.7 us -> none  [the longest x2 5.46 us: left_factor(): return jnp.dot(matrix, factor, preferred_element_type=jnp.float32)]
    ppermute x0 -> x18, waiting for transfers between devices: none -> 10.4 us  [swap(): lax.ppermute(value, axis, [(source, source ^ bit) for source in range(cou...]
    sub x2 -> x0, other arithmetic: 2.27 us -> none  [the longest x1 1.14 us: on_device(): weight_q_new = weight_q - step_size * momentum_q_new]
  transfers between devices with their start and end apart: 2 -> 18, of which waited for: 2 -> 8; matrix products, arithmetic and copies ran while one was open for 0% -> 0% of each run, Pallas kernels for 0% -> 23%
where the time goes in v4:
time: 61.1 us; the launch traced here: 60.9 us
  starting transfers between devices  30.7 us (50%)
  Pallas kernels  18.9 us (31%)
  waiting for transfers between devices  10.4 us (17%)
  between operations  0.86 us (1%)
    ppermute x18, starting transfers between devices, swap(): lax.ppermute(value, axis, [(source, source ^ bit) for source in range(cou...  30.7 us
    pallas_call x27, Pallas kernels, launch(): pl.pallas_call(body, in_specs=list(specs) + [in_place] * len(after), cost...  18.9 us
    ppermute x18, waiting for transfers between devices, swap(): lax.ppermute(value, axis, [(source, source ^ bit) for source in range(cou...  10.4 us
  transfers between devices with their start and end apart: 18, of which 8 were waited for; matrix products, arithmetic and copies ran while one was open for 0% of the time, Pallas kernels for 23%

profile of v4, /device:TPU:0, one launch (start us, length us, event | category | flops | bytes accessed | tf_op | source)
XLA Modules:
  0.0 60.9 jit_solution(4535214169906805085)
XLA Ops:
  0.6 2.8 %project_far_o.1 = (bf16[256,2048]{1,0:T(8,128)(2,1)S(1)}, bf16[32,384]{1,0:T(8,128)(2,1)S(1)}, f32[16,128]{1,0:T(8,128)S(1)}) custom-call(bf16[32,2048]{1,0:T(8,128)(2,1)} %bitcast.5, bf16[512,2048]{1,0:T(8,128)(2,1)} %refs_1_.7, bf16[512,2048]{1,0:T(8,128)(2,1)} %refs_2_.10, bf16[1,1,4096]{2,1,0:T(2,128)(2,1)} %refs_3_.1), custom_call_target="tpu_custom_call" | custom-call | flops 1 | bytes 1 | tf_op jit(solution)/shard_map/project_far_o/pallas_call | solution.py:53
  3.5 3.0 %collective-permute-start.8 = (bf16[32,384]{1,0:T(8,128)(2,1)S(1)}, bf16[32,384]{1,0:T(8,128)(2,1)S(1)}, u32[]{:S(2)}, u32[]{:S(2)}) collective-permute-start(bf16[32,384]{1,0:T(8,128)(2,1)S(1)} %get-tuple-element.42), channel_id=1, source_target_pairs={{0,4},{4,0},{8,12},{12,8},{16,20},{20,16},{24,28},{28,24},{1,5},{5... | collective-permute-start | bytes 73736 | tf_op jit(solution)/shard_map/ppermute | solution.py:397
  6.5 2.1 %project_near_o.1 = (bf16[256,2048]{1,0:T(8,128)(2,1)S(1)}, f32[32,256]{1,0:T(8,128)S(1)}) custom-call(bf16[32,2048]{1,0:T(8,128)(2,1)} %bitcast.6, bf16[512,2048]{1,0:T(8,128)(2,1)} %refs_1_.7, bf16[512,2048]{1,0:T(8,128)(2,1)} %refs_2_.10), custom_call_target="tpu_custom_call" | custom-call | flops 1 | bytes 1 | tf_op jit(solution)/shard_map/project_near_o/pallas_call | solution.py:53
  8.7 1.8 %collective-permute-start.9 = (bf16[32,384]{1,0:T(8,128)(2,1)S(1)}, bf16[32,384]{1,0:T(8,128)(2,1)S(1)}, u32[]{:S(2)}, u32[]{:S(2)}) collective-permute-start(bf16[32,384]{1,0:T(8,128)(2,1)S(1)} %first_sum_o.2.refs_0_), channel_id=1, source_target_pairs={{0,8},{4,12},{8,0},{12,4},{16,24},{20,28},{24,16},{28,20},{1,9},{5... | collective-permute-start | bytes 73736 | tf_op jit(solution)/shard_map/ppermute | solution.py:397
  10.5 2.2 %project_far_q.1 = (bf16[1024,512]{1,0:T(8,128)(2,1)S(1)}, bf16[32,1024]{1,0:T(8,128)(2,1)S(1)}) custom-call(bf16[32,512]{1,0:T(8,128)(2,1)} %bitcast.7, bf16[2048,512]{1,0:T(8,128)(2,1)} %refs_1_.5, bf16[2048,512]{1,0:T(8,128)(2,1)} %refs_2_.7), custom_call_target="tpu_custom_call" | custom-call | flops 1 | bytes 1 | tf_op jit(solution)/shard_map/project_far_q/pallas_call | solution.py:53
  12.7 1.6 %collective-permute-start = (bf16[32,1024]{1,0:T(8,128)(2,1)S(1)}, bf16[32,1024]{1,0:T(8,128)(2,1)S(1)}, u32[]{:S(2)}, u32[]{:S(2)}) collective-permute-start(bf16[32,1024]{1,0:T(8,128)(2,1)S(1)} %get-tuple-element.31), channel_id=1, source_target_pairs={{0,4},{4,0},{8,12},{12,8},{16,20},{20,16},{24,28},{28,24},{1,5},{5... | collective-permute-start | bytes 196616 | tf_op jit(solution)/shard_map/ppermute | solution.py:397
  14.3 2.7 %collective-permute-start.10 = (bf16[32,384]{1,0:T(8,128)(2,1)S(1)}, bf16[32,384]{1,0:T(8,128)(2,1)S(1)}, u32[]{:S(2)}, u32[]{:S(2)}) collective-permute-start(bf16[32,384]{1,0:T(8,128)(2,1)S(1)} %sum_o.2.refs_0_), channel_id=1, source_target_pairs={{0,16},{4,20},{8,24},{12,28},{16,0},{20,4},{24,8},{28,12},{1,17},{... | collective-permute-start | bytes 73736 | tf_op jit(solution)/shard_map/ppermute | solution.py:397
  16.9 2.3 %collective-permute-done.10.refs_1_ = bf16[32,384]{1,0:T(8,128)(2,1)S(1)} collective-permute-done((bf16[32,384]{1,0:T(8,128)(2,1)S(1)}, bf16[32,384]{1,0:T(8,128)(2,1)S(1)}, u32[]{:S(2)}, u32[]{:S(2)}) %collective-permute-start.10) | collective-permute-done | bytes 24608 | tf_op jit(solution)/shard_map/ppermute | solution.py:397
  19.8 2.2 %project_near_q.1 = (bf16[1024,512]{1,0:T(8,128)(2,1)S(1)}, f32[32,1024]{1,0:T(8,128)S(1)}) custom-call(bf16[32,512]{1,0:T(8,128)(2,1)} %bitcast.8, bf16[2048,512]{1,0:T(8,128)(2,1)} %refs_1_.5, bf16[2048,512]{1,0:T(8,128)(2,1)} %refs_2_.7), custom_call_target="tpu_custom_call" | custom-call | flops 1 | bytes 1 | tf_op jit(solution)/shard_map/project_near_q/pallas_call | solution.py:53
  22.0 1.1 %collective-permute-start.1 = (bf16[32,1024]{1,0:T(8,128)(2,1)S(1)}, bf16[32,1024]{1,0:T(8,128)(2,1)S(1)}, u32[]{:S(2)}, u32[]{:S(2)}) collective-permute-start(bf16[32,1024]{1,0:T(8,128)(2,1)S(1)} %first_sum_q.2.refs_0_), channel_id=1, source_target_pairs={{0,8},{4,12},{8,0},{12,4},{16,24},{20,28},{24,16},{28,20},{1,9},{5... | collective-permute-start | bytes 196616 | tf_op jit(solution)/shard_map/ppermute | solution.py:397
  24.8 1.6 %collective-permute-done.1.refs_1_ = bf16[32,1024]{1,0:T(8,128)(2,1)S(1)} collective-permute-done((bf16[32,1024]{1,0:T(8,128)(2,1)S(1)}, bf16[32,1024]{1,0:T(8,128)(2,1)S(1)}, u32[]{:S(2)}, u32[]{:S(2)}) %collective-permute-start.1) | collective-permute-done | bytes 65568 | tf_op jit(solution)/shard_map/ppermute | solution.py:397
  26.4 2.7 %collective-permute-start.2 = (bf16[32,1024]{1,0:T(8,128)(2,1)S(1)}, bf16[32,1024]{1,0:T(8,128)(2,1)S(1)}, u32[]{:S(2)}, u32[]{:S(2)}) collective-permute-start(bf16[32,1024]{1,0:T(8,128)(2,1)S(1)} %sum_q.2.refs_0_), channel_id=1, source_target_pairs={{0,16},{4,20},{8,24},{12,28},{16,0},{20,4},{24,8},{28,12},{1,17},{... | collective-permute-start | bytes 196616 | tf_op jit(solution)/shard_map/ppermute | solution.py:397
  29.2 2.0 %collective-permute-start.13 = (bf16[32,1024]{1,0:T(8,128)(2,1)S(1)}, bf16[32,1024]{1,0:T(8,128)(2,1)S(1)}, u32[]{:S(2)}, u32[]{:S(2)}) collective-permute-start(bf16[32,1024]{1,0:T(8,128)(2,1)S(1)} %first_sum_o.3.refs_0_.refs_2_), channel_id=1, source_target_pairs={{0,8},{4,12},{8,0},{12,4},{16,24},{20,28},{24,16},{28,20},{1,9},{5... | collective-permute-start | bytes 196616 | tf_op jit(solution)/shard_map/ppermute | solution.py:397
  31.9 4.2 %collective-permute-start.3 = (bf16[32,1024]{1,0:T(8,128)(2,1)S(1)}, bf16[32,1024]{1,0:T(8,128)(2,1)S(1)}, u32[]{:S(2)}, u32[]{:S(2)}) collective-permute-start(bf16[32,1024]{1,0:T(8,128)(2,1)S(1)} %hat_q.1.refs_0_), channel_id=1, source_target_pairs={{0,4},{4,0},{8,12},{12,8},{16,20},{20,16},{24,28},{28,24},{1,5},{5... | collective-permute-start | bytes 196616 | tf_op jit(solution)/shard_map/ppermute | solution.py:397
  37.2 1.2 %collective-permute-done.3.refs_0_.refs_1_ = bf16[32,1024]{1,0:T(8,128)(2,1)S(1)} collective-permute-done((bf16[32,1024]{1,0:T(8,128)(2,1)S(1)}, bf16[32,1024]{1,0:T(8,128)(2,1)S(1)}, u32[]{:S(2)}, u32[]{:S(2)}) %collective-permute-start.3) | collective-permute-done | bytes 65568 | tf_op jit(solution)/shard_map/ppermute | solution.py:397
  38.7 2.1 %collective-permute-start.4 = (bf16[32,256]{1,0:T(8,128)(2,1)S(1)}, bf16[32,256]{1,0:T(8,128)(2,1)S(1)}, u32[]{:S(2)}, u32[]{:S(2)}) collective-permute-start(bf16[32,256]{1,0:T(8,128)(2,1)S(1)} %get-tuple-element.35), channel_id=1, source_target_pairs={{0,4},{4,0},{8,12},{12,8},{16,20},{20,16},{24,28},{28,24},{1,5},{5... | collective-permute-start | bytes 49160 | tf_op jit(solution)/shard_map/ppermute | solution.py:397
  43.3 3.0 %collective-permute-done.5.refs_1_ = bf16[32,256]{1,0:T(8,128)(2,1)S(1)} collective-permute-done((bf16[32,256]{1,0:T(8,128)(2,1)S(1)}, bf16[32,256]{1,0:T(8,128)(2,1)S(1)}, u32[]{:S(2)}, u32[]{:S(2)}) %collective-permute-start.5) | collective-permute-done | bytes 16416 | tf_op jit(solution)/shard_map/ppermute | solution.py:397
  46.3 2.0 %collective-permute-start.6 = (bf16[32,256]{1,0:T(8,128)(2,1)S(1)}, bf16[32,256]{1,0:T(8,128)(2,1)S(1)}, u32[]{:S(2)}, u32[]{:S(2)}) collective-permute-start(bf16[32,256]{1,0:T(8,128)(2,1)S(1)} %sum_q.3.refs_0_), channel_id=1, source_target_pairs={{0,16},{4,20},{8,24},{12,28},{16,0},{20,4},{24,8},{28,12},{1,17},{... | collective-permute-start | bytes 49160 | tf_op jit(solution)/shard_map/ppermute | solution.py:397
  48.3 1.5 %collective-permute-start.17 = (f32[32,128]{1,0:T(8,128)S(1)}, f32[32,128]{1,0:T(8,128)S(1)}, u32[]{:S(2)}, u32[]{:S(2)}) collective-permute-start(f32[32,128]{1,0:T(8,128)S(1)} %norm_add.2.refs_0_), channel_id=1, source_target_pairs={{0,2},{1,3},{2,0},{3,1},{4,6},{5,7},{6,4},{7,5},{8,10},{9,11},{10,... | collective-permute-start | bytes 49160 | tf_op jit(solution)/shard_map/ppermute | solution.py:397
  50.9 2.0 %collective-permute-start.7 = (bf16[32,256]{1,0:T(8,128)(2,1)S(1)}, bf16[32,256]{1,0:T(8,128)(2,1)S(1)}, u32[]{:S(2)}, u32[]{:S(2)}) collective-permute-start(bf16[32,256]{1,0:T(8,128)(2,1)S(1)} %mean_q.1.refs_4_), channel_id=1, source_target_pairs={{0,4},{4,0},{8,12},{12,8},{16,20},{20,16},{24,28},{28,24},{1,5},{5... | collective-permute-start | bytes 49160 | tf_op jit(solution)/shard_map/ppermute | solution.py:397
  53.0 1.2 %finish_near_o.1.refs_6_ = bf16[512,2048]{1,0:T(8,128)(2,1)} custom-call(bf16[32,384]{1,0:T(8,128)(2,1)S(1)} %hat_o.1.refs_0_, bf16[32,384]{1,0:T(8,128)(2,1)S(1)} %collective-permute-done.11.refs_0_.refs_1_, bf16[256,2048]{1,0:T(8,128)(2,1)S(1)} %get-tuple-element.43.refs_1_.refs_2_, bf16[256,2048]{1,0:T(8,128)(2,1)S(1)} %get-tuple-element.44.refs_1_.refs_3_, ...), custom_call_target="tpu_custom_call" | custom-call | flops 1 | bytes 1 | tf_op jit(solution)/shard_map/finish_near_o/pallas_call | solution.py:53
  54.9 1.3 %finish_near_q.1.refs_6_ = bf16[2048,512]{1,0:T(8,128)(2,1)} custom-call(bf16[32,1024]{1,0:T(8,128)(2,1)S(1)} %hat_q.1.refs_0_, bf16[32,1024]{1,0:T(8,128)(2,1)S(1)} %collective-permute-done.3.refs_0_.refs_1_, bf16[1024,512]{1,0:T(8,128)(2,1)S(1)} %get-tuple-element.32.refs_1_.refs_2_, bf16[1024,512]{1,0:T(8,128)(2,1)S(1)} %get-tuple-element.33.refs_1_.refs_3_, ...), custom_call_target="tpu_custom_call" | custom-call | flops 1 | bytes 1 | tf_op jit(solution)/shard_map/finish_near_q/pallas_call | solution.py:53
  56.3 2.3 %finish_far_q.1 = (bf16[2048,512]{1,0:T(8,128)(2,1)}, bf16[32,512]{1,0:T(8,128)(2,1)}, f32[256,512]{1,0:T(8,128)}, f32[256,512]{1,0:T(8,128)}) custom-call(bf16[32,1024]{1,0:T(8,128)(2,1)S(1)} %hat_q.1.refs_0_, bf16[32,1024]{1,0:T(8,128)(2,1)S(1)} %collective-permute-done.3.refs_0_.refs_1_, ...), custom_call_target="tpu_custom_call", output_to_operand_aliasing={{0}: (6, {})} | custom-call | flops 1 | bytes 1 | tf_op jit(solution)/shard_map/finish_far_q/pallas_call | solution.py:53
  58.6 2.3 %finish_far_o.1 = (bf16[512,2048]{1,0:T(8,128)(2,1)}, bf16[32,2048]{1,0:T(8,128)(2,1)}, f32[512,256]{1,0:T(8,128)}, f32[512,256]{1,0:T(8,128)}) custom-call(bf16[32,384]{1,0:T(8,128)(2,1)S(1)} %hat_o.1.refs_0_, bf16[32,384]{1,0:T(8,128)(2,1)S(1)} %collective-permute-done.11.refs_0_.refs_1_, ...), custom_call_target="tpu_custom_call", output_to_operand_aliasing={{0}: (6, {})} | custom-call | flops 1 | bytes 1 | tf_op jit(solution)/shard_map/finish_far_o/pallas_call | solution.py:53
  (51 shorter events, 8.7 us)
Async XLA Ops:
  3.5 5.2 %collective-permute-start.8 = (bf16[32,384]{1,0:T(8,128)(2,1)S(1)}, bf16[32,384]{1,0:T(8,128)(2,1)S(1)}, u32[]{:S(2)}, u32[]{:S(2)}) collective-permute-start(bf16[32,384]{1,0:T(8,128)(2,1)S(1)} %get-tuple-element.42), channel_id=1, source_target_pairs={{0,4},{4,0},{8,12},{12,8},{16,20},{20,16},{24,28},{28,24},{1,5},{5... | collective-permute-start | bytes 73736 | tf_op jit(solution)/shard_map/ppermute | solution.py:397
  8.7 5.6 %collective-permute-start.9 = (bf16[32,384]{1,0:T(8,128)(2,1)S(1)}, bf16[32,384]{1,0:T(8,128)(2,1)S(1)}, u32[]{:S(2)}, u32[]{:S(2)}) collective-permute-start(bf16[32,384]{1,0:T(8,128)(2,1)S(1)} %first_sum_o.2.refs_0_), channel_id=1, source_target_pairs={{0,8},{4,12},{8,0},{12,4},{16,24},{20,28},{24,16},{28,20},{1,9},{5... | collective-permute-start | bytes 73736 | tf_op jit(solution)/shard_map/ppermute | solution.py:397
  10.5 8.7 %copy-start.4 = (f32[32,32]{1,0:T(8,128)S(1)}, f32[32,32]{1,0:T(8,128)}, u32[]{:S(2)}) copy-start(f32[32,32]{1,0:T(8,128)} %refs_2_.11) | copy-start | bytes 12292
  12.7 9.3 %collective-permute-start = (bf16[32,1024]{1,0:T(8,128)(2,1)S(1)}, bf16[32,1024]{1,0:T(8,128)(2,1)S(1)}, u32[]{:S(2)}, u32[]{:S(2)}) collective-permute-start(bf16[32,1024]{1,0:T(8,128)(2,1)S(1)} %get-tuple-element.31), channel_id=1, source_target_pairs={{0,4},{4,0},{8,12},{12,8},{16,20},{20,16},{24,28},{28,24},{1,5},{5... | collective-permute-start | bytes 196616 | tf_op jit(solution)/shard_map/ppermute | solution.py:397
  14.3 4.9 %collective-permute-start.10 = (bf16[32,384]{1,0:T(8,128)(2,1)S(1)}, bf16[32,384]{1,0:T(8,128)(2,1)S(1)}, u32[]{:S(2)}, u32[]{:S(2)}) collective-permute-start(bf16[32,384]{1,0:T(8,128)(2,1)S(1)} %sum_o.2.refs_0_), channel_id=1, source_target_pairs={{0,16},{4,20},{8,24},{12,28},{16,0},{20,4},{24,8},{28,12},{1,17},{... | collective-permute-start | bytes 73736 | tf_op jit(solution)/shard_map/ppermute | solution.py:397
  19.4 4.1 %collective-permute-start.11 = (bf16[32,384]{1,0:T(8,128)(2,1)S(1)}, bf16[32,384]{1,0:T(8,128)(2,1)S(1)}, u32[]{:S(2)}, u32[]{:S(2)}) collective-permute-start(bf16[32,384]{1,0:T(8,128)(2,1)S(1)} %hat_o.1.refs_0_), channel_id=1, source_target_pairs={{0,4},{4,0},{8,12},{12,8},{16,20},{20,16},{24,28},{28,24},{1,5},{5... | collective-permute-start | bytes 73736 | tf_op jit(solution)/shard_map/ppermute | solution.py:397
  22.0 9.6 %copy-start.5 = (f32[32,32]{1,0:T(8,128)S(1)}, f32[32,32]{1,0:T(8,128)}, u32[]{:S(2)}) copy-start(f32[32,32]{1,0:T(8,128)} %refs_2_.8) | copy-start | bytes 12292
  22.0 4.3 %collective-permute-start.1 = (bf16[32,1024]{1,0:T(8,128)(2,1)S(1)}, bf16[32,1024]{1,0:T(8,128)(2,1)S(1)}, u32[]{:S(2)}, u32[]{:S(2)}) collective-permute-start(bf16[32,1024]{1,0:T(8,128)(2,1)S(1)} %first_sum_q.2.refs_0_), channel_id=1, source_target_pairs={{0,8},{4,12},{8,0},{12,4},{16,24},{20,28},{24,16},{28,20},{1,9},{5... | collective-permute-start | bytes 196616 | tf_op jit(solution)/shard_map/ppermute | solution.py:397
  23.9 5.3 %collective-permute-start.12 = (bf16[32,1024]{1,0:T(8,128)(2,1)S(1)}, bf16[32,1024]{1,0:T(8,128)(2,1)S(1)}, u32[]{:S(2)}, u32[]{:S(2)}) collective-permute-start(bf16[32,1024]{1,0:T(8,128)(2,1)S(1)} %get-tuple-element.46), channel_id=1, source_target_pairs={{0,4},{4,0},{8,12},{12,8},{16,20},{20,16},{24,28},{28,24},{1,5},{5... | collective-permute-start | bytes 196616 | tf_op jit(solution)/shard_map/ppermute | solution.py:397
  26.4 5.2 %collective-permute-start.2 = (bf16[32,1024]{1,0:T(8,128)(2,1)S(1)}, bf16[32,1024]{1,0:T(8,128)(2,1)S(1)}, u32[]{:S(2)}, u32[]{:S(2)}) collective-permute-start(bf16[32,1024]{1,0:T(8,128)(2,1)S(1)} %sum_q.2.refs_0_), channel_id=1, source_target_pairs={{0,16},{4,20},{8,24},{12,28},{16,0},{20,4},{24,8},{28,12},{1,17},{... | collective-permute-start | bytes 196616 | tf_op jit(solution)/shard_map/ppermute | solution.py:397
  29.2 7.0 %collective-permute-start.13 = (bf16[32,1024]{1,0:T(8,128)(2,1)S(1)}, bf16[32,1024]{1,0:T(8,128)(2,1)S(1)}, u32[]{:S(2)}, u32[]{:S(2)}) collective-permute-start(bf16[32,1024]{1,0:T(8,128)(2,1)S(1)} %first_sum_o.3.refs_0_.refs_2_), channel_id=1, source_target_pairs={{0,8},{4,12},{8,0},{12,4},{16,24},{20,28},{24,16},{28,20},{1,9},{5... | collective-permute-start | bytes 196616 | tf_op jit(solution)/shard_map/ppermute | solution.py:397
  31.9 6.4 %collective-permute-start.3 = (bf16[32,1024]{1,0:T(8,128)(2,1)S(1)}, bf16[32,1024]{1,0:T(8,128)(2,1)S(1)}, u32[]{:S(2)}, u32[]{:S(2)}) collective-permute-start(bf16[32,1024]{1,0:T(8,128)(2,1)S(1)} %hat_q.1.refs_0_), channel_id=1, source_target_pairs={{0,4},{4,0},{8,12},{12,8},{16,20},{20,16},{24,28},{28,24},{1,5},{5... | collective-permute-start | bytes 196616 | tf_op jit(solution)/shard_map/ppermute | solution.py:397
  36.2 5.2 %collective-permute-start.14 = (bf16[32,1024]{1,0:T(8,128)(2,1)S(1)}, bf16[32,1024]{1,0:T(8,128)(2,1)S(1)}, u32[]{:S(2)}, u32[]{:S(2)}) collective-permute-start(bf16[32,1024]{1,0:T(8,128)(2,1)S(1)} %sum_o.3.refs_0_.refs_2_), channel_id=1, source_target_pairs={{0,16},{4,20},{8,24},{12,28},{16,0},{20,4},{24,8},{28,12},{1,17},{... | collective-permute-start | bytes 196616 | tf_op jit(solution)/shard_map/ppermute | solution.py:397
  38.7 3.8 %collective-permute-start.4 = (bf16[32,256]{1,0:T(8,128)(2,1)S(1)}, bf16[32,256]{1,0:T(8,128)(2,1)S(1)}, u32[]{:S(2)}, u32[]{:S(2)}) collective-permute-start(bf16[32,256]{1,0:T(8,128)(2,1)S(1)} %get-tuple-element.35), channel_id=1, source_target_pairs={{0,4},{4,0},{8,12},{12,8},{16,20},{20,16},{24,28},{28,24},{1,5},{5... | collective-permute-start | bytes 49160 | tf_op jit(solution)/shard_map/ppermute | solution.py:397
  41.4 17.1 %collective-permute-start.15 = (bf16[32,1024]{1,0:T(8,128)(2,1)S(1)}, bf16[32,1024]{1,0:T(8,128)(2,1)S(1)}, u32[]{:S(2)}, u32[]{:S(2)}) collective-permute-start(bf16[32,1024]{1,0:T(8,128)(2,1)S(1)} %mean_o.1.refs_4_.refs_2_), channel_id=1, source_target_pairs={{0,4},{4,0},{8,12},{12,8},{16,20},{20,16},{24,28},{28,24},{1,5},{5... | collective-permute-start | bytes 196616 | tf_op jit(solution)/shard_map/ppermute | solution.py:397
  42.5 3.8 %collective-permute-start.5 = (bf16[32,256]{1,0:T(8,128)(2,1)S(1)}, bf16[32,256]{1,0:T(8,128)(2,1)S(1)}, u32[]{:S(2)}, u32[]{:S(2)}) collective-permute-start(bf16[32,256]{1,0:T(8,128)(2,1)S(1)} %first_sum_q.3.refs_0_), channel_id=1, source_target_pairs={{0,8},{4,12},{8,0},{12,4},{16,24},{20,28},{24,16},{28,20},{1,9},{5... | collective-permute-start | bytes 49160 | tf_op jit(solution)/shard_map/ppermute | solution.py:397
  43.3 5.0 %collective-permute-start.16 = (f32[32,128]{1,0:T(8,128)S(1)}, f32[32,128]{1,0:T(8,128)S(1)}, u32[]{:S(2)}, u32[]{:S(2)}) collective-permute-start(f32[32,128]{1,0:T(8,128)S(1)} %norm_join.1.refs_0_), channel_id=1, source_target_pairs={{0,1},{1,0},{2,3},{3,2},{4,5},{5,4},{6,7},{7,6},{8,9},{9,8},{10,11... | collective-permute-start | bytes 49160 | tf_op jit(solution)/shard_map/ppermute | solution.py:397
  46.3 4.6 %collective-permute-start.6 = (bf16[32,256]{1,0:T(8,128)(2,1)S(1)}, bf16[32,256]{1,0:T(8,128)(2,1)S(1)}, u32[]{:S(2)}, u32[]{:S(2)}) collective-permute-start(bf16[32,256]{1,0:T(8,128)(2,1)S(1)} %sum_q.3.refs_0_), channel_id=1, source_target_pairs={{0,16},{4,20},{8,24},{12,28},{16,0},{20,4},{24,8},{28,12},{1,17},{... | collective-permute-start | bytes 49160 | tf_op jit(solution)/shard_map/ppermute | solution.py:397
  48.3 5.9 %collective-permute-start.17 = (f32[32,128]{1,0:T(8,128)S(1)}, f32[32,128]{1,0:T(8,128)S(1)}, u32[]{:S(2)}, u32[]{:S(2)}) collective-permute-start(f32[32,128]{1,0:T(8,128)S(1)} %norm_add.2.refs_0_), channel_id=1, source_target_pairs={{0,2},{1,3},{2,0},{3,1},{4,6},{5,7},{6,4},{7,5},{8,10},{9,11},{10,... | collective-permute-start | bytes 49160 | tf_op jit(solution)/shard_map/ppermute | solution.py:397
  50.9 5.3 %collective-permute-start.7 = (bf16[32,256]{1,0:T(8,128)(2,1)S(1)}, bf16[32,256]{1,0:T(8,128)(2,1)S(1)}, u32[]{:S(2)}, u32[]{:S(2)}) collective-permute-start(bf16[32,256]{1,0:T(8,128)(2,1)S(1)} %mean_q.1.refs_4_), channel_id=1, source_target_pairs={{0,4},{4,0},{8,12},{12,8},{16,20},{20,16},{24,28},{28,24},{1,5},{5... | collective-permute-start | bytes 49160 | tf_op jit(solution)/shard_map/ppermute | solution.py:397
  54.9 1.4 %copy-start = (f32[256,512]{1,0:T(8,128)S(1)}, f32[256,512]{1,0:T(8,128)}, u32[]{:S(2)}) copy-start(f32[256,512]{1,0:T(8,128)} %refs_7_.2) | copy-start | bytes 1572868
  54.9 1.4 %copy-start.1 = (f32[256,512]{1,0:T(8,128)S(1)}, f32[256,512]{1,0:T(8,128)}, u32[]{:S(2)}) copy-start(f32[256,512]{1,0:T(8,128)} %refs_8_.2) | copy-start | bytes 1572868
  56.2 2.4 %copy-start.2 = (f32[512,256]{1,0:T(8,128)S(1)}, f32[512,256]{1,0:T(8,128)}, u32[]{:S(2)}) copy-start(f32[512,256]{1,0:T(8,128)} %refs_7_.3) | copy-start | bytes 1572868
  56.2 2.4 %copy-start.3 = (f32[512,256]{1,0:T(8,128)S(1)}, f32[512,256]{1,0:T(8,128)}, u32[]{:S(2)}) copy-start(f32[512,256]{1,0:T(8,128)} %refs_8_.3) | copy-start | bytes 1572868

commit v5 on v3

v5 whole, which is shorter than its diff:
```python
import functools

import jax
import jax.numpy as jnp
from jax import lax
from jax.experimental import pallas as pl
from jax.experimental.pallas import tpu as pltpu
from jax.sharding import PartitionSpec as P

momentum_decay = 0.9
step_size = 0.5
lanes = 128
mib = 1024 * 1024
bf16 = jnp.bfloat16
f32 = jnp.float32

whole = pl.BlockSpec(memory_space=pltpu.VMEM)
in_place = pl.BlockSpec(memory_space=pl.ANY)


def dot(left, right, left_dim, right_dim, precision=None):
    return lax.dot_general(
        left,
        right,
        (((left_dim,), (right_dim,)), ((), ())),
        precision=precision,
        preferred_element_type=f32,
    )


def params(limit):
    return pltpu.CompilerParams(vmem_limit_bytes=limit * mib)


def cost(flops, moved):
    return pl.CostEstimate(flops=flops, bytes_accessed=moved, transcendentals=0)


def in_hbm(value):
    return pltpu.with_memory_space_constraint(value, pltpu.HBM)


def in_vmem(value):
    return pltpu.with_memory_space_constraint(value, pltpu.VMEM)


def shaped(shape, dtype):
    return jax.ShapeDtypeStruct(shape, dtype)


def parity():
    return lax.rem(lax.axis_index("replica"), 2)


def half_at(which, size):
    return pl.ds(pl.multiple_of(which * size, size), size)


def load(source, target, sem):
    copy = pltpu.make_async_copy(source, target, sem)
    copy.start()
    return copy


def project_half(
    which, fac_q_h, fac_o_h, grad_q, error_q, grad_o, error_o, mat_q, mat_o, store,
    fac_q, fac_o, grad_q_v, error_q_v, grad_o_v, error_o_v, sems,
):
    half_q, half_o = mat_q.shape[0], mat_o.shape[0]
    jobs = []
    fac_copies = [load(fac_q_h, fac_q, sems.at[0]), load(fac_o_h, fac_o, sems.at[1])]
    chunks_q, chunks_o = 4, 2
    rows_q, rows_o = half_q // chunks_q, half_o // chunks_o
    slot = 2
    for chunk in range(chunks_q):
        part = pl.ds(chunk * rows_q, rows_q)
        there = pl.ds(pl.multiple_of(which * half_q + chunk * rows_q, rows_q), rows_q)
        jobs.append((grad_q_v, error_q_v, mat_q, fac_q, part, chunk * rows_q, (
            load(grad_q.at[there], grad_q_v.at[part], sems.at[slot]),
            load(error_q.at[there], error_q_v.at[part], sems.at[slot + 1]),
        )))
        slot += 2
        if chunk % 2 == 0:
            continue
        chunk = chunk // 2
        part = pl.ds(chunk * rows_o, rows_o)
        there = pl.ds(pl.multiple_of(which * half_o + chunk * rows_o, rows_o), rows_o)
        jobs.append((grad_o_v, error_o_v, mat_o, fac_o, part, half_q + chunk * rows_o, (
            load(grad_o.at[there], grad_o_v.at[part], sems.at[slot]),
            load(error_o.at[there], error_o_v.at[part], sems.at[slot + 1]),
        )))
        slot += 2
    for copy in fac_copies:
        copy.wait()
    for grad_v, error_v, mat, fac, part, column, copies in jobs:
        for copy in copies:
            copy.wait()
        block = (grad_v[part].astype(f32) + error_v[part].astype(f32)).astype(bf16)
        mat[part] = block
        store(column, dot(fac[...], block, 1, 1))


def far_kernel(
    fac_q_h, fac_o_h, grad_q, error_q, grad_o, error_o, mat_q, mat_o, send, *scratch
):
    def store(column, value):
        send[:, column:column + value.shape[1]] = value.astype(bf16)

    project_half(
        1 - parity(), fac_q_h, fac_o_h, grad_q, error_q, grad_o, error_o,
        mat_q, mat_o, store, *scratch
    )


def near_kernel(
    fac_q_h, fac_o_h, grad_q, error_q, grad_o, error_o, norm_grads,
    mat_q, mat_o, part, norm, *scratch
):
    def store(column, value):
        part[:, column:column + value.shape[1]] = value

    project_half(
        parity(), fac_q_h, fac_o_h, grad_q, error_q, grad_o, error_o,
        mat_q, mat_o, store, *scratch
    )
    values = norm_grads[0].astype(f32)
    for row in range(norm.shape[0]):
        norm[row:row + 1, :] = values[:, row * lanes:(row + 1) * lanes]


def project(grad_q, error_q, grad_o, error_o, fac_q, fac_o, norm_grads):
    rank = fac_q.shape[0]
    half_q = (grad_q.shape[0] // 2, grad_q.shape[1])
    half_o = (grad_o.shape[0] // 2, grad_o.shape[1])
    columns = half_q[0] + half_o[0]
    norm_rows = norm_grads.size // lanes
    mats = (pltpu.VMEM(half_q, bf16), pltpu.VMEM(half_o, bf16))
    scratch = [
        pltpu.VMEM(fac_q.shape, bf16),
        pltpu.VMEM(fac_o.shape, bf16),
        pltpu.VMEM(half_q, bf16),
        pltpu.VMEM(half_q, bf16),
        pltpu.VMEM(half_o, bf16),
        pltpu.VMEM(half_o, bf16),
        pltpu.SemaphoreType.DMA((14,)),
    ]
    operands = [
        in_hbm(value) for value in (fac_q, fac_o, grad_q, error_q, grad_o, error_o)
    ]
    effort = cost(2 * rank * (grad_q.size + grad_o.size) // 2, 4 * grad_q.size)
    mat_q_far, mat_o_far, send = pl.pallas_call(
        far_kernel,
        out_shape=mats + (shaped((rank, columns), bf16),),
        in_specs=[in_place] * 6,
        out_specs=(whole,) * 3,
        scratch_shapes=scratch,
        compiler_params=params(16),
        cost_estimate=effort,
        name="project_far",
    )(*operands)
    mat_q_near, mat_o_near, part, norm = pl.pallas_call(
        near_kernel,
        out_shape=mats + (shaped((rank, columns), f32), shaped((norm_rows, lanes), f32)),
        in_specs=[in_place] * 6 + [whole],
        out_specs=(whole,) * 4,
        scratch_shapes=scratch,
        compiler_params=params(16),
        cost_estimate=effort,
        name="project_near",
    )(*operands, norm_grads)
    return mat_q_far, mat_o_far, send, mat_q_near, mat_o_near, part, norm


def small(kernel, name, outs, *operands):
    return pl.pallas_call(
        kernel,
        out_shape=outs,
        in_specs=[whole] * len(operands),
        out_specs=(whole,) * len(outs) if isinstance(outs, tuple) else whole,
        compiler_params=params(8),
        name=name,
    )(*operands)


def tree(parts):
    while len(parts) > 1:
        parts = [parts[place] + parts[place + 1] for place in range(0, len(parts), 2)]
    return parts[0]


def total_of(states, columns):
    return tree([state[:, :columns].astype(f32) for state in states])


def norm_of(states, columns):
    parts = []
    for state in states:
        part = state[:, columns:columns + lanes].astype(f32)
        if state.shape[1] > columns + lanes:
            part = part + state[:, columns + lanes:columns + 2 * lanes].astype(f32)
        parts.append(part)
    return tree(parts)


def store_norm(state, columns, total):
    high = total.astype(bf16)
    state[:, columns:columns + lanes] = high
    state[:, columns + lanes:columns + 2 * lanes] = (total - high.astype(f32)).astype(bf16)


def first_sum_kernel(part, norm, got, state):
    columns = part.shape[1]
    state[:, :columns] = (part[...] + got[...].astype(f32)).astype(bf16)
    state[:, columns:] = norm[...].astype(bf16)


def norm_sum_kernel(columns, *refs):
    *states, out = refs
    out[:, :columns] = total_of(states, columns).astype(bf16)
    store_norm(out, columns, norm_of(states, columns))


def plain_sum_kernel(*refs):
    *states, out = refs
    out[...] = total_of(states, out.shape[1]).astype(bf16)


def hat_kernel(size_q, columns, ginv_q, ginv_o, *refs):
    *states, out = refs
    total = total_of(states, columns)
    highest = lax.Precision.HIGHEST
    out[:, :size_q] = dot(ginv_q[...].T, total[:, :size_q], 1, 0, highest).astype(bf16)
    out[:, size_q:columns] = dot(ginv_o[...].T, total[:, size_q:], 1, 0, highest).astype(bf16)
    store_norm(out, columns, norm_of(states, columns))


def mean_kernel(count, norm, norm_got, *refs):
    *states, new, norm_sum = refs
    new[...] = (total_of(states, new.shape[1]) / count).astype(bf16)
    norm_sum[...] = norm[...] + norm_got[...]


def right_near_kernel(hat, mat_q, mat_o, part_q, part_o):
    size_q, size_o = mat_q.shape[0], mat_o.shape[0]
    part_q[...] = dot(hat[:, :size_q], mat_q[...], 1, 0)
    part_o[...] = dot(hat[:, size_q:size_q + size_o], mat_o[...], 1, 0)


def right_near(hat, mat_q, mat_o):
    rank = hat.shape[0]
    return pl.pallas_call(
        right_near_kernel,
        out_shape=(shaped((rank, mat_q.shape[1]), f32), shaped((rank, mat_o.shape[1]), f32)),
        in_specs=[whole] * 3,
        out_specs=(whole,) * 2,
        compiler_params=params(8),
        cost_estimate=cost(2 * rank * (mat_q.size + mat_o.size), 2 * (mat_q.size + mat_o.size)),
        name="right_near",
    )(hat, in_vmem(mat_q), in_vmem(mat_o))


def right_far_kernel(hat, mat_q, mat_o, part_q, part_o, hat_near, send, near, norm, all_q, all_o):
    size_q, size_o = mat_q.shape[0], mat_o.shape[0]
    all_q[...] = part_q[...] + dot(hat[:, :size_q], mat_q[...], 1, 0)
    all_o[...] = part_o[...] + dot(hat[:, size_q:size_q + size_o], mat_o[...], 1, 0)
    mine = parity()
    half_q, half_o = all_q.shape[1] // 2, all_o.shape[1] // 2
    send[:, :half_q] = all_q[:, half_at(1 - mine, half_q)].astype(bf16)
    send[:, half_q:] = all_o[:, half_at(1 - mine, half_o)].astype(bf16)
    near[:, :half_q] = all_q[:, half_at(mine, half_q)]
    near[:, half_q:] = all_o[:, half_at(mine, half_o)]
    norm[...] = norm_of([hat_near, hat], size_q + size_o)


def right_far(hat, mat_q, mat_o, part_q, part_o, hat_near, norm_rows):
    rank = hat.shape[0]
    columns = (mat_q.shape[1] + mat_o.shape[1]) // 2
    return pl.pallas_call(
        right_far_kernel,
        out_shape=(
            shaped((rank, columns), bf16),
            shaped((rank, columns), f32),
            shaped((norm_rows, lanes), f32),
        ),
        in_specs=[whole] * 6,
        out_specs=(whole,) * 3,
        scratch_shapes=[pltpu.VMEM(part_q.shape, f32), pltpu.VMEM(part_o.shape, f32)],
        compiler_params=params(8),
        cost_estimate=cost(2 * rank * (mat_q.size + mat_o.size), 2 * (mat_q.size + mat_o.size)),
        name="right_far",
    )(hat, in_vmem(mat_q), in_vmem(mat_o), part_q, part_o, hat_near)


def near_sum_kernel(near, got, norm, state, norm_out):
    state[...] = (near[...] + got[...].astype(f32)).astype(bf16)
    norm_out[...] = norm[...]


def error_columns(column, hat, hat_row, half, mat_q, mat_o, new, error_q, error_o, stage_q, stage_o, sems, slot):
    size_q, size_o = mat_q.shape[0], mat_o.shape[0]
    wide_q, wide_o = stage_q.shape[1], stage_o.shape[1]
    copies = []
    chunk_q, chunk_o = size_q // 2, size_o // 2
    cols_q, cols_o = half_at(column, wide_q), half_at(column, wide_o)
    for chunk in range(2):
        part = pl.ds(chunk * chunk_q, chunk_q)
        stage = pl.ds(hat_row * size_q + chunk * chunk_q, chunk_q)
        approx = dot(hat[:, part], new[:, :wide_q], 0, 0)
        stage_q[stage] = (mat_q[part, cols_q].astype(f32) - approx).astype(bf16)
        there = pl.ds(pl.multiple_of(half * size_q + chunk * chunk_q, chunk_q), chunk_q)
        copies.append(load(stage_q.at[stage], error_q.at[there, cols_q], sems.at[slot]))
        part = pl.ds(chunk * chunk_o, chunk_o)
        stage = pl.ds(hat_row * size_o + chunk * chunk_o, chunk_o)
        approx = dot(hat[:, size_q + chunk * chunk_o:size_q + (chunk + 1) * chunk_o], new[:, wide_q:], 0, 0)
        stage_o[stage] = (mat_o[part, cols_o].astype(f32) - approx).astype(bf16)
        there = pl.ds(pl.multiple_of(half * size_o + chunk * chunk_o, chunk_o), chunk_o)
        copies.append(load(stage_o.at[stage], error_o.at[there, cols_o], sems.at[slot + 1]))
        slot += 2
    return copies


def finish_near_kernel(
    hat_near, hat_far, mat_q_near, mat_o_near, mat_q_far, mat_o_far, new,
    error_q, error_o, stage_q, stage_o, sems
):
    mine = parity()
    copies = error_columns(
        mine, hat_near, 0, mine, mat_q_near, mat_o_near, new, error_q, error_o, stage_q, stage_o, sems, 0
    ) + error_columns(
        mine, hat_far, 1, 1 - mine, mat_q_far, mat_o_far, new, error_q, error_o, stage_q, stage_o, sems, 4
    )
    for copy in copies:
        copy.wait()


def piece_of(near, far, index, count, size, pieces):
    half = count // 2
    here = index // half == parity()
    slot = lax.rem(index, half)
    if size % lanes == 0:
        part = half_at(slot, size)
        return jnp.where(here, near[:, part].astype(f32), far[:, part].astype(f32)).astype(bf16)
    width = half * size
    chosen = jnp.where(here, near[:, :width].astype(f32), far[:, :width].astype(f32))
    for place in range(half):
        pieces[place] = chosen[:, place * size:(place + 1) * size]
    return pieces[slot].astype(bf16)


def finish_far_kernel(
    count, norm_count, hat_near, hat_far, mat_q_near, mat_o_near, mat_q_far, mat_o_far,
    new_near, new_far, weight_q, momentum_q, weight_o, momentum_o, norm, norm_got,
    error_q_in, error_o_in,
    error_q, error_o, new_q_h, new_o_h, momentum_q_h, weight_q_h, momentum_o_h, weight_o_h, norm_h,
    stage_q, stage_o, new_q, new_o, momentum_q_new, weight_q_new, momentum_o_new, weight_o_new,
    norm_mean, pieces_q, pieces_o, sems, out_sems
):
    mine = parity()
    me = lax.axis_index("replica")
    wide_q, wide_o = stage_q.shape[1], stage_o.shape[1]
    size_q = mat_q_near.shape[0]
    size_o = mat_o_near.shape[0]
    new_q[:, half_at(mine, wide_q)] = new_near[:, :wide_q]
    new_q[:, half_at(1 - mine, wide_q)] = new_far[:, :wide_q]
    new_o[:, half_at(mine, wide_o)] = new_near[:, wide_q:]
    new_o[:, half_at(1 - mine, wide_o)] = new_far[:, wide_q:]
    norm_mean[...] = (norm[...] + norm_got[...]) / norm_count
    copies = [
        load(new_q, new_q_h, out_sems.at[0]),
        load(new_o, new_o_h, out_sems.at[1]),
        load(norm_mean, norm_h, out_sems.at[2]),
    ]
    copies += error_columns(
        1 - mine, hat_near, 0, mine, mat_q_near, mat_o_near, new_far,
        error_q, error_o, stage_q, stage_o, sems, 0
    )
    piece = piece_of(hat_near, hat_far, me, count, weight_q.shape[0], pieces_q)
    moved = momentum_decay * momentum_q[...] + dot(piece, new_q[...], 0, 0)
    momentum_q_new[...] = moved
    weight_q_new[...] = weight_q[...] - step_size * moved
    copies.append(load(momentum_q_new, momentum_q_h, out_sems.at[3]))
    copies.append(load(weight_q_new, weight_q_h, out_sems.at[4]))
    copies += error_columns(
        1 - mine, hat_far, 1, 1 - mine, mat_q_far, mat_o_far, new_far,
        error_q, error_o, stage_q, stage_o, sems, 4
    )
    piece = piece_of(
        new_near.at[:, wide_q:], new_far.at[:, wide_q:], me, count, weight_o.shape[1], pieces_o
    )
    for which, hat in ((mine, hat_near), (1 - mine, hat_far)):
        rows = half_at(which, size_o)
        moved = momentum_decay * momentum_o[rows] + dot(hat[:, size_q:size_q + size_o], piece, 0, 0)
        momentum_o_new[rows] = moved
        weight_o_new[rows] = weight_o[rows] - step_size * moved
    copies.append(load(momentum_o_new, momentum_o_h, out_sems.at[5]))
    copies.append(load(weight_o_new, weight_o_h, out_sems.at[6]))
    for copy in copies:
        copy.wait()


def finish(
    count, norm_count, hat_near, hat_far, mats, new_near, weights, norm
):
    mat_q, mat_o = mats[0], mats[1]
    weight_q, _, weight_o, _ = weights
    rank = hat_near.shape[0]
    size_q, size_o = mat_q.shape[0], mat_o.shape[0]
    error_q = shaped((2 * size_q, mat_q.shape[1]), bf16)
    error_o = shaped((2 * size_o, mat_o.shape[1]), bf16)
    stages = [
        pltpu.VMEM((2 * size_q, mat_q.shape[1] // 2), bf16),
        pltpu.VMEM((2 * size_o, mat_o.shape[1] // 2), bf16),
    ]
    moved = 4 * (mat_q.size + mat_o.size)
    mats = [in_vmem(mat) for mat in mats]
    new_far = swap(new_near, 1)
    norm_got = swap(norm, 2, "tensor")
    error_q_part, error_o_part = pl.pallas_call(
        finish_near_kernel,
        out_shape=(error_q, error_o),
        in_specs=[whole] * 7,
        out_specs=(in_place,) * 2,
        scratch_shapes=stages + [pltpu.SemaphoreType.DMA((8,))],
        compiler_params=params(12),
        cost_estimate=cost(2 * rank * (mat_q.size + mat_o.size), moved),
        name="finish_near",
    )(hat_near, hat_far, *mats, new_near)
    outs = (
        error_q,
        error_o,
        shaped((rank, mat_q.shape[1]), bf16),
        shaped((rank, mat_o.shape[1]), bf16),
        shaped(weight_q.shape, f32),
        shaped(weight_q.shape, f32),
        shaped(weight_o.shape, f32),
        shaped(weight_o.shape, f32),
        shaped(norm.shape, f32),
    )
    return pl.pallas_call(
        functools.partial(finish_far_kernel, count, norm_count),
        out_shape=outs,
        in_specs=[whole] * 14 + [in_place] * 2,
        out_specs=(in_place,) * len(outs),
        scratch_shapes=stages + [pltpu.VMEM(out.shape, out.dtype) for out in outs[2:]] + [
            pltpu.VMEM((count // 2, rank, weight_q.shape[0]), f32),
            pltpu.VMEM((count // 2, rank, weight_o.shape[1]), f32),
            pltpu.SemaphoreType.DMA((8,)),
            pltpu.SemaphoreType.DMA((7,)),
        ],
        input_output_aliases={14: 0, 15: 1},
        compiler_params=params(16),
        cost_estimate=cost(2 * rank * (mat_q.size + mat_o.size), moved),
        name="finish_far",
    )(
        hat_near, hat_far, *mats, new_near, new_far, *(in_vmem(value) for value in weights),
        norm, norm_got, error_q_part, error_o_part,
    )


def swap(value, bit, axis="replica"):
    count = lax.axis_size(axis)
    return lax.ppermute(value, axis, [(source, source ^ bit) for source in range(count)])


def exchange(state, bits):
    offsets = [0]
    for bit in bits:
        offsets += [offset | bit for offset in offsets]
    got = {0: state}
    for offset in offsets[:0:-1]:
        got[offset] = swap(state, offset)
    return [got[offset] for offset in offsets]


def rounds_of(count):
    bits = [1 << place for place in range(1, count.bit_length() - 1)]
    return [bits[place:place + 2] for place in range(0, len(bits), 2)]


def on_device(
    grad_q,
    error_q,
    qfac_q,
    ginv_q,
    weight_q,
    momentum_q,
    grad_o,
    error_o,
    qfac_o,
    ginv_o,
    weight_o,
    momentum_o,
    norm_grads,
):
    replicas = lax.axis_size("replica")
    tensors = lax.axis_size("tensor")
    rank = qfac_q.shape[1]
    half_q = grad_q.shape[0] // 2
    norm_rows = norm_grads.size // lanes
    mat_q_far, mat_o_far, send, mat_q_near, mat_o_near, part, norm = project(
        grad_q, error_q, grad_o, error_o, qfac_q.T, qfac_o.T, norm_grads
    )
    columns = part.shape[1]
    rounds = rounds_of(replicas)
    state = small(
        first_sum_kernel, "first_sum", shaped((rank, columns + lanes), bf16), part, norm, swap(send, 1)
    )
    wide = shaped((rank, columns + 2 * lanes), bf16)
    for bits in rounds[:-1]:
        state = small(
            functools.partial(norm_sum_kernel, columns), "norm_sum", wide, *exchange(state, bits)
        )
    hat_near = small(
        functools.partial(hat_kernel, half_q, columns), "hats", wide,
        ginv_q, ginv_o, *exchange(state, rounds[-1]),
    )
    hat_far = swap(hat_near, 1)
    part_q, part_o = right_near(hat_near, mat_q_near, mat_o_near)
    send, near, norm = right_far(
        hat_far, mat_q_far, mat_o_far, part_q, part_o, hat_near, norm_rows
    )
    state, norm = small(
        near_sum_kernel, "near_sum", (shaped(send.shape, bf16), shaped(norm.shape, f32)),
        near, swap(send, 1), norm,
    )
    for bits in rounds[:-1]:
        state = small(
            plain_sum_kernel, "plain_sum", shaped(state.shape, bf16), *exchange(state, bits)
        )
    states = exchange(state, rounds[-1])
    new_near, norm = small(
        functools.partial(mean_kernel, replicas), "mean",
        (shaped(state.shape, bf16), shaped(norm.shape, f32)),
        norm, swap(norm, 1, "tensor"), *states,
    )
    (
        error_q_new, error_o_new, new_q, new_o,
        momentum_q_new, weight_q_new, momentum_o_new, weight_o_new, norm_mean,
    ) = finish(
        replicas, replicas * tensors, hat_near, hat_far,
        (mat_q_near, mat_o_near, mat_q_far, mat_o_far), new_near,
        (weight_q, momentum_q, weight_o, momentum_o), norm,
    )
    return (
        error_q_new,
        new_q.T,
        momentum_q_new,
        weight_q_new,
        error_o_new,
        new_o.T,
        momentum_o_new,
        weight_o_new,
        norm_mean.reshape(-1),
    )


def solution(mesh):
    in_specs = (
        P("replica", "tensor"),
        P("replica", "tensor"),
        P("tensor", None),
        P("tensor", None),
        P("replica", "tensor"),
        P("replica", "tensor"),
        P(("replica", "tensor"), None),
        P(("replica", "tensor"), None),
        P("tensor", None),
        P("tensor", None),
        P("tensor", "replica"),
        P("tensor", "replica"),
        P("replica", "tensor", None),
    )
    out_specs = (
        P("replica", "tensor"),
        P("tensor", None),
        P("replica", "tensor"),
        P("replica", "tensor"),
        P(("replica", "tensor"), None),
        P("tensor", None),
        P("tensor", "replica"),
        P("tensor", "replica"),
        P(),
    )
    return jax.shard_map(
        on_device, mesh=mesh, in_specs=in_specs, out_specs=out_specs, check_vma=False
    )
```

time: 54.8 us -> 46.6 us (0.85)
  Pallas kernels: 15.7 us -> 11.8 us
  waiting for transfers between devices: 21.5 us -> 17.8 us
  starting transfers between devices: 16.6 us -> 16 us
    pallas_call x12 -> x9, Pallas kernels: 13.9 us -> 10.1 us  [the longest x1 3.1 us: project(): pl.pallas_call(far_kernel, out_shape=mats + (shaped((rank, columns), bf16...]
    ppermute x11 -> x12, waiting for transfers between devices: 21.5 us -> 17.8 us  [swap(): lax.ppermute(value, axis, [(source, source ^ bit) for source in range(cou...]
    ppermute x11 -> x12, starting transfers between devices: 16.6 us -> 16 us  [swap(): lax.ppermute(value, axis, [(source, source ^ bit) for source in range(cou...]
  transfers between devices with their start and end apart: 11 -> 12, of which waited for: 8 -> 8; matrix products, arithmetic and copies ran while one was open for 0% -> 0% of each run, Pallas kernels for 11% -> 11%
where the time goes in v5:
time: 46.6 us; the launch traced here: 46.4 us
  waiting for transfers between devices  17.8 us (38%)
  starting transfers between devices  16 us (34%)
  Pallas kernels  11.8 us (25%)
  between operations  0.77 us (2%)
    ppermute x12, waiting for transfers between devices, swap(): lax.ppermute(value, axis, [(source, source ^ bit) for source in range(cou...  17.8 us
    ppermute x12, starting transfers between devices, swap(): lax.ppermute(value, axis, [(source, source ^ bit) for source in range(cou...  16 us
    pallas_call x1, Pallas kernels, project(): pl.pallas_call(far_kernel, out_shape=mats + (shaped((rank, columns), bf16...  3.1 us
    pallas_call x1, Pallas kernels, project(): pl.pallas_call(near_kernel, out_shape=mats + (shaped((rank, columns), f32...  3.09 us
    pallas_call x1, Pallas kernels, finish(): pl.pallas_call(functools.partial(finish_far_kernel, count, norm_count), o...  2.54 us
    pallas_call x1, Pallas kernels, finish(): pl.pallas_call(finish_near_kernel, out_shape=(error_q, error_o), in_specs...  1.71 us
  transfers between devices with their start and end apart: 12, of which 8 were waited for; matrix products, arithmetic and copies ran while one was open for 0% of the time, Pallas kernels for 11%

profile of v5, /device:TPU:0, one launch (start us, length us, event | category | flops | bytes accessed | tf_op | source)
XLA Modules:
  0.0 46.4 jit_solution(2110591114631771837)
XLA Ops:
  0.7 3.1 %project_far.1 = (bf16[1024,512]{1,0:T(8,128)(2,1)S(1)}, bf16[256,2048]{1,0:T(8,128)(2,1)S(1)}, bf16[32,1280]{1,0:T(8,128)(2,1)S(1)}) custom-call(bf16[32,512]{1,0:T(8,128)(2,1)} %bitcast.7, bf16[32,2048]{1,0:T(8,128)(2,1)} %bitcast.5, bf16[2048,512]{1,0:T(8,128)(2,1)} %grad_q.3, bf16[2048,512]{1,0:T(8,128)(2,1)} %error_q.3, bf16[512,2048]{1,0:T(8,128)(2,1)} %grad_o.3, ...), custom_call_target="tpu_custom_call" | custom-call | flops 67108864 | bytes 4194304 | tf_op jit(solution)/shard_map/project_far/pallas_call | solution.py:151
  3.8 3.0 %collective-permute-start = (bf16[32,1280]{1,0:T(8,128)(2,1)S(1)}, bf16[32,1280]{1,0:T(8,128)(2,1)S(1)}, u32[]{:S(2)}, u32[]{:S(2)}) collective-permute-start(bf16[32,1280]{1,0:T(8,128)(2,1)S(1)} %get-tuple-element.38), channel_id=1, source_target_pairs={{0,4},{4,0},{8,12},{12,8},{16,20},{20,16},{24,28},{28,24},{1,5},{5... | collective-permute-start | bytes 245768 | tf_op jit(solution)/shard_map/ppermute | solution.py:462
  6.8 3.1 %project_near.1 = (bf16[1024,512]{1,0:T(8,128)(2,1)S(1)}, bf16[256,2048]{1,0:T(8,128)(2,1)S(1)}, f32[32,1280]{1,0:T(8,128)S(1)}, f32[32,128]{1,0:T(8,128)S(1)}) custom-call(bf16[32,512]{1,0:T(8,128)(2,1)} %bitcast.8, bf16[32,2048]{1,0:T(8,128)(2,1)} %bitcast.6, bf16[2048,512]{1,0:T(8,128)(2,1)} %grad_q.3, bf16[2048,512]{1,0:T(8,128)(2,1)} %error_q.3, ...), custom_call_target="tpu_custom_call" | custom-call | flops 67108864 | bytes 4194304 | tf_op jit(solution)/shard_map/project_near/pallas_call | solution.py:161
  10.0 3.7 %collective-permute-start.3 = (bf16[32,1408]{1,0:T(8,128)(2,1)S(1)}, bf16[32,1408]{1,0:T(8,128)(2,1)S(1)}, u32[]{:S(2)}, u32[]{:S(2)}) collective-permute-start(bf16[32,1408]{1,0:T(8,128)(2,1)S(1)} %first_sum.1.refs_0_), channel_id=1, source_target_pairs={{0,24},{4,28},{8,16},{12,20},{16,8},{20,12},{24,0},{28,4},{1,25},{... | collective-permute-start | bytes 270344 | tf_op jit(solution)/shard_map/ppermute | solution.py:462
  13.6 0.8 %collective-permute-start.1 = (bf16[32,1408]{1,0:T(8,128)(2,1)S(1)}, bf16[32,1408]{1,0:T(8,128)(2,1)S(1)}, u32[]{:S(2)}, u32[]{:S(2)}) collective-permute-start(bf16[32,1408]{1,0:T(8,128)(2,1)S(1)} %first_sum.1.refs_0_), channel_id=1, source_target_pairs={{0,8},{4,12},{8,0},{12,4},{16,24},{20,28},{24,16},{28,20},{1,9},{5... | collective-permute-start | bytes 270344 | tf_op jit(solution)/shard_map/ppermute | solution.py:462
  14.4 3.0 %collective-permute-done.3.refs_3_ = bf16[32,1408]{1,0:T(8,128)(2,1)S(1)} collective-permute-done((bf16[32,1408]{1,0:T(8,128)(2,1)S(1)}, bf16[32,1408]{1,0:T(8,128)(2,1)S(1)}, u32[]{:S(2)}, u32[]{:S(2)}) %collective-permute-start.3) | collective-permute-done | bytes 90144 | tf_op jit(solution)/shard_map/ppermute | solution.py:462
  17.4 3.5 %collective-permute-done.2.refs_2_ = bf16[32,1408]{1,0:T(8,128)(2,1)S(1)} collective-permute-done((bf16[32,1408]{1,0:T(8,128)(2,1)S(1)}, bf16[32,1408]{1,0:T(8,128)(2,1)S(1)}, u32[]{:S(2)}, u32[]{:S(2)}) %collective-permute-start.2) | collective-permute-done | bytes 90144 | tf_op jit(solution)/shard_map/ppermute | solution.py:462
  20.9 0.3 hats.1.hat.hat_near
  21.3 0.8 %collective-permute-start.4 = (bf16[32,1536]{1,0:T(8,128)(2,1)S(1)}, bf16[32,1536]{1,0:T(8,128)(2,1)S(1)}, u32[]{:S(2)}, u32[]{:S(2)}) collective-permute-start(bf16[32,1536]{1,0:T(8,128)(2,1)S(1)} %hats.1.hat.hat_near), channel_id=1, source_target_pairs={{0,4},{4,0},{8,12},{12,8},{16,20},{20,16},{24,28},{28,24},{1,5},{5... | collective-permute-start | bytes 294920 | tf_op jit(solution)/shard_map/ppermute | solution.py:462
  22.1 0.5 right_near.1
  22.6 3.4 %collective-permute-done.4.hat.hat_far = bf16[32,1536]{1,0:T(8,128)(2,1)S(1)} collective-permute-done((bf16[32,1536]{1,0:T(8,128)(2,1)S(1)}, bf16[32,1536]{1,0:T(8,128)(2,1)S(1)}, u32[]{:S(2)}, u32[]{:S(2)}) %collective-permute-start.4) | collective-permute-done | bytes 98336 | tf_op jit(solution)/shard_map/ppermute | solution.py:462
  25.9 0.5 %right_far.1 = (bf16[32,1280]{1,0:T(8,128)(2,1)S(1)}, f32[32,1280]{1,0:T(8,128)S(1)}, f32[32,128]{1,0:T(8,128)S(1)}) custom-call(bf16[32,1536]{1,0:T(8,128)(2,1)S(1)} %collective-permute-done.4.hat.hat_far, bf16[1024,512]{1,0:T(8,128)(2,1)S(1)} %get-tuple-element.41.mat_q.mat_q_far, bf16[256,2048]{1,0:T(8,128)(2,1)S(1)} %get-tuple-element.42.mat_o.mat_o_far, ...), custom_call_target="tpu_custom_call" | custom-call | flops 67108864 | bytes 2097152 | tf_op jit(solution)/shard_map/right_far/pallas_call | solution.py:278
  26.4 0.8 %collective-permute-start.5 = (bf16[32,1280]{1,0:T(8,128)(2,1)S(1)}, bf16[32,1280]{1,0:T(8,128)(2,1)S(1)}, u32[]{:S(2)}, u32[]{:S(2)}) collective-permute-start(bf16[32,1280]{1,0:T(8,128)(2,1)S(1)} %get-tuple-element.46), channel_id=1, source_target_pairs={{0,4},{4,0},{8,12},{12,8},{16,20},{20,16},{24,28},{28,24},{1,5},{5... | collective-permute-start | bytes 245768 | tf_op jit(solution)/shard_map/ppermute | solution.py:462
  27.3 3.7 %collective-permute-done.5.got = bf16[32,1280]{1,0:T(8,128)(2,1)S(1)} collective-permute-done((bf16[32,1280]{1,0:T(8,128)(2,1)S(1)}, bf16[32,1280]{1,0:T(8,128)(2,1)S(1)}, u32[]{:S(2)}, u32[]{:S(2)}) %collective-permute-start.5) | collective-permute-done | bytes 81952 | tf_op jit(solution)/shard_map/ppermute | solution.py:462
  31.0 2.8 %collective-permute-start.9 = (bf16[32,1280]{1,0:T(8,128)(2,1)S(1)}, bf16[32,1280]{1,0:T(8,128)(2,1)S(1)}, u32[]{:S(2)}, u32[]{:S(2)}) collective-permute-start(bf16[32,1280]{1,0:T(8,128)(2,1)S(1)} %get-tuple-element.49.refs_0_), channel_id=1, source_target_pairs={{0,24},{4,28},{8,16},{12,20},{16,8},{20,12},{24,0},{28,4},{1,25},{... | collective-permute-start | bytes 245768 | tf_op jit(solution)/shard_map/ppermute | solution.py:462
  33.8 1.6 %collective-permute-start.7 = (bf16[32,1280]{1,0:T(8,128)(2,1)S(1)}, bf16[32,1280]{1,0:T(8,128)(2,1)S(1)}, u32[]{:S(2)}, u32[]{:S(2)}) collective-permute-start(bf16[32,1280]{1,0:T(8,128)(2,1)S(1)} %get-tuple-element.49.refs_0_), channel_id=1, source_target_pairs={{0,8},{4,12},{8,0},{12,4},{16,24},{20,28},{24,16},{28,20},{1,9},{5... | collective-permute-start | bytes 245768 | tf_op jit(solution)/shard_map/ppermute | solution.py:462
  35.4 1.2 %collective-permute-done.6.norm_got = f32[32,128]{1,0:T(8,128)S(1)} collective-permute-done((f32[32,128]{1,0:T(8,128)S(1)}, f32[32,128]{1,0:T(8,128)S(1)}, u32[]{:S(2)}, u32[]{:S(2)}) %collective-permute-start.6) | collective-permute-done | bytes 16416 | tf_op jit(solution)/shard_map/ppermute | solution.py:462
  36.6 0.7 %collective-permute-done.9.refs_3_ = bf16[32,1280]{1,0:T(8,128)(2,1)S(1)} collective-permute-done((bf16[32,1280]{1,0:T(8,128)(2,1)S(1)}, bf16[32,1280]{1,0:T(8,128)(2,1)S(1)}, u32[]{:S(2)}, u32[]{:S(2)}) %collective-permute-start.9) | collective-permute-done | bytes 81952 | tf_op jit(solution)/shard_map/ppermute | solution.py:462
  37.3 1.9 %collective-permute-done.8.refs_2_ = bf16[32,1280]{1,0:T(8,128)(2,1)S(1)} collective-permute-done((bf16[32,1280]{1,0:T(8,128)(2,1)S(1)}, bf16[32,1280]{1,0:T(8,128)(2,1)S(1)}, u32[]{:S(2)}, u32[]{:S(2)}) %collective-permute-start.8) | collective-permute-done | bytes 81952 | tf_op jit(solution)/shard_map/ppermute | solution.py:462
  39.2 0.8 %collective-permute-start.10 = (bf16[32,1280]{1,0:T(8,128)(2,1)S(1)}, bf16[32,1280]{1,0:T(8,128)(2,1)S(1)}, u32[]{:S(2)}, u32[]{:S(2)}) collective-permute-start(bf16[32,1280]{1,0:T(8,128)(2,1)S(1)} %get-tuple-element.50.new.new_near), channel_id=1, source_target_pairs={{0,4},{4,0},{8,12},{12,8},{16,20},{20,16},{24,28},{28,24},{1,5},{5... | collective-permute-start | bytes 245768 | tf_op jit(solution)/shard_map/ppermute | solution.py:462
  40.0 1.6 %collective-permute-start.11 = (f32[32,128]{1,0:T(8,128)S(1)}, f32[32,128]{1,0:T(8,128)S(1)}, u32[]{:S(2)}, u32[]{:S(2)}) collective-permute-start(f32[32,128]{1,0:T(8,128)S(1)} %get-tuple-element.51.norm), channel_id=1, source_target_pairs={{0,2},{1,3},{2,0},{3,1},{4,6},{5,7},{6,4},{7,5},{8,10},{9,11},{10,... | collective-permute-start | bytes 49160 | tf_op jit(solution)/shard_map/ppermute | solution.py:462
  41.6 1.7 %finish_near.1 = (bf16[2048,512]{1,0:T(8,128)(2,1)}, bf16[512,2048]{1,0:T(8,128)(2,1)}) custom-call(bf16[32,1536]{1,0:T(8,128)(2,1)S(1)} %hats.1.hat.hat_near, bf16[32,1536]{1,0:T(8,128)(2,1)S(1)} %collective-permute-done.4.hat.hat_far, bf16[1024,512]{1,0:T(8,128)(2,1)S(1)} %get-tuple-element.39.mat_q.mat_q_near, ...), custom_call_target="tpu_custom_call" | custom-call | flops 67108864 | bytes 4194304 | tf_op jit(solution)/shard_map/finish_near/pallas_call | solution.py:418
  43.3 0.5 %collective-permute-done.11.norm_got = f32[32,128]{1,0:T(8,128)S(1)} collective-permute-done((f32[32,128]{1,0:T(8,128)S(1)}, f32[32,128]{1,0:T(8,128)S(1)}, u32[]{:S(2)}, u32[]{:S(2)}) %collective-permute-start.11) | collective-permute-done | bytes 16416 | tf_op jit(solution)/shard_map/ppermute | solution.py:462
  43.9 2.5 %finish_far.1 = (bf16[2048,512]{1,0:T(8,128)(2,1)}, bf16[512,2048]{1,0:T(8,128)(2,1)}, bf16[32,512]{1,0:T(8,128)(2,1)}, bf16[32,2048]{1,0:T(8,128)(2,1)}, f32[25...) custom-call(bf16[32,1536]{1,0:T(8,128)(2,1)S(1)} %hats.1.hat.hat_nea, ...), custom_call_target="tpu_custom_call", output_to_operand_aliasing={{0}: (14, {}), {1}: (15, {})} | custom-call | flops 67108864 | bytes 4194304 | tf_op jit(solution)/shard_map/finish_far/pallas_call | solution.py:439
  (24 shorter events, 0.1 us)
Async XLA Ops:
  0.6 6.2 %copy-start.4 = (bf16[1,1,4096]{2,1,0:T(2,128)(2,1)S(1)}, bf16[1,1,4096]{2,1,0:T(2,128)(2,1)}, u32[]{:S(2)}) copy-start(bf16[1,1,4096]{2,1,0:T(2,128)(2,1)} %norm_grads.1) | copy-start | bytes 24580
  3.8 17.2 %copy-start.5 = (f32[32,32]{1,0:T(8,128)S(1)}, f32[32,32]{1,0:T(8,128)}, u32[]{:S(2)}) copy-start(f32[32,32]{1,0:T(8,128)} %ginv_q.1) | copy-start | bytes 12292
  3.8 17.1 %copy-start.6 = (f32[32,32]{1,0:T(8,128)S(1)}, f32[32,32]{1,0:T(8,128)}, u32[]{:S(2)}) copy-start(f32[32,32]{1,0:T(8,128)} %ginv_o.1) | copy-start | bytes 12292
  3.8 6.1 %collective-permute-start = (bf16[32,1280]{1,0:T(8,128)(2,1)S(1)}, bf16[32,1280]{1,0:T(8,128)(2,1)S(1)}, u32[]{:S(2)}, u32[]{:S(2)}) collective-permute-start(bf16[32,1280]{1,0:T(8,128)(2,1)S(1)} %get-tuple-element.38), channel_id=1, source_target_pairs={{0,4},{4,0},{8,12},{12,8},{16,20},{20,16},{24,28},{28,24},{1,5},{5... | collective-permute-start | bytes 245768 | tf_op jit(solution)/shard_map/ppermute | solution.py:462
  10.0 7.4 %collective-permute-start.3 = (bf16[32,1408]{1,0:T(8,128)(2,1)S(1)}, bf16[32,1408]{1,0:T(8,128)(2,1)S(1)}, u32[]{:S(2)}, u32[]{:S(2)}) collective-permute-start(bf16[32,1408]{1,0:T(8,128)(2,1)S(1)} %first_sum.1.refs_0_), channel_id=1, source_target_pairs={{0,24},{4,28},{8,16},{12,20},{16,8},{20,12},{24,0},{28,4},{1,25},{... | collective-permute-start | bytes 270344 | tf_op jit(solution)/shard_map/ppermute | solution.py:462
  13.6 7.3 %collective-permute-start.2 = (bf16[32,1408]{1,0:T(8,128)(2,1)S(1)}, bf16[32,1408]{1,0:T(8,128)(2,1)S(1)}, u32[]{:S(2)}, u32[]{:S(2)}) collective-permute-start(bf16[32,1408]{1,0:T(8,128)(2,1)S(1)} %first_sum.1.refs_0_), channel_id=1, source_target_pairs={{0,16},{4,20},{8,24},{12,28},{16,0},{20,4},{24,8},{28,12},{1,17},{... | collective-permute-start | bytes 270344 | tf_op jit(solution)/shard_map/ppermute | solution.py:462
  13.6 7.3 %collective-permute-start.1 = (bf16[32,1408]{1,0:T(8,128)(2,1)S(1)}, bf16[32,1408]{1,0:T(8,128)(2,1)S(1)}, u32[]{:S(2)}, u32[]{:S(2)}) collective-permute-start(bf16[32,1408]{1,0:T(8,128)(2,1)S(1)} %first_sum.1.refs_0_), channel_id=1, source_target_pairs={{0,8},{4,12},{8,0},{12,4},{16,24},{20,28},{24,16},{28,20},{1,9},{5... | collective-permute-start | bytes 270344 | tf_op jit(solution)/shard_map/ppermute | solution.py:462
  21.3 4.7 %collective-permute-start.4 = (bf16[32,1536]{1,0:T(8,128)(2,1)S(1)}, bf16[32,1536]{1,0:T(8,128)(2,1)S(1)}, u32[]{:S(2)}, u32[]{:S(2)}) collective-permute-start(bf16[32,1536]{1,0:T(8,128)(2,1)S(1)} %hats.1.hat.hat_near), channel_id=1, source_target_pairs={{0,4},{4,0},{8,12},{12,8},{16,20},{20,16},{24,28},{28,24},{1,5},{5... | collective-permute-start | bytes 294920 | tf_op jit(solution)/shard_map/ppermute | solution.py:462
  26.4 4.5 %collective-permute-start.5 = (bf16[32,1280]{1,0:T(8,128)(2,1)S(1)}, bf16[32,1280]{1,0:T(8,128)(2,1)S(1)}, u32[]{:S(2)}, u32[]{:S(2)}) collective-permute-start(bf16[32,1280]{1,0:T(8,128)(2,1)S(1)} %get-tuple-element.46), channel_id=1, source_target_pairs={{0,4},{4,0},{8,12},{12,8},{16,20},{20,16},{24,28},{28,24},{1,5},{5... | collective-permute-start | bytes 245768 | tf_op jit(solution)/shard_map/ppermute | solution.py:462
  31.0 6.3 %collective-permute-start.9 = (bf16[32,1280]{1,0:T(8,128)(2,1)S(1)}, bf16[32,1280]{1,0:T(8,128)(2,1)S(1)}, u32[]{:S(2)}, u32[]{:S(2)}) collective-permute-start(bf16[32,1280]{1,0:T(8,128)(2,1)S(1)} %get-tuple-element.49.refs_0_), channel_id=1, source_target_pairs={{0,24},{4,28},{8,16},{12,20},{16,8},{20,12},{24,0},{28,4},{1,25},{... | collective-permute-start | bytes 245768 | tf_op jit(solution)/shard_map/ppermute | solution.py:462
  33.8 5.3 %collective-permute-start.8 = (bf16[32,1280]{1,0:T(8,128)(2,1)S(1)}, bf16[32,1280]{1,0:T(8,128)(2,1)S(1)}, u32[]{:S(2)}, u32[]{:S(2)}) collective-permute-start(bf16[32,1280]{1,0:T(8,128)(2,1)S(1)} %get-tuple-element.49.refs_0_), channel_id=1, source_target_pairs={{0,16},{4,20},{8,24},{12,28},{16,0},{20,4},{24,8},{28,12},{1,17},{... | collective-permute-start | bytes 245768 | tf_op jit(solution)/shard_map/ppermute | solution.py:462
  33.8 5.3 %collective-permute-start.7 = (bf16[32,1280]{1,0:T(8,128)(2,1)S(1)}, bf16[32,1280]{1,0:T(8,128)(2,1)S(1)}, u32[]{:S(2)}, u32[]{:S(2)}) collective-permute-start(bf16[32,1280]{1,0:T(8,128)(2,1)S(1)} %get-tuple-element.49.refs_0_), channel_id=1, source_target_pairs={{0,8},{4,12},{8,0},{12,4},{16,24},{20,28},{24,16},{28,20},{1,9},{5... | collective-permute-start | bytes 245768 | tf_op jit(solution)/shard_map/ppermute | solution.py:462
  35.4 1.2 %collective-permute-start.6 = (f32[32,128]{1,0:T(8,128)S(1)}, f32[32,128]{1,0:T(8,128)S(1)}, u32[]{:S(2)}, u32[]{:S(2)}) collective-permute-start(f32[32,128]{1,0:T(8,128)S(1)} %get-tuple-element.48.norm), channel_id=1, source_target_pairs={{0,1},{1,0},{2,3},{3,2},{4,5},{5,4},{6,7},{7,6},{8,9},{9,8},{10,11... | collective-permute-start | bytes 49160 | tf_op jit(solution)/shard_map/ppermute | solution.py:462
  39.2 4.6 %collective-permute-start.10 = (bf16[32,1280]{1,0:T(8,128)(2,1)S(1)}, bf16[32,1280]{1,0:T(8,128)(2,1)S(1)}, u32[]{:S(2)}, u32[]{:S(2)}) collective-permute-start(bf16[32,1280]{1,0:T(8,128)(2,1)S(1)} %get-tuple-element.50.new.new_near), channel_id=1, source_target_pairs={{0,4},{4,0},{8,12},{12,8},{16,20},{20,16},{24,28},{28,24},{1,5},{5... | collective-permute-start | bytes 245768 | tf_op jit(solution)/shard_map/ppermute | solution.py:462
  40.0 3.8 %copy-start = (f32[256,512]{1,0:T(8,128)S(1)}, f32[256,512]{1,0:T(8,128)}, u32[]{:S(2)}) copy-start(f32[256,512]{1,0:T(8,128)} %weight_q.1) | copy-start | bytes 1572868
  40.0 3.8 %copy-start.1 = (f32[256,512]{1,0:T(8,128)S(1)}, f32[256,512]{1,0:T(8,128)}, u32[]{:S(2)}) copy-start(f32[256,512]{1,0:T(8,128)} %momentum_q.1) | copy-start | bytes 1572868
  40.0 3.8 %copy-start.2 = (f32[512,256]{1,0:T(8,128)S(1)}, f32[512,256]{1,0:T(8,128)}, u32[]{:S(2)}) copy-start(f32[512,256]{1,0:T(8,128)} %weight_o.1) | copy-start | bytes 1572868
  40.0 3.8 %copy-start.3 = (f32[512,256]{1,0:T(8,128)S(1)}, f32[512,256]{1,0:T(8,128)}, u32[]{:S(2)}) copy-start(f32[512,256]{1,0:T(8,128)} %momentum_o.1) | copy-start | bytes 1572868
  40.0 3.8 %collective-permute-start.11 = (f32[32,128]{1,0:T(8,128)S(1)}, f32[32,128]{1,0:T(8,128)S(1)}, u32[]{:S(2)}, u32[]{:S(2)}) collective-permute-start(f32[32,128]{1,0:T(8,128)S(1)} %get-tuple-element.51.norm), channel_id=1, source_target_pairs={{0,2},{1,3},{2,0},{3,1},{4,6},{5,7},{6,4},{7,5},{8,10},{9,11},{10,... | collective-permute-start | bytes 49160 | tf_op jit(solution)/shard_map/ppermute | solution.py:462

commit v6 on v5

--- a/solution.py
+++ b/solution.py
@@ -49,7 +49,9 @@
 
 
 def parity():
-    return lax.rem(lax.axis_index("replica"), 2)
+    replica = lax.axis_index("replica")
+    odd = lax.rem(lax.axis_index("tensor"), 2) == 1
+    return jnp.where(odd, replica // (lax.axis_size("replica") // 2), lax.rem(replica, 2))
 
 
 def half_at(which, size):
@@ -259,36 +261,56 @@
     )(hat, in_vmem(mat_q), in_vmem(mat_o))
 
 
-def right_far_kernel(hat, mat_q, mat_o, part_q, part_o, hat_near, send, near, norm, all_q, all_o):
+def right_half(which, hat, mat_q, mat_o, part_q, part_o, store):
     size_q, size_o = mat_q.shape[0], mat_o.shape[0]
-    all_q[...] = part_q[...] + dot(hat[:, :size_q], mat_q[...], 1, 0)
-    all_o[...] = part_o[...] + dot(hat[:, size_q:size_q + size_o], mat_o[...], 1, 0)
-    mine = parity()
-    half_q, half_o = all_q.shape[1] // 2, all_o.shape[1] // 2
-    send[:, :half_q] = all_q[:, half_at(1 - mine, half_q)].astype(bf16)
-    send[:, half_q:] = all_o[:, half_at(1 - mine, half_o)].astype(bf16)
-    near[:, :half_q] = all_q[:, half_at(mine, half_q)]
-    near[:, half_q:] = all_o[:, half_at(mine, half_o)]
-    norm[...] = norm_of([hat_near, hat], size_q + size_o)
+    half_q, half_o = mat_q.shape[1] // 2, mat_o.shape[1] // 2
+    columns = half_at(which, half_q)
+    store(0, half_q, part_q[:, columns] + dot(hat[:, :size_q], mat_q[:, columns], 1, 0))
+    columns = half_at(which, half_o)
+    store(half_q, half_o, part_o[:, columns] + dot(
+        hat[:, size_q:size_q + size_o], mat_o[:, columns], 1, 0
+    ))
+
+
+def right_send_kernel(hat, mat_q, mat_o, part_q, part_o, send):
+    def store(column, width, value):
+        send[:, column:column + width] = value.astype(bf16)
+
+    right_half(1 - parity(), hat, mat_q, mat_o, part_q, part_o, store)
+
+
+def right_keep_kernel(hat, mat_q, mat_o, part_q, part_o, hat_near, near, norm):
+    def store(column, width, value):
+        near[:, column:column + width] = value
+
+    right_half(parity(), hat, mat_q, mat_o, part_q, part_o, store)
+    norm[...] = norm_of([hat_near, hat], mat_q.shape[0] + mat_o.shape[0])
 
 
 def right_far(hat, mat_q, mat_o, part_q, part_o, hat_near, norm_rows):
     rank = hat.shape[0]
     columns = (mat_q.shape[1] + mat_o.shape[1]) // 2
-    return pl.pallas_call(
-        right_far_kernel,
-        out_shape=(
-            shaped((rank, columns), bf16),
-            shaped((rank, columns), f32),
-            shaped((norm_rows, lanes), f32),
-        ),
+    operands = (hat, in_vmem(mat_q), in_vmem(mat_o), part_q, part_o)
+    effort = cost(rank * (mat_q.size + mat_o.size), mat_q.size + mat_o.size)
+    send = pl.pallas_call(
+        right_send_kernel,
+        out_shape=shaped((rank, columns), bf16),
+        in_specs=[whole] * 5,
+        out_specs=whole,
+        compiler_params=params(8),
+        cost_estimate=effort,
+        name="right_send",
+    )(*operands)
+    near, norm = pl.pallas_call(
+        right_keep_kernel,
+        out_shape=(shaped((rank, columns), f32), shaped((norm_rows, lanes), f32)),
         in_specs=[whole] * 6,
-        out_specs=(whole,) * 3,
-        scratch_shapes=[pltpu.VMEM(part_q.shape, f32), pltpu.VMEM(part_o.shape, f32)],
+        out_specs=(whole,) * 2,
         compiler_params=params(8),
-        cost_estimate=cost(2 * rank * (mat_q.size + mat_o.size), 2 * (mat_q.size + mat_o.size)),
-        name="right_far",
-    )(hat, in_vmem(mat_q), in_vmem(mat_o), part_q, part_o, hat_near)
+        cost_estimate=effort,
+        name="right_keep",
+    )(*operands, hat_near)
+    return send, near, norm
 
 
 def near_sum_kernel(near, got, norm, state, norm_out):
@@ -413,8 +435,8 @@
     ]
     moved = 4 * (mat_q.size + mat_o.size)
     mats = [in_vmem(mat) for mat in mats]
-    new_far = swap(new_near, 1)
-    norm_got = swap(norm, 2, "tensor")
+    new_far = swap_halves(new_near)
+    norm_got = swap_tensor(norm, 2)
     error_q_part, error_o_part = pl.pallas_call(
         finish_near_kernel,
         out_shape=(error_q, error_o),
@@ -457,23 +479,36 @@
     )
 
 
-def swap(value, bit, axis="replica"):
-    count = lax.axis_size(axis)
-    return lax.ppermute(value, axis, [(source, source ^ bit) for source in range(count)])
+def swap(value, even, odd):
+    replicas, tensors = lax.axis_size("replica"), lax.axis_size("tensor")
+    pairs = []
+    for replica in range(replicas):
+        for tensor in range(tensors):
+            target = replica ^ (odd if tensor % 2 else even)
+            pairs.append((replica * tensors + tensor, target * tensors + tensor))
+    return lax.ppermute(value, ("replica", "tensor"), pairs)
+
+
+def swap_halves(value):
+    return swap(value, 1, lax.axis_size("replica") // 2)
+
+
+def swap_tensor(value, bit):
+    count = lax.axis_size("tensor")
+    return lax.ppermute(value, "tensor", [(source, source ^ bit) for source in range(count)])
 
 
 def exchange(state, bits):
-    offsets = [0]
-    for bit in bits:
-        offsets += [offset | bit for offset in offsets]
-    got = {0: state}
-    for offset in offsets[:0:-1]:
-        got[offset] = swap(state, offset)
-    return [got[offset] for offset in offsets]
+    offsets = [(0, 0)]
+    for even, odd in bits:
+        offsets += [(first | even, second | odd) for first, second in offsets]
+    got = [swap(state, *offset) for offset in offsets[:0:-1]]
+    return [state] + got[::-1]
 
 
 def rounds_of(count):
-    bits = [1 << place for place in range(1, count.bit_length() - 1)]
+    places = range(1, count.bit_length() - 1)
+    bits = [(1 << place, 1 << (place - 1)) for place in places]
     return [bits[place:place + 2] for place in range(0, len(bits), 2)]
 
 
@@ -503,7 +538,7 @@
     columns = part.shape[1]
     rounds = rounds_of(replicas)
     state = small(
-        first_sum_kernel, "first_sum", shaped((rank, columns + lanes), bf16), part, norm, swap(send, 1)
+        first_sum_kernel, "first_sum", shaped((rank, columns + lanes), bf16), part, norm, swap_halves(send)
     )
     wide = shaped((rank, columns + 2 * lanes), bf16)
     for bits in rounds[:-1]:
@@ -514,14 +549,14 @@
         functools.partial(hat_kernel, half_q, columns), "hats", wide,
         ginv_q, ginv_o, *exchange(state, rounds[-1]),
     )
-    hat_far = swap(hat_near, 1)
+    hat_far = swap_halves(hat_near)
     part_q, part_o = right_near(hat_near, mat_q_near, mat_o_near)
     send, near, norm = right_far(
         hat_far, mat_q_far, mat_o_far, part_q, part_o, hat_near, norm_rows
     )
     state, norm = small(
         near_sum_kernel, "near_sum", (shaped(send.shape, bf16), shaped(norm.shape, f32)),
-        near, swap(send, 1), norm,
+        near, swap_halves(send), norm,
     )
     for bits in rounds[:-1]:
         state = small(
@@ -531,7 +566,7 @@
     new_near, norm = small(
         functools.partial(mean_kernel, replicas), "mean",
         (shaped(state.shape, bf16), shaped(norm.shape, f32)),
-        norm, swap(norm, 1, "tensor"), *states,
+        norm, swap_tensor(norm, 1), *states,
     )
     (
         error_q_new, error_o_new, new_q, new_o,

time: 46.6 us -> 45.5 us (0.976)
  waiting for transfers between devices: 17.8 us -> 14.8 us
  starting transfers between devices: 16 us -> 17.9 us
    ppermute x12, waiting for transfers between devices: 17.8 us -> 14.8 us  [the longest x10 13 us: swap(): return lax.ppermute(value, ('replica', 'tensor'), pairs)]
    ppermute x12, starting transfers between devices: 16 us -> 17.9 us  [the longest x10 16.3 us: swap(): return lax.ppermute(value, ('replica', 'tensor'), pairs)]
  transfers between devices with their start and end apart: 12 -> 12, of which waited for: 8 -> 8; matrix products, arithmetic and copies ran while one was open for 0% -> 0% of each run, Pallas kernels for 11% -> 12%
where the time goes in v6:
time: 45.5 us; the launch traced here: 45.4 us
  starting transfers between devices  17.9 us (39%)
  waiting for transfers between devices  14.8 us (33%)
  Pallas kernels  11.9 us (26%)
  between operations  0.78 us (2%)
    ppermute x10, starting transfers between devices, swap(): return lax.ppermute(value, ('replica', 'tensor'), pairs)  16.3 us
    ppermute x10, waiting for transfers between devices, swap(): return lax.ppermute(value, ('replica', 'tensor'), pairs)  13 us
    pallas_call x1, Pallas kernels, project(): pl.pallas_call(far_kernel, out_shape=mats + (shaped((rank, columns), bf16...  3.1 us
    pallas_call x1, Pallas kernels, project(): pl.pallas_call(near_kernel, out_shape=mats + (shaped((rank, columns), f32...  3.09 us
    pallas_call x1, Pallas kernels, finish(): pl.pallas_call(functools.partial(finish_far_kernel, count, norm_count), o...  2.54 us
    ppermute x2, waiting for transfers between devices, swap_tensor(): lax.ppermute(value, 'tensor', [(source, source ^ bit) for source in range...  1.71 us
    pallas_call x1, Pallas kernels, finish(): pl.pallas_call(finish_near_kernel, out_shape=(error_q, error_o), in_specs...  1.71 us
    ppermute x2, starting transfers between devices, swap_tensor(): lax.ppermute(value, 'tensor', [(source, source ^ bit) for source in range...  1.56 us
  transfers between devices with their start and end apart: 12, of which 8 were waited for; matrix products, arithmetic and copies ran while one was open for 0% of the time, Pallas kernels for 12%

profile of v6, /device:TPU:0, one launch (start us, length us, event | category | flops | bytes accessed | tf_op | source)
XLA Modules:
  0.0 45.4 jit_solution(16978168471068119343)
XLA Ops:
  0.7 3.1 %project_far.1 = (bf16[1024,512]{1,0:T(8,128)(2,1)S(1)}, bf16[256,2048]{1,0:T(8,128)(2,1)S(1)}, bf16[32,1280]{1,0:T(8,128)(2,1)S(1)}) custom-call(bf16[32,512]{1,0:T(8,128)(2,1)} %bitcast.7, bf16[32,2048]{1,0:T(8,128)(2,1)} %bitcast.5, bf16[2048,512]{1,0:T(8,128)(2,1)} %grad_q.3, bf16[2048,512]{1,0:T(8,128)(2,1)} %error_q.3, bf16[512,2048]{1,0:T(8,128)(2,1)} %grad_o.3, ...), custom_call_target="tpu_custom_call" | custom-call | flops 67108864 | bytes 4194304 | tf_op jit(solution)/shard_map/project_far/pallas_call | solution.py:153
  3.8 3.0 %collective-permute-start = (bf16[32,1280]{1,0:T(8,128)(2,1)S(1)}, bf16[32,1280]{1,0:T(8,128)(2,1)S(1)}, u32[]{:S(2)}, u32[]{:S(2)}) collective-permute-start(bf16[32,1280]{1,0:T(8,128)(2,1)S(1)} %get-tuple-element.37), channel_id=1, source_target_pairs={{0,4},{1,17},{2,6},{3,19},{4,0},{5,21},{6,2},{7,23},{8,12},{9,25},... | collective-permute-start | bytes 245768 | tf_op jit(solution)/shard_map/ppermute | solution.py:489
  6.8 3.1 %project_near.1 = (bf16[1024,512]{1,0:T(8,128)(2,1)S(1)}, bf16[256,2048]{1,0:T(8,128)(2,1)S(1)}, f32[32,1280]{1,0:T(8,128)S(1)}, f32[32,128]{1,0:T(8,128)S(1)}) custom-call(bf16[32,512]{1,0:T(8,128)(2,1)} %bitcast.8, bf16[32,2048]{1,0:T(8,128)(2,1)} %bitcast.6, bf16[2048,512]{1,0:T(8,128)(2,1)} %grad_q.3, bf16[2048,512]{1,0:T(8,128)(2,1)} %error_q.3, ...), custom_call_target="tpu_custom_call" | custom-call | flops 67108864 | bytes 4194304 | tf_op jit(solution)/shard_map/project_near/pallas_call | solution.py:163
  10.0 3.7 %collective-permute-start.3 = (bf16[32,1408]{1,0:T(8,128)(2,1)S(1)}, bf16[32,1408]{1,0:T(8,128)(2,1)S(1)}, u32[]{:S(2)}, u32[]{:S(2)}) collective-permute-start(bf16[32,1408]{1,0:T(8,128)(2,1)S(1)} %first_sum.1.refs_0_), channel_id=1, source_target_pairs={{0,24},{1,13},{2,26},{3,15},{4,28},{5,9},{6,30},{7,11},{8,16},{9,5... | collective-permute-start | bytes 270344 | tf_op jit(solution)/shard_map/ppermute | solution.py:489
  13.6 0.8 %collective-permute-start.1 = (bf16[32,1408]{1,0:T(8,128)(2,1)S(1)}, bf16[32,1408]{1,0:T(8,128)(2,1)S(1)}, u32[]{:S(2)}, u32[]{:S(2)}) collective-permute-start(bf16[32,1408]{1,0:T(8,128)(2,1)S(1)} %first_sum.1.refs_0_), channel_id=1, source_target_pairs={{0,8},{1,5},{2,10},{3,7},{4,12},{5,1},{6,14},{7,3},{8,0},{9,13},{1... | collective-permute-start | bytes 270344 | tf_op jit(solution)/shard_map/ppermute | solution.py:489
  14.4 2.6 %collective-permute-done.3.refs_3_ = bf16[32,1408]{1,0:T(8,128)(2,1)S(1)} collective-permute-done((bf16[32,1408]{1,0:T(8,128)(2,1)S(1)}, bf16[32,1408]{1,0:T(8,128)(2,1)S(1)}, u32[]{:S(2)}, u32[]{:S(2)}) %collective-permute-start.3) | collective-permute-done | bytes 90144 | tf_op jit(solution)/shard_map/ppermute | solution.py:489
  17.0 2.5 %collective-permute-done.2.refs_2_ = bf16[32,1408]{1,0:T(8,128)(2,1)S(1)} collective-permute-done((bf16[32,1408]{1,0:T(8,128)(2,1)S(1)}, bf16[32,1408]{1,0:T(8,128)(2,1)S(1)}, u32[]{:S(2)}, u32[]{:S(2)}) %collective-permute-start.2) | collective-permute-done | bytes 90144 | tf_op jit(solution)/shard_map/ppermute | solution.py:489
  19.5 0.3 hats.1.hat.hat_near
  19.9 1.5 %collective-permute-start.4 = (bf16[32,1536]{1,0:T(8,128)(2,1)S(1)}, bf16[32,1536]{1,0:T(8,128)(2,1)S(1)}, u32[]{:S(2)}, u32[]{:S(2)}) collective-permute-start(bf16[32,1536]{1,0:T(8,128)(2,1)S(1)} %hats.1.hat.hat_near), channel_id=1, source_target_pairs={{0,4},{1,17},{2,6},{3,19},{4,0},{5,21},{6,2},{7,23},{8,12},{9,25},... | collective-permute-start | bytes 294920 | tf_op jit(solution)/shard_map/ppermute | solution.py:489
  21.3 0.5 %right_near.1 = (f32[32,512]{1,0:T(8,128)S(1)}, f32[32,2048]{1,0:T(8,128)S(1)}) custom-call(bf16[32,1536]{1,0:T(8,128)(2,1)S(1)} %hats.1.hat.hat_near, bf16[1024,512]{1,0:T(8,128)(2,1)S(1)} %get-tuple-element.38.mat_q.mat_q_near, bf16[256,2048]{1,0:T(8,128)(2,1)S(1)} %get-tuple-element.39.mat_o.mat_o_near), custom_call_target="tpu_custom_call" | custom-call | flops 67108864 | bytes 2097152 | tf_op jit(solution)/shard_map/right_near/pallas_call | solution.py:253
  21.8 2.8 %collective-permute-done.4.hat.hat_far = bf16[32,1536]{1,0:T(8,128)(2,1)S(1)} collective-permute-done((bf16[32,1536]{1,0:T(8,128)(2,1)S(1)}, bf16[32,1536]{1,0:T(8,128)(2,1)S(1)}, u32[]{:S(2)}, u32[]{:S(2)}) %collective-permute-start.4) | collective-permute-done | bytes 98336 | tf_op jit(solution)/shard_map/ppermute | solution.py:489
  24.6 0.3 right_send.1
  24.9 1.5 %collective-permute-start.5 = (bf16[32,1280]{1,0:T(8,128)(2,1)S(1)}, bf16[32,1280]{1,0:T(8,128)(2,1)S(1)}, u32[]{:S(2)}, u32[]{:S(2)}) collective-permute-start(bf16[32,1280]{1,0:T(8,128)(2,1)S(1)} %right_send.1), channel_id=1, source_target_pairs={{0,4},{1,17},{2,6},{3,19},{4,0},{5,21},{6,2},{7,23},{8,12},{9,25},... | collective-permute-start | bytes 245768 | tf_op jit(solution)/shard_map/ppermute | solution.py:489
  26.6 2.8 %collective-permute-done.5.got = bf16[32,1280]{1,0:T(8,128)(2,1)S(1)} collective-permute-done((bf16[32,1280]{1,0:T(8,128)(2,1)S(1)}, bf16[32,1280]{1,0:T(8,128)(2,1)S(1)}, u32[]{:S(2)}, u32[]{:S(2)}) %collective-permute-start.5) | collective-permute-done | bytes 81952 | tf_op jit(solution)/shard_map/ppermute | solution.py:489
  29.4 2.7 %collective-permute-start.9 = (bf16[32,1280]{1,0:T(8,128)(2,1)S(1)}, bf16[32,1280]{1,0:T(8,128)(2,1)S(1)}, u32[]{:S(2)}, u32[]{:S(2)}) collective-permute-start(bf16[32,1280]{1,0:T(8,128)(2,1)S(1)} %get-tuple-element.47.refs_0_), channel_id=1, source_target_pairs={{0,24},{1,13},{2,26},{3,15},{4,28},{5,9},{6,30},{7,11},{8,16},{9,5... | collective-permute-start | bytes 245768 | tf_op jit(solution)/shard_map/ppermute | solution.py:489
  32.1 1.8 %collective-permute-start.7 = (bf16[32,1280]{1,0:T(8,128)(2,1)S(1)}, bf16[32,1280]{1,0:T(8,128)(2,1)S(1)}, u32[]{:S(2)}, u32[]{:S(2)}) collective-permute-start(bf16[32,1280]{1,0:T(8,128)(2,1)S(1)} %get-tuple-element.47.refs_0_), channel_id=1, source_target_pairs={{0,8},{1,5},{2,10},{3,7},{4,12},{5,1},{6,14},{7,3},{8,0},{9,13},{1... | collective-permute-start | bytes 245768 | tf_op jit(solution)/shard_map/ppermute | solution.py:489
  33.8 1.2 %collective-permute-done.6.norm_got = f32[32,128]{1,0:T(8,128)S(1)} collective-permute-done((f32[32,128]{1,0:T(8,128)S(1)}, f32[32,128]{1,0:T(8,128)S(1)}, u32[]{:S(2)}, u32[]{:S(2)}) %collective-permute-start.6) | collective-permute-done | bytes 16416 | tf_op jit(solution)/shard_map/ppermute | solution.py:498
  35.0 0.7 %collective-permute-done.9.refs_3_ = bf16[32,1280]{1,0:T(8,128)(2,1)S(1)} collective-permute-done((bf16[32,1280]{1,0:T(8,128)(2,1)S(1)}, bf16[32,1280]{1,0:T(8,128)(2,1)S(1)}, u32[]{:S(2)}, u32[]{:S(2)}) %collective-permute-start.9) | collective-permute-done | bytes 81952 | tf_op jit(solution)/shard_map/ppermute | solution.py:489
  35.7 1.8 %collective-permute-done.8.refs_2_ = bf16[32,1280]{1,0:T(8,128)(2,1)S(1)} collective-permute-done((bf16[32,1280]{1,0:T(8,128)(2,1)S(1)}, bf16[32,1280]{1,0:T(8,128)(2,1)S(1)}, u32[]{:S(2)}, u32[]{:S(2)}) %collective-permute-start.8) | collective-permute-done | bytes 81952 | tf_op jit(solution)/shard_map/ppermute | solution.py:489
  37.5 1.5 %collective-permute-start.10 = (bf16[32,1280]{1,0:T(8,128)(2,1)S(1)}, bf16[32,1280]{1,0:T(8,128)(2,1)S(1)}, u32[]{:S(2)}, u32[]{:S(2)}) collective-permute-start(bf16[32,1280]{1,0:T(8,128)(2,1)S(1)} %get-tuple-element.48.new.new_near), channel_id=1, source_target_pairs={{0,4},{1,17},{2,6},{3,19},{4,0},{5,21},{6,2},{7,23},{8,12},{9,25},... | collective-permute-start | bytes 245768 | tf_op jit(solution)/shard_map/ppermute | solution.py:489
  39.0 1.6 %collective-permute-start.11 = (f32[32,128]{1,0:T(8,128)S(1)}, f32[32,128]{1,0:T(8,128)S(1)}, u32[]{:S(2)}, u32[]{:S(2)}) collective-permute-start(f32[32,128]{1,0:T(8,128)S(1)} %get-tuple-element.49.norm), channel_id=1, source_target_pairs={{0,2},{1,3},{2,0},{3,1},{4,6},{5,7},{6,4},{7,5},{8,10},{9,11},{10,... | collective-permute-start | bytes 49160 | tf_op jit(solution)/shard_map/ppermute | solution.py:498
  40.5 1.7 %finish_near.1 = (bf16[2048,512]{1,0:T(8,128)(2,1)}, bf16[512,2048]{1,0:T(8,128)(2,1)}) custom-call(bf16[32,1536]{1,0:T(8,128)(2,1)S(1)} %hats.1.hat.hat_near, bf16[32,1536]{1,0:T(8,128)(2,1)S(1)} %collective-permute-done.4.hat.hat_far, bf16[1024,512]{1,0:T(8,128)(2,1)S(1)} %get-tuple-element.38.mat_q.mat_q_near, ...), custom_call_target="tpu_custom_call" | custom-call | flops 67108864 | bytes 4194304 | tf_op jit(solution)/shard_map/finish_near/pallas_call | solution.py:440
  42.2 0.5 %collective-permute-done.11.norm_got = f32[32,128]{1,0:T(8,128)S(1)} collective-permute-done((f32[32,128]{1,0:T(8,128)S(1)}, f32[32,128]{1,0:T(8,128)S(1)}, u32[]{:S(2)}, u32[]{:S(2)}) %collective-permute-start.11) | collective-permute-done | bytes 16416 | tf_op jit(solution)/shard_map/ppermute | solution.py:498
  42.8 2.5 %finish_far.1 = (bf16[2048,512]{1,0:T(8,128)(2,1)}, bf16[512,2048]{1,0:T(8,128)(2,1)}, bf16[32,512]{1,0:T(8,128)(2,1)}, bf16[32,2048]{1,0:T(8,128)(2,1)}, f32[25...) custom-call(bf16[32,1536]{1,0:T(8,128)(2,1)S(1)} %hats.1.hat.hat_nea, ...), custom_call_target="tpu_custom_call", output_to_operand_aliasing={{0}: (14, {}), {1}: (15, {})} | custom-call | flops 67108864 | bytes 4194304 | tf_op jit(solution)/shard_map/finish_far/pallas_call | solution.py:461
  (25 shorter events, 0.4 us)
Async XLA Ops:
  0.6 6.2 %copy-start.4 = (bf16[1,1,4096]{2,1,0:T(2,128)(2,1)S(1)}, bf16[1,1,4096]{2,1,0:T(2,128)(2,1)}, u32[]{:S(2)}) copy-start(bf16[1,1,4096]{2,1,0:T(2,128)(2,1)} %norm_grads.1) | copy-start | bytes 24580
  3.8 15.8 %copy-start.5 = (f32[32,32]{1,0:T(8,128)S(1)}, f32[32,32]{1,0:T(8,128)}, u32[]{:S(2)}) copy-start(f32[32,32]{1,0:T(8,128)} %ginv_q.1) | copy-start | bytes 12292
  3.8 15.7 %copy-start.6 = (f32[32,32]{1,0:T(8,128)S(1)}, f32[32,32]{1,0:T(8,128)}, u32[]{:S(2)}) copy-start(f32[32,32]{1,0:T(8,128)} %ginv_o.1) | copy-start | bytes 12292
  3.8 6.1 %collective-permute-start = (bf16[32,1280]{1,0:T(8,128)(2,1)S(1)}, bf16[32,1280]{1,0:T(8,128)(2,1)S(1)}, u32[]{:S(2)}, u32[]{:S(2)}) collective-permute-start(bf16[32,1280]{1,0:T(8,128)(2,1)S(1)} %get-tuple-element.37), channel_id=1, source_target_pairs={{0,4},{1,17},{2,6},{3,19},{4,0},{5,21},{6,2},{7,23},{8,12},{9,25},... | collective-permute-start | bytes 245768 | tf_op jit(solution)/shard_map/ppermute | solution.py:489
  10.0 7.1 %collective-permute-start.3 = (bf16[32,1408]{1,0:T(8,128)(2,1)S(1)}, bf16[32,1408]{1,0:T(8,128)(2,1)S(1)}, u32[]{:S(2)}, u32[]{:S(2)}) collective-permute-start(bf16[32,1408]{1,0:T(8,128)(2,1)S(1)} %first_sum.1.refs_0_), channel_id=1, source_target_pairs={{0,24},{1,13},{2,26},{3,15},{4,28},{5,9},{6,30},{7,11},{8,16},{9,5... | collective-permute-start | bytes 270344 | tf_op jit(solution)/shard_map/ppermute | solution.py:489
  13.6 5.9 %collective-permute-start.2 = (bf16[32,1408]{1,0:T(8,128)(2,1)S(1)}, bf16[32,1408]{1,0:T(8,128)(2,1)S(1)}, u32[]{:S(2)}, u32[]{:S(2)}) collective-permute-start(bf16[32,1408]{1,0:T(8,128)(2,1)S(1)} %first_sum.1.refs_0_), channel_id=1, source_target_pairs={{0,16},{1,9},{2,18},{3,11},{4,20},{5,13},{6,22},{7,15},{8,24},{9,1... | collective-permute-start | bytes 270344 | tf_op jit(solution)/shard_map/ppermute | solution.py:489
  13.6 5.9 %collective-permute-start.1 = (bf16[32,1408]{1,0:T(8,128)(2,1)S(1)}, bf16[32,1408]{1,0:T(8,128)(2,1)S(1)}, u32[]{:S(2)}, u32[]{:S(2)}) collective-permute-start(bf16[32,1408]{1,0:T(8,128)(2,1)S(1)} %first_sum.1.refs_0_), channel_id=1, source_target_pairs={{0,8},{1,5},{2,10},{3,7},{4,12},{5,1},{6,14},{7,3},{8,0},{9,13},{1... | collective-permute-start | bytes 270344 | tf_op jit(solution)/shard_map/ppermute | solution.py:489
  19.9 4.7 %collective-permute-start.4 = (bf16[32,1536]{1,0:T(8,128)(2,1)S(1)}, bf16[32,1536]{1,0:T(8,128)(2,1)S(1)}, u32[]{:S(2)}, u32[]{:S(2)}) collective-permute-start(bf16[32,1536]{1,0:T(8,128)(2,1)S(1)} %hats.1.hat.hat_near), channel_id=1, source_target_pairs={{0,4},{1,17},{2,6},{3,19},{4,0},{5,21},{6,2},{7,23},{8,12},{9,25},... | collective-permute-start | bytes 294920 | tf_op jit(solution)/shard_map/ppermute | solution.py:489
  24.9 4.5 %collective-permute-start.5 = (bf16[32,1280]{1,0:T(8,128)(2,1)S(1)}, bf16[32,1280]{1,0:T(8,128)(2,1)S(1)}, u32[]{:S(2)}, u32[]{:S(2)}) collective-permute-start(bf16[32,1280]{1,0:T(8,128)(2,1)S(1)} %right_send.1), channel_id=1, source_target_pairs={{0,4},{1,17},{2,6},{3,19},{4,0},{5,21},{6,2},{7,23},{8,12},{9,25},... | collective-permute-start | bytes 245768 | tf_op jit(solution)/shard_map/ppermute | solution.py:489
  29.4 6.3 %collective-permute-start.9 = (bf16[32,1280]{1,0:T(8,128)(2,1)S(1)}, bf16[32,1280]{1,0:T(8,128)(2,1)S(1)}, u32[]{:S(2)}, u32[]{:S(2)}) collective-permute-start(bf16[32,1280]{1,0:T(8,128)(2,1)S(1)} %get-tuple-element.47.refs_0_), channel_id=1, source_target_pairs={{0,24},{1,13},{2,26},{3,15},{4,28},{5,9},{6,30},{7,11},{8,16},{9,5... | collective-permute-start | bytes 245768 | tf_op jit(solution)/shard_map/ppermute | solution.py:489
  32.1 5.4 %collective-permute-start.8 = (bf16[32,1280]{1,0:T(8,128)(2,1)S(1)}, bf16[32,1280]{1,0:T(8,128)(2,1)S(1)}, u32[]{:S(2)}, u32[]{:S(2)}) collective-permute-start(bf16[32,1280]{1,0:T(8,128)(2,1)S(1)} %get-tuple-element.47.refs_0_), channel_id=1, source_target_pairs={{0,16},{1,9},{2,18},{3,11},{4,20},{5,13},{6,22},{7,15},{8,24},{9,1... | collective-permute-start | bytes 245768 | tf_op jit(solution)/shard_map/ppermute | solution.py:489
  32.1 5.4 %collective-permute-start.7 = (bf16[32,1280]{1,0:T(8,128)(2,1)S(1)}, bf16[32,1280]{1,0:T(8,128)(2,1)S(1)}, u32[]{:S(2)}, u32[]{:S(2)}) collective-permute-start(bf16[32,1280]{1,0:T(8,128)(2,1)S(1)} %get-tuple-element.47.refs_0_), channel_id=1, source_target_pairs={{0,8},{1,5},{2,10},{3,7},{4,12},{5,1},{6,14},{7,3},{8,0},{9,13},{1... | collective-permute-start | bytes 245768 | tf_op jit(solution)/shard_map/ppermute | solution.py:489
  33.8 1.2 %collective-permute-start.6 = (f32[32,128]{1,0:T(8,128)S(1)}, f32[32,128]{1,0:T(8,128)S(1)}, u32[]{:S(2)}, u32[]{:S(2)}) collective-permute-start(f32[32,128]{1,0:T(8,128)S(1)} %get-tuple-element.46.norm), channel_id=1, source_target_pairs={{0,1},{1,0},{2,3},{3,2},{4,5},{5,4},{6,7},{7,6},{8,9},{9,8},{10,11... | collective-permute-start | bytes 49160 | tf_op jit(solution)/shard_map/ppermute | solution.py:498
  37.5 5.3 %collective-permute-start.10 = (bf16[32,1280]{1,0:T(8,128)(2,1)S(1)}, bf16[32,1280]{1,0:T(8,128)(2,1)S(1)}, u32[]{:S(2)}, u32[]{:S(2)}) collective-permute-start(bf16[32,1280]{1,0:T(8,128)(2,1)S(1)} %get-tuple-element.48.new.new_near), channel_id=1, source_target_pairs={{0,4},{1,17},{2,6},{3,19},{4,0},{5,21},{6,2},{7,23},{8,12},{9,25},... | collective-permute-start | bytes 245768 | tf_op jit(solution)/shard_map/ppermute | solution.py:489
  39.0 3.8 %copy-start = (f32[256,512]{1,0:T(8,128)S(1)}, f32[256,512]{1,0:T(8,128)}, u32[]{:S(2)}) copy-start(f32[256,512]{1,0:T(8,128)} %weight_q.1) | copy-start | bytes 1572868
  39.0 3.8 %copy-start.1 = (f32[256,512]{1,0:T(8,128)S(1)}, f32[256,512]{1,0:T(8,128)}, u32[]{:S(2)}) copy-start(f32[256,512]{1,0:T(8,128)} %momentum_q.1) | copy-start | bytes 1572868
  39.0 3.8 %copy-start.2 = (f32[512,256]{1,0:T(8,128)S(1)}, f32[512,256]{1,0:T(8,128)}, u32[]{:S(2)}) copy-start(f32[512,256]{1,0:T(8,128)} %weight_o.1) | copy-start | bytes 1572868
  39.0 3.8 %copy-start.3 = (f32[512,256]{1,0:T(8,128)S(1)}, f32[512,256]{1,0:T(8,128)}, u32[]{:S(2)}) copy-start(f32[512,256]{1,0:T(8,128)} %momentum_o.1) | copy-start | bytes 1572868
  39.0 3.8 %collective-permute-start.11 = (f32[32,128]{1,0:T(8,128)S(1)}, f32[32,128]{1,0:T(8,128)S(1)}, u32[]{:S(2)}, u32[]{:S(2)}) collective-permute-start(f32[32,128]{1,0:T(8,128)S(1)} %get-tuple-element.49.norm), channel_id=1, source_target_pairs={{0,2},{1,3},{2,0},{3,1},{4,6},{5,7},{6,4},{7,5},{8,10},{9,11},{10,... | collective-permute-start | bytes 49160 | tf_op jit(solution)/shard_map/ppermute | solution.py:498

commit v7 on v6

--- a/solution.py
+++ b/solution.py
@@ -97,9 +97,9 @@
     for grad_v, error_v, mat, fac, part, column, copies in jobs:
         for copy in copies:
             copy.wait()
-        block = (grad_v[part].astype(f32) + error_v[part].astype(f32)).astype(bf16)
+        block = grad_v[part] + error_v[part]
         mat[part] = block
-        store(column, dot(fac[...], block, 1, 1))
+        store(column, dot(block, fac[...], 1, 1).T)
 
 
 def far_kernel(
@@ -236,10 +236,14 @@
     store_norm(out, columns, norm_of(states, columns))
 
 
-def mean_kernel(count, norm, norm_got, *refs):
-    *states, new, norm_sum = refs
+def norm_add_kernel(mine, got, total):
+    total[...] = mine[...] + got[...]
+
+
+def mean_kernel(count, norm_count, norm, norm_got, *refs):
+    *states, new, norm_mean = refs
     new[...] = (total_of(states, new.shape[1]) / count).astype(bf16)
-    norm_sum[...] = norm[...] + norm_got[...]
+    norm_mean[...] = (norm[...] + norm_got[...]) / norm_count
 
 
 def right_near_kernel(hat, mat_q, mat_o, part_q, part_o):
@@ -341,20 +345,6 @@
     return copies
 
 
-def finish_near_kernel(
-    hat_near, hat_far, mat_q_near, mat_o_near, mat_q_far, mat_o_far, new,
-    error_q, error_o, stage_q, stage_o, sems
-):
-    mine = parity()
-    copies = error_columns(
-        mine, hat_near, 0, mine, mat_q_near, mat_o_near, new, error_q, error_o, stage_q, stage_o, sems, 0
-    ) + error_columns(
-        mine, hat_far, 1, 1 - mine, mat_q_far, mat_o_far, new, error_q, error_o, stage_q, stage_o, sems, 4
-    )
-    for copy in copies:
-        copy.wait()
-
-
 def piece_of(near, far, index, count, size, pieces):
     half = count // 2
     here = index // half == parity()
@@ -369,13 +359,48 @@
     return pieces[slot].astype(bf16)
 
 
+def finish_near_kernel(
+    count, hat_near, hat_far, mat_q_near, mat_o_near, mat_q_far, mat_o_far, new, weight_q, momentum_q,
+    error_q, error_o, momentum_q_h, weight_q_h,
+    stage_q, stage_o, momentum_q_new, weight_q_new, pieces, sems, out_sems
+):
+    mine = parity()
+    me = lax.axis_index("replica")
+    copies = error_columns(
+        mine, hat_near, 0, mine, mat_q_near, mat_o_near, new, error_q, error_o, stage_q, stage_o, sems, 0
+    ) + error_columns(
+        mine, hat_far, 1, 1 - mine, mat_q_far, mat_o_far, new, error_q, error_o, stage_q, stage_o, sems, 4
+    )
+    piece = piece_of(hat_near, hat_far, me, count, weight_q.shape[0], pieces)
+    copies += query_columns(
+        mine, piece, new, weight_q, momentum_q, momentum_q_new, weight_q_new,
+        momentum_q_h, weight_q_h, out_sems
+    )
+    for copy in copies:
+        copy.wait()
+
+
+def query_columns(
+    which, piece, new, weight, momentum, momentum_new, weight_new, momentum_h, weight_h, sems
+):
+    wide = momentum_new.shape[1]
+    columns = half_at(which, wide)
+    moved = momentum_decay * momentum[:, columns] + dot(piece, new[:, :wide], 0, 0)
+    momentum_new[...] = moved
+    weight_new[...] = weight[:, columns] - step_size * moved
+    return [
+        load(momentum_new, momentum_h.at[:, columns], sems.at[0]),
+        load(weight_new, weight_h.at[:, columns], sems.at[1]),
+    ]
+
+
 def finish_far_kernel(
-    count, norm_count, hat_near, hat_far, mat_q_near, mat_o_near, mat_q_far, mat_o_far,
-    new_near, new_far, weight_q, momentum_q, weight_o, momentum_o, norm, norm_got,
-    error_q_in, error_o_in,
-    error_q, error_o, new_q_h, new_o_h, momentum_q_h, weight_q_h, momentum_o_h, weight_o_h, norm_h,
-    stage_q, stage_o, new_q, new_o, momentum_q_new, weight_q_new, momentum_o_new, weight_o_new,
-    norm_mean, pieces_q, pieces_o, sems, out_sems
+    count, hat_near, hat_far, mat_q_near, mat_o_near, mat_q_far, mat_o_far,
+    new_near, new_far, weight_q, momentum_q, weight_o, momentum_o, norm,
+    error_q_in, error_o_in, momentum_q_in, weight_q_in,
+    error_q, error_o, momentum_q_h, weight_q_h, new_q_h, new_o_h, momentum_o_h, weight_o_h, norm_h,
+    stage_q, stage_o, momentum_q_new, weight_q_new, new_q, new_o, momentum_o_new, weight_o_new,
+    pieces_q, pieces_o, sems, out_sems
 ):
     mine = parity()
     me = lax.axis_index("replica")
@@ -386,25 +411,14 @@
     new_q[:, half_at(1 - mine, wide_q)] = new_far[:, :wide_q]
     new_o[:, half_at(mine, wide_o)] = new_near[:, wide_q:]
     new_o[:, half_at(1 - mine, wide_o)] = new_far[:, wide_q:]
-    norm_mean[...] = (norm[...] + norm_got[...]) / norm_count
     copies = [
         load(new_q, new_q_h, out_sems.at[0]),
         load(new_o, new_o_h, out_sems.at[1]),
-        load(norm_mean, norm_h, out_sems.at[2]),
+        load(norm, norm_h, out_sems.at[2]),
     ]
     copies += error_columns(
         1 - mine, hat_near, 0, mine, mat_q_near, mat_o_near, new_far,
         error_q, error_o, stage_q, stage_o, sems, 0
-    )
-    piece = piece_of(hat_near, hat_far, me, count, weight_q.shape[0], pieces_q)
-    moved = momentum_decay * momentum_q[...] + dot(piece, new_q[...], 0, 0)
-    momentum_q_new[...] = moved
-    weight_q_new[...] = weight_q[...] - step_size * moved
-    copies.append(load(momentum_q_new, momentum_q_h, out_sems.at[3]))
-    copies.append(load(weight_q_new, weight_q_h, out_sems.at[4]))
-    copies += error_columns(
-        1 - mine, hat_far, 1, 1 - mine, mat_q_far, mat_o_far, new_far,
-        error_q, error_o, stage_q, stage_o, sems, 4
     )
     piece = piece_of(
         new_near.at[:, wide_q:], new_far.at[:, wide_q:], me, count, weight_o.shape[1], pieces_o
@@ -414,69 +428,76 @@
         moved = momentum_decay * momentum_o[rows] + dot(hat[:, size_q:size_q + size_o], piece, 0, 0)
         momentum_o_new[rows] = moved
         weight_o_new[rows] = weight_o[rows] - step_size * moved
-    copies.append(load(momentum_o_new, momentum_o_h, out_sems.at[5]))
-    copies.append(load(weight_o_new, weight_o_h, out_sems.at[6]))
+    copies.append(load(momentum_o_new, momentum_o_h, out_sems.at[3]))
+    copies.append(load(weight_o_new, weight_o_h, out_sems.at[4]))
+    copies += error_columns(
+        1 - mine, hat_far, 1, 1 - mine, mat_q_far, mat_o_far, new_far,
+        error_q, error_o, stage_q, stage_o, sems, 4
+    )
+    piece = piece_of(hat_near, hat_far, me, count, weight_q.shape[0], pieces_q)
+    copies += query_columns(
+        1 - mine, piece, new_far, weight_q, momentum_q, momentum_q_new, weight_q_new,
+        momentum_q_h, weight_q_h, out_sems.at[5:7]
+    )
     for copy in copies:
         copy.wait()
 
 
-def finish(
-    count, norm_count, hat_near, hat_far, mats, new_near, weights, norm
-):
+def finish(count, hat_near, hat_far, mats, new_near, weights, norm):
     mat_q, mat_o = mats[0], mats[1]
     weight_q, _, weight_o, _ = weights
     rank = hat_near.shape[0]
     size_q, size_o = mat_q.shape[0], mat_o.shape[0]
-    error_q = shaped((2 * size_q, mat_q.shape[1]), bf16)
-    error_o = shaped((2 * size_o, mat_o.shape[1]), bf16)
+    early = (
+        shaped((2 * size_q, mat_q.shape[1]), bf16),
+        shaped((2 * size_o, mat_o.shape[1]), bf16),
+        shaped(weight_q.shape, f32),
+        shaped(weight_q.shape, f32),
+    )
+    late = (
+        shaped((rank, mat_q.shape[1]), bf16),
+        shaped((rank, mat_o.shape[1]), bf16),
+        shaped(weight_o.shape, f32),
+        shaped(weight_o.shape, f32),
+    )
+    piece_q = (weight_q.shape[0], weight_q.shape[1] // 2)
     stages = [
         pltpu.VMEM((2 * size_q, mat_q.shape[1] // 2), bf16),
         pltpu.VMEM((2 * size_o, mat_o.shape[1] // 2), bf16),
+        pltpu.VMEM(piece_q, f32),
+        pltpu.VMEM(piece_q, f32),
     ]
+    pieces_q = pltpu.VMEM((count // 2, rank, weight_q.shape[0]), f32)
+    pieces_o = pltpu.VMEM((count // 2, rank, weight_o.shape[1]), f32)
     moved = 4 * (mat_q.size + mat_o.size)
     mats = [in_vmem(mat) for mat in mats]
+    weights = [in_vmem(value) for value in weights]
     new_far = swap_halves(new_near)
-    norm_got = swap_tensor(norm, 2)
-    error_q_part, error_o_part = pl.pallas_call(
-        finish_near_kernel,
-        out_shape=(error_q, error_o),
-        in_specs=[whole] * 7,
-        out_specs=(in_place,) * 2,
-        scratch_shapes=stages + [pltpu.SemaphoreType.DMA((8,))],
+    parts = pl.pallas_call(
+        functools.partial(finish_near_kernel, count),
+        out_shape=early,
+        in_specs=[whole] * 9,
+        out_specs=(in_place,) * 4,
+        scratch_shapes=stages + [
+            pieces_q, pltpu.SemaphoreType.DMA((8,)), pltpu.SemaphoreType.DMA((2,))
+        ],
         compiler_params=params(12),
         cost_estimate=cost(2 * rank * (mat_q.size + mat_o.size), moved),
         name="finish_near",
-    )(hat_near, hat_far, *mats, new_near)
-    outs = (
-        error_q,
-        error_o,
-        shaped((rank, mat_q.shape[1]), bf16),
-        shaped((rank, mat_o.shape[1]), bf16),
-        shaped(weight_q.shape, f32),
-        shaped(weight_q.shape, f32),
-        shaped(weight_o.shape, f32),
-        shaped(weight_o.shape, f32),
-        shaped(norm.shape, f32),
-    )
+    )(hat_near, hat_far, *mats, new_near, *weights[:2])
     return pl.pallas_call(
-        functools.partial(finish_far_kernel, count, norm_count),
-        out_shape=outs,
-        in_specs=[whole] * 14 + [in_place] * 2,
-        out_specs=(in_place,) * len(outs),
-        scratch_shapes=stages + [pltpu.VMEM(out.shape, out.dtype) for out in outs[2:]] + [
-            pltpu.VMEM((count // 2, rank, weight_q.shape[0]), f32),
-            pltpu.VMEM((count // 2, rank, weight_o.shape[1]), f32),
-            pltpu.SemaphoreType.DMA((8,)),
-            pltpu.SemaphoreType.DMA((7,)),
+        functools.partial(finish_far_kernel, count),
+        out_shape=early + late + (shaped(norm.shape, f32),),
+        in_specs=[whole] * 13 + [in_place] * 4,
+        out_specs=(in_place,) * 9,
+        scratch_shapes=stages + [pltpu.VMEM(out.shape, out.dtype) for out in late] + [
+            pieces_q, pieces_o, pltpu.SemaphoreType.DMA((8,)), pltpu.SemaphoreType.DMA((7,))
         ],
-        input_output_aliases={14: 0, 15: 1},
+        input_output_aliases={13: 0, 14: 1, 15: 2, 16: 3},
         compiler_params=params(16),
         cost_estimate=cost(2 * rank * (mat_q.size + mat_o.size), moved),
         name="finish_far",
-    )(
-        hat_near, hat_far, *mats, new_near, new_far, *(in_vmem(value) for value in weights),
-        norm, norm_got, error_q_part, error_o_part,
-    )
+    )(hat_near, hat_far, *mats, new_near, new_far, *weights, norm, *parts)
 
 
 def swap(value, even, odd):
@@ -563,16 +584,19 @@
             plain_sum_kernel, "plain_sum", shaped(state.shape, bf16), *exchange(state, bits)
         )
     states = exchange(state, rounds[-1])
+    norm = small(
+        norm_add_kernel, "norm_add", shaped(norm.shape, f32), norm, swap_tensor(norm, 1)
+    )
     new_near, norm = small(
-        functools.partial(mean_kernel, replicas), "mean",
+        functools.partial(mean_kernel, replicas, replicas * tensors), "mean",
         (shaped(state.shape, bf16), shaped(norm.shape, f32)),
-        norm, swap_tensor(norm, 1), *states,
+        norm, swap_tensor(norm, 2), *states,
     )
     (
-        error_q_new, error_o_new, new_q, new_o,
-        momentum_q_new, weight_q_new, momentum_o_new, weight_o_new, norm_mean,
+        error_q_new, error_o_new, momentum_q_new, weight_q_new,
+        new_q, new_o, momentum_o_new, weight_o_new, norm_mean,
     ) = finish(
-        replicas, replicas * tensors, hat_near, hat_far,
+        replicas, hat_near, hat_far,
         (mat_q_near, mat_o_near, mat_q_far, mat_o_far), new_near,
         (weight_q, momentum_q, weight_o, momentum_o), norm,
     )

time: 45.5 us -> 46.4 us (1.020)
  waiting for transfers between devices: 14.8 us -> 15.9 us
  starting transfers between devices: 17.9 us -> 17.1 us
    ppermute x2, waiting for transfers between devices: 1.71 us -> 3.43 us  [swap_tensor(): lax.ppermute(value, 'tensor', [(source, source ^ bit) for source in range...]
    ppermute x10, starting transfers between devices: 16.3 us -> 15.6 us  [swap(): return lax.ppermute(value, ('replica', 'tensor'), pairs)]
    ppermute x10, waiting for transfers between devices: 13 us -> 12.5 us  [swap(): return lax.ppermute(value, ('replica', 'tensor'), pairs)]
  transfers between devices with their start and end apart: 12 -> 12, of which waited for: 8 -> 7; matrix products, arithmetic and copies ran while one was open for 0% -> 0% of each run, Pallas kernels for 12% -> 13%
where the time goes in v7:
time: 46.4 us; the launch traced here: 46.2 us
  starting transfers between devices  17.1 us (37%)
  waiting for transfers between devices  15.9 us (34%)
  Pallas kernels  12.3 us (27%)
  between operations  0.8 us (2%)
    ppermute x10, starting transfers between devices, swap(): return lax.ppermute(value, ('replica', 'tensor'), pairs)  15.6 us
    ppermute x10, waiting for transfers between devices, swap(): return lax.ppermute(value, ('replica', 'tensor'), pairs)  12.5 us
    ppermute x2, waiting for transfers between devices, swap_tensor(): lax.ppermute(value, 'tensor', [(source, source ^ bit) for source in range...  3.43 us
    pallas_call x1, Pallas kernels, project(): pl.pallas_call(far_kernel, out_shape=mats + (shaped((rank, columns), bf16...  3.35 us
    pallas_call x1, Pallas kernels, project(): pl.pallas_call(near_kernel, out_shape=mats + (shaped((rank, columns), f32...  3.33 us
    pallas_call x1, Pallas kernels, finish(): pl.pallas_call(functools.partial(finish_far_kernel, count), out_shape=ear...  2.33 us
    pallas_call x1, Pallas kernels, finish(): pl.pallas_call(functools.partial(finish_near_kernel, count), out_shape=ea...  1.86 us
    ppermute x2, starting transfers between devices, swap_tensor(): lax.ppermute(value, 'tensor', [(source, source ^ bit) for source in range...  1.49 us
  transfers between devices with their start and end apart: 12, of which 7 were waited for; matrix products, arithmetic and copies ran while one was open for 0% of the time, Pallas kernels for 13%

profile of v7, /device:TPU:0, one launch (start us, length us, event | category | flops | bytes accessed | tf_op | source)
XLA Modules:
  0.0 46.2 jit_solution(12823036769287617891)
XLA Ops:
  0.7 3.3 %project_far.1 = (bf16[1024,512]{1,0:T(8,128)(2,1)S(1)}, bf16[256,2048]{1,0:T(8,128)(2,1)S(1)}, bf16[32,1280]{1,0:T(8,128)(2,1)S(1)}) custom-call(bf16[32,512]{1,0:T(8,128)(2,1)} %bitcast.7, bf16[32,2048]{1,0:T(8,128)(2,1)} %bitcast.5, bf16[2048,512]{1,0:T(8,128)(2,1)} %grad_q.3, bf16[2048,512]{1,0:T(8,128)(2,1)} %error_q.3, bf16[512,2048]{1,0:T(8,128)(2,1)} %grad_o.3, ...), custom_call_target="tpu_custom_call" | custom-call | flops 67108864 | bytes 4194304 | tf_op jit(solution)/shard_map/project_far/pallas_call | solution.py:153
  4.0 3.0 %collective-permute-start = (bf16[32,1280]{1,0:T(8,128)(2,1)S(1)}, bf16[32,1280]{1,0:T(8,128)(2,1)S(1)}, u32[]{:S(2)}, u32[]{:S(2)}) collective-permute-start(bf16[32,1280]{1,0:T(8,128)(2,1)S(1)} %get-tuple-element.39), channel_id=1, source_target_pairs={{0,4},{1,17},{2,6},{3,19},{4,0},{5,21},{6,2},{7,23},{8,12},{9,25},... | collective-permute-start | bytes 245768 | tf_op jit(solution)/shard_map/ppermute | solution.py:510
  7.1 3.3 %project_near.1 = (bf16[1024,512]{1,0:T(8,128)(2,1)S(1)}, bf16[256,2048]{1,0:T(8,128)(2,1)S(1)}, f32[32,1280]{1,0:T(8,128)S(1)}, f32[32,128]{1,0:T(8,128)S(1)}) custom-call(bf16[32,512]{1,0:T(8,128)(2,1)} %bitcast.8, bf16[32,2048]{1,0:T(8,128)(2,1)} %bitcast.6, bf16[2048,512]{1,0:T(8,128)(2,1)} %grad_q.3, bf16[2048,512]{1,0:T(8,128)(2,1)} %error_q.3, ...), custom_call_target="tpu_custom_call" | custom-call | flops 67108864 | bytes 4194304 | tf_op jit(solution)/shard_map/project_near/pallas_call | solution.py:163
  10.4 3.7 %collective-permute-start.3 = (bf16[32,1408]{1,0:T(8,128)(2,1)S(1)}, bf16[32,1408]{1,0:T(8,128)(2,1)S(1)}, u32[]{:S(2)}, u32[]{:S(2)}) collective-permute-start(bf16[32,1408]{1,0:T(8,128)(2,1)S(1)} %first_sum.1.refs_0_), channel_id=1, source_target_pairs={{0,24},{1,13},{2,26},{3,15},{4,28},{5,9},{6,30},{7,11},{8,16},{9,5... | collective-permute-start | bytes 270344 | tf_op jit(solution)/shard_map/ppermute | solution.py:510
  14.1 0.8 %collective-permute-start.1 = (bf16[32,1408]{1,0:T(8,128)(2,1)S(1)}, bf16[32,1408]{1,0:T(8,128)(2,1)S(1)}, u32[]{:S(2)}, u32[]{:S(2)}) collective-permute-start(bf16[32,1408]{1,0:T(8,128)(2,1)S(1)} %first_sum.1.refs_0_), channel_id=1, source_target_pairs={{0,8},{1,5},{2,10},{3,7},{4,12},{5,1},{6,14},{7,3},{8,0},{9,13},{1... | collective-permute-start | bytes 270344 | tf_op jit(solution)/shard_map/ppermute | solution.py:510
  14.9 2.4 %collective-permute-done.3.refs_3_ = bf16[32,1408]{1,0:T(8,128)(2,1)S(1)} collective-permute-done((bf16[32,1408]{1,0:T(8,128)(2,1)S(1)}, bf16[32,1408]{1,0:T(8,128)(2,1)S(1)}, u32[]{:S(2)}, u32[]{:S(2)}) %collective-permute-start.3) | collective-permute-done | bytes 90144 | tf_op jit(solution)/shard_map/ppermute | solution.py:510
  17.3 2.7 %collective-permute-done.2.refs_2_ = bf16[32,1408]{1,0:T(8,128)(2,1)S(1)} collective-permute-done((bf16[32,1408]{1,0:T(8,128)(2,1)S(1)}, bf16[32,1408]{1,0:T(8,128)(2,1)S(1)}, u32[]{:S(2)}, u32[]{:S(2)}) %collective-permute-start.2) | collective-permute-done | bytes 90144 | tf_op jit(solution)/shard_map/ppermute | solution.py:510
  20.0 0.3 hats.1.hat.hat_near
  20.3 1.2 %collective-permute-start.4 = (bf16[32,1536]{1,0:T(8,128)(2,1)S(1)}, bf16[32,1536]{1,0:T(8,128)(2,1)S(1)}, u32[]{:S(2)}, u32[]{:S(2)}) collective-permute-start(bf16[32,1536]{1,0:T(8,128)(2,1)S(1)} %hats.1.hat.hat_near), channel_id=1, source_target_pairs={{0,4},{1,17},{2,6},{3,19},{4,0},{5,21},{6,2},{7,23},{8,12},{9,25},... | collective-permute-start | bytes 294920 | tf_op jit(solution)/shard_map/ppermute | solution.py:510
  21.6 0.5 right_near.1
  22.0 3.0 %collective-permute-done.4.hat.hat_far = bf16[32,1536]{1,0:T(8,128)(2,1)S(1)} collective-permute-done((bf16[32,1536]{1,0:T(8,128)(2,1)S(1)}, bf16[32,1536]{1,0:T(8,128)(2,1)S(1)}, u32[]{:S(2)}, u32[]{:S(2)}) %collective-permute-start.4) | collective-permute-done | bytes 98336 | tf_op jit(solution)/shard_map/ppermute | solution.py:510
  25.0 0.3 right_send.1
  25.4 1.2 %collective-permute-start.5 = (bf16[32,1280]{1,0:T(8,128)(2,1)S(1)}, bf16[32,1280]{1,0:T(8,128)(2,1)S(1)}, u32[]{:S(2)}, u32[]{:S(2)}) collective-permute-start(bf16[32,1280]{1,0:T(8,128)(2,1)S(1)} %right_send.1), channel_id=1, source_target_pairs={{0,4},{1,17},{2,6},{3,19},{4,0},{5,21},{6,2},{7,23},{8,12},{9,25},... | collective-permute-start | bytes 245768 | tf_op jit(solution)/shard_map/ppermute | solution.py:510
  26.6 0.3 right_keep.1
  26.9 3.0 %collective-permute-done.5.got = bf16[32,1280]{1,0:T(8,128)(2,1)S(1)} collective-permute-done((bf16[32,1280]{1,0:T(8,128)(2,1)S(1)}, bf16[32,1280]{1,0:T(8,128)(2,1)S(1)}, u32[]{:S(2)}, u32[]{:S(2)}) %collective-permute-start.5) | collective-permute-done | bytes 81952 | tf_op jit(solution)/shard_map/ppermute | solution.py:510
  29.9 2.5 %collective-permute-start.10 = (bf16[32,1280]{1,0:T(8,128)(2,1)S(1)}, bf16[32,1280]{1,0:T(8,128)(2,1)S(1)}, u32[]{:S(2)}, u32[]{:S(2)}) collective-permute-start(bf16[32,1280]{1,0:T(8,128)(2,1)S(1)} %get-tuple-element.49.refs_0_), channel_id=1, source_target_pairs={{0,24},{1,13},{2,26},{3,15},{4,28},{5,9},{6,30},{7,11},{8,16},{9,5... | collective-permute-start | bytes 245768 | tf_op jit(solution)/shard_map/ppermute | solution.py:510
  32.5 1.8 %collective-permute-start.8 = (bf16[32,1280]{1,0:T(8,128)(2,1)S(1)}, bf16[32,1280]{1,0:T(8,128)(2,1)S(1)}, u32[]{:S(2)}, u32[]{:S(2)}) collective-permute-start(bf16[32,1280]{1,0:T(8,128)(2,1)S(1)} %get-tuple-element.49.refs_0_), channel_id=1, source_target_pairs={{0,8},{1,5},{2,10},{3,7},{4,12},{5,1},{6,14},{7,3},{8,0},{9,13},{1... | collective-permute-start | bytes 245768 | tf_op jit(solution)/shard_map/ppermute | solution.py:510
  34.3 1.2 %collective-permute-done.6.got = f32[32,128]{1,0:T(8,128)S(1)} collective-permute-done((f32[32,128]{1,0:T(8,128)S(1)}, f32[32,128]{1,0:T(8,128)S(1)}, u32[]{:S(2)}, u32[]{:S(2)}) %collective-permute-start.6) | collective-permute-done | bytes 16416 | tf_op jit(solution)/shard_map/ppermute | solution.py:519
  35.5 1.5 %collective-permute-start.7 = (f32[32,128]{1,0:T(8,128)S(1)}, f32[32,128]{1,0:T(8,128)S(1)}, u32[]{:S(2)}, u32[]{:S(2)}) collective-permute-start(f32[32,128]{1,0:T(8,128)S(1)} %norm_add.1.norm), channel_id=1, source_target_pairs={{0,2},{1,3},{2,0},{3,1},{4,6},{5,7},{6,4},{7,5},{8,10},{9,11},{10,... | collective-permute-start | bytes 49160 | tf_op jit(solution)/shard_map/ppermute | solution.py:519
  37.0 2.2 %collective-permute-done.7.norm_got = f32[32,128]{1,0:T(8,128)S(1)} collective-permute-done((f32[32,128]{1,0:T(8,128)S(1)}, f32[32,128]{1,0:T(8,128)S(1)}, u32[]{:S(2)}, u32[]{:S(2)}) %collective-permute-start.7) | collective-permute-done | bytes 16416 | tf_op jit(solution)/shard_map/ppermute | solution.py:519
  39.4 1.2 %collective-permute-start.11 = (bf16[32,1280]{1,0:T(8,128)(2,1)S(1)}, bf16[32,1280]{1,0:T(8,128)(2,1)S(1)}, u32[]{:S(2)}, u32[]{:S(2)}) collective-permute-start(bf16[32,1280]{1,0:T(8,128)(2,1)S(1)} %get-tuple-element.50.new.new_near), channel_id=1, source_target_pairs={{0,4},{1,17},{2,6},{3,19},{4,0},{5,21},{6,2},{7,23},{8,12},{9,25},... | collective-permute-start | bytes 245768 | tf_op jit(solution)/shard_map/ppermute | solution.py:510
  40.6 1.9 %finish_near.1 = (bf16[2048,512]{1,0:T(8,128)(2,1)}, bf16[512,2048]{1,0:T(8,128)(2,1)}, f32[256,512]{1,0:T(8,128)}, f32[256,512]{1,0:T(8,128)}) custom-call(bf16[32,1536]{1,0:T(8,128)(2,1)S(1)} %hats.1.hat.hat_near, bf16[32,1536]{1,0:T(8,128)(2,1)S(1)} %collective-permute-done.4.hat.hat_far, bf16[1024,512]{1,0:T(8,128)(2,1)S(1)} %get-tuple-element.40.mat_q.mat_q_near, ...), custom_call_target="tpu_custom_call" | custom-call | flops 67108864 | bytes 4194304 | tf_op jit(solution)/shard_map/finish_near/pallas_call | solution.py:476
  42.5 1.4 %collective-permute-done.11.new_far = bf16[32,1280]{1,0:T(8,128)(2,1)S(1)} collective-permute-done((bf16[32,1280]{1,0:T(8,128)(2,1)S(1)}, bf16[32,1280]{1,0:T(8,128)(2,1)S(1)}, u32[]{:S(2)}, u32[]{:S(2)}) %collective-permute-start.11) | collective-permute-done | bytes 81952 | tf_op jit(solution)/shard_map/ppermute | solution.py:510
  43.9 2.3 %finish_far.1 = (bf16[2048,512]{1,0:T(8,128)(2,1)}, bf16[512,2048]{1,0:T(8,128)(2,1)}, f32[256,512]{1,0:T(8,128)}, f32[256,512]{1,0:T(8,128)}, bf16[32,512]{1,0:...) custom-call(bf16[32,1536]{1,0:T(8,128)(2,1)S(1)} %hats.1.hat.hat_nea, ...), custom_call_target="tpu_custom_call", output_to_operand_aliasing={{0}: (13, {}), {1}: (14, {}), {2}: (15, {}), {3}: (16, {})} | custom-call | flops 67108864 | bytes 4194304 | tf_op jit(solution)/shard_map/finish_far/pallas_call | solution.py:488
  (26 shorter events, 0.3 us)
Async XLA Ops:
  0.6 6.4 %copy-start.4 = (bf16[1,1,4096]{2,1,0:T(2,128)(2,1)S(1)}, bf16[1,1,4096]{2,1,0:T(2,128)(2,1)}, u32[]{:S(2)}) copy-start(bf16[1,1,4096]{2,1,0:T(2,128)(2,1)} %norm_grads.1) | copy-start | bytes 24580
  4.0 16.0 %copy-start.5 = (f32[32,32]{1,0:T(8,128)S(1)}, f32[32,32]{1,0:T(8,128)}, u32[]{:S(2)}) copy-start(f32[32,32]{1,0:T(8,128)} %ginv_q.1) | copy-start | bytes 12292
  4.0 16.0 %copy-start.6 = (f32[32,32]{1,0:T(8,128)S(1)}, f32[32,32]{1,0:T(8,128)}, u32[]{:S(2)}) copy-start(f32[32,32]{1,0:T(8,128)} %ginv_o.1) | copy-start | bytes 12292
  4.0 6.4 %collective-permute-start = (bf16[32,1280]{1,0:T(8,128)(2,1)S(1)}, bf16[32,1280]{1,0:T(8,128)(2,1)S(1)}, u32[]{:S(2)}, u32[]{:S(2)}) collective-permute-start(bf16[32,1280]{1,0:T(8,128)(2,1)S(1)} %get-tuple-element.39), channel_id=1, source_target_pairs={{0,4},{1,17},{2,6},{3,19},{4,0},{5,21},{6,2},{7,23},{8,12},{9,25},... | collective-permute-start | bytes 245768 | tf_op jit(solution)/shard_map/ppermute | solution.py:510
  10.4 6.9 %collective-permute-start.3 = (bf16[32,1408]{1,0:T(8,128)(2,1)S(1)}, bf16[32,1408]{1,0:T(8,128)(2,1)S(1)}, u32[]{:S(2)}, u32[]{:S(2)}) collective-permute-start(bf16[32,1408]{1,0:T(8,128)(2,1)S(1)} %first_sum.1.refs_0_), channel_id=1, source_target_pairs={{0,24},{1,13},{2,26},{3,15},{4,28},{5,9},{6,30},{7,11},{8,16},{9,5... | collective-permute-start | bytes 270344 | tf_op jit(solution)/shard_map/ppermute | solution.py:510
  14.1 5.9 %collective-permute-start.2 = (bf16[32,1408]{1,0:T(8,128)(2,1)S(1)}, bf16[32,1408]{1,0:T(8,128)(2,1)S(1)}, u32[]{:S(2)}, u32[]{:S(2)}) collective-permute-start(bf16[32,1408]{1,0:T(8,128)(2,1)S(1)} %first_sum.1.refs_0_), channel_id=1, source_target_pairs={{0,16},{1,9},{2,18},{3,11},{4,20},{5,13},{6,22},{7,15},{8,24},{9,1... | collective-permute-start | bytes 270344 | tf_op jit(solution)/shard_map/ppermute | solution.py:510
  14.1 5.9 %collective-permute-start.1 = (bf16[32,1408]{1,0:T(8,128)(2,1)S(1)}, bf16[32,1408]{1,0:T(8,128)(2,1)S(1)}, u32[]{:S(2)}, u32[]{:S(2)}) collective-permute-start(bf16[32,1408]{1,0:T(8,128)(2,1)S(1)} %first_sum.1.refs_0_), channel_id=1, source_target_pairs={{0,8},{1,5},{2,10},{3,7},{4,12},{5,1},{6,14},{7,3},{8,0},{9,13},{1... | collective-permute-start | bytes 270344 | tf_op jit(solution)/shard_map/ppermute | solution.py:510
  20.3 4.7 %collective-permute-start.4 = (bf16[32,1536]{1,0:T(8,128)(2,1)S(1)}, bf16[32,1536]{1,0:T(8,128)(2,1)S(1)}, u32[]{:S(2)}, u32[]{:S(2)}) collective-permute-start(bf16[32,1536]{1,0:T(8,128)(2,1)S(1)} %hats.1.hat.hat_near), channel_id=1, source_target_pairs={{0,4},{1,17},{2,6},{3,19},{4,0},{5,21},{6,2},{7,23},{8,12},{9,25},... | collective-permute-start | bytes 294920 | tf_op jit(solution)/shard_map/ppermute | solution.py:510
  25.3 15.3 %copy-start = (f32[256,512]{1,0:T(8,128)S(1)}, f32[256,512]{1,0:T(8,128)}, u32[]{:S(2)}) copy-start(f32[256,512]{1,0:T(8,128)} %weight_q.3) | copy-start | bytes 1572868
  25.3 15.3 %copy-start.1 = (f32[256,512]{1,0:T(8,128)S(1)}, f32[256,512]{1,0:T(8,128)}, u32[]{:S(2)}) copy-start(f32[256,512]{1,0:T(8,128)} %momentum_q.3) | copy-start | bytes 1572868
  25.4 4.5 %collective-permute-start.5 = (bf16[32,1280]{1,0:T(8,128)(2,1)S(1)}, bf16[32,1280]{1,0:T(8,128)(2,1)S(1)}, u32[]{:S(2)}, u32[]{:S(2)}) collective-permute-start(bf16[32,1280]{1,0:T(8,128)(2,1)S(1)} %right_send.1), channel_id=1, source_target_pairs={{0,4},{1,17},{2,6},{3,19},{4,0},{5,21},{6,2},{7,23},{8,12},{9,25},... | collective-permute-start | bytes 245768 | tf_op jit(solution)/shard_map/ppermute | solution.py:510
  29.9 9.4 %collective-permute-start.10 = (bf16[32,1280]{1,0:T(8,128)(2,1)S(1)}, bf16[32,1280]{1,0:T(8,128)(2,1)S(1)}, u32[]{:S(2)}, u32[]{:S(2)}) collective-permute-start(bf16[32,1280]{1,0:T(8,128)(2,1)S(1)} %get-tuple-element.49.refs_0_), channel_id=1, source_target_pairs={{0,24},{1,13},{2,26},{3,15},{4,28},{5,9},{6,30},{7,11},{8,16},{9,5... | collective-permute-start | bytes 245768 | tf_op jit(solution)/shard_map/ppermute | solution.py:510
  32.3 6.9 %collective-permute-start.9 = (bf16[32,1280]{1,0:T(8,128)(2,1)S(1)}, bf16[32,1280]{1,0:T(8,128)(2,1)S(1)}, u32[]{:S(2)}, u32[]{:S(2)}) collective-permute-start(bf16[32,1280]{1,0:T(8,128)(2,1)S(1)} %get-tuple-element.49.refs_0_), channel_id=1, source_target_pairs={{0,16},{1,9},{2,18},{3,11},{4,20},{5,13},{6,22},{7,15},{8,24},{9,1... | collective-permute-start | bytes 245768 | tf_op jit(solution)/shard_map/ppermute | solution.py:510
  32.5 6.8 %collective-permute-start.8 = (bf16[32,1280]{1,0:T(8,128)(2,1)S(1)}, bf16[32,1280]{1,0:T(8,128)(2,1)S(1)}, u32[]{:S(2)}, u32[]{:S(2)}) collective-permute-start(bf16[32,1280]{1,0:T(8,128)(2,1)S(1)} %get-tuple-element.49.refs_0_), channel_id=1, source_target_pairs={{0,8},{1,5},{2,10},{3,7},{4,12},{5,1},{6,14},{7,3},{8,0},{9,13},{1... | collective-permute-start | bytes 245768 | tf_op jit(solution)/shard_map/ppermute | solution.py:510
  34.3 1.2 %collective-permute-start.6 = (f32[32,128]{1,0:T(8,128)S(1)}, f32[32,128]{1,0:T(8,128)S(1)}, u32[]{:S(2)}, u32[]{:S(2)}) collective-permute-start(f32[32,128]{1,0:T(8,128)S(1)} %get-tuple-element.48.mine), channel_id=1, source_target_pairs={{0,1},{1,0},{2,3},{3,2},{4,5},{5,4},{6,7},{7,6},{8,9},{9,8},{10,11... | collective-permute-start | bytes 49160 | tf_op jit(solution)/shard_map/ppermute | solution.py:519
  35.5 3.7 %collective-permute-start.7 = (f32[32,128]{1,0:T(8,128)S(1)}, f32[32,128]{1,0:T(8,128)S(1)}, u32[]{:S(2)}, u32[]{:S(2)}) collective-permute-start(f32[32,128]{1,0:T(8,128)S(1)} %norm_add.1.norm), channel_id=1, source_target_pairs={{0,2},{1,3},{2,0},{3,1},{4,6},{5,7},{6,4},{7,5},{8,10},{9,11},{10,... | collective-permute-start | bytes 49160 | tf_op jit(solution)/shard_map/ppermute | solution.py:519
  39.3 4.5 %copy-start.2 = (f32[512,256]{1,0:T(8,128)S(1)}, f32[512,256]{1,0:T(8,128)}, u32[]{:S(2)}) copy-start(f32[512,256]{1,0:T(8,128)} %weight_o.1) | copy-start | bytes 1572868
  39.3 4.5 %copy-start.3 = (f32[512,256]{1,0:T(8,128)S(1)}, f32[512,256]{1,0:T(8,128)}, u32[]{:S(2)}) copy-start(f32[512,256]{1,0:T(8,128)} %momentum_o.1) | copy-start | bytes 1572868
  39.4 4.5 %collective-permute-start.11 = (bf16[32,1280]{1,0:T(8,128)(2,1)S(1)}, bf16[32,1280]{1,0:T(8,128)(2,1)S(1)}, u32[]{:S(2)}, u32[]{:S(2)}) collective-permute-start(bf16[32,1280]{1,0:T(8,128)(2,1)S(1)} %get-tuple-element.50.new.new_near), channel_id=1, source_target_pairs={{0,4},{1,17},{2,6},{3,19},{4,0},{5,21},{6,2},{7,23},{8,12},{9,25},... | collective-permute-start | bytes 245768 | tf_op jit(solution)/shard_map/ppermute | solution.py:510

commit v8 on v7

--- a/solution.py
+++ b/solution.py
@@ -99,7 +99,7 @@
             copy.wait()
         block = grad_v[part] + error_v[part]
         mat[part] = block
-        store(column, dot(block, fac[...], 1, 1).T)
+        store(column, dot(fac[...], block, 1, 1))
 
 
 def far_kernel(
@@ -236,10 +236,6 @@
     store_norm(out, columns, norm_of(states, columns))
 
 
-def norm_add_kernel(mine, got, total):
-    total[...] = mine[...] + got[...]
-
-
 def mean_kernel(count, norm_count, norm, norm_got, *refs):
     *states, new, norm_mean = refs
     new[...] = (total_of(states, new.shape[1]) / count).astype(bf16)
@@ -317,9 +313,9 @@
     return send, near, norm
 
 
-def near_sum_kernel(near, got, norm, state, norm_out):
+def near_sum_kernel(near, got, norm, norm_got, state, norm_sum):
     state[...] = (near[...] + got[...].astype(f32)).astype(bf16)
-    norm_out[...] = norm[...]
+    norm_sum[...] = norm[...] + norm_got[...]
 
 
 def error_columns(column, hat, hat_row, half, mat_q, mat_o, new, error_q, error_o, stage_q, stage_o, sems, slot):
@@ -577,16 +573,13 @@
     )
     state, norm = small(
         near_sum_kernel, "near_sum", (shaped(send.shape, bf16), shaped(norm.shape, f32)),
-        near, swap_halves(send), norm,
+        near, swap_halves(send), norm, swap_tensor(norm, 1),
     )
     for bits in rounds[:-1]:
         state = small(
             plain_sum_kernel, "plain_sum", shaped(state.shape, bf16), *exchange(state, bits)
         )
     states = exchange(state, rounds[-1])
-    norm = small(
-        norm_add_kernel, "norm_add", shaped(norm.shape, f32), norm, swap_tensor(norm, 1)
-    )
     new_near, norm = small(
         functools.partial(mean_kernel, replicas, replicas * tensors), "mean",
         (shaped(state.shape, bf16), shaped(norm.shape, f32)),

time: 46.4 us -> 45.6 us (0.983)
  waiting for transfers between devices: 15.9 us -> 13.7 us
  starting transfers between devices: 17.1 us -> 19.1 us
  Pallas kernels: 12.3 us -> 11.8 us
    ppermute x10, waiting for transfers between devices: 12.5 us -> 10.2 us  [swap(): return lax.ppermute(value, ('replica', 'tensor'), pairs)]
    ppermute x10, starting transfers between devices: 15.6 us -> 17.6 us  [swap(): return lax.ppermute(value, ('replica', 'tensor'), pairs)]
  transfers between devices with their start and end apart: 12 -> 12, of which waited for: 7 -> 8; matrix products, arithmetic and copies ran while one was open for 0% -> 0% of each run, Pallas kernels for 13% -> 13%
where the time goes in v8:
time: 45.6 us; the launch traced here: 45.4 us
  starting transfers between devices  19.1 us (42%)
  waiting for transfers between devices  13.7 us (30%)
  Pallas kernels  11.8 us (26%)
  between operations  0.8 us (2%)
    ppermute x10, starting transfers between devices, swap(): return lax.ppermute(value, ('replica', 'tensor'), pairs)  17.6 us
    ppermute x10, waiting for transfers between devices, swap(): return lax.ppermute(value, ('replica', 'tensor'), pairs)  10.2 us
    ppermute x2, waiting for transfers between devices, swap_tensor(): lax.ppermute(value, 'tensor', [(source, source ^ bit) for source in range...  3.42 us
    pallas_call x1, Pallas kernels, project(): pl.pallas_call(far_kernel, out_shape=mats + (shaped((rank, columns), bf16...  3.09 us
    pallas_call x1, Pallas kernels, project(): pl.pallas_call(near_kernel, out_shape=mats + (shaped((rank, columns), f32...  3.08 us
    pallas_call x1, Pallas kernels, finish(): pl.pallas_call(functools.partial(finish_far_kernel, count), out_shape=ear...  2.32 us
    pallas_call x1, Pallas kernels, finish(): pl.pallas_call(functools.partial(finish_near_kernel, count), out_shape=ea...  1.87 us
    ppermute x2, starting transfers between devices, swap_tensor(): lax.ppermute(value, 'tensor', [(source, source ^ bit) for source in range...  1.56 us
  transfers between devices with their start and end apart: 12, of which 8 were waited for; matrix products, arithmetic and copies ran while one was open for 0% of the time, Pallas kernels for 13%

profile of v8, /device:TPU:0, one launch (start us, length us, event | category | flops | bytes accessed | tf_op | source)
XLA Modules:
  0.0 45.4 jit_solution(18297860055123749829)
XLA Ops:
  0.7 3.1 %project_far.1 = (bf16[1024,512]{1,0:T(8,128)(2,1)S(1)}, bf16[256,2048]{1,0:T(8,128)(2,1)S(1)}, bf16[32,1280]{1,0:T(8,128)(2,1)S(1)}) custom-call(bf16[32,512]{1,0:T(8,128)(2,1)} %bitcast.7, bf16[32,2048]{1,0:T(8,128)(2,1)} %bitcast.5, bf16[2048,512]{1,0:T(8,128)(2,1)} %grad_q.3, bf16[2048,512]{1,0:T(8,128)(2,1)} %error_q.3, bf16[512,2048]{1,0:T(8,128)(2,1)} %grad_o.3, ...), custom_call_target="tpu_custom_call" | custom-call | flops 67108864 | bytes 4194304 | tf_op jit(solution)/shard_map/project_far/pallas_call | solution.py:153
  3.8 3.0 %collective-permute-start = (bf16[32,1280]{1,0:T(8,128)(2,1)S(1)}, bf16[32,1280]{1,0:T(8,128)(2,1)S(1)}, u32[]{:S(2)}, u32[]{:S(2)}) collective-permute-start(bf16[32,1280]{1,0:T(8,128)(2,1)S(1)} %get-tuple-element.39), channel_id=1, source_target_pairs={{0,4},{1,17},{2,6},{3,19},{4,0},{5,21},{6,2},{7,23},{8,12},{9,25},... | collective-permute-start | bytes 245768 | tf_op jit(solution)/shard_map/ppermute | solution.py:506
  6.8 3.1 %project_near.1 = (bf16[1024,512]{1,0:T(8,128)(2,1)S(1)}, bf16[256,2048]{1,0:T(8,128)(2,1)S(1)}, f32[32,1280]{1,0:T(8,128)S(1)}, f32[32,128]{1,0:T(8,128)S(1)}) custom-call(bf16[32,512]{1,0:T(8,128)(2,1)} %bitcast.8, bf16[32,2048]{1,0:T(8,128)(2,1)} %bitcast.6, bf16[2048,512]{1,0:T(8,128)(2,1)} %grad_q.3, bf16[2048,512]{1,0:T(8,128)(2,1)} %error_q.3, ...), custom_call_target="tpu_custom_call" | custom-call | flops 67108864 | bytes 4194304 | tf_op jit(solution)/shard_map/project_near/pallas_call | solution.py:163
  9.9 3.7 %collective-permute-start.3 = (bf16[32,1408]{1,0:T(8,128)(2,1)S(1)}, bf16[32,1408]{1,0:T(8,128)(2,1)S(1)}, u32[]{:S(2)}, u32[]{:S(2)}) collective-permute-start(bf16[32,1408]{1,0:T(8,128)(2,1)S(1)} %first_sum.1.refs_0_), channel_id=1, source_target_pairs={{0,24},{1,13},{2,26},{3,15},{4,28},{5,9},{6,30},{7,11},{8,16},{9,5... | collective-permute-start | bytes 270344 | tf_op jit(solution)/shard_map/ppermute | solution.py:506
  13.6 0.8 %collective-permute-start.1 = (bf16[32,1408]{1,0:T(8,128)(2,1)S(1)}, bf16[32,1408]{1,0:T(8,128)(2,1)S(1)}, u32[]{:S(2)}, u32[]{:S(2)}) collective-permute-start(bf16[32,1408]{1,0:T(8,128)(2,1)S(1)} %first_sum.1.refs_0_), channel_id=1, source_target_pairs={{0,8},{1,5},{2,10},{3,7},{4,12},{5,1},{6,14},{7,3},{8,0},{9,13},{1... | collective-permute-start | bytes 270344 | tf_op jit(solution)/shard_map/ppermute | solution.py:506
  14.4 2.7 %collective-permute-done.3.refs_3_ = bf16[32,1408]{1,0:T(8,128)(2,1)S(1)} collective-permute-done((bf16[32,1408]{1,0:T(8,128)(2,1)S(1)}, bf16[32,1408]{1,0:T(8,128)(2,1)S(1)}, u32[]{:S(2)}, u32[]{:S(2)}) %collective-permute-start.3) | collective-permute-done | bytes 90144 | tf_op jit(solution)/shard_map/ppermute | solution.py:506
  17.1 2.4 %collective-permute-done.2.refs_2_ = bf16[32,1408]{1,0:T(8,128)(2,1)S(1)} collective-permute-done((bf16[32,1408]{1,0:T(8,128)(2,1)S(1)}, bf16[32,1408]{1,0:T(8,128)(2,1)S(1)}, u32[]{:S(2)}, u32[]{:S(2)}) %collective-permute-start.2) | collective-permute-done | bytes 90144 | tf_op jit(solution)/shard_map/ppermute | solution.py:506
  19.5 0.3 hats.1.hat.hat_near
  19.8 1.5 %collective-permute-start.4 = (bf16[32,1536]{1,0:T(8,128)(2,1)S(1)}, bf16[32,1536]{1,0:T(8,128)(2,1)S(1)}, u32[]{:S(2)}, u32[]{:S(2)}) collective-permute-start(bf16[32,1536]{1,0:T(8,128)(2,1)S(1)} %hats.1.hat.hat_near), channel_id=1, source_target_pairs={{0,4},{1,17},{2,6},{3,19},{4,0},{5,21},{6,2},{7,23},{8,12},{9,25},... | collective-permute-start | bytes 294920 | tf_op jit(solution)/shard_map/ppermute | solution.py:506
  21.3 0.5 %right_near.1 = (f32[32,512]{1,0:T(8,128)S(1)}, f32[32,2048]{1,0:T(8,128)S(1)}) custom-call(bf16[32,1536]{1,0:T(8,128)(2,1)S(1)} %hats.1.hat.hat_near, bf16[1024,512]{1,0:T(8,128)(2,1)S(1)} %get-tuple-element.40.mat_q.mat_q_near, bf16[256,2048]{1,0:T(8,128)(2,1)S(1)} %get-tuple-element.41.mat_o.mat_o_near), custom_call_target="tpu_custom_call" | custom-call | flops 67108864 | bytes 2097152 | tf_op jit(solution)/shard_map/right_near/pallas_call | solution.py:253
  21.8 2.7 %collective-permute-done.4.hat.hat_far = bf16[32,1536]{1,0:T(8,128)(2,1)S(1)} collective-permute-done((bf16[32,1536]{1,0:T(8,128)(2,1)S(1)}, bf16[32,1536]{1,0:T(8,128)(2,1)S(1)}, u32[]{:S(2)}, u32[]{:S(2)}) %collective-permute-start.4) | collective-permute-done | bytes 98336 | tf_op jit(solution)/shard_map/ppermute | solution.py:506
  24.5 0.3 right_send.1
  24.8 1.5 %collective-permute-start.5 = (bf16[32,1280]{1,0:T(8,128)(2,1)S(1)}, bf16[32,1280]{1,0:T(8,128)(2,1)S(1)}, u32[]{:S(2)}, u32[]{:S(2)}) collective-permute-start(bf16[32,1280]{1,0:T(8,128)(2,1)S(1)} %right_send.1), channel_id=1, source_target_pairs={{0,4},{1,17},{2,6},{3,19},{4,0},{5,21},{6,2},{7,23},{8,12},{9,25},... | collective-permute-start | bytes 245768 | tf_op jit(solution)/shard_map/ppermute | solution.py:506
  26.7 1.2 %collective-permute-done.6.norm_got = f32[32,128]{1,0:T(8,128)S(1)} collective-permute-done((f32[32,128]{1,0:T(8,128)S(1)}, f32[32,128]{1,0:T(8,128)S(1)}, u32[]{:S(2)}, u32[]{:S(2)}) %collective-permute-start.6) | collective-permute-done | bytes 16416 | tf_op jit(solution)/shard_map/ppermute | solution.py:515
  27.9 1.5 %collective-permute-done.5.got = bf16[32,1280]{1,0:T(8,128)(2,1)S(1)} collective-permute-done((bf16[32,1280]{1,0:T(8,128)(2,1)S(1)}, bf16[32,1280]{1,0:T(8,128)(2,1)S(1)}, u32[]{:S(2)}, u32[]{:S(2)}) %collective-permute-start.5) | collective-permute-done | bytes 81952 | tf_op jit(solution)/shard_map/ppermute | solution.py:506
  29.4 2.7 %collective-permute-start.10 = (bf16[32,1280]{1,0:T(8,128)(2,1)S(1)}, bf16[32,1280]{1,0:T(8,128)(2,1)S(1)}, u32[]{:S(2)}, u32[]{:S(2)}) collective-permute-start(bf16[32,1280]{1,0:T(8,128)(2,1)S(1)} %get-tuple-element.49.refs_0_), channel_id=1, source_target_pairs={{0,24},{1,13},{2,26},{3,15},{4,28},{5,9},{6,30},{7,11},{8,16},{9,5... | collective-permute-start | bytes 245768 | tf_op jit(solution)/shard_map/ppermute | solution.py:506
  32.1 1.7 %collective-permute-start.8 = (bf16[32,1280]{1,0:T(8,128)(2,1)S(1)}, bf16[32,1280]{1,0:T(8,128)(2,1)S(1)}, u32[]{:S(2)}, u32[]{:S(2)}) collective-permute-start(bf16[32,1280]{1,0:T(8,128)(2,1)S(1)} %get-tuple-element.49.refs_0_), channel_id=1, source_target_pairs={{0,8},{1,5},{2,10},{3,7},{4,12},{5,1},{6,14},{7,3},{8,0},{9,13},{1... | collective-permute-start | bytes 245768 | tf_op jit(solution)/shard_map/ppermute | solution.py:506
  33.8 1.5 %collective-permute-start.7 = (f32[32,128]{1,0:T(8,128)S(1)}, f32[32,128]{1,0:T(8,128)S(1)}, u32[]{:S(2)}, u32[]{:S(2)}) collective-permute-start(f32[32,128]{1,0:T(8,128)S(1)} %get-tuple-element.48.norm), channel_id=1, source_target_pairs={{0,2},{1,3},{2,0},{3,1},{4,6},{5,7},{6,4},{7,5},{8,10},{9,11},{10,... | collective-permute-start | bytes 49160 | tf_op jit(solution)/shard_map/ppermute | solution.py:515
  35.3 2.2 %collective-permute-done.7.norm_got = f32[32,128]{1,0:T(8,128)S(1)} collective-permute-done((f32[32,128]{1,0:T(8,128)S(1)}, f32[32,128]{1,0:T(8,128)S(1)}, u32[]{:S(2)}, u32[]{:S(2)}) %collective-permute-start.7) | collective-permute-done | bytes 16416 | tf_op jit(solution)/shard_map/ppermute | solution.py:515
  37.6 0.4 collective-permute-done.9.refs_2_
  38.0 2.7 %collective-permute-start.11 = (bf16[32,1280]{1,0:T(8,128)(2,1)S(1)}, bf16[32,1280]{1,0:T(8,128)(2,1)S(1)}, u32[]{:S(2)}, u32[]{:S(2)}) collective-permute-start(bf16[32,1280]{1,0:T(8,128)(2,1)S(1)} %get-tuple-element.50.new.new_near), channel_id=1, source_target_pairs={{0,4},{1,17},{2,6},{3,19},{4,0},{5,21},{6,2},{7,23},{8,12},{9,25},... | collective-permute-start | bytes 245768 | tf_op jit(solution)/shard_map/ppermute | solution.py:506
  40.7 1.9 %finish_near.1 = (bf16[2048,512]{1,0:T(8,128)(2,1)}, bf16[512,2048]{1,0:T(8,128)(2,1)}, f32[256,512]{1,0:T(8,128)}, f32[256,512]{1,0:T(8,128)}) custom-call(bf16[32,1536]{1,0:T(8,128)(2,1)S(1)} %hats.1.hat.hat_near, bf16[32,1536]{1,0:T(8,128)(2,1)S(1)} %collective-permute-done.4.hat.hat_far, bf16[1024,512]{1,0:T(8,128)(2,1)S(1)} %get-tuple-element.40.mat_q.mat_q_near, ...), custom_call_target="tpu_custom_call" | custom-call | flops 67108864 | bytes 4194304 | tf_op jit(solution)/shard_map/finish_near/pallas_call | solution.py:472
  42.5 0.5 %collective-permute-done.11.new_far = bf16[32,1280]{1,0:T(8,128)(2,1)S(1)} collective-permute-done((bf16[32,1280]{1,0:T(8,128)(2,1)S(1)}, bf16[32,1280]{1,0:T(8,128)(2,1)S(1)}, u32[]{:S(2)}, u32[]{:S(2)}) %collective-permute-start.11) | collective-permute-done | bytes 81952 | tf_op jit(solution)/shard_map/ppermute | solution.py:506
  43.1 2.3 %finish_far.1 = (bf16[2048,512]{1,0:T(8,128)(2,1)}, bf16[512,2048]{1,0:T(8,128)(2,1)}, f32[256,512]{1,0:T(8,128)}, f32[256,512]{1,0:T(8,128)}, bf16[32,512]{1,0:...) custom-call(bf16[32,1536]{1,0:T(8,128)(2,1)S(1)} %hats.1.hat.hat_nea, ...), custom_call_target="tpu_custom_call", output_to_operand_aliasing={{0}: (13, {}), {1}: (14, {}), {2}: (15, {}), {3}: (16, {})} | custom-call | flops 67108864 | bytes 4194304 | tf_op jit(solution)/shard_map/finish_far/pallas_call | solution.py:484
  (25 shorter events, 0.5 us)
Async XLA Ops:
  0.6 6.2 %copy-start.4 = (bf16[1,1,4096]{2,1,0:T(2,128)(2,1)S(1)}, bf16[1,1,4096]{2,1,0:T(2,128)(2,1)}, u32[]{:S(2)}) copy-start(bf16[1,1,4096]{2,1,0:T(2,128)(2,1)} %norm_grads.1) | copy-start | bytes 24580
  3.7 15.7 %copy-start.5 = (f32[32,32]{1,0:T(8,128)S(1)}, f32[32,32]{1,0:T(8,128)}, u32[]{:S(2)}) copy-start(f32[32,32]{1,0:T(8,128)} %ginv_q.1) | copy-start | bytes 12292
  3.8 15.7 %copy-start.6 = (f32[32,32]{1,0:T(8,128)S(1)}, f32[32,32]{1,0:T(8,128)}, u32[]{:S(2)}) copy-start(f32[32,32]{1,0:T(8,128)} %ginv_o.1) | copy-start | bytes 12292
  3.8 6.1 %collective-permute-start = (bf16[32,1280]{1,0:T(8,128)(2,1)S(1)}, bf16[32,1280]{1,0:T(8,128)(2,1)S(1)}, u32[]{:S(2)}, u32[]{:S(2)}) collective-permute-start(bf16[32,1280]{1,0:T(8,128)(2,1)S(1)} %get-tuple-element.39), channel_id=1, source_target_pairs={{0,4},{1,17},{2,6},{3,19},{4,0},{5,21},{6,2},{7,23},{8,12},{9,25},... | collective-permute-start | bytes 245768 | tf_op jit(solution)/shard_map/ppermute | solution.py:506
  9.9 7.2 %collective-permute-start.3 = (bf16[32,1408]{1,0:T(8,128)(2,1)S(1)}, bf16[32,1408]{1,0:T(8,128)(2,1)S(1)}, u32[]{:S(2)}, u32[]{:S(2)}) collective-permute-start(bf16[32,1408]{1,0:T(8,128)(2,1)S(1)} %first_sum.1.refs_0_), channel_id=1, source_target_pairs={{0,24},{1,13},{2,26},{3,15},{4,28},{5,9},{6,30},{7,11},{8,16},{9,5... | collective-permute-start | bytes 270344 | tf_op jit(solution)/shard_map/ppermute | solution.py:506
  13.6 5.9 %collective-permute-start.2 = (bf16[32,1408]{1,0:T(8,128)(2,1)S(1)}, bf16[32,1408]{1,0:T(8,128)(2,1)S(1)}, u32[]{:S(2)}, u32[]{:S(2)}) collective-permute-start(bf16[32,1408]{1,0:T(8,128)(2,1)S(1)} %first_sum.1.refs_0_), channel_id=1, source_target_pairs={{0,16},{1,9},{2,18},{3,11},{4,20},{5,13},{6,22},{7,15},{8,24},{9,1... | collective-permute-start | bytes 270344 | tf_op jit(solution)/shard_map/ppermute | solution.py:506
  13.6 5.9 %collective-permute-start.1 = (bf16[32,1408]{1,0:T(8,128)(2,1)S(1)}, bf16[32,1408]{1,0:T(8,128)(2,1)S(1)}, u32[]{:S(2)}, u32[]{:S(2)}) collective-permute-start(bf16[32,1408]{1,0:T(8,128)(2,1)S(1)} %first_sum.1.refs_0_), channel_id=1, source_target_pairs={{0,8},{1,5},{2,10},{3,7},{4,12},{5,1},{6,14},{7,3},{8,0},{9,13},{1... | collective-permute-start | bytes 270344 | tf_op jit(solution)/shard_map/ppermute | solution.py:506
  19.8 4.7 %collective-permute-start.4 = (bf16[32,1536]{1,0:T(8,128)(2,1)S(1)}, bf16[32,1536]{1,0:T(8,128)(2,1)S(1)}, u32[]{:S(2)}, u32[]{:S(2)}) collective-permute-start(bf16[32,1536]{1,0:T(8,128)(2,1)S(1)} %hats.1.hat.hat_near), channel_id=1, source_target_pairs={{0,4},{1,17},{2,6},{3,19},{4,0},{5,21},{6,2},{7,23},{8,12},{9,25},... | collective-permute-start | bytes 294920 | tf_op jit(solution)/shard_map/ppermute | solution.py:506
  24.8 15.8 %copy-start = (f32[256,512]{1,0:T(8,128)S(1)}, f32[256,512]{1,0:T(8,128)}, u32[]{:S(2)}) copy-start(f32[256,512]{1,0:T(8,128)} %weight_q.3) | copy-start | bytes 1572868
  24.8 15.8 %copy-start.1 = (f32[256,512]{1,0:T(8,128)S(1)}, f32[256,512]{1,0:T(8,128)}, u32[]{:S(2)}) copy-start(f32[256,512]{1,0:T(8,128)} %momentum_q.3) | copy-start | bytes 1572868
  24.8 4.5 %collective-permute-start.5 = (bf16[32,1280]{1,0:T(8,128)(2,1)S(1)}, bf16[32,1280]{1,0:T(8,128)(2,1)S(1)}, u32[]{:S(2)}, u32[]{:S(2)}) collective-permute-start(bf16[32,1280]{1,0:T(8,128)(2,1)S(1)} %right_send.1), channel_id=1, source_target_pairs={{0,4},{1,17},{2,6},{3,19},{4,0},{5,21},{6,2},{7,23},{8,12},{9,25},... | collective-permute-start | bytes 245768 | tf_op jit(solution)/shard_map/ppermute | solution.py:506
  26.6 1.2 %collective-permute-start.6 = (f32[32,128]{1,0:T(8,128)S(1)}, f32[32,128]{1,0:T(8,128)S(1)}, u32[]{:S(2)}, u32[]{:S(2)}) collective-permute-start(f32[32,128]{1,0:T(8,128)S(1)} %get-tuple-element.47.norm), channel_id=1, source_target_pairs={{0,1},{1,0},{2,3},{3,2},{4,5},{5,4},{6,7},{7,6},{8,9},{9,8},{10,11... | collective-permute-start | bytes 49160 | tf_op jit(solution)/shard_map/ppermute | solution.py:515
  29.4 8.2 %collective-permute-start.10 = (bf16[32,1280]{1,0:T(8,128)(2,1)S(1)}, bf16[32,1280]{1,0:T(8,128)(2,1)S(1)}, u32[]{:S(2)}, u32[]{:S(2)}) collective-permute-start(bf16[32,1280]{1,0:T(8,128)(2,1)S(1)} %get-tuple-element.49.refs_0_), channel_id=1, source_target_pairs={{0,24},{1,13},{2,26},{3,15},{4,28},{5,9},{6,30},{7,11},{8,16},{9,5... | collective-permute-start | bytes 245768 | tf_op jit(solution)/shard_map/ppermute | solution.py:506
  32.1 5.8 %collective-permute-start.9 = (bf16[32,1280]{1,0:T(8,128)(2,1)S(1)}, bf16[32,1280]{1,0:T(8,128)(2,1)S(1)}, u32[]{:S(2)}, u32[]{:S(2)}) collective-permute-start(bf16[32,1280]{1,0:T(8,128)(2,1)S(1)} %get-tuple-element.49.refs_0_), channel_id=1, source_target_pairs={{0,16},{1,9},{2,18},{3,11},{4,20},{5,13},{6,22},{7,15},{8,24},{9,1... | collective-permute-start | bytes 245768 | tf_op jit(solution)/shard_map/ppermute | solution.py:506
  32.1 5.8 %collective-permute-start.8 = (bf16[32,1280]{1,0:T(8,128)(2,1)S(1)}, bf16[32,1280]{1,0:T(8,128)(2,1)S(1)}, u32[]{:S(2)}, u32[]{:S(2)}) collective-permute-start(bf16[32,1280]{1,0:T(8,128)(2,1)S(1)} %get-tuple-element.49.refs_0_), channel_id=1, source_target_pairs={{0,8},{1,5},{2,10},{3,7},{4,12},{5,1},{6,14},{7,3},{8,0},{9,13},{1... | collective-permute-start | bytes 245768 | tf_op jit(solution)/shard_map/ppermute | solution.py:506
  33.8 3.7 %collective-permute-start.7 = (f32[32,128]{1,0:T(8,128)S(1)}, f32[32,128]{1,0:T(8,128)S(1)}, u32[]{:S(2)}, u32[]{:S(2)}) collective-permute-start(f32[32,128]{1,0:T(8,128)S(1)} %get-tuple-element.48.norm), channel_id=1, source_target_pairs={{0,2},{1,3},{2,0},{3,1},{4,6},{5,7},{6,4},{7,5},{8,10},{9,11},{10,... | collective-permute-start | bytes 49160 | tf_op jit(solution)/shard_map/ppermute | solution.py:515
  38.0 5.1 %copy-start.2 = (f32[512,256]{1,0:T(8,128)S(1)}, f32[512,256]{1,0:T(8,128)}, u32[]{:S(2)}) copy-start(f32[512,256]{1,0:T(8,128)} %weight_o.1) | copy-start | bytes 1572868
  38.0 5.1 %copy-start.3 = (f32[512,256]{1,0:T(8,128)S(1)}, f32[512,256]{1,0:T(8,128)}, u32[]{:S(2)}) copy-start(f32[512,256]{1,0:T(8,128)} %momentum_o.1) | copy-start | bytes 1572868
  38.0 5.1 %collective-permute-start.11 = (bf16[32,1280]{1,0:T(8,128)(2,1)S(1)}, bf16[32,1280]{1,0:T(8,128)(2,1)S(1)}, u32[]{:S(2)}, u32[]{:S(2)}) collective-permute-start(bf16[32,1280]{1,0:T(8,128)(2,1)S(1)} %get-tuple-element.50.new.new_near), channel_id=1, source_target_pairs={{0,4},{1,17},{2,6},{3,19},{4,0},{5,21},{6,2},{7,23},{8,12},{9,25},... | collective-permute-start | bytes 245768 | tf_op jit(solution)/shard_map/ppermute | solution.py:506

commit v9 on v8

--- a/solution.py
+++ b/solution.py
@@ -58,9 +58,9 @@
     return pl.ds(pl.multiple_of(which * size, size), size)
 
 
-def load(source, target, sem):
+def load(source, target, sem, queue=0):
     copy = pltpu.make_async_copy(source, target, sem)
-    copy.start()
+    copy.start(priority=queue)
     return copy
 
 
@@ -70,28 +70,21 @@
 ):
     half_q, half_o = mat_q.shape[0], mat_o.shape[0]
     jobs = []
-    fac_copies = [load(fac_q_h, fac_q, sems.at[0]), load(fac_o_h, fac_o, sems.at[1])]
-    chunks_q, chunks_o = 4, 2
-    rows_q, rows_o = half_q // chunks_q, half_o // chunks_o
+    fac_copies = [load(fac_o_h, fac_o, sems.at[0]), load(fac_q_h, fac_q, sems.at[1], 1)]
     slot = 2
-    for chunk in range(chunks_q):
-        part = pl.ds(chunk * rows_q, rows_q)
-        there = pl.ds(pl.multiple_of(which * half_q + chunk * rows_q, rows_q), rows_q)
-        jobs.append((grad_q_v, error_q_v, mat_q, fac_q, part, chunk * rows_q, (
-            load(grad_q.at[there], grad_q_v.at[part], sems.at[slot]),
-            load(error_q.at[there], error_q_v.at[part], sems.at[slot + 1]),
-        )))
-        slot += 2
-        if chunk % 2 == 0:
-            continue
-        chunk = chunk // 2
-        part = pl.ds(chunk * rows_o, rows_o)
-        there = pl.ds(pl.multiple_of(which * half_o + chunk * rows_o, rows_o), rows_o)
-        jobs.append((grad_o_v, error_o_v, mat_o, fac_o, part, half_q + chunk * rows_o, (
-            load(grad_o.at[there], grad_o_v.at[part], sems.at[slot]),
-            load(error_o.at[there], error_o_v.at[part], sems.at[slot + 1]),
-        )))
-        slot += 2
+    for chunks, half, column, grad, error, grad_v, error_v, mat, fac in (
+        (2, half_o, half_q, grad_o, error_o, grad_o_v, error_o_v, mat_o, fac_o),
+        (4, half_q, 0, grad_q, error_q, grad_q_v, error_q_v, mat_q, fac_q),
+    ):
+        rows = half // chunks
+        for chunk in range(chunks):
+            part = pl.ds(chunk * rows, rows)
+            there = pl.ds(pl.multiple_of(which * half + chunk * rows, rows), rows)
+            jobs.append((grad_v, error_v, mat, fac, part, column + chunk * rows, (
+                load(grad.at[there], grad_v.at[part], sems.at[slot]),
+                load(error.at[there], error_v.at[part], sems.at[slot + 1], 1),
+            )))
+            slot += 2
     for copy in fac_copies:
         copy.wait()
     for grad_v, error_v, mat, fac, part, column, copies in jobs:
@@ -336,7 +329,7 @@
         approx = dot(hat[:, size_q + chunk * chunk_o:size_q + (chunk + 1) * chunk_o], new[:, wide_q:], 0, 0)
         stage_o[stage] = (mat_o[part, cols_o].astype(f32) - approx).astype(bf16)
         there = pl.ds(pl.multiple_of(half * size_o + chunk * chunk_o, chunk_o), chunk_o)
-        copies.append(load(stage_o.at[stage], error_o.at[there, cols_o], sems.at[slot + 1]))
+        copies.append(load(stage_o.at[stage], error_o.at[there, cols_o], sems.at[slot + 1], 1))
         slot += 2
     return copies
 
@@ -386,7 +379,7 @@
     weight_new[...] = weight[:, columns] - step_size * moved
     return [
         load(momentum_new, momentum_h.at[:, columns], sems.at[0]),
-        load(weight_new, weight_h.at[:, columns], sems.at[1]),
+        load(weight_new, weight_h.at[:, columns], sems.at[1], 1),
     ]
 
 
@@ -409,7 +402,7 @@
     new_o[:, half_at(1 - mine, wide_o)] = new_far[:, wide_q:]
     copies = [
         load(new_q, new_q_h, out_sems.at[0]),
-        load(new_o, new_o_h, out_sems.at[1]),
+        load(new_o, new_o_h, out_sems.at[1], 1),
         load(norm, norm_h, out_sems.at[2]),
     ]
     copies += error_columns(
@@ -425,7 +418,7 @@
         momentum_o_new[rows] = moved
         weight_o_new[rows] = weight_o[rows] - step_size * moved
     copies.append(load(momentum_o_new, momentum_o_h, out_sems.at[3]))
-    copies.append(load(weight_o_new, weight_o_h, out_sems.at[4]))
+    copies.append(load(weight_o_new, weight_o_h, out_sems.at[4], 1))
     copies += error_columns(
         1 - mine, hat_far, 1, 1 - mine, mat_q_far, mat_o_far, new_far,
         error_q, error_o, stage_q, stage_o, sems, 4

time: 45.6 us -> 45.8 us (level)
  starting transfers between devices: 19.1 us -> 16.5 us
  waiting for transfers between devices: 13.7 us -> 15.1 us
  Pallas kernels: 11.8 us -> 13.1 us
    ppermute x10, starting transfers between devices: 17.6 us -> 15 us  [swap(): return lax.ppermute(value, ('replica', 'tensor'), pairs)]
    ppermute x10, waiting for transfers between devices: 10.2 us -> 11.7 us  [swap(): return lax.ppermute(value, ('replica', 'tensor'), pairs)]
    pallas_call x1, Pallas kernels: 3.09 us -> 3.72 us  [project(): pl.pallas_call(far_kernel, out_shape=mats + (shaped((rank, columns), bf16...]
    pallas_call x1, Pallas kernels: 3.08 us -> 3.71 us  [project(): pl.pallas_call(near_kernel, out_shape=mats + (shaped((rank, columns), f32...]
  transfers between devices with their start and end apart: 12 -> 12, of which waited for: 8 -> 7; matrix products, arithmetic and copies ran while one was open for 0% -> 0% of each run, Pallas kernels for 13% -> 14%
where the time goes in v9:
time: 45.8 us; the launch traced here: 45.6 us
  starting transfers between devices  16.5 us (36%)
  waiting for transfers between devices  15.1 us (33%)
  Pallas kernels  13.1 us (29%)
  between operations  0.8 us (2%)
    ppermute x10, starting transfers between devices, swap(): return lax.ppermute(value, ('replica', 'tensor'), pairs)  15 us
    ppermute x10, waiting for transfers between devices, swap(): return lax.ppermute(value, ('replica', 'tensor'), pairs)  11.7 us
    pallas_call x1, Pallas kernels, project(): pl.pallas_call(far_kernel, out_shape=mats + (shaped((rank, columns), bf16...  3.72 us
    pallas_call x1, Pallas kernels, project(): pl.pallas_call(near_kernel, out_shape=mats + (shaped((rank, columns), f32...  3.71 us
    ppermute x2, waiting for transfers between devices, swap_tensor(): lax.ppermute(value, 'tensor', [(source, source ^ bit) for source in range...  3.42 us
    pallas_call x1, Pallas kernels, finish(): pl.pallas_call(functools.partial(finish_far_kernel, count), out_shape=ear...  2.33 us
    pallas_call x1, Pallas kernels, finish(): pl.pallas_call(functools.partial(finish_near_kernel, count), out_shape=ea...  1.86 us
    ppermute x2, starting transfers between devices, swap_tensor(): lax.ppermute(value, 'tensor', [(source, source ^ bit) for source in range...  1.56 us
  transfers between devices with their start and end apart: 12, of which 7 were waited for; matrix products, arithmetic and copies ran while one was open for 0% of the time, Pallas kernels for 14%

profile of v9, /device:TPU:0, one launch (start us, length us, event | category | flops | bytes accessed | tf_op | source)
XLA Modules:
  0.0 45.6 jit_solution(5297413550130296738)
XLA Ops:
  0.7 3.7 %project_far.1 = (bf16[1024,512]{1,0:T(8,128)(2,1)S(1)}, bf16[256,2048]{1,0:T(8,128)(2,1)S(1)}, bf16[32,1280]{1,0:T(8,128)(2,1)S(1)}) custom-call(bf16[32,512]{1,0:T(8,128)(2,1)} %bitcast.7, bf16[32,2048]{1,0:T(8,128)(2,1)} %bitcast.5, bf16[2048,512]{1,0:T(8,128)(2,1)} %grad_q.3, bf16[2048,512]{1,0:T(8,128)(2,1)} %error_q.3, bf16[512,2048]{1,0:T(8,128)(2,1)} %grad_o.3, ...), custom_call_target="tpu_custom_call" | custom-call | flops 67108864 | bytes 4194304 | tf_op jit(solution)/shard_map/project_far/pallas_call | solution.py:146
  4.4 3.0 %collective-permute-start = (bf16[32,1280]{1,0:T(8,128)(2,1)S(1)}, bf16[32,1280]{1,0:T(8,128)(2,1)S(1)}, u32[]{:S(2)}, u32[]{:S(2)}) collective-permute-start(bf16[32,1280]{1,0:T(8,128)(2,1)S(1)} %get-tuple-element.39), channel_id=1, source_target_pairs={{0,4},{1,17},{2,6},{3,19},{4,0},{5,21},{6,2},{7,23},{8,12},{9,25},... | collective-permute-start | bytes 245768 | tf_op jit(solution)/shard_map/ppermute | solution.py:499
  7.4 3.7 %project_near.1 = (bf16[1024,512]{1,0:T(8,128)(2,1)S(1)}, bf16[256,2048]{1,0:T(8,128)(2,1)S(1)}, f32[32,1280]{1,0:T(8,128)S(1)}, f32[32,128]{1,0:T(8,128)S(1)}) custom-call(bf16[32,512]{1,0:T(8,128)(2,1)} %bitcast.8, bf16[32,2048]{1,0:T(8,128)(2,1)} %bitcast.6, bf16[2048,512]{1,0:T(8,128)(2,1)} %grad_q.3, bf16[2048,512]{1,0:T(8,128)(2,1)} %error_q.3, ...), custom_call_target="tpu_custom_call" | custom-call | flops 67108864 | bytes 4194304 | tf_op jit(solution)/shard_map/project_near/pallas_call | solution.py:156
  11.2 3.7 %collective-permute-start.3 = (bf16[32,1408]{1,0:T(8,128)(2,1)S(1)}, bf16[32,1408]{1,0:T(8,128)(2,1)S(1)}, u32[]{:S(2)}, u32[]{:S(2)}) collective-permute-start(bf16[32,1408]{1,0:T(8,128)(2,1)S(1)} %first_sum.1.refs_0_), channel_id=1, source_target_pairs={{0,24},{1,13},{2,26},{3,15},{4,28},{5,9},{6,30},{7,11},{8,16},{9,5... | collective-permute-start | bytes 270344 | tf_op jit(solution)/shard_map/ppermute | solution.py:499
  14.9 0.8 %collective-permute-start.1 = (bf16[32,1408]{1,0:T(8,128)(2,1)S(1)}, bf16[32,1408]{1,0:T(8,128)(2,1)S(1)}, u32[]{:S(2)}, u32[]{:S(2)}) collective-permute-start(bf16[32,1408]{1,0:T(8,128)(2,1)S(1)} %first_sum.1.refs_0_), channel_id=1, source_target_pairs={{0,8},{1,5},{2,10},{3,7},{4,12},{5,1},{6,14},{7,3},{8,0},{9,13},{1... | collective-permute-start | bytes 270344 | tf_op jit(solution)/shard_map/ppermute | solution.py:499
  15.6 2.2 %collective-permute-done.3.refs_3_ = bf16[32,1408]{1,0:T(8,128)(2,1)S(1)} collective-permute-done((bf16[32,1408]{1,0:T(8,128)(2,1)S(1)}, bf16[32,1408]{1,0:T(8,128)(2,1)S(1)}, u32[]{:S(2)}, u32[]{:S(2)}) %collective-permute-start.3) | collective-permute-done | bytes 90144 | tf_op jit(solution)/shard_map/ppermute | solution.py:499
  17.8 2.8 %collective-permute-done.2.refs_2_ = bf16[32,1408]{1,0:T(8,128)(2,1)S(1)} collective-permute-done((bf16[32,1408]{1,0:T(8,128)(2,1)S(1)}, bf16[32,1408]{1,0:T(8,128)(2,1)S(1)}, u32[]{:S(2)}, u32[]{:S(2)}) %collective-permute-start.2) | collective-permute-done | bytes 90144 | tf_op jit(solution)/shard_map/ppermute | solution.py:499
  20.6 0.3 hats.1.hat.hat_near
  20.9 1.0 %collective-permute-start.4 = (bf16[32,1536]{1,0:T(8,128)(2,1)S(1)}, bf16[32,1536]{1,0:T(8,128)(2,1)S(1)}, u32[]{:S(2)}, u32[]{:S(2)}) collective-permute-start(bf16[32,1536]{1,0:T(8,128)(2,1)S(1)} %hats.1.hat.hat_near), channel_id=1, source_target_pairs={{0,4},{1,17},{2,6},{3,19},{4,0},{5,21},{6,2},{7,23},{8,12},{9,25},... | collective-permute-start | bytes 294920 | tf_op jit(solution)/shard_map/ppermute | solution.py:499
  22.0 0.5 right_near.1
  22.4 3.2 %collective-permute-done.4.hat.hat_far = bf16[32,1536]{1,0:T(8,128)(2,1)S(1)} collective-permute-done((bf16[32,1536]{1,0:T(8,128)(2,1)S(1)}, bf16[32,1536]{1,0:T(8,128)(2,1)S(1)}, u32[]{:S(2)}, u32[]{:S(2)}) %collective-permute-start.4) | collective-permute-done | bytes 98336 | tf_op jit(solution)/shard_map/ppermute | solution.py:499
  25.6 0.3 right_send.1
  25.9 1.0 %collective-permute-start.5 = (bf16[32,1280]{1,0:T(8,128)(2,1)S(1)}, bf16[32,1280]{1,0:T(8,128)(2,1)S(1)}, u32[]{:S(2)}, u32[]{:S(2)}) collective-permute-start(bf16[32,1280]{1,0:T(8,128)(2,1)S(1)} %right_send.1), channel_id=1, source_target_pairs={{0,4},{1,17},{2,6},{3,19},{4,0},{5,21},{6,2},{7,23},{8,12},{9,25},... | collective-permute-start | bytes 245768 | tf_op jit(solution)/shard_map/ppermute | solution.py:499
  27.3 1.2 %collective-permute-done.6.norm_got = f32[32,128]{1,0:T(8,128)S(1)} collective-permute-done((f32[32,128]{1,0:T(8,128)S(1)}, f32[32,128]{1,0:T(8,128)S(1)}, u32[]{:S(2)}, u32[]{:S(2)}) %collective-permute-start.6) | collective-permute-done | bytes 16416 | tf_op jit(solution)/shard_map/ppermute | solution.py:508
  28.5 2.0 %collective-permute-done.5.got = bf16[32,1280]{1,0:T(8,128)(2,1)S(1)} collective-permute-done((bf16[32,1280]{1,0:T(8,128)(2,1)S(1)}, bf16[32,1280]{1,0:T(8,128)(2,1)S(1)}, u32[]{:S(2)}, u32[]{:S(2)}) %collective-permute-start.5) | collective-permute-done | bytes 81952 | tf_op jit(solution)/shard_map/ppermute | solution.py:499
  30.5 2.2 %collective-permute-start.10 = (bf16[32,1280]{1,0:T(8,128)(2,1)S(1)}, bf16[32,1280]{1,0:T(8,128)(2,1)S(1)}, u32[]{:S(2)}, u32[]{:S(2)}) collective-permute-start(bf16[32,1280]{1,0:T(8,128)(2,1)S(1)} %get-tuple-element.49.refs_0_), channel_id=1, source_target_pairs={{0,24},{1,13},{2,26},{3,15},{4,28},{5,9},{6,30},{7,11},{8,16},{9,5... | collective-permute-start | bytes 245768 | tf_op jit(solution)/shard_map/ppermute | solution.py:499
  32.7 0.5 %collective-permute-start.9 = (bf16[32,1280]{1,0:T(8,128)(2,1)S(1)}, bf16[32,1280]{1,0:T(8,128)(2,1)S(1)}, u32[]{:S(2)}, u32[]{:S(2)}) collective-permute-start(bf16[32,1280]{1,0:T(8,128)(2,1)S(1)} %get-tuple-element.49.refs_0_), channel_id=1, source_target_pairs={{0,16},{1,9},{2,18},{3,11},{4,20},{5,13},{6,22},{7,15},{8,24},{9,1... | collective-permute-start | bytes 245768 | tf_op jit(solution)/shard_map/ppermute | solution.py:499
  33.2 1.7 %collective-permute-start.8 = (bf16[32,1280]{1,0:T(8,128)(2,1)S(1)}, bf16[32,1280]{1,0:T(8,128)(2,1)S(1)}, u32[]{:S(2)}, u32[]{:S(2)}) collective-permute-start(bf16[32,1280]{1,0:T(8,128)(2,1)S(1)} %get-tuple-element.49.refs_0_), channel_id=1, source_target_pairs={{0,8},{1,5},{2,10},{3,7},{4,12},{5,1},{6,14},{7,3},{8,0},{9,13},{1... | collective-permute-start | bytes 245768 | tf_op jit(solution)/shard_map/ppermute | solution.py:499
  34.9 1.5 %collective-permute-start.7 = (f32[32,128]{1,0:T(8,128)S(1)}, f32[32,128]{1,0:T(8,128)S(1)}, u32[]{:S(2)}, u32[]{:S(2)}) collective-permute-start(f32[32,128]{1,0:T(8,128)S(1)} %get-tuple-element.48.norm), channel_id=1, source_target_pairs={{0,2},{1,3},{2,0},{3,1},{4,6},{5,7},{6,4},{7,5},{8,10},{9,11},{10,... | collective-permute-start | bytes 49160 | tf_op jit(solution)/shard_map/ppermute | solution.py:508
  36.4 2.2 %collective-permute-done.7.norm_got = f32[32,128]{1,0:T(8,128)S(1)} collective-permute-done((f32[32,128]{1,0:T(8,128)S(1)}, f32[32,128]{1,0:T(8,128)S(1)}, u32[]{:S(2)}, u32[]{:S(2)}) %collective-permute-start.7) | collective-permute-done | bytes 16416 | tf_op jit(solution)/shard_map/ppermute | solution.py:508
  38.8 1.0 %collective-permute-start.11 = (bf16[32,1280]{1,0:T(8,128)(2,1)S(1)}, bf16[32,1280]{1,0:T(8,128)(2,1)S(1)}, u32[]{:S(2)}, u32[]{:S(2)}) collective-permute-start(bf16[32,1280]{1,0:T(8,128)(2,1)S(1)} %get-tuple-element.50.new.new_near), channel_id=1, source_target_pairs={{0,4},{1,17},{2,6},{3,19},{4,0},{5,21},{6,2},{7,23},{8,12},{9,25},... | collective-permute-start | bytes 245768 | tf_op jit(solution)/shard_map/ppermute | solution.py:499
  39.8 1.9 %finish_near.1 = (bf16[2048,512]{1,0:T(8,128)(2,1)}, bf16[512,2048]{1,0:T(8,128)(2,1)}, f32[256,512]{1,0:T(8,128)}, f32[256,512]{1,0:T(8,128)}) custom-call(bf16[32,1536]{1,0:T(8,128)(2,1)S(1)} %hats.1.hat.hat_near, bf16[32,1536]{1,0:T(8,128)(2,1)S(1)} %collective-permute-done.4.hat.hat_far, bf16[1024,512]{1,0:T(8,128)(2,1)S(1)} %get-tuple-element.40.mat_q.mat_q_near, ...), custom_call_target="tpu_custom_call" | custom-call | flops 67108864 | bytes 4194304 | tf_op jit(solution)/shard_map/finish_near/pallas_call | solution.py:465
  41.6 1.6 %collective-permute-done.11.new_far = bf16[32,1280]{1,0:T(8,128)(2,1)S(1)} collective-permute-done((bf16[32,1280]{1,0:T(8,128)(2,1)S(1)}, bf16[32,1280]{1,0:T(8,128)(2,1)S(1)}, u32[]{:S(2)}, u32[]{:S(2)}) %collective-permute-start.11) | collective-permute-done | bytes 81952 | tf_op jit(solution)/shard_map/ppermute | solution.py:499
  43.3 2.3 %finish_far.1 = (bf16[2048,512]{1,0:T(8,128)(2,1)}, bf16[512,2048]{1,0:T(8,128)(2,1)}, f32[256,512]{1,0:T(8,128)}, f32[256,512]{1,0:T(8,128)}, bf16[32,512]{1,0:...) custom-call(bf16[32,1536]{1,0:T(8,128)(2,1)S(1)} %hats.1.hat.hat_nea, ...), custom_call_target="tpu_custom_call", output_to_operand_aliasing={{0}: (13, {}), {1}: (14, {}), {2}: (15, {}), {3}: (16, {})} | custom-call | flops 67108864 | bytes 4194304 | tf_op jit(solution)/shard_map/finish_far/pallas_call | solution.py:477
  (25 shorter events, 0.5 us)
Async XLA Ops:
  0.6 6.8 %copy-start.4 = (bf16[1,1,4096]{2,1,0:T(2,128)(2,1)S(1)}, bf16[1,1,4096]{2,1,0:T(2,128)(2,1)}, u32[]{:S(2)}) copy-start(bf16[1,1,4096]{2,1,0:T(2,128)(2,1)} %norm_grads.1) | copy-start | bytes 24580
  4.4 16.2 %copy-start.5 = (f32[32,32]{1,0:T(8,128)S(1)}, f32[32,32]{1,0:T(8,128)}, u32[]{:S(2)}) copy-start(f32[32,32]{1,0:T(8,128)} %ginv_q.1) | copy-start | bytes 12292
  4.4 16.2 %copy-start.6 = (f32[32,32]{1,0:T(8,128)S(1)}, f32[32,32]{1,0:T(8,128)}, u32[]{:S(2)}) copy-start(f32[32,32]{1,0:T(8,128)} %ginv_o.1) | copy-start | bytes 12292
  4.4 6.8 %collective-permute-start = (bf16[32,1280]{1,0:T(8,128)(2,1)S(1)}, bf16[32,1280]{1,0:T(8,128)(2,1)S(1)}, u32[]{:S(2)}, u32[]{:S(2)}) collective-permute-start(bf16[32,1280]{1,0:T(8,128)(2,1)S(1)} %get-tuple-element.39), channel_id=1, source_target_pairs={{0,4},{1,17},{2,6},{3,19},{4,0},{5,21},{6,2},{7,23},{8,12},{9,25},... | collective-permute-start | bytes 245768 | tf_op jit(solution)/shard_map/ppermute | solution.py:499
  11.2 6.6 %collective-permute-start.3 = (bf16[32,1408]{1,0:T(8,128)(2,1)S(1)}, bf16[32,1408]{1,0:T(8,128)(2,1)S(1)}, u32[]{:S(2)}, u32[]{:S(2)}) collective-permute-start(bf16[32,1408]{1,0:T(8,128)(2,1)S(1)} %first_sum.1.refs_0_), channel_id=1, source_target_pairs={{0,24},{1,13},{2,26},{3,15},{4,28},{5,9},{6,30},{7,11},{8,16},{9,5... | collective-permute-start | bytes 270344 | tf_op jit(solution)/shard_map/ppermute | solution.py:499
  14.9 5.7 %collective-permute-start.2 = (bf16[32,1408]{1,0:T(8,128)(2,1)S(1)}, bf16[32,1408]{1,0:T(8,128)(2,1)S(1)}, u32[]{:S(2)}, u32[]{:S(2)}) collective-permute-start(bf16[32,1408]{1,0:T(8,128)(2,1)S(1)} %first_sum.1.refs_0_), channel_id=1, source_target_pairs={{0,16},{1,9},{2,18},{3,11},{4,20},{5,13},{6,22},{7,15},{8,24},{9,1... | collective-permute-start | bytes 270344 | tf_op jit(solution)/shard_map/ppermute | solution.py:499
  14.9 5.7 %collective-permute-start.1 = (bf16[32,1408]{1,0:T(8,128)(2,1)S(1)}, bf16[32,1408]{1,0:T(8,128)(2,1)S(1)}, u32[]{:S(2)}, u32[]{:S(2)}) collective-permute-start(bf16[32,1408]{1,0:T(8,128)(2,1)S(1)} %first_sum.1.refs_0_), channel_id=1, source_target_pairs={{0,8},{1,5},{2,10},{3,7},{4,12},{5,1},{6,14},{7,3},{8,0},{9,13},{1... | collective-permute-start | bytes 270344 | tf_op jit(solution)/shard_map/ppermute | solution.py:499
  20.9 4.7 %collective-permute-start.4 = (bf16[32,1536]{1,0:T(8,128)(2,1)S(1)}, bf16[32,1536]{1,0:T(8,128)(2,1)S(1)}, u32[]{:S(2)}, u32[]{:S(2)}) collective-permute-start(bf16[32,1536]{1,0:T(8,128)(2,1)S(1)} %hats.1.hat.hat_near), channel_id=1, source_target_pairs={{0,4},{1,17},{2,6},{3,19},{4,0},{5,21},{6,2},{7,23},{8,12},{9,25},... | collective-permute-start | bytes 294920 | tf_op jit(solution)/shard_map/ppermute | solution.py:499
  25.9 13.9 %copy-start = (f32[256,512]{1,0:T(8,128)S(1)}, f32[256,512]{1,0:T(8,128)}, u32[]{:S(2)}) copy-start(f32[256,512]{1,0:T(8,128)} %weight_q.3) | copy-start | bytes 1572868
  25.9 13.8 %copy-start.1 = (f32[256,512]{1,0:T(8,128)S(1)}, f32[256,512]{1,0:T(8,128)}, u32[]{:S(2)}) copy-start(f32[256,512]{1,0:T(8,128)} %momentum_q.3) | copy-start | bytes 1572868
  25.9 4.5 %collective-permute-start.5 = (bf16[32,1280]{1,0:T(8,128)(2,1)S(1)}, bf16[32,1280]{1,0:T(8,128)(2,1)S(1)}, u32[]{:S(2)}, u32[]{:S(2)}) collective-permute-start(bf16[32,1280]{1,0:T(8,128)(2,1)S(1)} %right_send.1), channel_id=1, source_target_pairs={{0,4},{1,17},{2,6},{3,19},{4,0},{5,21},{6,2},{7,23},{8,12},{9,25},... | collective-permute-start | bytes 245768 | tf_op jit(solution)/shard_map/ppermute | solution.py:499
  27.2 1.2 %collective-permute-start.6 = (f32[32,128]{1,0:T(8,128)S(1)}, f32[32,128]{1,0:T(8,128)S(1)}, u32[]{:S(2)}, u32[]{:S(2)}) collective-permute-start(f32[32,128]{1,0:T(8,128)S(1)} %get-tuple-element.47.norm), channel_id=1, source_target_pairs={{0,1},{1,0},{2,3},{3,2},{4,5},{5,4},{6,7},{7,6},{8,9},{9,8},{10,11... | collective-permute-start | bytes 49160 | tf_op jit(solution)/shard_map/ppermute | solution.py:508
  30.5 8.2 %collective-permute-start.10 = (bf16[32,1280]{1,0:T(8,128)(2,1)S(1)}, bf16[32,1280]{1,0:T(8,128)(2,1)S(1)}, u32[]{:S(2)}, u32[]{:S(2)}) collective-permute-start(bf16[32,1280]{1,0:T(8,128)(2,1)S(1)} %get-tuple-element.49.refs_0_), channel_id=1, source_target_pairs={{0,24},{1,13},{2,26},{3,15},{4,28},{5,9},{6,30},{7,11},{8,16},{9,5... | collective-permute-start | bytes 245768 | tf_op jit(solution)/shard_map/ppermute | solution.py:499
  32.7 6.0 %collective-permute-start.9 = (bf16[32,1280]{1,0:T(8,128)(2,1)S(1)}, bf16[32,1280]{1,0:T(8,128)(2,1)S(1)}, u32[]{:S(2)}, u32[]{:S(2)}) collective-permute-start(bf16[32,1280]{1,0:T(8,128)(2,1)S(1)} %get-tuple-element.49.refs_0_), channel_id=1, source_target_pairs={{0,16},{1,9},{2,18},{3,11},{4,20},{5,13},{6,22},{7,15},{8,24},{9,1... | collective-permute-start | bytes 245768 | tf_op jit(solution)/shard_map/ppermute | solution.py:499
  33.2 5.4 %collective-permute-start.8 = (bf16[32,1280]{1,0:T(8,128)(2,1)S(1)}, bf16[32,1280]{1,0:T(8,128)(2,1)S(1)}, u32[]{:S(2)}, u32[]{:S(2)}) collective-permute-start(bf16[32,1280]{1,0:T(8,128)(2,1)S(1)} %get-tuple-element.49.refs_0_), channel_id=1, source_target_pairs={{0,8},{1,5},{2,10},{3,7},{4,12},{5,1},{6,14},{7,3},{8,0},{9,13},{1... | collective-permute-start | bytes 245768 | tf_op jit(solution)/shard_map/ppermute | solution.py:499
  34.9 3.7 %collective-permute-start.7 = (f32[32,128]{1,0:T(8,128)S(1)}, f32[32,128]{1,0:T(8,128)S(1)}, u32[]{:S(2)}, u32[]{:S(2)}) collective-permute-start(f32[32,128]{1,0:T(8,128)S(1)} %get-tuple-element.48.norm), channel_id=1, source_target_pairs={{0,2},{1,3},{2,0},{3,1},{4,6},{5,7},{6,4},{7,5},{8,10},{9,11},{10,... | collective-permute-start | bytes 49160 | tf_op jit(solution)/shard_map/ppermute | solution.py:508
  38.7 4.5 %copy-start.2 = (f32[512,256]{1,0:T(8,128)S(1)}, f32[512,256]{1,0:T(8,128)}, u32[]{:S(2)}) copy-start(f32[512,256]{1,0:T(8,128)} %weight_o.1) | copy-start | bytes 1572868
  38.8 4.5 %copy-start.3 = (f32[512,256]{1,0:T(8,128)S(1)}, f32[512,256]{1,0:T(8,128)}, u32[]{:S(2)}) copy-start(f32[512,256]{1,0:T(8,128)} %momentum_o.1) | copy-start | bytes 1572868
  38.8 4.5 %collective-permute-start.11 = (bf16[32,1280]{1,0:T(8,128)(2,1)S(1)}, bf16[32,1280]{1,0:T(8,128)(2,1)S(1)}, u32[]{:S(2)}, u32[]{:S(2)}) collective-permute-start(bf16[32,1280]{1,0:T(8,128)(2,1)S(1)} %get-tuple-element.50.new.new_near), channel_id=1, source_target_pairs={{0,4},{1,17},{2,6},{3,19},{4,0},{5,21},{6,2},{7,23},{8,12},{9,25},... | collective-permute-start | bytes 245768 | tf_op jit(solution)/shard_map/ppermute | solution.py:499

commit v10 on v8

--- a/solution.py
+++ b/solution.py
@@ -69,37 +69,34 @@
     fac_q, fac_o, grad_q_v, error_q_v, grad_o_v, error_o_v, sems,
 ):
     half_q, half_o = mat_q.shape[0], mat_o.shape[0]
+    steps = 4
+    rows_q, rows_o = half_q // steps, half_o // steps
+    fac_copies = [load(fac_q_h, fac_q, sems.at[0]), load(fac_o_h, fac_o, sems.at[1])]
     jobs = []
-    fac_copies = [load(fac_q_h, fac_q, sems.at[0]), load(fac_o_h, fac_o, sems.at[1])]
-    chunks_q, chunks_o = 4, 2
-    rows_q, rows_o = half_q // chunks_q, half_o // chunks_o
-    slot = 2
-    for chunk in range(chunks_q):
-        part = pl.ds(chunk * rows_q, rows_q)
-        there = pl.ds(pl.multiple_of(which * half_q + chunk * rows_q, rows_q), rows_q)
-        jobs.append((grad_q_v, error_q_v, mat_q, fac_q, part, chunk * rows_q, (
-            load(grad_q.at[there], grad_q_v.at[part], sems.at[slot]),
-            load(error_q.at[there], error_q_v.at[part], sems.at[slot + 1]),
+    for step in range(steps):
+        slot = 2 + 4 * step
+        part_q = pl.ds(step * rows_q, rows_q)
+        part_o = pl.ds(step * rows_o, rows_o)
+        there_q = pl.ds(pl.multiple_of(which * half_q + step * rows_q, rows_q), rows_q)
+        there_o = pl.ds(pl.multiple_of(which * half_o + step * rows_o, rows_o), rows_o)
+        jobs.append((step, part_q, part_o, (
+            load(grad_q.at[there_q], grad_q_v.at[part_q], sems.at[slot]),
+            load(error_q.at[there_q], error_q_v.at[part_q], sems.at[slot + 1]),
+            load(grad_o.at[there_o], grad_o_v.at[part_o], sems.at[slot + 2]),
+            load(error_o.at[there_o], error_o_v.at[part_o], sems.at[slot + 3]),
         )))
-        slot += 2
-        if chunk % 2 == 0:
-            continue
-        chunk = chunk // 2
-        part = pl.ds(chunk * rows_o, rows_o)
-        there = pl.ds(pl.multiple_of(which * half_o + chunk * rows_o, rows_o), rows_o)
-        jobs.append((grad_o_v, error_o_v, mat_o, fac_o, part, half_q + chunk * rows_o, (
-            load(grad_o.at[there], grad_o_v.at[part], sems.at[slot]),
-            load(error_o.at[there], error_o_v.at[part], sems.at[slot + 1]),
-        )))
-        slot += 2
     for copy in fac_copies:
         copy.wait()
-    for grad_v, error_v, mat, fac, part, column, copies in jobs:
+    columns_o = fac_o[...].T
+    for step, part_q, part_o, copies in jobs:
         for copy in copies:
             copy.wait()
-        block = grad_v[part] + error_v[part]
-        mat[part] = block
-        store(column, dot(fac[...], block, 1, 1))
+        block_q = grad_q_v[part_q] + error_q_v[part_q]
+        block_o = grad_o_v[part_o] + error_o_v[part_o]
+        mat_q[part_q] = block_q
+        mat_o[part_o] = block_o
+        store(step * rows_q, dot(fac_q[...], block_q, 1, 1))
+        store(half_q + step * rows_o, dot(block_o, columns_o, 1, 0).T)
 
 
 def far_kernel(
@@ -144,7 +141,7 @@
         pltpu.VMEM(half_q, bf16),
         pltpu.VMEM(half_o, bf16),
         pltpu.VMEM(half_o, bf16),
-        pltpu.SemaphoreType.DMA((14,)),
+        pltpu.SemaphoreType.DMA((18,)),
     ]
     operands = [
         in_hbm(value) for value in (fac_q, fac_o, grad_q, error_q, grad_o, error_o)

time: 45.6 us -> 45.6 us (level)
  starting transfers between devices: 19.1 us -> 19.7 us
    ppermute x10, starting transfers between devices: 17.6 us -> 18.1 us  [swap(): return lax.ppermute(value, ('replica', 'tensor'), pairs)]
  transfers between devices with their start and end apart: 12 -> 12, of which waited for: 8 -> 8; matrix products, arithmetic and copies ran while one was open for 0% -> 0% of each run, Pallas kernels for 13% -> 12%
where the time goes in v10:
time: 45.6 us; the launch traced here: 45.4 us
  starting transfers between devices  19.7 us (43%)
  waiting for transfers between devices  13.5 us (30%)
  Pallas kernels  11.4 us (25%)
  between operations  0.8 us (2%)
    ppermute x10, starting transfers between devices, swap(): return lax.ppermute(value, ('replica', 'tensor'), pairs)  18.1 us
    ppermute x10, waiting for transfers between devices, swap(): return lax.ppermute(value, ('replica', 'tensor'), pairs)  10 us
    ppermute x2, waiting for transfers between devices, swap_tensor(): lax.ppermute(value, 'tensor', [(source, source ^ bit) for source in range...  3.42 us
    pallas_call x1, Pallas kernels, project(): pl.pallas_call(far_kernel, out_shape=mats + (shaped((rank, columns), bf16...  2.91 us
    pallas_call x1, Pallas kernels, project(): pl.pallas_call(near_kernel, out_shape=mats + (shaped((rank, columns), f32...  2.9 us
    pallas_call x1, Pallas kernels, finish(): pl.pallas_call(functools.partial(finish_far_kernel, count), out_shape=ear...  2.32 us
    pallas_call x1, Pallas kernels, finish(): pl.pallas_call(functools.partial(finish_near_kernel, count), out_shape=ea...  1.86 us
    ppermute x2, starting transfers between devices, swap_tensor(): lax.ppermute(value, 'tensor', [(source, source ^ bit) for source in range...  1.56 us
  transfers between devices with their start and end apart: 12, of which 8 were waited for; matrix products, arithmetic and copies ran while one was open for 0% of the time, Pallas kernels for 12%

profile of v10, /device:TPU:0, one launch (start us, length us, event | category | flops | bytes accessed | tf_op | source)
XLA Modules:
  0.0 45.4 jit_solution(18424408842726036583)
XLA Ops:
  0.7 2.9 %project_far.1 = (bf16[1024,512]{1,0:T(8,128)(2,1)S(1)}, bf16[256,2048]{1,0:T(8,128)(2,1)S(1)}, bf16[32,1280]{1,0:T(8,128)(2,1)S(1)}) custom-call(bf16[32,512]{1,0:T(8,128)(2,1)} %bitcast.7, bf16[32,2048]{1,0:T(8,128)(2,1)} %bitcast.5, bf16[2048,512]{1,0:T(8,128)(2,1)} %grad_q.3, bf16[2048,512]{1,0:T(8,128)(2,1)} %error_q.3, bf16[512,2048]{1,0:T(8,128)(2,1)} %grad_o.3, ...), custom_call_target="tpu_custom_call" | custom-call | flops 67108864 | bytes 4194304 | tf_op jit(solution)/shard_map/project_far/pallas_call | solution.py:150
  3.6 3.0 %collective-permute-start = (bf16[32,1280]{1,0:T(8,128)(2,1)S(1)}, bf16[32,1280]{1,0:T(8,128)(2,1)S(1)}, u32[]{:S(2)}, u32[]{:S(2)}) collective-permute-start(bf16[32,1280]{1,0:T(8,128)(2,1)S(1)} %get-tuple-element.39), channel_id=1, source_target_pairs={{0,4},{1,17},{2,6},{3,19},{4,0},{5,21},{6,2},{7,23},{8,12},{9,25},... | collective-permute-start | bytes 245768 | tf_op jit(solution)/shard_map/ppermute | solution.py:503
  6.6 2.9 %project_near.1 = (bf16[1024,512]{1,0:T(8,128)(2,1)S(1)}, bf16[256,2048]{1,0:T(8,128)(2,1)S(1)}, f32[32,1280]{1,0:T(8,128)S(1)}, f32[32,128]{1,0:T(8,128)S(1)}) custom-call(bf16[32,512]{1,0:T(8,128)(2,1)} %bitcast.8, bf16[32,2048]{1,0:T(8,128)(2,1)} %bitcast.6, bf16[2048,512]{1,0:T(8,128)(2,1)} %grad_q.3, bf16[2048,512]{1,0:T(8,128)(2,1)} %error_q.3, ...), custom_call_target="tpu_custom_call" | custom-call | flops 67108864 | bytes 4194304 | tf_op jit(solution)/shard_map/project_near/pallas_call | solution.py:160
  9.6 3.7 %collective-permute-start.3 = (bf16[32,1408]{1,0:T(8,128)(2,1)S(1)}, bf16[32,1408]{1,0:T(8,128)(2,1)S(1)}, u32[]{:S(2)}, u32[]{:S(2)}) collective-permute-start(bf16[32,1408]{1,0:T(8,128)(2,1)S(1)} %first_sum.1.refs_0_), channel_id=1, source_target_pairs={{0,24},{1,13},{2,26},{3,15},{4,28},{5,9},{6,30},{7,11},{8,16},{9,5... | collective-permute-start | bytes 270344 | tf_op jit(solution)/shard_map/ppermute | solution.py:503
  13.2 0.8 %collective-permute-start.1 = (bf16[32,1408]{1,0:T(8,128)(2,1)S(1)}, bf16[32,1408]{1,0:T(8,128)(2,1)S(1)}, u32[]{:S(2)}, u32[]{:S(2)}) collective-permute-start(bf16[32,1408]{1,0:T(8,128)(2,1)S(1)} %first_sum.1.refs_0_), channel_id=1, source_target_pairs={{0,8},{1,5},{2,10},{3,7},{4,12},{5,1},{6,14},{7,3},{8,0},{9,13},{1... | collective-permute-start | bytes 270344 | tf_op jit(solution)/shard_map/ppermute | solution.py:503
  14.0 2.9 %collective-permute-done.3.refs_3_ = bf16[32,1408]{1,0:T(8,128)(2,1)S(1)} collective-permute-done((bf16[32,1408]{1,0:T(8,128)(2,1)S(1)}, bf16[32,1408]{1,0:T(8,128)(2,1)S(1)}, u32[]{:S(2)}, u32[]{:S(2)}) %collective-permute-start.3) | collective-permute-done | bytes 90144 | tf_op jit(solution)/shard_map/ppermute | solution.py:503
  16.9 2.2 %collective-permute-done.2.refs_2_ = bf16[32,1408]{1,0:T(8,128)(2,1)S(1)} collective-permute-done((bf16[32,1408]{1,0:T(8,128)(2,1)S(1)}, bf16[32,1408]{1,0:T(8,128)(2,1)S(1)}, u32[]{:S(2)}, u32[]{:S(2)}) %collective-permute-start.2) | collective-permute-done | bytes 90144 | tf_op jit(solution)/shard_map/ppermute | solution.py:503
  19.1 0.3 hats.1.hat.hat_near
  19.5 1.7 %collective-permute-start.4 = (bf16[32,1536]{1,0:T(8,128)(2,1)S(1)}, bf16[32,1536]{1,0:T(8,128)(2,1)S(1)}, u32[]{:S(2)}, u32[]{:S(2)}) collective-permute-start(bf16[32,1536]{1,0:T(8,128)(2,1)S(1)} %hats.1.hat.hat_near), channel_id=1, source_target_pairs={{0,4},{1,17},{2,6},{3,19},{4,0},{5,21},{6,2},{7,23},{8,12},{9,25},... | collective-permute-start | bytes 294920 | tf_op jit(solution)/shard_map/ppermute | solution.py:503
  21.1 0.5 %right_near.1 = (f32[32,512]{1,0:T(8,128)S(1)}, f32[32,2048]{1,0:T(8,128)S(1)}) custom-call(bf16[32,1536]{1,0:T(8,128)(2,1)S(1)} %hats.1.hat.hat_near, bf16[1024,512]{1,0:T(8,128)(2,1)S(1)} %get-tuple-element.40.mat_q.mat_q_near, bf16[256,2048]{1,0:T(8,128)(2,1)S(1)} %get-tuple-element.41.mat_o.mat_o_near), custom_call_target="tpu_custom_call" | custom-call | flops 67108864 | bytes 2097152 | tf_op jit(solution)/shard_map/right_near/pallas_call | solution.py:250
  21.6 2.6 %collective-permute-done.4.hat.hat_far = bf16[32,1536]{1,0:T(8,128)(2,1)S(1)} collective-permute-done((bf16[32,1536]{1,0:T(8,128)(2,1)S(1)}, bf16[32,1536]{1,0:T(8,128)(2,1)S(1)}, u32[]{:S(2)}, u32[]{:S(2)}) %collective-permute-start.4) | collective-permute-done | bytes 98336 | tf_op jit(solution)/shard_map/ppermute | solution.py:503
  24.2 0.3 right_send.1
  24.5 1.7 %collective-permute-start.5 = (bf16[32,1280]{1,0:T(8,128)(2,1)S(1)}, bf16[32,1280]{1,0:T(8,128)(2,1)S(1)}, u32[]{:S(2)}, u32[]{:S(2)}) collective-permute-start(bf16[32,1280]{1,0:T(8,128)(2,1)S(1)} %right_send.1), channel_id=1, source_target_pairs={{0,4},{1,17},{2,6},{3,19},{4,0},{5,21},{6,2},{7,23},{8,12},{9,25},... | collective-permute-start | bytes 245768 | tf_op jit(solution)/shard_map/ppermute | solution.py:503
  26.5 1.2 %collective-permute-done.6.norm_got = f32[32,128]{1,0:T(8,128)S(1)} collective-permute-done((f32[32,128]{1,0:T(8,128)S(1)}, f32[32,128]{1,0:T(8,128)S(1)}, u32[]{:S(2)}, u32[]{:S(2)}) %collective-permute-start.6) | collective-permute-done | bytes 16416 | tf_op jit(solution)/shard_map/ppermute | solution.py:512
  27.7 1.3 %collective-permute-done.5.got = bf16[32,1280]{1,0:T(8,128)(2,1)S(1)} collective-permute-done((bf16[32,1280]{1,0:T(8,128)(2,1)S(1)}, bf16[32,1280]{1,0:T(8,128)(2,1)S(1)}, u32[]{:S(2)}, u32[]{:S(2)}) %collective-permute-start.5) | collective-permute-done | bytes 81952 | tf_op jit(solution)/shard_map/ppermute | solution.py:503
  29.0 2.9 %collective-permute-start.10 = (bf16[32,1280]{1,0:T(8,128)(2,1)S(1)}, bf16[32,1280]{1,0:T(8,128)(2,1)S(1)}, u32[]{:S(2)}, u32[]{:S(2)}) collective-permute-start(bf16[32,1280]{1,0:T(8,128)(2,1)S(1)} %get-tuple-element.49.refs_0_), channel_id=1, source_target_pairs={{0,24},{1,13},{2,26},{3,15},{4,28},{5,9},{6,30},{7,11},{8,16},{9,5... | collective-permute-start | bytes 245768 | tf_op jit(solution)/shard_map/ppermute | solution.py:503
  31.9 1.6 %collective-permute-start.8 = (bf16[32,1280]{1,0:T(8,128)(2,1)S(1)}, bf16[32,1280]{1,0:T(8,128)(2,1)S(1)}, u32[]{:S(2)}, u32[]{:S(2)}) collective-permute-start(bf16[32,1280]{1,0:T(8,128)(2,1)S(1)} %get-tuple-element.49.refs_0_), channel_id=1, source_target_pairs={{0,8},{1,5},{2,10},{3,7},{4,12},{5,1},{6,14},{7,3},{8,0},{9,13},{1... | collective-permute-start | bytes 245768 | tf_op jit(solution)/shard_map/ppermute | solution.py:503
  33.5 1.5 %collective-permute-start.7 = (f32[32,128]{1,0:T(8,128)S(1)}, f32[32,128]{1,0:T(8,128)S(1)}, u32[]{:S(2)}, u32[]{:S(2)}) collective-permute-start(f32[32,128]{1,0:T(8,128)S(1)} %get-tuple-element.48.norm), channel_id=1, source_target_pairs={{0,2},{1,3},{2,0},{3,1},{4,6},{5,7},{6,4},{7,5},{8,10},{9,11},{10,... | collective-permute-start | bytes 49160 | tf_op jit(solution)/shard_map/ppermute | solution.py:512
  35.0 2.2 %collective-permute-done.7.norm_got = f32[32,128]{1,0:T(8,128)S(1)} collective-permute-done((f32[32,128]{1,0:T(8,128)S(1)}, f32[32,128]{1,0:T(8,128)S(1)}, u32[]{:S(2)}, u32[]{:S(2)}) %collective-permute-start.7) | collective-permute-done | bytes 16416 | tf_op jit(solution)/shard_map/ppermute | solution.py:512
  37.2 0.5 %collective-permute-done.9.refs_2_ = bf16[32,1280]{1,0:T(8,128)(2,1)S(1)} collective-permute-done((bf16[32,1280]{1,0:T(8,128)(2,1)S(1)}, bf16[32,1280]{1,0:T(8,128)(2,1)S(1)}, u32[]{:S(2)}, u32[]{:S(2)}) %collective-permute-start.9) | collective-permute-done | bytes 81952 | tf_op jit(solution)/shard_map/ppermute | solution.py:503
  37.8 2.9 %collective-permute-start.11 = (bf16[32,1280]{1,0:T(8,128)(2,1)S(1)}, bf16[32,1280]{1,0:T(8,128)(2,1)S(1)}, u32[]{:S(2)}, u32[]{:S(2)}) collective-permute-start(bf16[32,1280]{1,0:T(8,128)(2,1)S(1)} %get-tuple-element.50.new.new_near), channel_id=1, source_target_pairs={{0,4},{1,17},{2,6},{3,19},{4,0},{5,21},{6,2},{7,23},{8,12},{9,25},... | collective-permute-start | bytes 245768 | tf_op jit(solution)/shard_map/ppermute | solution.py:503
  40.7 1.9 %finish_near.1 = (bf16[2048,512]{1,0:T(8,128)(2,1)}, bf16[512,2048]{1,0:T(8,128)(2,1)}, f32[256,512]{1,0:T(8,128)}, f32[256,512]{1,0:T(8,128)}) custom-call(bf16[32,1536]{1,0:T(8,128)(2,1)S(1)} %hats.1.hat.hat_near, bf16[32,1536]{1,0:T(8,128)(2,1)S(1)} %collective-permute-done.4.hat.hat_far, bf16[1024,512]{1,0:T(8,128)(2,1)S(1)} %get-tuple-element.40.mat_q.mat_q_near, ...), custom_call_target="tpu_custom_call" | custom-call | flops 67108864 | bytes 4194304 | tf_op jit(solution)/shard_map/finish_near/pallas_call | solution.py:469
  42.5 0.5 %collective-permute-done.11.new_far = bf16[32,1280]{1,0:T(8,128)(2,1)S(1)} collective-permute-done((bf16[32,1280]{1,0:T(8,128)(2,1)S(1)}, bf16[32,1280]{1,0:T(8,128)(2,1)S(1)}, u32[]{:S(2)}, u32[]{:S(2)}) %collective-permute-start.11) | collective-permute-done | bytes 81952 | tf_op jit(solution)/shard_map/ppermute | solution.py:503
  43.1 2.3 %finish_far.1 = (bf16[2048,512]{1,0:T(8,128)(2,1)}, bf16[512,2048]{1,0:T(8,128)(2,1)}, f32[256,512]{1,0:T(8,128)}, f32[256,512]{1,0:T(8,128)}, bf16[32,512]{1,0:...) custom-call(bf16[32,1536]{1,0:T(8,128)(2,1)S(1)} %hats.1.hat.hat_nea, ...), custom_call_target="tpu_custom_call", output_to_operand_aliasing={{0}: (13, {}), {1}: (14, {}), {2}: (15, {}), {3}: (16, {})} | custom-call | flops 67108864 | bytes 4194304 | tf_op jit(solution)/shard_map/finish_far/pallas_call | solution.py:481
  (25 shorter events, 0.5 us)
Async XLA Ops:
  0.6 6.0 %copy-start.4 = (bf16[1,1,4096]{2,1,0:T(2,128)(2,1)S(1)}, bf16[1,1,4096]{2,1,0:T(2,128)(2,1)}, u32[]{:S(2)}) copy-start(bf16[1,1,4096]{2,1,0:T(2,128)(2,1)} %norm_grads.1) | copy-start | bytes 24580
  3.6 15.6 %copy-start.5 = (f32[32,32]{1,0:T(8,128)S(1)}, f32[32,32]{1,0:T(8,128)}, u32[]{:S(2)}) copy-start(f32[32,32]{1,0:T(8,128)} %ginv_q.1) | copy-start | bytes 12292
  3.6 15.6 %copy-start.6 = (f32[32,32]{1,0:T(8,128)S(1)}, f32[32,32]{1,0:T(8,128)}, u32[]{:S(2)}) copy-start(f32[32,32]{1,0:T(8,128)} %ginv_o.1) | copy-start | bytes 12292
  3.6 5.9 %collective-permute-start = (bf16[32,1280]{1,0:T(8,128)(2,1)S(1)}, bf16[32,1280]{1,0:T(8,128)(2,1)S(1)}, u32[]{:S(2)}, u32[]{:S(2)}) collective-permute-start(bf16[32,1280]{1,0:T(8,128)(2,1)S(1)} %get-tuple-element.39), channel_id=1, source_target_pairs={{0,4},{1,17},{2,6},{3,19},{4,0},{5,21},{6,2},{7,23},{8,12},{9,25},... | collective-permute-start | bytes 245768 | tf_op jit(solution)/shard_map/ppermute | solution.py:503
  9.6 7.3 %collective-permute-start.3 = (bf16[32,1408]{1,0:T(8,128)(2,1)S(1)}, bf16[32,1408]{1,0:T(8,128)(2,1)S(1)}, u32[]{:S(2)}, u32[]{:S(2)}) collective-permute-start(bf16[32,1408]{1,0:T(8,128)(2,1)S(1)} %first_sum.1.refs_0_), channel_id=1, source_target_pairs={{0,24},{1,13},{2,26},{3,15},{4,28},{5,9},{6,30},{7,11},{8,16},{9,5... | collective-permute-start | bytes 270344 | tf_op jit(solution)/shard_map/ppermute | solution.py:503
  13.2 5.9 %collective-permute-start.2 = (bf16[32,1408]{1,0:T(8,128)(2,1)S(1)}, bf16[32,1408]{1,0:T(8,128)(2,1)S(1)}, u32[]{:S(2)}, u32[]{:S(2)}) collective-permute-start(bf16[32,1408]{1,0:T(8,128)(2,1)S(1)} %first_sum.1.refs_0_), channel_id=1, source_target_pairs={{0,16},{1,9},{2,18},{3,11},{4,20},{5,13},{6,22},{7,15},{8,24},{9,1... | collective-permute-start | bytes 270344 | tf_op jit(solution)/shard_map/ppermute | solution.py:503
  13.2 5.9 %collective-permute-start.1 = (bf16[32,1408]{1,0:T(8,128)(2,1)S(1)}, bf16[32,1408]{1,0:T(8,128)(2,1)S(1)}, u32[]{:S(2)}, u32[]{:S(2)}) collective-permute-start(bf16[32,1408]{1,0:T(8,128)(2,1)S(1)} %first_sum.1.refs_0_), channel_id=1, source_target_pairs={{0,8},{1,5},{2,10},{3,7},{4,12},{5,1},{6,14},{7,3},{8,0},{9,13},{1... | collective-permute-start | bytes 270344 | tf_op jit(solution)/shard_map/ppermute | solution.py:503
  19.5 4.7 %collective-permute-start.4 = (bf16[32,1536]{1,0:T(8,128)(2,1)S(1)}, bf16[32,1536]{1,0:T(8,128)(2,1)S(1)}, u32[]{:S(2)}, u32[]{:S(2)}) collective-permute-start(bf16[32,1536]{1,0:T(8,128)(2,1)S(1)} %hats.1.hat.hat_near), channel_id=1, source_target_pairs={{0,4},{1,17},{2,6},{3,19},{4,0},{5,21},{6,2},{7,23},{8,12},{9,25},... | collective-permute-start | bytes 294920 | tf_op jit(solution)/shard_map/ppermute | solution.py:503
  24.5 16.2 %copy-start = (f32[256,512]{1,0:T(8,128)S(1)}, f32[256,512]{1,0:T(8,128)}, u32[]{:S(2)}) copy-start(f32[256,512]{1,0:T(8,128)} %weight_q.3) | copy-start | bytes 1572868
  24.5 16.2 %copy-start.1 = (f32[256,512]{1,0:T(8,128)S(1)}, f32[256,512]{1,0:T(8,128)}, u32[]{:S(2)}) copy-start(f32[256,512]{1,0:T(8,128)} %momentum_q.3) | copy-start | bytes 1572868
  24.5 4.5 %collective-permute-start.5 = (bf16[32,1280]{1,0:T(8,128)(2,1)S(1)}, bf16[32,1280]{1,0:T(8,128)(2,1)S(1)}, u32[]{:S(2)}, u32[]{:S(2)}) collective-permute-start(bf16[32,1280]{1,0:T(8,128)(2,1)S(1)} %right_send.1), channel_id=1, source_target_pairs={{0,4},{1,17},{2,6},{3,19},{4,0},{5,21},{6,2},{7,23},{8,12},{9,25},... | collective-permute-start | bytes 245768 | tf_op jit(solution)/shard_map/ppermute | solution.py:503
  26.4 1.2 %collective-permute-start.6 = (f32[32,128]{1,0:T(8,128)S(1)}, f32[32,128]{1,0:T(8,128)S(1)}, u32[]{:S(2)}, u32[]{:S(2)}) collective-permute-start(f32[32,128]{1,0:T(8,128)S(1)} %get-tuple-element.47.norm), channel_id=1, source_target_pairs={{0,1},{1,0},{2,3},{3,2},{4,5},{5,4},{6,7},{7,6},{8,9},{9,8},{10,11... | collective-permute-start | bytes 49160 | tf_op jit(solution)/shard_map/ppermute | solution.py:512
  29.0 8.2 %collective-permute-start.10 = (bf16[32,1280]{1,0:T(8,128)(2,1)S(1)}, bf16[32,1280]{1,0:T(8,128)(2,1)S(1)}, u32[]{:S(2)}, u32[]{:S(2)}) collective-permute-start(bf16[32,1280]{1,0:T(8,128)(2,1)S(1)} %get-tuple-element.49.refs_0_), channel_id=1, source_target_pairs={{0,24},{1,13},{2,26},{3,15},{4,28},{5,9},{6,30},{7,11},{8,16},{9,5... | collective-permute-start | bytes 245768 | tf_op jit(solution)/shard_map/ppermute | solution.py:503
  31.9 5.8 %collective-permute-start.9 = (bf16[32,1280]{1,0:T(8,128)(2,1)S(1)}, bf16[32,1280]{1,0:T(8,128)(2,1)S(1)}, u32[]{:S(2)}, u32[]{:S(2)}) collective-permute-start(bf16[32,1280]{1,0:T(8,128)(2,1)S(1)} %get-tuple-element.49.refs_0_), channel_id=1, source_target_pairs={{0,16},{1,9},{2,18},{3,11},{4,20},{5,13},{6,22},{7,15},{8,24},{9,1... | collective-permute-start | bytes 245768 | tf_op jit(solution)/shard_map/ppermute | solution.py:503
  31.9 5.8 %collective-permute-start.8 = (bf16[32,1280]{1,0:T(8,128)(2,1)S(1)}, bf16[32,1280]{1,0:T(8,128)(2,1)S(1)}, u32[]{:S(2)}, u32[]{:S(2)}) collective-permute-start(bf16[32,1280]{1,0:T(8,128)(2,1)S(1)} %get-tuple-element.49.refs_0_), channel_id=1, source_target_pairs={{0,8},{1,5},{2,10},{3,7},{4,12},{5,1},{6,14},{7,3},{8,0},{9,13},{1... | collective-permute-start | bytes 245768 | tf_op jit(solution)/shard_map/ppermute | solution.py:503
  33.5 3.7 %collective-permute-start.7 = (f32[32,128]{1,0:T(8,128)S(1)}, f32[32,128]{1,0:T(8,128)S(1)}, u32[]{:S(2)}, u32[]{:S(2)}) collective-permute-start(f32[32,128]{1,0:T(8,128)S(1)} %get-tuple-element.48.norm), channel_id=1, source_target_pairs={{0,2},{1,3},{2,0},{3,1},{4,6},{5,7},{6,4},{7,5},{8,10},{9,11},{10,... | collective-permute-start | bytes 49160 | tf_op jit(solution)/shard_map/ppermute | solution.py:512
  37.8 5.3 %copy-start.2 = (f32[512,256]{1,0:T(8,128)S(1)}, f32[512,256]{1,0:T(8,128)}, u32[]{:S(2)}) copy-start(f32[512,256]{1,0:T(8,128)} %weight_o.1) | copy-start | bytes 1572868
  37.8 5.3 %copy-start.3 = (f32[512,256]{1,0:T(8,128)S(1)}, f32[512,256]{1,0:T(8,128)}, u32[]{:S(2)}) copy-start(f32[512,256]{1,0:T(8,128)} %momentum_o.1) | copy-start | bytes 1572868
  37.8 5.3 %collective-permute-start.11 = (bf16[32,1280]{1,0:T(8,128)(2,1)S(1)}, bf16[32,1280]{1,0:T(8,128)(2,1)S(1)}, u32[]{:S(2)}, u32[]{:S(2)}) collective-permute-start(bf16[32,1280]{1,0:T(8,128)(2,1)S(1)} %get-tuple-element.50.new.new_near), channel_id=1, source_target_pairs={{0,4},{1,17},{2,6},{3,19},{4,0},{5,21},{6,2},{7,23},{8,12},{9,25},... | collective-permute-start | bytes 245768 | tf_op jit(solution)/shard_map/ppermute | solution.py:503

commit v11 on v10

--- a/solution.py
+++ b/solution.py
@@ -181,6 +181,11 @@
     )(*operands)
 
 
+def store_all(out, column, value):
+    for slot in range(out.shape[0]):
+        out[slot, :, column:column + value.shape[1]] = value
+
+
 def tree(parts):
     while len(parts) > 1:
         parts = [parts[place] + parts[place + 1] for place in range(0, len(parts), 2)]
@@ -188,11 +193,13 @@
 
 
 def total_of(states, columns):
-    return tree([state[:, :columns].astype(f32) for state in states])
+    return tree([states[slot, :, :columns].astype(f32) for slot in range(states.shape[0])])
 
 
 def norm_of(states, columns):
     parts = []
+    if not isinstance(states, list):
+        states = [states.at[slot] for slot in range(states.shape[0])]
     for state in states:
         part = state[:, columns:columns + lanes].astype(f32)
         if state.shape[1] > columns + lanes:
@@ -208,24 +215,23 @@
 
 
 def first_sum_kernel(part, norm, got, state):
-    columns = part.shape[1]
-    state[:, :columns] = (part[...] + got[...].astype(f32)).astype(bf16)
-    state[:, columns:] = norm[...].astype(bf16)
-
-
-def norm_sum_kernel(columns, *refs):
-    *states, out = refs
-    out[:, :columns] = total_of(states, columns).astype(bf16)
-    store_norm(out, columns, norm_of(states, columns))
-
-
-def plain_sum_kernel(*refs):
-    *states, out = refs
-    out[...] = total_of(states, out.shape[1]).astype(bf16)
-
-
-def hat_kernel(size_q, columns, ginv_q, ginv_o, *refs):
-    *states, out = refs
+    store_all(state, 0, (part[...] + got[...].astype(f32)).astype(bf16))
+    store_all(state, part.shape[1], norm[...].astype(bf16))
+
+
+def norm_sum_kernel(columns, states, out):
+    store_all(out, 0, total_of(states, columns).astype(bf16))
+    total = norm_of(states, columns)
+    high = total.astype(bf16)
+    store_all(out, columns, high)
+    store_all(out, columns + lanes, (total - high.astype(f32)).astype(bf16))
+
+
+def plain_sum_kernel(states, out):
+    store_all(out, 0, total_of(states, out.shape[2]).astype(bf16))
+
+
+def hat_kernel(size_q, columns, ginv_q, ginv_o, states, out):
     total = total_of(states, columns)
     highest = lax.Precision.HIGHEST
     out[:, :size_q] = dot(ginv_q[...].T, total[:, :size_q], 1, 0, highest).astype(bf16)
@@ -233,8 +239,7 @@
     store_norm(out, columns, norm_of(states, columns))
 
 
-def mean_kernel(count, norm_count, norm, norm_got, *refs):
-    *states, new, norm_mean = refs
+def mean_kernel(count, norm_count, norm, norm_got, states, new, norm_mean):
     new[...] = (total_of(states, new.shape[1]) / count).astype(bf16)
     norm_mean[...] = (norm[...] + norm_got[...]) / norm_count
 
@@ -311,7 +316,7 @@
 
 
 def near_sum_kernel(near, got, norm, norm_got, state, norm_sum):
-    state[...] = (near[...] + got[...].astype(f32)).astype(bf16)
+    store_all(state, 0, (near[...] + got[...].astype(f32)).astype(bf16))
     norm_sum[...] = norm[...] + norm_got[...]
 
 
@@ -512,12 +517,19 @@
     return lax.ppermute(value, "tensor", [(source, source ^ bit) for source in range(count)])
 
 
-def exchange(state, bits):
-    offsets = [(0, 0)]
-    for even, odd in bits:
-        offsets += [(first | even, second | odd) for first, second in offsets]
-    got = [swap(state, *offset) for offset in offsets[:0:-1]]
-    return [state] + got[::-1]
+def exchange(states, bits):
+    replicas, tensors = lax.axis_size("replica"), lax.axis_size("tensor")
+    groups = []
+    for tensor in range(tensors):
+        offsets = [0]
+        for pair in bits:
+            offsets += [offset | pair[tensor % 2] for offset in offsets]
+        for base in range(replicas):
+            if not base & offsets[-1]:
+                groups.append([(base | offset) * tensors + tensor for offset in offsets])
+    return lax.all_to_all(
+        states, ("replica", "tensor"), 0, 0, axis_index_groups=groups, tiled=True
+    )
 
 
 def rounds_of(count):
@@ -551,36 +563,39 @@
     )
     columns = part.shape[1]
     rounds = rounds_of(replicas)
-    state = small(
-        first_sum_kernel, "first_sum", shaped((rank, columns + lanes), bf16), part, norm, swap_halves(send)
-    )
-    wide = shaped((rank, columns + 2 * lanes), bf16)
-    for bits in rounds[:-1]:
-        state = small(
-            functools.partial(norm_sum_kernel, columns), "norm_sum", wide, *exchange(state, bits)
+    sizes = [1 << len(bits) for bits in rounds] + [1]
+    states = small(
+        first_sum_kernel, "first_sum", shaped((sizes[0], rank, columns + lanes), bf16),
+        part, norm, swap_halves(send),
+    )
+    wide = (rank, columns + 2 * lanes)
+    for bits, size in zip(rounds[:-1], sizes[1:]):
+        states = small(
+            functools.partial(norm_sum_kernel, columns), "norm_sum", shaped((size,) + wide, bf16),
+            exchange(states, bits),
         )
     hat_near = small(
-        functools.partial(hat_kernel, half_q, columns), "hats", wide,
-        ginv_q, ginv_o, *exchange(state, rounds[-1]),
+        functools.partial(hat_kernel, half_q, columns), "hats", shaped(wide, bf16),
+        ginv_q, ginv_o, exchange(states, rounds[-1]),
     )
     hat_far = swap_halves(hat_near)
     part_q, part_o = right_near(hat_near, mat_q_near, mat_o_near)
     send, near, norm = right_far(
         hat_far, mat_q_far, mat_o_far, part_q, part_o, hat_near, norm_rows
     )
-    state, norm = small(
-        near_sum_kernel, "near_sum", (shaped(send.shape, bf16), shaped(norm.shape, f32)),
+    states, norm = small(
+        near_sum_kernel, "near_sum",
+        (shaped((sizes[0],) + send.shape, bf16), shaped(norm.shape, f32)),
         near, swap_halves(send), norm, swap_tensor(norm, 1),
     )
-    for bits in rounds[:-1]:
-        state = small(
-            plain_sum_kernel, "plain_sum", shaped(state.shape, bf16), *exchange(state, bits)
+    for bits, size in zip(rounds[:-1], sizes[1:]):
+        states = small(
+            plain_sum_kernel, "plain_sum", shaped((size,) + send.shape, bf16), exchange(states, bits)
         )
-    states = exchange(state, rounds[-1])
     new_near, norm = small(
         functools.partial(mean_kernel, replicas, replicas * tensors), "mean",
-        (shaped(state.shape, bf16), shaped(norm.shape, f32)),
-        norm, swap_tensor(norm, 2), *states,
+        (shaped(send.shape, bf16), shaped(norm.shape, f32)),
+        norm, swap_tensor(norm, 2), exchange(states, rounds[-1]),
     )
     (
         error_q_new, error_o_new, momentum_q_new, weight_q_new,

time: 45.6 us -> 55.9 us (1.23)
  blocking collectives: 0 us -> 12.9 us
  starting transfers between devices: 19.7 us -> 14.5 us
  local copies, waits for them, and re-layouts: 0.04 us -> 4.41 us
  waiting for transfers between devices: 13.5 us -> 10.4 us
  Pallas kernels: 11.4 us -> 12.4 us
    all_to_all x0 -> x1, blocking collectives: none -> 12.9 us  [exchange(): lax.all_to_all(states, ('replica', 'tensor'), 0, 0, axis_index_groups=gro...]
    ppermute x10 -> x4, starting transfers between devices: 18.1 us -> 8.75 us  [swap(): return lax.ppermute(value, ('replica', 'tensor'), pairs)]
    ppermute x10 -> x4, waiting for transfers between devices: 10 us -> 3.38 us  [swap(): return lax.ppermute(value, ('replica', 'tensor'), pairs)]
    unnamed x14 -> x22, local copies, waits for them, and re-layouts: 0.04 us -> 4.41 us
    all_to_all x0 -> x1, starting transfers between devices: none -> 4.1 us  [exchange(): lax.all_to_all(states, ('replica', 'tensor'), 0, 0, axis_index_groups=gro...]
    all_to_all x0 -> x1, waiting for transfers between devices: none -> 3.56 us  [exchange(): lax.all_to_all(states, ('replica', 'tensor'), 0, 0, axis_index_groups=gro...]
    pallas_call x4, Pallas kernels: 0.42 us -> 1.41 us  [small(): pl.pallas_call(kernel, out_shape=outs, in_specs=[whole] * len(operands),...]
  transfers between devices with their start and end apart: 12 -> 7, of which waited for: 8 -> 5; matrix products, arithmetic and copies ran while one was open for 0% -> 0% of each run, Pallas kernels for 12% -> 10%
where the time goes in v11:
time: 55.9 us; the launch traced here: 55.4 us
  starting transfers between devices  14.5 us (26%)
  blocking collectives  12.9 us (23%)
  Pallas kernels  12.4 us (22%)
  waiting for transfers between devices  10.4 us (19%)
  local copies, waits for them, and re-layouts  4.41 us (8%)
  between operations  0.82 us (1%)
    all_to_all x1, blocking collectives, exchange(): lax.all_to_all(states, ('replica', 'tensor'), 0, 0, axis_index_groups=gro...  12.9 us
    ppermute x4, starting transfers between devices, swap(): return lax.ppermute(value, ('replica', 'tensor'), pairs)  8.75 us
    unnamed x22, local copies, waits for them, and re-layouts  4.41 us
    all_to_all x1, starting transfers between devices, exchange(): lax.all_to_all(states, ('replica', 'tensor'), 0, 0, axis_index_groups=gro...  4.1 us
    all_to_all x1, waiting for transfers between devices, exchange(): lax.all_to_all(states, ('replica', 'tensor'), 0, 0, axis_index_groups=gro...  3.56 us
    ppermute x2, waiting for transfers between devices, swap_tensor(): lax.ppermute(value, 'tensor', [(source, source ^ bit) for source in range...  3.42 us
    ppermute x4, waiting for transfers between devices, swap(): return lax.ppermute(value, ('replica', 'tensor'), pairs)  3.38 us
    pallas_call x1, Pallas kernels, project(): pl.pallas_call(far_kernel, out_shape=mats + (shaped((rank, columns), bf16...  2.91 us
  transfers between devices with their start and end apart: 7, of which 5 were waited for; matrix products, arithmetic and copies ran while one was open for 0% of the time, Pallas kernels for 10%

profile of v11, /device:TPU:0, one launch (start us, length us, event | category | flops | bytes accessed | tf_op | source)
XLA Modules:
  0.0 55.4 jit_solution(7319705651412621471)
XLA Ops:
  0.7 2.9 %project_far.1 = (bf16[1024,512]{1,0:T(8,128)(2,1)S(1)}, bf16[256,2048]{1,0:T(8,128)(2,1)S(1)}, bf16[32,1280]{1,0:T(8,128)(2,1)S(1)}) custom-call(bf16[32,512]{1,0:T(8,128)(2,1)} %bitcast.7, bf16[32,2048]{1,0:T(8,128)(2,1)} %bitcast.5, bf16[2048,512]{1,0:T(8,128)(2,1)} %grad_q.3, bf16[2048,512]{1,0:T(8,128)(2,1)} %error_q.3, bf16[512,2048]{1,0:T(8,128)(2,1)} %grad_o.3, ...), custom_call_target="tpu_custom_call" | custom-call | flops 67108864 | bytes 4194304 | tf_op jit(solution)/shard_map/project_far/pallas_call | solution.py:150
  3.6 3.0 %collective-permute-start = (bf16[32,1280]{1,0:T(8,128)(2,1)S(1)}, bf16[32,1280]{1,0:T(8,128)(2,1)S(1)}, u32[]{:S(2)}, u32[]{:S(2)}) collective-permute-start(bf16[32,1280]{1,0:T(8,128)(2,1)S(1)} %get-tuple-element.39), channel_id=1, source_target_pairs={{0,4},{1,17},{2,6},{3,19},{4,0},{5,21},{6,2},{7,23},{8,12},{9,25},... | collective-permute-start | bytes 245768 | tf_op jit(solution)/shard_map/ppermute | solution.py:508
  6.6 2.9 %project_near.1 = (bf16[1024,512]{1,0:T(8,128)(2,1)S(1)}, bf16[256,2048]{1,0:T(8,128)(2,1)S(1)}, f32[32,1280]{1,0:T(8,128)S(1)}, f32[32,128]{1,0:T(8,128)S(1)}) custom-call(bf16[32,512]{1,0:T(8,128)(2,1)} %bitcast.8, bf16[32,2048]{1,0:T(8,128)(2,1)} %bitcast.6, bf16[2048,512]{1,0:T(8,128)(2,1)} %grad_q.3, bf16[2048,512]{1,0:T(8,128)(2,1)} %error_q.3, ...), custom_call_target="tpu_custom_call" | custom-call | flops 67108864 | bytes 4194304 | tf_op jit(solution)/shard_map/project_near/pallas_call | solution.py:160
  9.6 12.9 %all_to_all.10.states = bf16[4,32,1408]{2,1,0:T(8,128)(2,1)S(1)} all-to-all(bf16[4,32,1408]{2,1,0:T(8,128)(2,1)S(1)} %first_sum.1), channel_id=1, replica_groups={{0,8,16,24},{4,12,20,28},{1,5,9,13},{17,21,25,29},{2,10,18,26},{6,14,22..., dimensions={0} | all-to-all | bytes 720896 | tf_op jit(solution)/shard_map/all_to_all | solution.py:530
  22.5 0.3 hats.1.hat.hat_near
  22.9 1.9 %collective-permute-start.1 = (bf16[32,1536]{1,0:T(8,128)(2,1)S(1)}, bf16[32,1536]{1,0:T(8,128)(2,1)S(1)}, u32[]{:S(2)}, u32[]{:S(2)}) collective-permute-start(bf16[32,1536]{1,0:T(8,128)(2,1)S(1)} %hats.1.hat.hat_near), channel_id=1, source_target_pairs={{0,4},{1,17},{2,6},{3,19},{4,0},{5,21},{6,2},{7,23},{8,12},{9,25},... | collective-permute-start | bytes 294920 | tf_op jit(solution)/shard_map/ppermute | solution.py:508
  24.8 0.5 right_near.1
  25.3 2.3 %collective-permute-done.1.hat.hat_far = bf16[32,1536]{1,0:T(8,128)(2,1)S(1)} collective-permute-done((bf16[32,1536]{1,0:T(8,128)(2,1)S(1)}, bf16[32,1536]{1,0:T(8,128)(2,1)S(1)}, u32[]{:S(2)}, u32[]{:S(2)}) %collective-permute-start.1) | collective-permute-done | bytes 98336 | tf_op jit(solution)/shard_map/ppermute | solution.py:508
  27.9 1.9 %collective-permute-start.2 = (bf16[32,1280]{1,0:T(8,128)(2,1)S(1)}, bf16[32,1280]{1,0:T(8,128)(2,1)S(1)}, u32[]{:S(2)}, u32[]{:S(2)}) collective-permute-start(bf16[32,1280]{1,0:T(8,128)(2,1)S(1)} %right_send.1), channel_id=1, source_target_pairs={{0,4},{1,17},{2,6},{3,19},{4,0},{5,21},{6,2},{7,23},{8,12},{9,25},... | collective-permute-start | bytes 245768 | tf_op jit(solution)/shard_map/ppermute | solution.py:508
  30.2 1.2 %collective-permute-done.3.norm_got = f32[32,128]{1,0:T(8,128)S(1)} collective-permute-done((f32[32,128]{1,0:T(8,128)S(1)}, f32[32,128]{1,0:T(8,128)S(1)}, u32[]{:S(2)}, u32[]{:S(2)}) %collective-permute-start.3) | collective-permute-done | bytes 16416 | tf_op jit(solution)/shard_map/ppermute | solution.py:517
  31.3 1.1 %collective-permute-done.2.got = bf16[32,1280]{1,0:T(8,128)(2,1)S(1)} collective-permute-done((bf16[32,1280]{1,0:T(8,128)(2,1)S(1)}, bf16[32,1280]{1,0:T(8,128)(2,1)S(1)}, u32[]{:S(2)}, u32[]{:S(2)}) %collective-permute-start.2) | collective-permute-done | bytes 81952 | tf_op jit(solution)/shard_map/ppermute | solution.py:508
  32.4 0.7 %copy-done.7 = bf16[4,32,1280]{2,1,0:T(8,128)(2,1)} copy-done((bf16[4,32,1280]{2,1,0:T(8,128)(2,1)}, bf16[4,32,1280]{2,1,0:T(8,128)(2,1)S(1)}, u32[]{:S(2)}) %copy-start.7) | copy-done | bytes 327704
  33.1 4.1 %all-to-all-start.1 = ((bf16[4,32,1280]{2,1,0:T(8,128)(2,1)}), bf16[4,32,1280]{2,1,0:T(8,128)(2,1)}, u32[]{:S(2)}, u32[]{:S(2)}) async-start(bf16[4,32,1280]{2,1,0:T(8,128)(2,1)} %copy-done.7), calls=%async_computation.1 | async-start | bytes 655360 | tf_op jit(solution)/shard_map/all_to_all | solution.py:530
  37.3 1.6 %collective-permute-start.4 = (f32[32,128]{1,0:T(8,128)S(1)}, f32[32,128]{1,0:T(8,128)S(1)}, u32[]{:S(2)}, u32[]{:S(2)}) collective-permute-start(f32[32,128]{1,0:T(8,128)S(1)} %get-tuple-element.48.norm), channel_id=1, source_target_pairs={{0,2},{1,3},{2,0},{3,1},{4,6},{5,7},{6,4},{7,5},{8,10},{9,11},{10,... | collective-permute-start | bytes 49160 | tf_op jit(solution)/shard_map/ppermute | solution.py:517
  38.8 2.2 %collective-permute-done.4.norm_got = f32[32,128]{1,0:T(8,128)S(1)} collective-permute-done((f32[32,128]{1,0:T(8,128)S(1)}, f32[32,128]{1,0:T(8,128)S(1)}, u32[]{:S(2)}, u32[]{:S(2)}) %collective-permute-start.4) | collective-permute-done | bytes 16416 | tf_op jit(solution)/shard_map/ppermute | solution.py:517
  41.1 3.6 %all-to-all-done.1.states = bf16[4,32,1280]{2,1,0:T(8,128)(2,1)} async-done(((bf16[4,32,1280]{2,1,0:T(8,128)(2,1)}), bf16[4,32,1280]{2,1,0:T(8,128)(2,1)}, u32[]{:S(2)}, u32[]{:S(2)}) %all-to-all-start.1) | async-done | bytes 327712 | tf_op jit(solution)/shard_map/all_to_all | solution.py:530
  44.6 1.0 %mean.1 = (bf16[32,1280]{1,0:T(8,128)(2,1)S(1)}, f32[32,128]{1,0:T(8,128)S(1)}) custom-call(f32[32,128]{1,0:T(8,128)S(1)} %get-tuple-element.48.norm, f32[32,128]{1,0:T(8,128)S(1)} %collective-permute-done.4.norm_got, bf16[4,32,1280]{2,1,0:T(8,128)(2,1)} %all-to-all-done.1.states), custom_call_target="tpu_custom_call" | custom-call | tf_op jit(solution)/shard_map/mean/pallas_call | solution.py:174
  45.6 1.9 %collective-permute-start.5 = (bf16[32,1280]{1,0:T(8,128)(2,1)S(1)}, bf16[32,1280]{1,0:T(8,128)(2,1)S(1)}, u32[]{:S(2)}, u32[]{:S(2)}) collective-permute-start(bf16[32,1280]{1,0:T(8,128)(2,1)S(1)} %get-tuple-element.50.new.new_near), channel_id=1, source_target_pairs={{0,4},{1,17},{2,6},{3,19},{4,0},{5,21},{6,2},{7,23},{8,12},{9,25},... | collective-permute-start | bytes 245768 | tf_op jit(solution)/shard_map/ppermute | solution.py:508
  47.6 1.2 %copy-done.1 = bf16[256,2048]{1,0:T(8,128)(2,1)S(1)} copy-done((bf16[256,2048]{1,0:T(8,128)(2,1)S(1)}, bf16[256,2048]{1,0:T(8,128)(2,1)}, u32[]{:S(2)}) %copy-start.1) | copy-done | bytes 1048600
  48.8 1.0 %copy-done.3 = f32[256,512]{1,0:T(8,128)S(1)} copy-done((f32[256,512]{1,0:T(8,128)S(1)}, f32[256,512]{1,0:T(8,128)}, u32[]{:S(2)}) %copy-start.3) | copy-done | bytes 524312
  49.8 1.0 %copy-done.4 = f32[256,512]{1,0:T(8,128)S(1)} copy-done((f32[256,512]{1,0:T(8,128)S(1)}, f32[256,512]{1,0:T(8,128)}, u32[]{:S(2)}) %copy-start.4) | copy-done | bytes 524312
  50.9 1.9 %finish_near.1 = (bf16[2048,512]{1,0:T(8,128)(2,1)}, bf16[512,2048]{1,0:T(8,128)(2,1)}, f32[256,512]{1,0:T(8,128)}, f32[256,512]{1,0:T(8,128)}) custom-call(bf16[32,1536]{1,0:T(8,128)(2,1)S(1)} %hats.1.hat.hat_near, bf16[32,1536]{1,0:T(8,128)(2,1)S(1)} %collective-permute-done.1.hat.hat_far, bf16[1024,512]{1,0:T(8,128)(2,1)S(1)} %get-tuple-element.40.mat_q.mat_q_near, ...), custom_call_target="tpu_custom_call" | custom-call | flops 67108864 | bytes 4194304 | tf_op jit(solution)/shard_map/finish_near/pallas_call | solution.py:474
  52.8 0.4 copy-done.6
  53.1 2.3 %finish_far.1 = (bf16[2048,512]{1,0:T(8,128)(2,1)}, bf16[512,2048]{1,0:T(8,128)(2,1)}, f32[256,512]{1,0:T(8,128)}, f32[256,512]{1,0:T(8,128)}, bf16[32,512]{1,0:...) custom-call(bf16[32,1536]{1,0:T(8,128)(2,1)S(1)} %hats.1.hat.hat_nea, ...), custom_call_target="tpu_custom_call", output_to_operand_aliasing={{0}: (13, {}), {1}: (14, {}), {2}: (15, {}), {3}: (16, {})} | custom-call | flops 67108864 | bytes 4194304 | tf_op jit(solution)/shard_map/finish_far/pallas_call | solution.py:486
  (24 shorter events, 0.7 us)
Async XLA Ops:
  0.6 6.0 %copy-start.8 = (bf16[1,1,4096]{2,1,0:T(2,128)(2,1)S(1)}, bf16[1,1,4096]{2,1,0:T(2,128)(2,1)}, u32[]{:S(2)}) copy-start(bf16[1,1,4096]{2,1,0:T(2,128)(2,1)} %norm_grads.1) | copy-start | bytes 24580
  3.6 19.0 %copy-start.9 = (f32[32,32]{1,0:T(8,128)S(1)}, f32[32,32]{1,0:T(8,128)}, u32[]{:S(2)}) copy-start(f32[32,32]{1,0:T(8,128)} %ginv_q.1) | copy-start | bytes 12292
  3.6 19.0 %copy-start.10 = (f32[32,32]{1,0:T(8,128)S(1)}, f32[32,32]{1,0:T(8,128)}, u32[]{:S(2)}) copy-start(f32[32,32]{1,0:T(8,128)} %ginv_o.1) | copy-start | bytes 12292
  3.6 6.0 %collective-permute-start = (bf16[32,1280]{1,0:T(8,128)(2,1)S(1)}, bf16[32,1280]{1,0:T(8,128)(2,1)S(1)}, u32[]{:S(2)}, u32[]{:S(2)}) collective-permute-start(bf16[32,1280]{1,0:T(8,128)(2,1)S(1)} %get-tuple-element.39), channel_id=1, source_target_pairs={{0,4},{1,17},{2,6},{3,19},{4,0},{5,21},{6,2},{7,23},{8,12},{9,25},... | collective-permute-start | bytes 245768 | tf_op jit(solution)/shard_map/ppermute | solution.py:508
  9.5 18.3 %copy-start = (bf16[256,2048]{1,0:T(8,128)(2,1)}, bf16[256,2048]{1,0:T(8,128)(2,1)S(1)}, u32[]{:S(2)}) copy-start(bf16[256,2048]{1,0:T(8,128)(2,1)S(1)} %get-tuple-element.41.mat_o.mat_o_near) | copy-start | bytes 3145732
  22.9 4.7 %collective-permute-start.1 = (bf16[32,1536]{1,0:T(8,128)(2,1)S(1)}, bf16[32,1536]{1,0:T(8,128)(2,1)S(1)}, u32[]{:S(2)}, u32[]{:S(2)}) collective-permute-start(bf16[32,1536]{1,0:T(8,128)(2,1)S(1)} %hats.1.hat.hat_near), channel_id=1, source_target_pairs={{0,4},{1,17},{2,6},{3,19},{4,0},{5,21},{6,2},{7,23},{8,12},{9,25},... | collective-permute-start | bytes 294920 | tf_op jit(solution)/shard_map/ppermute | solution.py:508
  27.9 4.5 %collective-permute-start.2 = (bf16[32,1280]{1,0:T(8,128)(2,1)S(1)}, bf16[32,1280]{1,0:T(8,128)(2,1)S(1)}, u32[]{:S(2)}, u32[]{:S(2)}) collective-permute-start(bf16[32,1280]{1,0:T(8,128)(2,1)S(1)} %right_send.1), channel_id=1, source_target_pairs={{0,4},{1,17},{2,6},{3,19},{4,0},{5,21},{6,2},{7,23},{8,12},{9,25},... | collective-permute-start | bytes 245768 | tf_op jit(solution)/shard_map/ppermute | solution.py:508
  30.1 1.2 %collective-permute-start.3 = (f32[32,128]{1,0:T(8,128)S(1)}, f32[32,128]{1,0:T(8,128)S(1)}, u32[]{:S(2)}, u32[]{:S(2)}) collective-permute-start(f32[32,128]{1,0:T(8,128)S(1)} %get-tuple-element.47.norm), channel_id=1, source_target_pairs={{0,1},{1,0},{2,3},{3,2},{4,5},{5,4},{6,7},{7,6},{8,9},{9,8},{10,11... | collective-permute-start | bytes 49160 | tf_op jit(solution)/shard_map/ppermute | solution.py:517
  32.4 0.7 %copy-start.7 = (bf16[4,32,1280]{2,1,0:T(8,128)(2,1)}, bf16[4,32,1280]{2,1,0:T(8,128)(2,1)S(1)}, u32[]{:S(2)}) copy-start(bf16[4,32,1280]{2,1,0:T(8,128)(2,1)S(1)} %get-tuple-element.49) | copy-start | bytes 983044
  33.1 11.5 %all-to-all-start.1 = ((bf16[4,32,1280]{2,1,0:T(8,128)(2,1)}), bf16[4,32,1280]{2,1,0:T(8,128)(2,1)}, u32[]{:S(2)}, u32[]{:S(2)}) async-start(bf16[4,32,1280]{2,1,0:T(8,128)(2,1)} %copy-done.7), calls=%async_computation.1 | async-start | bytes 655360 | tf_op jit(solution)/shard_map/all_to_all | solution.py:530
  37.3 3.8 %collective-permute-start.4 = (f32[32,128]{1,0:T(8,128)S(1)}, f32[32,128]{1,0:T(8,128)S(1)}, u32[]{:S(2)}, u32[]{:S(2)}) collective-permute-start(f32[32,128]{1,0:T(8,128)S(1)} %get-tuple-element.48.norm), channel_id=1, source_target_pairs={{0,2},{1,3},{2,0},{3,1},{4,6},{5,7},{6,4},{7,5},{8,10},{9,11},{10,... | collective-permute-start | bytes 49160 | tf_op jit(solution)/shard_map/ppermute | solution.py:517
  45.6 7.1 %collective-permute-start.5 = (bf16[32,1280]{1,0:T(8,128)(2,1)S(1)}, bf16[32,1280]{1,0:T(8,128)(2,1)S(1)}, u32[]{:S(2)}, u32[]{:S(2)}) collective-permute-start(bf16[32,1280]{1,0:T(8,128)(2,1)S(1)} %get-tuple-element.50.new.new_near), channel_id=1, source_target_pairs={{0,4},{1,17},{2,6},{3,19},{4,0},{5,21},{6,2},{7,23},{8,12},{9,25},... | collective-permute-start | bytes 245768 | tf_op jit(solution)/shard_map/ppermute | solution.py:508
  47.6 1.2 %copy-start.1 = (bf16[256,2048]{1,0:T(8,128)(2,1)S(1)}, bf16[256,2048]{1,0:T(8,128)(2,1)}, u32[]{:S(2)}) copy-start(bf16[256,2048]{1,0:T(8,128)(2,1)} %copy-done) | copy-start | bytes 3145732
  48.8 1.0 %copy-start.3 = (f32[256,512]{1,0:T(8,128)S(1)}, f32[256,512]{1,0:T(8,128)}, u32[]{:S(2)}) copy-start(f32[256,512]{1,0:T(8,128)} %weight_q.3) | copy-start | bytes 1572868
  49.8 1.0 %copy-start.4 = (f32[256,512]{1,0:T(8,128)S(1)}, f32[256,512]{1,0:T(8,128)}, u32[]{:S(2)}) copy-start(f32[256,512]{1,0:T(8,128)} %momentum_q.3) | copy-start | bytes 1572868
  50.9 1.9 %copy-start.2 = (bf16[256,2048]{1,0:T(8,128)(2,1)S(1)}, bf16[256,2048]{1,0:T(8,128)(2,1)}, u32[]{:S(2)}) copy-start(bf16[256,2048]{1,0:T(8,128)(2,1)} %copy-done) | copy-start | bytes 3145732
  50.9 1.9 %copy-start.5 = (f32[512,256]{1,0:T(8,128)S(1)}, f32[512,256]{1,0:T(8,128)}, u32[]{:S(2)}) copy-start(f32[512,256]{1,0:T(8,128)} %weight_o.1) | copy-start | bytes 1572868
  50.9 2.3 %copy-start.6 = (f32[512,256]{1,0:T(8,128)S(1)}, f32[512,256]{1,0:T(8,128)}, u32[]{:S(2)}) copy-start(f32[512,256]{1,0:T(8,128)} %momentum_o.1) | copy-start | bytes 1572868

commit v12 on v10

--- a/solution.py
+++ b/solution.py
@@ -319,9 +319,9 @@
     size_q, size_o = mat_q.shape[0], mat_o.shape[0]
     wide_q, wide_o = stage_q.shape[1], stage_o.shape[1]
     copies = []
-    chunk_q, chunk_o = size_q // 2, size_o // 2
+    chunk_q, chunk_o = size_q // 4, size_o // 4
     cols_q, cols_o = half_at(column, wide_q), half_at(column, wide_o)
-    for chunk in range(2):
+    for chunk in range(4):
         part = pl.ds(chunk * chunk_q, chunk_q)
         stage = pl.ds(hat_row * size_q + chunk * chunk_q, chunk_q)
         approx = dot(hat[:, part], new[:, :wide_q], 0, 0)
@@ -362,7 +362,7 @@
     copies = error_columns(
         mine, hat_near, 0, mine, mat_q_near, mat_o_near, new, error_q, error_o, stage_q, stage_o, sems, 0
     ) + error_columns(
-        mine, hat_far, 1, 1 - mine, mat_q_far, mat_o_far, new, error_q, error_o, stage_q, stage_o, sems, 4
+        mine, hat_far, 1, 1 - mine, mat_q_far, mat_o_far, new, error_q, error_o, stage_q, stage_o, sems, 8
     )
     piece = piece_of(hat_near, hat_far, me, count, weight_q.shape[0], pieces)
     copies += query_columns(
@@ -425,7 +425,7 @@
     copies.append(load(weight_o_new, weight_o_h, out_sems.at[4]))
     copies += error_columns(
         1 - mine, hat_far, 1, 1 - mine, mat_q_far, mat_o_far, new_far,
-        error_q, error_o, stage_q, stage_o, sems, 4
+        error_q, error_o, stage_q, stage_o, sems, 8
     )
     piece = piece_of(hat_near, hat_far, me, count, weight_q.shape[0], pieces_q)
     copies += query_columns(
@@ -472,7 +472,7 @@
         in_specs=[whole] * 9,
         out_specs=(in_place,) * 4,
         scratch_shapes=stages + [
-            pieces_q, pltpu.SemaphoreType.DMA((8,)), pltpu.SemaphoreType.DMA((2,))
+            pieces_q, pltpu.SemaphoreType.DMA((16,)), pltpu.SemaphoreType.DMA((2,))
         ],
         compiler_params=params(12),
         cost_estimate=cost(2 * rank * (mat_q.size + mat_o.size), moved),
@@ -484,7 +484,7 @@
         in_specs=[whole] * 13 + [in_place] * 4,
         out_specs=(in_place,) * 9,
         scratch_shapes=stages + [pltpu.VMEM(out.shape, out.dtype) for out in late] + [
-            pieces_q, pieces_o, pltpu.SemaphoreType.DMA((8,)), pltpu.SemaphoreType.DMA((7,))
+            pieces_q, pieces_o, pltpu.SemaphoreType.DMA((16,)), pltpu.SemaphoreType.DMA((7,))
         ],
         input_output_aliases={13: 0, 14: 1, 15: 2, 16: 3},
         compiler_params=params(16),
@@ -516,8 +516,9 @@
     offsets = [(0, 0)]
     for even, odd in bits:
         offsets += [(first | even, second | odd) for first, second in offsets]
-    got = [swap(state, *offset) for offset in offsets[:0:-1]]
-    return [state] + got[::-1]
+    if len(offsets) == 4:
+        offsets = [offsets[place] for place in (0, 1, 3, 2)]
+    return [state] + [swap(state, *offset) for offset in offsets[1:]]
 
 
 def rounds_of(count):

time: 45.6 us -> 44.2 us (0.969)
  starting transfers between devices: 19.7 us -> 17 us
  waiting for transfers between devices: 13.5 us -> 14.7 us
    ppermute x10, starting transfers between devices: 18.1 us -> 15.5 us  [swap(): return lax.ppermute(value, ('replica', 'tensor'), pairs)]
    ppermute x10, waiting for transfers between devices: 10 us -> 11.3 us  [swap(): return lax.ppermute(value, ('replica', 'tensor'), pairs)]
  transfers between devices with their start and end apart: 12 -> 12, of which waited for: 8 -> 10; matrix products, arithmetic and copies ran while one was open for 0% -> 0% of each run, Pallas kernels for 12% -> 13%
where the time goes in v12:
time: 44.2 us; the launch traced here: 44 us
  starting transfers between devices  17 us (38%)
  waiting for transfers between devices  14.7 us (33%)
  Pallas kernels  11.5 us (26%)
  between operations  0.79 us (2%)
    ppermute x10, starting transfers between devices, swap(): return lax.ppermute(value, ('replica', 'tensor'), pairs)  15.5 us
    ppermute x10, waiting for transfers between devices, swap(): return lax.ppermute(value, ('replica', 'tensor'), pairs)  11.3 us
    ppermute x2, waiting for transfers between devices, swap_tensor(): lax.ppermute(value, 'tensor', [(source, source ^ bit) for source in range...  3.41 us
    pallas_call x1, Pallas kernels, project(): pl.pallas_call(far_kernel, out_shape=mats + (shaped((rank, columns), bf16...  2.91 us
    pallas_call x1, Pallas kernels, project(): pl.pallas_call(near_kernel, out_shape=mats + (shaped((rank, columns), f32...  2.9 us
    pallas_call x1, Pallas kernels, finish(): pl.pallas_call(functools.partial(finish_far_kernel, count), out_shape=ear...  2.34 us
    pallas_call x1, Pallas kernels, finish(): pl.pallas_call(functools.partial(finish_near_kernel, count), out_shape=ea...  1.88 us
    ppermute x2, starting transfers between devices, swap_tensor(): lax.ppermute(value, 'tensor', [(source, source ^ bit) for source in range...  1.57 us
  transfers between devices with their start and end apart: 12, of which 10 were waited for; matrix products, arithmetic and copies ran while one was open for 0% of the time, Pallas kernels for 13%

profile of v12, /device:TPU:0, one launch (start us, length us, event | category | flops | bytes accessed | tf_op | source)
XLA Modules:
  0.0 44.0 jit_solution(11795975504791059230)
XLA Ops:
  0.7 2.9 %project_far.1 = (bf16[1024,512]{1,0:T(8,128)(2,1)S(1)}, bf16[256,2048]{1,0:T(8,128)(2,1)S(1)}, bf16[32,1280]{1,0:T(8,128)(2,1)S(1)}) custom-call(bf16[32,512]{1,0:T(8,128)(2,1)} %bitcast.7, bf16[32,2048]{1,0:T(8,128)(2,1)} %bitcast.5, bf16[2048,512]{1,0:T(8,128)(2,1)} %grad_q.3, bf16[2048,512]{1,0:T(8,128)(2,1)} %error_q.3, bf16[512,2048]{1,0:T(8,128)(2,1)} %grad_o.3, ...), custom_call_target="tpu_custom_call" | custom-call | flops 67108864 | bytes 4194304 | tf_op jit(solution)/shard_map/project_far/pallas_call | solution.py:150
  3.6 3.0 %collective-permute-start = (bf16[32,1280]{1,0:T(8,128)(2,1)S(1)}, bf16[32,1280]{1,0:T(8,128)(2,1)S(1)}, u32[]{:S(2)}, u32[]{:S(2)}) collective-permute-start(bf16[32,1280]{1,0:T(8,128)(2,1)S(1)} %get-tuple-element.39), channel_id=1, source_target_pairs={{0,4},{1,17},{2,6},{3,19},{4,0},{5,21},{6,2},{7,23},{8,12},{9,25},... | collective-permute-start | bytes 245768 | tf_op jit(solution)/shard_map/ppermute | solution.py:503
  6.6 2.9 %project_near.1 = (bf16[1024,512]{1,0:T(8,128)(2,1)S(1)}, bf16[256,2048]{1,0:T(8,128)(2,1)S(1)}, f32[32,1280]{1,0:T(8,128)S(1)}, f32[32,128]{1,0:T(8,128)S(1)}) custom-call(bf16[32,512]{1,0:T(8,128)(2,1)} %bitcast.8, bf16[32,2048]{1,0:T(8,128)(2,1)} %bitcast.6, bf16[2048,512]{1,0:T(8,128)(2,1)} %grad_q.3, bf16[2048,512]{1,0:T(8,128)(2,1)} %error_q.3, ...), custom_call_target="tpu_custom_call" | custom-call | flops 67108864 | bytes 4194304 | tf_op jit(solution)/shard_map/project_near/pallas_call | solution.py:160
  9.6 2.7 %collective-permute-start.3 = (bf16[32,1408]{1,0:T(8,128)(2,1)S(1)}, bf16[32,1408]{1,0:T(8,128)(2,1)S(1)}, u32[]{:S(2)}, u32[]{:S(2)}) collective-permute-start(bf16[32,1408]{1,0:T(8,128)(2,1)S(1)} %first_sum.1.refs_0_), channel_id=1, source_target_pairs={{0,16},{1,9},{2,18},{3,11},{4,20},{5,13},{6,22},{7,15},{8,24},{9,1... | collective-permute-start | bytes 270344 | tf_op jit(solution)/shard_map/ppermute | solution.py:503
  12.2 1.4 %collective-permute-start.2 = (bf16[32,1408]{1,0:T(8,128)(2,1)S(1)}, bf16[32,1408]{1,0:T(8,128)(2,1)S(1)}, u32[]{:S(2)}, u32[]{:S(2)}) collective-permute-start(bf16[32,1408]{1,0:T(8,128)(2,1)S(1)} %first_sum.1.refs_0_), channel_id=1, source_target_pairs={{0,24},{1,13},{2,26},{3,15},{4,28},{5,9},{6,30},{7,11},{8,16},{9,5... | collective-permute-start | bytes 270344 | tf_op jit(solution)/shard_map/ppermute | solution.py:503
  13.8 1.3 %collective-permute-done.3.refs_3_ = bf16[32,1408]{1,0:T(8,128)(2,1)S(1)} collective-permute-done((bf16[32,1408]{1,0:T(8,128)(2,1)S(1)}, bf16[32,1408]{1,0:T(8,128)(2,1)S(1)}, u32[]{:S(2)}, u32[]{:S(2)}) %collective-permute-start.3) | collective-permute-done | bytes 90144 | tf_op jit(solution)/shard_map/ppermute | solution.py:503
  15.1 3.8 %collective-permute-done.2.refs_2_ = bf16[32,1408]{1,0:T(8,128)(2,1)S(1)} collective-permute-done((bf16[32,1408]{1,0:T(8,128)(2,1)S(1)}, bf16[32,1408]{1,0:T(8,128)(2,1)S(1)}, u32[]{:S(2)}, u32[]{:S(2)}) %collective-permute-start.2) | collective-permute-done | bytes 90144 | tf_op jit(solution)/shard_map/ppermute | solution.py:503
  19.1 0.3 hats.1.hat.hat_near
  19.4 1.6 %collective-permute-start.4 = (bf16[32,1536]{1,0:T(8,128)(2,1)S(1)}, bf16[32,1536]{1,0:T(8,128)(2,1)S(1)}, u32[]{:S(2)}, u32[]{:S(2)}) collective-permute-start(bf16[32,1536]{1,0:T(8,128)(2,1)S(1)} %hats.1.hat.hat_near), channel_id=1, source_target_pairs={{0,4},{1,17},{2,6},{3,19},{4,0},{5,21},{6,2},{7,23},{8,12},{9,25},... | collective-permute-start | bytes 294920 | tf_op jit(solution)/shard_map/ppermute | solution.py:503
  21.0 0.5 %right_near.1 = (f32[32,512]{1,0:T(8,128)S(1)}, f32[32,2048]{1,0:T(8,128)S(1)}) custom-call(bf16[32,1536]{1,0:T(8,128)(2,1)S(1)} %hats.1.hat.hat_near, bf16[1024,512]{1,0:T(8,128)(2,1)S(1)} %get-tuple-element.40.mat_q.mat_q_near, bf16[256,2048]{1,0:T(8,128)(2,1)S(1)} %get-tuple-element.41.mat_o.mat_o_near), custom_call_target="tpu_custom_call" | custom-call | flops 67108864 | bytes 2097152 | tf_op jit(solution)/shard_map/right_near/pallas_call | solution.py:250
  21.5 2.6 %collective-permute-done.4.hat.hat_far = bf16[32,1536]{1,0:T(8,128)(2,1)S(1)} collective-permute-done((bf16[32,1536]{1,0:T(8,128)(2,1)S(1)}, bf16[32,1536]{1,0:T(8,128)(2,1)S(1)}, u32[]{:S(2)}, u32[]{:S(2)}) %collective-permute-start.4) | collective-permute-done | bytes 98336 | tf_op jit(solution)/shard_map/ppermute | solution.py:503
  24.4 1.6 %collective-permute-start.5 = (bf16[32,1280]{1,0:T(8,128)(2,1)S(1)}, bf16[32,1280]{1,0:T(8,128)(2,1)S(1)}, u32[]{:S(2)}, u32[]{:S(2)}) collective-permute-start(bf16[32,1280]{1,0:T(8,128)(2,1)S(1)} %right_send.1), channel_id=1, source_target_pairs={{0,4},{1,17},{2,6},{3,19},{4,0},{5,21},{6,2},{7,23},{8,12},{9,25},... | collective-permute-start | bytes 245768 | tf_op jit(solution)/shard_map/ppermute | solution.py:503
  26.4 1.2 %collective-permute-done.6.norm_got = f32[32,128]{1,0:T(8,128)S(1)} collective-permute-done((f32[32,128]{1,0:T(8,128)S(1)}, f32[32,128]{1,0:T(8,128)S(1)}, u32[]{:S(2)}, u32[]{:S(2)}) %collective-permute-start.6) | collective-permute-done | bytes 16416 | tf_op jit(solution)/shard_map/ppermute | solution.py:512
  27.5 1.4 %collective-permute-done.5.got = bf16[32,1280]{1,0:T(8,128)(2,1)S(1)} collective-permute-done((bf16[32,1280]{1,0:T(8,128)(2,1)S(1)}, bf16[32,1280]{1,0:T(8,128)(2,1)S(1)}, u32[]{:S(2)}, u32[]{:S(2)}) %collective-permute-start.5) | collective-permute-done | bytes 81952 | tf_op jit(solution)/shard_map/ppermute | solution.py:503
  29.0 1.6 %collective-permute-start.10 = (bf16[32,1280]{1,0:T(8,128)(2,1)S(1)}, bf16[32,1280]{1,0:T(8,128)(2,1)S(1)}, u32[]{:S(2)}, u32[]{:S(2)}) collective-permute-start(bf16[32,1280]{1,0:T(8,128)(2,1)S(1)} %get-tuple-element.49.refs_0_), channel_id=1, source_target_pairs={{0,16},{1,9},{2,18},{3,11},{4,20},{5,13},{6,22},{7,15},{8,24},{9,1... | collective-permute-start | bytes 245768 | tf_op jit(solution)/shard_map/ppermute | solution.py:503
  30.6 1.2 %collective-permute-start.9 = (bf16[32,1280]{1,0:T(8,128)(2,1)S(1)}, bf16[32,1280]{1,0:T(8,128)(2,1)S(1)}, u32[]{:S(2)}, u32[]{:S(2)}) collective-permute-start(bf16[32,1280]{1,0:T(8,128)(2,1)S(1)} %get-tuple-element.49.refs_0_), channel_id=1, source_target_pairs={{0,24},{1,13},{2,26},{3,15},{4,28},{5,9},{6,30},{7,11},{8,16},{9,5... | collective-permute-start | bytes 245768 | tf_op jit(solution)/shard_map/ppermute | solution.py:503
  31.8 0.7 %collective-permute-start.8 = (bf16[32,1280]{1,0:T(8,128)(2,1)S(1)}, bf16[32,1280]{1,0:T(8,128)(2,1)S(1)}, u32[]{:S(2)}, u32[]{:S(2)}) collective-permute-start(bf16[32,1280]{1,0:T(8,128)(2,1)S(1)} %get-tuple-element.49.refs_0_), channel_id=1, source_target_pairs={{0,8},{1,5},{2,10},{3,7},{4,12},{5,1},{6,14},{7,3},{8,0},{9,13},{1... | collective-permute-start | bytes 245768 | tf_op jit(solution)/shard_map/ppermute | solution.py:503
  32.5 1.5 %collective-permute-start.7 = (f32[32,128]{1,0:T(8,128)S(1)}, f32[32,128]{1,0:T(8,128)S(1)}, u32[]{:S(2)}, u32[]{:S(2)}) collective-permute-start(f32[32,128]{1,0:T(8,128)S(1)} %get-tuple-element.48.norm), channel_id=1, source_target_pairs={{0,2},{1,3},{2,0},{3,1},{4,6},{5,7},{6,4},{7,5},{8,10},{9,11},{10,... | collective-permute-start | bytes 49160 | tf_op jit(solution)/shard_map/ppermute | solution.py:512
  34.0 2.2 %collective-permute-done.7.norm_got = f32[32,128]{1,0:T(8,128)S(1)} collective-permute-done((f32[32,128]{1,0:T(8,128)S(1)}, f32[32,128]{1,0:T(8,128)S(1)}, u32[]{:S(2)}, u32[]{:S(2)}) %collective-permute-start.7) | collective-permute-done | bytes 16416 | tf_op jit(solution)/shard_map/ppermute | solution.py:512
  36.3 0.7 %collective-permute-done.9.refs_2_ = bf16[32,1280]{1,0:T(8,128)(2,1)S(1)} collective-permute-done((bf16[32,1280]{1,0:T(8,128)(2,1)S(1)}, bf16[32,1280]{1,0:T(8,128)(2,1)S(1)}, u32[]{:S(2)}, u32[]{:S(2)}) %collective-permute-start.9) | collective-permute-done | bytes 81952 | tf_op jit(solution)/shard_map/ppermute | solution.py:503
  37.2 1.5 %collective-permute-start.11 = (bf16[32,1280]{1,0:T(8,128)(2,1)S(1)}, bf16[32,1280]{1,0:T(8,128)(2,1)S(1)}, u32[]{:S(2)}, u32[]{:S(2)}) collective-permute-start(bf16[32,1280]{1,0:T(8,128)(2,1)S(1)} %get-tuple-element.50.new.new_near), channel_id=1, source_target_pairs={{0,4},{1,17},{2,6},{3,19},{4,0},{5,21},{6,2},{7,23},{8,12},{9,25},... | collective-permute-start | bytes 245768 | tf_op jit(solution)/shard_map/ppermute | solution.py:503
  38.7 1.9 %finish_near.1 = (bf16[2048,512]{1,0:T(8,128)(2,1)}, bf16[512,2048]{1,0:T(8,128)(2,1)}, f32[256,512]{1,0:T(8,128)}, f32[256,512]{1,0:T(8,128)}) custom-call(bf16[32,1536]{1,0:T(8,128)(2,1)S(1)} %hats.1.hat.hat_near, bf16[32,1536]{1,0:T(8,128)(2,1)S(1)} %collective-permute-done.4.hat.hat_far, bf16[1024,512]{1,0:T(8,128)(2,1)S(1)} %get-tuple-element.40.mat_q.mat_q_near, ...), custom_call_target="tpu_custom_call" | custom-call | flops 67108864 | bytes 4194304 | tf_op jit(solution)/shard_map/finish_near/pallas_call | solution.py:469
  40.5 1.1 %collective-permute-done.11.new_far = bf16[32,1280]{1,0:T(8,128)(2,1)S(1)} collective-permute-done((bf16[32,1280]{1,0:T(8,128)(2,1)S(1)}, bf16[32,1280]{1,0:T(8,128)(2,1)S(1)}, u32[]{:S(2)}, u32[]{:S(2)}) %collective-permute-start.11) | collective-permute-done | bytes 81952 | tf_op jit(solution)/shard_map/ppermute | solution.py:503
  41.7 2.3 %finish_far.1 = (bf16[2048,512]{1,0:T(8,128)(2,1)}, bf16[512,2048]{1,0:T(8,128)(2,1)}, f32[256,512]{1,0:T(8,128)}, f32[256,512]{1,0:T(8,128)}, bf16[32,512]{1,0:...) custom-call(bf16[32,1536]{1,0:T(8,128)(2,1)S(1)} %hats.1.hat.hat_nea, ...), custom_call_target="tpu_custom_call", output_to_operand_aliasing={{0}: (13, {}), {1}: (14, {}), {2}: (15, {}), {3}: (16, {})} | custom-call | flops 67108864 | bytes 4194304 | tf_op jit(solution)/shard_map/finish_far/pallas_call | solution.py:481
  (25 shorter events, 1.4 us)
Async XLA Ops:
  0.6 6.0 %copy-start.4 = (bf16[1,1,4096]{2,1,0:T(2,128)(2,1)S(1)}, bf16[1,1,4096]{2,1,0:T(2,128)(2,1)}, u32[]{:S(2)}) copy-start(bf16[1,1,4096]{2,1,0:T(2,128)(2,1)} %norm_grads.1) | copy-start | bytes 24580
  3.6 15.5 %copy-start.5 = (f32[32,32]{1,0:T(8,128)S(1)}, f32[32,32]{1,0:T(8,128)}, u32[]{:S(2)}) copy-start(f32[32,32]{1,0:T(8,128)} %ginv_q.1) | copy-start | bytes 12292
  3.6 15.5 %copy-start.6 = (f32[32,32]{1,0:T(8,128)S(1)}, f32[32,32]{1,0:T(8,128)}, u32[]{:S(2)}) copy-start(f32[32,32]{1,0:T(8,128)} %ginv_o.1) | copy-start | bytes 12292
  3.6 5.9 %collective-permute-start = (bf16[32,1280]{1,0:T(8,128)(2,1)S(1)}, bf16[32,1280]{1,0:T(8,128)(2,1)S(1)}, u32[]{:S(2)}, u32[]{:S(2)}) collective-permute-start(bf16[32,1280]{1,0:T(8,128)(2,1)S(1)} %get-tuple-element.39), channel_id=1, source_target_pairs={{0,4},{1,17},{2,6},{3,19},{4,0},{5,21},{6,2},{7,23},{8,12},{9,25},... | collective-permute-start | bytes 245768 | tf_op jit(solution)/shard_map/ppermute | solution.py:503
  9.6 5.5 %collective-permute-start.3 = (bf16[32,1408]{1,0:T(8,128)(2,1)S(1)}, bf16[32,1408]{1,0:T(8,128)(2,1)S(1)}, u32[]{:S(2)}, u32[]{:S(2)}) collective-permute-start(bf16[32,1408]{1,0:T(8,128)(2,1)S(1)} %first_sum.1.refs_0_), channel_id=1, source_target_pairs={{0,16},{1,9},{2,18},{3,11},{4,20},{5,13},{6,22},{7,15},{8,24},{9,1... | collective-permute-start | bytes 270344 | tf_op jit(solution)/shard_map/ppermute | solution.py:503
  12.2 6.6 %collective-permute-start.2 = (bf16[32,1408]{1,0:T(8,128)(2,1)S(1)}, bf16[32,1408]{1,0:T(8,128)(2,1)S(1)}, u32[]{:S(2)}, u32[]{:S(2)}) collective-permute-start(bf16[32,1408]{1,0:T(8,128)(2,1)S(1)} %first_sum.1.refs_0_), channel_id=1, source_target_pairs={{0,24},{1,13},{2,26},{3,15},{4,28},{5,9},{6,30},{7,11},{8,16},{9,5... | collective-permute-start | bytes 270344 | tf_op jit(solution)/shard_map/ppermute | solution.py:503
  13.6 5.5 %collective-permute-start.1 = (bf16[32,1408]{1,0:T(8,128)(2,1)S(1)}, bf16[32,1408]{1,0:T(8,128)(2,1)S(1)}, u32[]{:S(2)}, u32[]{:S(2)}) collective-permute-start(bf16[32,1408]{1,0:T(8,128)(2,1)S(1)} %first_sum.1.refs_0_), channel_id=1, source_target_pairs={{0,8},{1,5},{2,10},{3,7},{4,12},{5,1},{6,14},{7,3},{8,0},{9,13},{1... | collective-permute-start | bytes 270344 | tf_op jit(solution)/shard_map/ppermute | solution.py:503
  19.4 4.7 %collective-permute-start.4 = (bf16[32,1536]{1,0:T(8,128)(2,1)S(1)}, bf16[32,1536]{1,0:T(8,128)(2,1)S(1)}, u32[]{:S(2)}, u32[]{:S(2)}) collective-permute-start(bf16[32,1536]{1,0:T(8,128)(2,1)S(1)} %hats.1.hat.hat_near), channel_id=1, source_target_pairs={{0,4},{1,17},{2,6},{3,19},{4,0},{5,21},{6,2},{7,23},{8,12},{9,25},... | collective-permute-start | bytes 294920 | tf_op jit(solution)/shard_map/ppermute | solution.py:503
  24.4 14.3 %copy-start = (f32[256,512]{1,0:T(8,128)S(1)}, f32[256,512]{1,0:T(8,128)}, u32[]{:S(2)}) copy-start(f32[256,512]{1,0:T(8,128)} %weight_q.3) | copy-start | bytes 1572868
  24.4 14.2 %copy-start.1 = (f32[256,512]{1,0:T(8,128)S(1)}, f32[256,512]{1,0:T(8,128)}, u32[]{:S(2)}) copy-start(f32[256,512]{1,0:T(8,128)} %momentum_q.3) | copy-start | bytes 1572868
  24.4 4.5 %collective-permute-start.5 = (bf16[32,1280]{1,0:T(8,128)(2,1)S(1)}, bf16[32,1280]{1,0:T(8,128)(2,1)S(1)}, u32[]{:S(2)}, u32[]{:S(2)}) collective-permute-start(bf16[32,1280]{1,0:T(8,128)(2,1)S(1)} %right_send.1), channel_id=1, source_target_pairs={{0,4},{1,17},{2,6},{3,19},{4,0},{5,21},{6,2},{7,23},{8,12},{9,25},... | collective-permute-start | bytes 245768 | tf_op jit(solution)/shard_map/ppermute | solution.py:503
  26.3 1.2 %collective-permute-start.6 = (f32[32,128]{1,0:T(8,128)S(1)}, f32[32,128]{1,0:T(8,128)S(1)}, u32[]{:S(2)}, u32[]{:S(2)}) collective-permute-start(f32[32,128]{1,0:T(8,128)S(1)} %get-tuple-element.47.norm), channel_id=1, source_target_pairs={{0,1},{1,0},{2,3},{3,2},{4,5},{5,4},{6,7},{7,6},{8,9},{9,8},{10,11... | collective-permute-start | bytes 49160 | tf_op jit(solution)/shard_map/ppermute | solution.py:512
  29.0 7.3 %collective-permute-start.10 = (bf16[32,1280]{1,0:T(8,128)(2,1)S(1)}, bf16[32,1280]{1,0:T(8,128)(2,1)S(1)}, u32[]{:S(2)}, u32[]{:S(2)}) collective-permute-start(bf16[32,1280]{1,0:T(8,128)(2,1)S(1)} %get-tuple-element.49.refs_0_), channel_id=1, source_target_pairs={{0,16},{1,9},{2,18},{3,11},{4,20},{5,13},{6,22},{7,15},{8,24},{9,1... | collective-permute-start | bytes 245768 | tf_op jit(solution)/shard_map/ppermute | solution.py:503
  30.6 6.4 %collective-permute-start.9 = (bf16[32,1280]{1,0:T(8,128)(2,1)S(1)}, bf16[32,1280]{1,0:T(8,128)(2,1)S(1)}, u32[]{:S(2)}, u32[]{:S(2)}) collective-permute-start(bf16[32,1280]{1,0:T(8,128)(2,1)S(1)} %get-tuple-element.49.refs_0_), channel_id=1, source_target_pairs={{0,24},{1,13},{2,26},{3,15},{4,28},{5,9},{6,30},{7,11},{8,16},{9,5... | collective-permute-start | bytes 245768 | tf_op jit(solution)/shard_map/ppermute | solution.py:503
  31.8 5.3 %collective-permute-start.8 = (bf16[32,1280]{1,0:T(8,128)(2,1)S(1)}, bf16[32,1280]{1,0:T(8,128)(2,1)S(1)}, u32[]{:S(2)}, u32[]{:S(2)}) collective-permute-start(bf16[32,1280]{1,0:T(8,128)(2,1)S(1)} %get-tuple-element.49.refs_0_), channel_id=1, source_target_pairs={{0,8},{1,5},{2,10},{3,7},{4,12},{5,1},{6,14},{7,3},{8,0},{9,13},{1... | collective-permute-start | bytes 245768 | tf_op jit(solution)/shard_map/ppermute | solution.py:503
  32.5 3.7 %collective-permute-start.7 = (f32[32,128]{1,0:T(8,128)S(1)}, f32[32,128]{1,0:T(8,128)S(1)}, u32[]{:S(2)}, u32[]{:S(2)}) collective-permute-start(f32[32,128]{1,0:T(8,128)S(1)} %get-tuple-element.48.norm), channel_id=1, source_target_pairs={{0,2},{1,3},{2,0},{3,1},{4,6},{5,7},{6,4},{7,5},{8,10},{9,11},{10,... | collective-permute-start | bytes 49160 | tf_op jit(solution)/shard_map/ppermute | solution.py:512
  37.1 4.5 %copy-start.2 = (f32[512,256]{1,0:T(8,128)S(1)}, f32[512,256]{1,0:T(8,128)}, u32[]{:S(2)}) copy-start(f32[512,256]{1,0:T(8,128)} %weight_o.1) | copy-start | bytes 1572868
  37.2 4.5 %copy-start.3 = (f32[512,256]{1,0:T(8,128)S(1)}, f32[512,256]{1,0:T(8,128)}, u32[]{:S(2)}) copy-start(f32[512,256]{1,0:T(8,128)} %momentum_o.1) | copy-start | bytes 1572868
  37.2 4.5 %collective-permute-start.11 = (bf16[32,1280]{1,0:T(8,128)(2,1)S(1)}, bf16[32,1280]{1,0:T(8,128)(2,1)S(1)}, u32[]{:S(2)}, u32[]{:S(2)}) collective-permute-start(bf16[32,1280]{1,0:T(8,128)(2,1)S(1)} %get-tuple-element.50.new.new_near), channel_id=1, source_target_pairs={{0,4},{1,17},{2,6},{3,19},{4,0},{5,21},{6,2},{7,23},{8,12},{9,25},... | collective-permute-start | bytes 245768 | tf_op jit(solution)/shard_map/ppermute | solution.py:503

commit v13 on v12

--- a/solution.py
+++ b/solution.py
@@ -89,13 +89,16 @@
         copy.wait()
     columns_o = fac_o[...].T
     for step, part_q, part_o, copies in jobs:
-        for copy in copies:
+        early = 2 if step == 0 else 4
+        for copy in copies[:early]:
             copy.wait()
         block_q = grad_q_v[part_q] + error_q_v[part_q]
+        mat_q[part_q] = block_q
+        store(step * rows_q, dot(fac_q[...], block_q, 1, 1))
+        for copy in copies[early:]:
+            copy.wait()
         block_o = grad_o_v[part_o] + error_o_v[part_o]
-        mat_q[part_q] = block_q
         mat_o[part_o] = block_o
-        store(step * rows_q, dot(fac_q[...], block_q, 1, 1))
         store(half_q + step * rows_o, dot(block_o, columns_o, 1, 0).T)
 
 

time: 44.2 us -> 44.4 us (level)
  no operation moved by 1% of the time
where the time goes in v13:
time: 44.4 us; the launch traced here: 44.2 us
  starting transfers between devices  16.8 us (38%)
  waiting for transfers between devices  15 us (34%)
  Pallas kernels  11.7 us (26%)
  between operations  0.79 us (2%)
    ppermute x10, starting transfers between devices, swap(): return lax.ppermute(value, ('replica', 'tensor'), pairs)  15.2 us
    ppermute x10, waiting for transfers between devices, swap(): return lax.ppermute(value, ('replica', 'tensor'), pairs)  11.5 us
    ppermute x2, waiting for transfers between devices, swap_tensor(): lax.ppermute(value, 'tensor', [(source, source ^ bit) for source in range...  3.42 us
    pallas_call x1, Pallas kernels, project(): pl.pallas_call(far_kernel, out_shape=mats + (shaped((rank, columns), bf16...  3 us
    pallas_call x1, Pallas kernels, project(): pl.pallas_call(near_kernel, out_shape=mats + (shaped((rank, columns), f32...  2.99 us
    pallas_call x1, Pallas kernels, finish(): pl.pallas_call(functools.partial(finish_far_kernel, count), out_shape=ear...  2.34 us
    pallas_call x1, Pallas kernels, finish(): pl.pallas_call(functools.partial(finish_near_kernel, count), out_shape=ea...  1.88 us
    ppermute x2, starting transfers between devices, swap_tensor(): lax.ppermute(value, 'tensor', [(source, source ^ bit) for source in range...  1.56 us
  transfers between devices with their start and end apart: 12, of which 10 were waited for; matrix products, arithmetic and copies ran while one was open for 0% of the time, Pallas kernels for 13%

profile of v13, /device:TPU:0, one launch (start us, length us, event | category | flops | bytes accessed | tf_op | source)
XLA Modules:
  0.0 44.2 jit_solution(3659529389848054524)
XLA Ops:
  0.7 3.0 %project_far.1 = (bf16[1024,512]{1,0:T(8,128)(2,1)S(1)}, bf16[256,2048]{1,0:T(8,128)(2,1)S(1)}, bf16[32,1280]{1,0:T(8,128)(2,1)S(1)}) custom-call(bf16[32,512]{1,0:T(8,128)(2,1)} %bitcast.7, bf16[32,2048]{1,0:T(8,128)(2,1)} %bitcast.5, bf16[2048,512]{1,0:T(8,128)(2,1)} %grad_q.3, bf16[2048,512]{1,0:T(8,128)(2,1)} %error_q.3, bf16[512,2048]{1,0:T(8,128)(2,1)} %grad_o.3, ...), custom_call_target="tpu_custom_call" | custom-call | flops 67108864 | bytes 4194304 | tf_op jit(solution)/shard_map/project_far/pallas_call | solution.py:153
  3.7 3.0 %collective-permute-start = (bf16[32,1280]{1,0:T(8,128)(2,1)S(1)}, bf16[32,1280]{1,0:T(8,128)(2,1)S(1)}, u32[]{:S(2)}, u32[]{:S(2)}) collective-permute-start(bf16[32,1280]{1,0:T(8,128)(2,1)S(1)} %get-tuple-element.39), channel_id=1, source_target_pairs={{0,4},{1,17},{2,6},{3,19},{4,0},{5,21},{6,2},{7,23},{8,12},{9,25},... | collective-permute-start | bytes 245768 | tf_op jit(solution)/shard_map/ppermute | solution.py:506
  6.7 3.0 %project_near.1 = (bf16[1024,512]{1,0:T(8,128)(2,1)S(1)}, bf16[256,2048]{1,0:T(8,128)(2,1)S(1)}, f32[32,1280]{1,0:T(8,128)S(1)}, f32[32,128]{1,0:T(8,128)S(1)}) custom-call(bf16[32,512]{1,0:T(8,128)(2,1)} %bitcast.8, bf16[32,2048]{1,0:T(8,128)(2,1)} %bitcast.6, bf16[2048,512]{1,0:T(8,128)(2,1)} %grad_q.3, bf16[2048,512]{1,0:T(8,128)(2,1)} %error_q.3, ...), custom_call_target="tpu_custom_call" | custom-call | flops 67108864 | bytes 4194304 | tf_op jit(solution)/shard_map/project_near/pallas_call | solution.py:163
  9.8 2.7 %collective-permute-start.3 = (bf16[32,1408]{1,0:T(8,128)(2,1)S(1)}, bf16[32,1408]{1,0:T(8,128)(2,1)S(1)}, u32[]{:S(2)}, u32[]{:S(2)}) collective-permute-start(bf16[32,1408]{1,0:T(8,128)(2,1)S(1)} %first_sum.1.refs_0_), channel_id=1, source_target_pairs={{0,16},{1,9},{2,18},{3,11},{4,20},{5,13},{6,22},{7,15},{8,24},{9,1... | collective-permute-start | bytes 270344 | tf_op jit(solution)/shard_map/ppermute | solution.py:506
  12.4 1.4 %collective-permute-start.2 = (bf16[32,1408]{1,0:T(8,128)(2,1)S(1)}, bf16[32,1408]{1,0:T(8,128)(2,1)S(1)}, u32[]{:S(2)}, u32[]{:S(2)}) collective-permute-start(bf16[32,1408]{1,0:T(8,128)(2,1)S(1)} %first_sum.1.refs_0_), channel_id=1, source_target_pairs={{0,24},{1,13},{2,26},{3,15},{4,28},{5,9},{6,30},{7,11},{8,16},{9,5... | collective-permute-start | bytes 270344 | tf_op jit(solution)/shard_map/ppermute | solution.py:506
  14.0 1.3 %collective-permute-done.3.refs_3_ = bf16[32,1408]{1,0:T(8,128)(2,1)S(1)} collective-permute-done((bf16[32,1408]{1,0:T(8,128)(2,1)S(1)}, bf16[32,1408]{1,0:T(8,128)(2,1)S(1)}, u32[]{:S(2)}, u32[]{:S(2)}) %collective-permute-start.3) | collective-permute-done | bytes 90144 | tf_op jit(solution)/shard_map/ppermute | solution.py:506
  15.3 3.7 %collective-permute-done.2.refs_2_ = bf16[32,1408]{1,0:T(8,128)(2,1)S(1)} collective-permute-done((bf16[32,1408]{1,0:T(8,128)(2,1)S(1)}, bf16[32,1408]{1,0:T(8,128)(2,1)S(1)}, u32[]{:S(2)}, u32[]{:S(2)}) %collective-permute-start.2) | collective-permute-done | bytes 90144 | tf_op jit(solution)/shard_map/ppermute | solution.py:506
  19.3 0.3 hats.1.hat.hat_near
  19.6 1.5 %collective-permute-start.4 = (bf16[32,1536]{1,0:T(8,128)(2,1)S(1)}, bf16[32,1536]{1,0:T(8,128)(2,1)S(1)}, u32[]{:S(2)}, u32[]{:S(2)}) collective-permute-start(bf16[32,1536]{1,0:T(8,128)(2,1)S(1)} %hats.1.hat.hat_near), channel_id=1, source_target_pairs={{0,4},{1,17},{2,6},{3,19},{4,0},{5,21},{6,2},{7,23},{8,12},{9,25},... | collective-permute-start | bytes 294920 | tf_op jit(solution)/shard_map/ppermute | solution.py:506
  21.1 0.5 %right_near.1 = (f32[32,512]{1,0:T(8,128)S(1)}, f32[32,2048]{1,0:T(8,128)S(1)}) custom-call(bf16[32,1536]{1,0:T(8,128)(2,1)S(1)} %hats.1.hat.hat_near, bf16[1024,512]{1,0:T(8,128)(2,1)S(1)} %get-tuple-element.40.mat_q.mat_q_near, bf16[256,2048]{1,0:T(8,128)(2,1)S(1)} %get-tuple-element.41.mat_o.mat_o_near), custom_call_target="tpu_custom_call" | custom-call | flops 67108864 | bytes 2097152 | tf_op jit(solution)/shard_map/right_near/pallas_call | solution.py:253
  21.5 2.7 %collective-permute-done.4.hat.hat_far = bf16[32,1536]{1,0:T(8,128)(2,1)S(1)} collective-permute-done((bf16[32,1536]{1,0:T(8,128)(2,1)S(1)}, bf16[32,1536]{1,0:T(8,128)(2,1)S(1)}, u32[]{:S(2)}, u32[]{:S(2)}) %collective-permute-start.4) | collective-permute-done | bytes 98336 | tf_op jit(solution)/shard_map/ppermute | solution.py:506
  24.6 1.5 %collective-permute-start.5 = (bf16[32,1280]{1,0:T(8,128)(2,1)S(1)}, bf16[32,1280]{1,0:T(8,128)(2,1)S(1)}, u32[]{:S(2)}, u32[]{:S(2)}) collective-permute-start(bf16[32,1280]{1,0:T(8,128)(2,1)S(1)} %right_send.1), channel_id=1, source_target_pairs={{0,4},{1,17},{2,6},{3,19},{4,0},{5,21},{6,2},{7,23},{8,12},{9,25},... | collective-permute-start | bytes 245768 | tf_op jit(solution)/shard_map/ppermute | solution.py:506
  26.5 1.2 %collective-permute-done.6.norm_got = f32[32,128]{1,0:T(8,128)S(1)} collective-permute-done((f32[32,128]{1,0:T(8,128)S(1)}, f32[32,128]{1,0:T(8,128)S(1)}, u32[]{:S(2)}, u32[]{:S(2)}) %collective-permute-start.6) | collective-permute-done | bytes 16416 | tf_op jit(solution)/shard_map/ppermute | solution.py:515
  27.6 1.5 %collective-permute-done.5.got = bf16[32,1280]{1,0:T(8,128)(2,1)S(1)} collective-permute-done((bf16[32,1280]{1,0:T(8,128)(2,1)S(1)}, bf16[32,1280]{1,0:T(8,128)(2,1)S(1)}, u32[]{:S(2)}, u32[]{:S(2)}) %collective-permute-start.5) | collective-permute-done | bytes 81952 | tf_op jit(solution)/shard_map/ppermute | solution.py:506
  29.1 1.6 %collective-permute-start.10 = (bf16[32,1280]{1,0:T(8,128)(2,1)S(1)}, bf16[32,1280]{1,0:T(8,128)(2,1)S(1)}, u32[]{:S(2)}, u32[]{:S(2)}) collective-permute-start(bf16[32,1280]{1,0:T(8,128)(2,1)S(1)} %get-tuple-element.49.refs_0_), channel_id=1, source_target_pairs={{0,16},{1,9},{2,18},{3,11},{4,20},{5,13},{6,22},{7,15},{8,24},{9,1... | collective-permute-start | bytes 245768 | tf_op jit(solution)/shard_map/ppermute | solution.py:506
  30.7 1.2 %collective-permute-start.9 = (bf16[32,1280]{1,0:T(8,128)(2,1)S(1)}, bf16[32,1280]{1,0:T(8,128)(2,1)S(1)}, u32[]{:S(2)}, u32[]{:S(2)}) collective-permute-start(bf16[32,1280]{1,0:T(8,128)(2,1)S(1)} %get-tuple-element.49.refs_0_), channel_id=1, source_target_pairs={{0,24},{1,13},{2,26},{3,15},{4,28},{5,9},{6,30},{7,11},{8,16},{9,5... | collective-permute-start | bytes 245768 | tf_op jit(solution)/shard_map/ppermute | solution.py:506
  32.0 0.7 %collective-permute-start.8 = (bf16[32,1280]{1,0:T(8,128)(2,1)S(1)}, bf16[32,1280]{1,0:T(8,128)(2,1)S(1)}, u32[]{:S(2)}, u32[]{:S(2)}) collective-permute-start(bf16[32,1280]{1,0:T(8,128)(2,1)S(1)} %get-tuple-element.49.refs_0_), channel_id=1, source_target_pairs={{0,8},{1,5},{2,10},{3,7},{4,12},{5,1},{6,14},{7,3},{8,0},{9,13},{1... | collective-permute-start | bytes 245768 | tf_op jit(solution)/shard_map/ppermute | solution.py:506
  32.7 1.5 %collective-permute-start.7 = (f32[32,128]{1,0:T(8,128)S(1)}, f32[32,128]{1,0:T(8,128)S(1)}, u32[]{:S(2)}, u32[]{:S(2)}) collective-permute-start(f32[32,128]{1,0:T(8,128)S(1)} %get-tuple-element.48.norm), channel_id=1, source_target_pairs={{0,2},{1,3},{2,0},{3,1},{4,6},{5,7},{6,4},{7,5},{8,10},{9,11},{10,... | collective-permute-start | bytes 49160 | tf_op jit(solution)/shard_map/ppermute | solution.py:515
  34.2 2.2 %collective-permute-done.7.norm_got = f32[32,128]{1,0:T(8,128)S(1)} collective-permute-done((f32[32,128]{1,0:T(8,128)S(1)}, f32[32,128]{1,0:T(8,128)S(1)}, u32[]{:S(2)}, u32[]{:S(2)}) %collective-permute-start.7) | collective-permute-done | bytes 16416 | tf_op jit(solution)/shard_map/ppermute | solution.py:515
  36.4 0.7 %collective-permute-done.9.refs_2_ = bf16[32,1280]{1,0:T(8,128)(2,1)S(1)} collective-permute-done((bf16[32,1280]{1,0:T(8,128)(2,1)S(1)}, bf16[32,1280]{1,0:T(8,128)(2,1)S(1)}, u32[]{:S(2)}, u32[]{:S(2)}) %collective-permute-start.9) | collective-permute-done | bytes 81952 | tf_op jit(solution)/shard_map/ppermute | solution.py:506
  37.4 1.4 %collective-permute-start.11 = (bf16[32,1280]{1,0:T(8,128)(2,1)S(1)}, bf16[32,1280]{1,0:T(8,128)(2,1)S(1)}, u32[]{:S(2)}, u32[]{:S(2)}) collective-permute-start(bf16[32,1280]{1,0:T(8,128)(2,1)S(1)} %get-tuple-element.50.new.new_near), channel_id=1, source_target_pairs={{0,4},{1,17},{2,6},{3,19},{4,0},{5,21},{6,2},{7,23},{8,12},{9,25},... | collective-permute-start | bytes 245768 | tf_op jit(solution)/shard_map/ppermute | solution.py:506
  38.8 1.9 %finish_near.1 = (bf16[2048,512]{1,0:T(8,128)(2,1)}, bf16[512,2048]{1,0:T(8,128)(2,1)}, f32[256,512]{1,0:T(8,128)}, f32[256,512]{1,0:T(8,128)}) custom-call(bf16[32,1536]{1,0:T(8,128)(2,1)S(1)} %hats.1.hat.hat_near, bf16[32,1536]{1,0:T(8,128)(2,1)S(1)} %collective-permute-done.4.hat.hat_far, bf16[1024,512]{1,0:T(8,128)(2,1)S(1)} %get-tuple-element.40.mat_q.mat_q_near, ...), custom_call_target="tpu_custom_call" | custom-call | flops 67108864 | bytes 4194304 | tf_op jit(solution)/shard_map/finish_near/pallas_call | solution.py:472
  40.7 1.2 %collective-permute-done.11.new_far = bf16[32,1280]{1,0:T(8,128)(2,1)S(1)} collective-permute-done((bf16[32,1280]{1,0:T(8,128)(2,1)S(1)}, bf16[32,1280]{1,0:T(8,128)(2,1)S(1)}, u32[]{:S(2)}, u32[]{:S(2)}) %collective-permute-start.11) | collective-permute-done | bytes 81952 | tf_op jit(solution)/shard_map/ppermute | solution.py:506
  41.9 2.3 %finish_far.1 = (bf16[2048,512]{1,0:T(8,128)(2,1)}, bf16[512,2048]{1,0:T(8,128)(2,1)}, f32[256,512]{1,0:T(8,128)}, f32[256,512]{1,0:T(8,128)}, bf16[32,512]{1,0:...) custom-call(bf16[32,1536]{1,0:T(8,128)(2,1)S(1)} %hats.1.hat.hat_nea, ...), custom_call_target="tpu_custom_call", output_to_operand_aliasing={{0}: (13, {}), {1}: (14, {}), {2}: (15, {}), {3}: (16, {})} | custom-call | flops 67108864 | bytes 4194304 | tf_op jit(solution)/shard_map/finish_far/pallas_call | solution.py:484
  (25 shorter events, 1.5 us)
Async XLA Ops:
  0.6 6.1 %copy-start.4 = (bf16[1,1,4096]{2,1,0:T(2,128)(2,1)S(1)}, bf16[1,1,4096]{2,1,0:T(2,128)(2,1)}, u32[]{:S(2)}) copy-start(bf16[1,1,4096]{2,1,0:T(2,128)(2,1)} %norm_grads.1) | copy-start | bytes 24580
  3.7 15.6 %copy-start.5 = (f32[32,32]{1,0:T(8,128)S(1)}, f32[32,32]{1,0:T(8,128)}, u32[]{:S(2)}) copy-start(f32[32,32]{1,0:T(8,128)} %ginv_q.1) | copy-start | bytes 12292
  3.7 15.6 %copy-start.6 = (f32[32,32]{1,0:T(8,128)S(1)}, f32[32,32]{1,0:T(8,128)}, u32[]{:S(2)}) copy-start(f32[32,32]{1,0:T(8,128)} %ginv_o.1) | copy-start | bytes 12292
  3.7 6.0 %collective-permute-start = (bf16[32,1280]{1,0:T(8,128)(2,1)S(1)}, bf16[32,1280]{1,0:T(8,128)(2,1)S(1)}, u32[]{:S(2)}, u32[]{:S(2)}) collective-permute-start(bf16[32,1280]{1,0:T(8,128)(2,1)S(1)} %get-tuple-element.39), channel_id=1, source_target_pairs={{0,4},{1,17},{2,6},{3,19},{4,0},{5,21},{6,2},{7,23},{8,12},{9,25},... | collective-permute-start | bytes 245768 | tf_op jit(solution)/shard_map/ppermute | solution.py:506
  9.8 5.5 %collective-permute-start.3 = (bf16[32,1408]{1,0:T(8,128)(2,1)S(1)}, bf16[32,1408]{1,0:T(8,128)(2,1)S(1)}, u32[]{:S(2)}, u32[]{:S(2)}) collective-permute-start(bf16[32,1408]{1,0:T(8,128)(2,1)S(1)} %first_sum.1.refs_0_), channel_id=1, source_target_pairs={{0,16},{1,9},{2,18},{3,11},{4,20},{5,13},{6,22},{7,15},{8,24},{9,1... | collective-permute-start | bytes 270344 | tf_op jit(solution)/shard_map/ppermute | solution.py:506
  12.4 6.6 %collective-permute-start.2 = (bf16[32,1408]{1,0:T(8,128)(2,1)S(1)}, bf16[32,1408]{1,0:T(8,128)(2,1)S(1)}, u32[]{:S(2)}, u32[]{:S(2)}) collective-permute-start(bf16[32,1408]{1,0:T(8,128)(2,1)S(1)} %first_sum.1.refs_0_), channel_id=1, source_target_pairs={{0,24},{1,13},{2,26},{3,15},{4,28},{5,9},{6,30},{7,11},{8,16},{9,5... | collective-permute-start | bytes 270344 | tf_op jit(solution)/shard_map/ppermute | solution.py:506
  13.8 5.5 %collective-permute-start.1 = (bf16[32,1408]{1,0:T(8,128)(2,1)S(1)}, bf16[32,1408]{1,0:T(8,128)(2,1)S(1)}, u32[]{:S(2)}, u32[]{:S(2)}) collective-permute-start(bf16[32,1408]{1,0:T(8,128)(2,1)S(1)} %first_sum.1.refs_0_), channel_id=1, source_target_pairs={{0,8},{1,5},{2,10},{3,7},{4,12},{5,1},{6,14},{7,3},{8,0},{9,13},{1... | collective-permute-start | bytes 270344 | tf_op jit(solution)/shard_map/ppermute | solution.py:506
  19.6 4.7 %collective-permute-start.4 = (bf16[32,1536]{1,0:T(8,128)(2,1)S(1)}, bf16[32,1536]{1,0:T(8,128)(2,1)S(1)}, u32[]{:S(2)}, u32[]{:S(2)}) collective-permute-start(bf16[32,1536]{1,0:T(8,128)(2,1)S(1)} %hats.1.hat.hat_near), channel_id=1, source_target_pairs={{0,4},{1,17},{2,6},{3,19},{4,0},{5,21},{6,2},{7,23},{8,12},{9,25},... | collective-permute-start | bytes 294920 | tf_op jit(solution)/shard_map/ppermute | solution.py:506
  24.6 14.2 %copy-start = (f32[256,512]{1,0:T(8,128)S(1)}, f32[256,512]{1,0:T(8,128)}, u32[]{:S(2)}) copy-start(f32[256,512]{1,0:T(8,128)} %weight_q.3) | copy-start | bytes 1572868
  24.6 14.2 %copy-start.1 = (f32[256,512]{1,0:T(8,128)S(1)}, f32[256,512]{1,0:T(8,128)}, u32[]{:S(2)}) copy-start(f32[256,512]{1,0:T(8,128)} %momentum_q.3) | copy-start | bytes 1572868
  24.6 4.5 %collective-permute-start.5 = (bf16[32,1280]{1,0:T(8,128)(2,1)S(1)}, bf16[32,1280]{1,0:T(8,128)(2,1)S(1)}, u32[]{:S(2)}, u32[]{:S(2)}) collective-permute-start(bf16[32,1280]{1,0:T(8,128)(2,1)S(1)} %right_send.1), channel_id=1, source_target_pairs={{0,4},{1,17},{2,6},{3,19},{4,0},{5,21},{6,2},{7,23},{8,12},{9,25},... | collective-permute-start | bytes 245768 | tf_op jit(solution)/shard_map/ppermute | solution.py:506
  26.4 1.2 %collective-permute-start.6 = (f32[32,128]{1,0:T(8,128)S(1)}, f32[32,128]{1,0:T(8,128)S(1)}, u32[]{:S(2)}, u32[]{:S(2)}) collective-permute-start(f32[32,128]{1,0:T(8,128)S(1)} %get-tuple-element.47.norm), channel_id=1, source_target_pairs={{0,1},{1,0},{2,3},{3,2},{4,5},{5,4},{6,7},{7,6},{8,9},{9,8},{10,11... | collective-permute-start | bytes 49160 | tf_op jit(solution)/shard_map/ppermute | solution.py:515
  29.1 7.3 %collective-permute-start.10 = (bf16[32,1280]{1,0:T(8,128)(2,1)S(1)}, bf16[32,1280]{1,0:T(8,128)(2,1)S(1)}, u32[]{:S(2)}, u32[]{:S(2)}) collective-permute-start(bf16[32,1280]{1,0:T(8,128)(2,1)S(1)} %get-tuple-element.49.refs_0_), channel_id=1, source_target_pairs={{0,16},{1,9},{2,18},{3,11},{4,20},{5,13},{6,22},{7,15},{8,24},{9,1... | collective-permute-start | bytes 245768 | tf_op jit(solution)/shard_map/ppermute | solution.py:506
  30.7 6.4 %collective-permute-start.9 = (bf16[32,1280]{1,0:T(8,128)(2,1)S(1)}, bf16[32,1280]{1,0:T(8,128)(2,1)S(1)}, u32[]{:S(2)}, u32[]{:S(2)}) collective-permute-start(bf16[32,1280]{1,0:T(8,128)(2,1)S(1)} %get-tuple-element.49.refs_0_), channel_id=1, source_target_pairs={{0,24},{1,13},{2,26},{3,15},{4,28},{5,9},{6,30},{7,11},{8,16},{9,5... | collective-permute-start | bytes 245768 | tf_op jit(solution)/shard_map/ppermute | solution.py:506
  32.0 5.3 %collective-permute-start.8 = (bf16[32,1280]{1,0:T(8,128)(2,1)S(1)}, bf16[32,1280]{1,0:T(8,128)(2,1)S(1)}, u32[]{:S(2)}, u32[]{:S(2)}) collective-permute-start(bf16[32,1280]{1,0:T(8,128)(2,1)S(1)} %get-tuple-element.49.refs_0_), channel_id=1, source_target_pairs={{0,8},{1,5},{2,10},{3,7},{4,12},{5,1},{6,14},{7,3},{8,0},{9,13},{1... | collective-permute-start | bytes 245768 | tf_op jit(solution)/shard_map/ppermute | solution.py:506
  32.7 3.7 %collective-permute-start.7 = (f32[32,128]{1,0:T(8,128)S(1)}, f32[32,128]{1,0:T(8,128)S(1)}, u32[]{:S(2)}, u32[]{:S(2)}) collective-permute-start(f32[32,128]{1,0:T(8,128)S(1)} %get-tuple-element.48.norm), channel_id=1, source_target_pairs={{0,2},{1,3},{2,0},{3,1},{4,6},{5,7},{6,4},{7,5},{8,10},{9,11},{10,... | collective-permute-start | bytes 49160 | tf_op jit(solution)/shard_map/ppermute | solution.py:515
  37.3 4.5 %copy-start.2 = (f32[512,256]{1,0:T(8,128)S(1)}, f32[512,256]{1,0:T(8,128)}, u32[]{:S(2)}) copy-start(f32[512,256]{1,0:T(8,128)} %weight_o.1) | copy-start | bytes 1572868
  37.3 4.5 %copy-start.3 = (f32[512,256]{1,0:T(8,128)S(1)}, f32[512,256]{1,0:T(8,128)}, u32[]{:S(2)}) copy-start(f32[512,256]{1,0:T(8,128)} %momentum_o.1) | copy-start | bytes 1572868
  37.4 4.5 %collective-permute-start.11 = (bf16[32,1280]{1,0:T(8,128)(2,1)S(1)}, bf16[32,1280]{1,0:T(8,128)(2,1)S(1)}, u32[]{:S(2)}, u32[]{:S(2)}) collective-permute-start(bf16[32,1280]{1,0:T(8,128)(2,1)S(1)} %get-tuple-element.50.new.new_near), channel_id=1, source_target_pairs={{0,4},{1,17},{2,6},{3,19},{4,0},{5,21},{6,2},{7,23},{8,12},{9,25},... | collective-permute-start | bytes 245768 | tf_op jit(solution)/shard_map/ppermute | solution.py:506
